TPU v7x, 32 devices: a whole 2x2x4 slice. The times are simulated.
32 devices in a mesh: rows: 8 (over y, x, core), chan: 4 (over z).
Axes of the slice: x: 2, y: 2, z: 4, core: 2. Of those that a mesh axis runs over, the one named last changes fastest.
Arguments:
- pixels: float32 [64, 2, 64, 512], P('rows', None, None, 'chan')
- cotangent: bfloat16 [64, 2, 64, 512], P('rows', None, None, 'chan'), may hold values from -6 to 6
- loss_weight: float32 [2], replicated, may hold values from 0.5 to 2
- timesteps: int32 [2], replicated, may hold values from 0 to 999
- clip_embed: float32 [2, 2048], replicated, may hold values from -6 to 6
- context: bfloat16 [2, 81, 2048], replicated, may hold values from -6 to 6
- text_len: int32 [2], replicated, may hold values from 1 to 77
- conv_first: float32 [9, 512, 512], P(None, 'rows', 'chan'), may hold values from -0.09375 to 0.09375
- conv_first_moment: float32 [9, 512, 512], P(None, 'rows', 'chan')
- conv_first_square: float32 [9, 512, 512], P(None, 'rows', 'chan'), as said below
- conv_second: float32 [9, 512, 512], P(None, 'rows', 'chan'), may hold values from -0.09375 to 0.09375
- conv_second_moment: float32 [9, 512, 512], P(None, 'rows', 'chan')
- conv_second_square: float32 [9, 512, 512], P(None, 'rows', 'chan')
- qkv_weight: float32 [512, 3, 512], P('rows', None, 'chan'), may hold values from -0.25 to 0.25
- qkv_weight_moment: float32 [512, 3, 512], P('rows', None, 'chan')
- qkv_weight_square: float32 [512, 3, 512], P('rows', None, 'chan')
- out_weight: float32 [512, 512], P('rows', 'chan'), may hold values from -4 to 4
- out_weight_moment: float32 [512, 512], P('rows', 'chan')
- out_weight_square: float32 [512, 512], P('rows', 'chan')
- embed_weight: float32 [2048, 2, 512], P('rows', None, 'chan'), may hold values from -0.0625 to 0.0625
- embed_weight_moment: float32 [2048, 2, 512], P('rows', None, 'chan')
- embed_weight_square: float32 [2048, 2, 512], P('rows', None, 'chan')
- context_weight: float32 [2048, 2, 512], P('rows', None, 'chan'), may hold values from -0.125 to 0.125
- context_weight_moment: float32 [2048, 2, 512], P('rows', None, 'chan')
- context_weight_square: float32 [2048, 2, 512], P('rows', None, 'chan')
- vectors: float32 [14, 512], P(None, 'chan')
- vectors_moment: float32 [14, 512], P(None, 'chan')
- vectors_square: float32 [14, 512], P(None, 'chan')
Outputs:
- activations: bfloat16 [64, 2, 64, 512], P('rows', None, None, 'chan')
- pixel_grad: float32 [64, 2, 64, 512], P('rows', None, None, 'chan')
- grad_norm: float32 [], replicated
- conv_first_new: float32 [9, 512, 512], P(None, 'rows', 'chan')
- conv_first_moment_new: float32 [9, 512, 512], P(None, 'rows', 'chan')
- conv_first_square_new: float32 [9, 512, 512], P(None, 'rows', 'chan')
- conv_first_low: bfloat16 [9, 512, 512], P(None, 'rows', 'chan')
- conv_second_new: float32 [9, 512, 512], P(None, 'rows', 'chan')
- conv_second_moment_new: float32 [9, 512, 512], P(None, 'rows', 'chan')
- conv_second_square_new: float32 [9, 512, 512], P(None, 'rows', 'chan')
- conv_second_low: bfloat16 [9, 512, 512], P(None, 'rows', 'chan')
- qkv_weight_new: float32 [512, 3, 512], P('rows', None, 'chan')
- qkv_weight_moment_new: float32 [512, 3, 512], P('rows', None, 'chan')
- qkv_weight_square_new: float32 [512, 3, 512], P('rows', None, 'chan')
- qkv_weight_low: bfloat16 [512, 3, 512], P('rows', None, 'chan')
- out_weight_new: float32 [512, 512], P('rows', 'chan')
- out_weight_moment_new: float32 [512, 512], P('rows', 'chan')
- out_weight_square_new: float32 [512, 512], P('rows', 'chan')
- out_weight_low: bfloat16 [512, 512], P('rows', 'chan')
- embed_weight_new: float32 [2048, 2, 512], P('rows', None, 'chan')
- embed_weight_moment_new: float32 [2048, 2, 512], P('rows', None, 'chan')
- embed_weight_square_new: float32 [2048, 2, 512], P('rows', None, 'chan')
- embed_weight_low: bfloat16 [2048, 2, 512], P('rows', None, 'chan')
- context_weight_new: float32 [2048, 2, 512], P('rows', None, 'chan')
- context_weight_moment_new: float32 [2048, 2, 512], P('rows', None, 'chan')
- context_weight_square_new: float32 [2048, 2, 512], P('rows', None, 'chan')
- context_weight_low: bfloat16 [2048, 2, 512], P('rows', None, 'chan')
- vectors_new: float32 [14, 512], P(None, 'chan')
- vectors_moment_new: float32 [14, 512], P(None, 'chan')
- vectors_square_new: float32 [14, 512], P(None, 'chan')
Inputs may be any that keep to these rules, and one draw needn't show every extreme that they name: `conv_first_square`: second moments are positive.
All inputs are finite; a program needn't handle non-finite values.
Results may differ from a plain program's by a relative error of at most 0.018.
The roundings to bfloat16 on the way count: a program that leaves them out, or rounds other values in their place, can miss the bound.
Values may be sent and summed in bfloat16 or wider, within the bound.
No kernel may reach another device: no remote copies, remote signals or barrier semaphores. Data moves between devices by JAX's collectives and lax.ppermute only.
A program may use at most 384 MiB of HBM per device.

v0:
```python
import math

import jax
import jax.numpy as jnp
from jax import lax
from jax.sharding import PartitionSpec as P

C = 512
GROUPS = 32
HEAD_DIM = 64
EMB = 2048
DCTX = 2048
IMG_H = 64
IMG_W = 64
CLIP_TOK = 4
STEP = 10
CTX = 81


highest = lax.Precision.HIGHEST
clip_limit = 1.0


def extended(x, sides, width):
    for axis, dim in sides:
        size, length = (lax.axis_size(axis), x.shape[dim])
        up = [(i, (i + 1) % size) for i in range(size - 1)]
        down = [(j, i) for i, j in up]
        last = lax.slice_in_dim(x, length - width, length, axis=dim)
        initial = lax.slice_in_dim(x, 0, width, axis=dim)
        before = lax.ppermute(last, axis, up)
        after = lax.ppermute(initial, axis, down)
        x = jnp.concatenate([before, x, after], axis=dim)
    return x


def to_heads(values):
    local_rows, images, image_width, channels = values.shape
    split_heads = values.reshape(local_rows, images, image_width, channels // HEAD_DIM, HEAD_DIM)
    return jnp.transpose(split_heads, (1, 3, 0, 2, 4)).reshape(
        images, channels // HEAD_DIM, local_rows * image_width, HEAD_DIM
    )


def from_heads(values, local_rows, image_width):
    images, heads_here, tokens, head_size = values.shape
    split_heads = values.reshape(images, heads_here, local_rows, image_width, head_size)
    return jnp.transpose(split_heads, (2, 0, 3, 1, 4)).reshape(
        local_rows, images, image_width, heads_here * head_size
    )


def context_heads(values):
    images, positions, channels = values.shape
    return jnp.transpose(
        values.reshape(images, positions, channels // HEAD_DIM, HEAD_DIM), (0, 2, 1, 3)
    )


def context_flat(values):
    images, heads_here, positions, head_size = values.shape
    return jnp.transpose(values, (0, 2, 1, 3)).reshape(images, positions, heads_here * head_size)


def group_totals(left_side, right_side, groups_here):
    local_rows, images, image_width, channels = left_side.shape
    group_shape = (local_rows, images, image_width, groups_here, channels // groups_here)
    left_grouped = left_side.reshape(group_shape)
    right_grouped = right_side.reshape(group_shape)
    return lax.psum(
        (
            jnp.sum(left_grouped, axis=(0, 2, 4)),
            jnp.sum(left_grouped * right_grouped, axis=(0, 2, 4)),
        ),
        "rows",
    )


def spread_groups(statistic, channels):
    return jnp.repeat(statistic, channels // statistic.shape[1], axis=1)[None, :, None, :]


def normalize(values, gain, offset, groups_here, group_count):
    total_one, total_two = group_totals(values, values, groups_here)
    average = total_one / group_count
    inverse = lax.rsqrt(total_two / group_count - average * average + 1e-05)
    channels = values.shape[3]
    centered = (values - spread_groups(average, channels)) * spread_groups(inverse, channels)
    return (centered, inverse, centered * gain + offset)


def normalize_back(gradient, centered, inverse, gain, groups_here, group_count):
    scaled = gradient * gain
    total_one, crossed = group_totals(scaled, centered, groups_here)
    channels = gradient.shape[3]
    result = spread_groups(inverse, channels) * (
        scaled
        - spread_groups(total_one / group_count, channels)
        - centered * spread_groups(crossed / group_count, channels)
    )
    return (result, jnp.sum(gradient * centered, axis=(0, 1, 2)), jnp.sum(gradient, axis=(0, 1, 2)))


def silu_slope(values):
    sigmoid = jax.nn.sigmoid(values)
    return sigmoid * (1.0 + values * (1.0 - sigmoid))


def with_rims(values):
    return extended(values, (("rows", 0),), 1)


def all_channels(values):
    return lax.all_gather(values, "chan", axis=3, tiled=True)


def channel_total(partial_value):
    return lax.psum_scatter(partial_value, "chan", scatter_dimension=3, tiled=True)


def gather_keys(keys_low, values_low):
    return (
        lax.all_gather(keys_low, "rows", axis=0, tiled=True),
        lax.all_gather(values_low, "rows", axis=0, tiled=True),
    )


def split_blocks(pair):
    rows_each = min(8, IMG_H)
    return tuple(
        (
            member.reshape((member.shape[0] // rows_each, rows_each) + member.shape[1:])
            for member in pair
        )
    )


def tap_stack(padded, local_rows, image_width, flipped):
    wide = jnp.pad(padded, ((0, 0), (0, 0), (1, 1), (0, 0)))
    pieces = []
    for tap_row in range(3):
        for tap_col in range(3):
            row_start = 2 - tap_row if flipped else tap_row
            col_start = 2 - tap_col if flipped else tap_col
            pieces.append(
                wide[row_start : row_start + local_rows, :, col_start : col_start + image_width, :]
            )
    return jnp.concatenate(pieces, axis=3)


def conv_forward(gathered, kernel, local_rows, image_width):
    patches = tap_stack(gathered, local_rows, image_width, False)
    result = jnp.dot(
        patches.reshape(-1, patches.shape[3]),
        kernel.reshape(-1, kernel.shape[2]),
        preferred_element_type=jnp.float32,
    )
    return result.reshape(local_rows, gathered.shape[1], image_width, kernel.shape[2])


def conv_backward(grad_low, kernel, gathered, local_rows, image_width):
    patches = tap_stack(gathered, local_rows, image_width, False)
    kernel_grad = jnp.einsum(
        "ti,to->io",
        patches.reshape(-1, patches.shape[3]),
        grad_low.reshape(-1, grad_low.shape[3]),
        preferred_element_type=jnp.float32,
    ).reshape(kernel.shape)
    flipped = tap_stack(with_rims(grad_low), local_rows, image_width, True)
    turned = jnp.transpose(kernel, (0, 2, 1)).reshape(-1, kernel.shape[1])
    partial_value = jnp.dot(
        flipped.reshape(-1, flipped.shape[3]), turned, preferred_element_type=jnp.float32
    )
    return (
        kernel_grad,
        channel_total(
            partial_value.reshape(local_rows, grad_low.shape[1], image_width, kernel.shape[1])
        ),
    )


def fold_keys(carry_state, pieces, query_heads):
    peak_score, weight_sum, accumulated = carry_state
    key_heads = to_heads(pieces[0])
    value_heads = to_heads(pieces[1])
    scores = (
        jnp.einsum("bhqd,bhkd->bhqk", query_heads, key_heads, preferred_element_type=jnp.float32)
        * 0.125
    )
    new_peak = jnp.maximum(peak_score, jnp.max(scores, axis=3))
    factor = jnp.exp(peak_score - new_peak)
    weights = jnp.exp(scores - new_peak[..., None])
    weight_sum = weight_sum * factor + jnp.sum(weights, axis=3)
    accumulated = accumulated * factor[..., None] + jnp.einsum(
        "bhqk,bhkd->bhqd", weights, value_heads.astype(jnp.float32), precision=highest
    )
    return (new_peak, weight_sum, accumulated)


def score_parts(query_heads, grad_heads, key_heads, value_heads, log_total, row_delta):
    scores = (
        jnp.einsum("bhqd,bhkd->bhqk", query_heads, key_heads, preferred_element_type=jnp.float32)
        * 0.125
    )
    probs = jnp.exp(scores - log_total[..., None])
    dprob = jnp.einsum(
        "bhqd,bhkd->bhqk", grad_heads, value_heads, preferred_element_type=jnp.float32
    )
    dscore = (probs * (dprob - row_delta[..., None])).astype(jnp.bfloat16)
    return (probs, dscore)


def key_block(carry_grad, pieces, query_heads, grad_heads, grad_wide, log_total, row_delta):
    key_heads = to_heads(pieces[0])
    value_heads = to_heads(pieces[1])
    block_rows = pieces[0].shape[0]
    image_width = pieces[0].shape[2]
    probs, dscore = score_parts(
        query_heads, grad_heads, key_heads, value_heads, log_total, row_delta
    )
    carry_grad = carry_grad + jnp.einsum(
        "bhqk,bhkd->bhqd", dscore, key_heads, preferred_element_type=jnp.float32
    )
    key_grad = (
        jnp.einsum("bhqk,bhqd->bhkd", dscore, query_heads, preferred_element_type=jnp.float32)
        * 0.125
    )
    value_grad = jnp.einsum("bhqk,bhqd->bhkd", probs, grad_wide, precision=highest)
    return (
        carry_grad,
        jnp.concatenate(
            (
                from_heads(key_grad, block_rows, image_width),
                from_heads(value_grad, block_rows, image_width),
            ),
            axis=3,
        ),
    )


def adamw(weight, moment, square, gradient, step_rate, weight_decay):
    moment_new = 0.9 * moment + 0.1 * gradient
    square_new = 0.999 * square + 0.001 * gradient * gradient
    corrected = moment_new / (1.0 - 0.9**STEP)
    scaled = square_new / (1.0 - 0.999**STEP)
    weight_new = weight - step_rate * (
        corrected / (jnp.sqrt(scaled) + 1e-08) + weight_decay * weight
    )
    return (weight_new, moment_new, square_new)


def body(
    pixels,
    cotangent,
    loss_weight,
    timesteps,
    clip_embed,
    context,
    text_len,
    conv_first,
    conv_first_moment,
    conv_first_square,
    conv_second,
    conv_second_moment,
    conv_second_square,
    qkv_weight,
    qkv_weight_moment,
    qkv_weight_square,
    out_weight,
    out_weight_moment,
    out_weight_square,
    embed_weight,
    embed_weight_moment,
    embed_weight_square,
    context_weight,
    context_weight_moment,
    context_weight_square,
    vectors,
    vectors_moment,
    vectors_square,
):
    row_count = lax.axis_size("rows")
    local_rows, images, image_width, local_channels = pixels.shape
    groups_here = GROUPS * local_channels // C
    group_count = IMG_H * IMG_W * (C // GROUPS)
    conv_one_low, conv_two_low, qkv_low, out_low, embed_low, context_low = (
        lax.all_gather(conv_first.astype(jnp.bfloat16), "rows", axis=1, tiled=True),
        lax.all_gather(conv_second.astype(jnp.bfloat16), "rows", axis=1, tiled=True),
        lax.all_gather(qkv_weight.astype(jnp.bfloat16), "rows", axis=0, tiled=True),
        lax.all_gather(out_weight.astype(jnp.bfloat16), "rows", axis=0, tiled=True),
        lax.all_gather(embed_weight.astype(jnp.bfloat16), "rows", axis=0, tiled=True),
        lax.all_gather(context_weight.astype(jnp.bfloat16), "rows", axis=0, tiled=True),
    )
    centered_one, inverse_one, normed_one = normalize(
        pixels, vectors[0], vectors[1], groups_here, group_count
    )
    active_one = jax.nn.silu(normed_one).astype(jnp.bfloat16)
    gathered_one = all_channels(with_rims(active_one))
    hidden_one = conv_forward(gathered_one, conv_one_low, local_rows, image_width) + vectors[2]
    half_width = EMB // 2
    frequency = jnp.exp(-math.log(10000.0) * jnp.arange(half_width, dtype=jnp.float32) / half_width)
    phases = timesteps.astype(jnp.float32)[:, None] * frequency[None, :]
    embedding = jax.nn.silu(
        jnp.concatenate((jnp.cos(phases), jnp.sin(phases)), axis=1) + clip_embed
    ).astype(jnp.bfloat16)
    modulation = jnp.einsum("be,esc->bsc", embedding, embed_low, preferred_element_type=jnp.float32)
    scale_rows = modulation[:, 0] + vectors[12]
    shift_rows = modulation[:, 1] + vectors[13]
    centered_two, inverse_two, normed_two = normalize(
        hidden_one, vectors[3], vectors[4], groups_here, group_count
    )
    shaped = normed_two * (1.0 + scale_rows[None, :, None, :]) + shift_rows[None, :, None, :]
    active_two = jax.nn.silu(shaped).astype(jnp.bfloat16)
    gathered_two = all_channels(with_rims(active_two))
    residual = (
        pixels + conv_forward(gathered_two, conv_two_low, local_rows, image_width) + vectors[5]
    )
    centered_three, inverse_three, normed_three = normalize(
        residual, vectors[6], vectors[7], groups_here, group_count
    )
    gathered_three = all_channels(normed_three.astype(jnp.bfloat16))
    projected = jnp.einsum(
        "hbwc,csd->hbwsd", gathered_three, qkv_low, preferred_element_type=jnp.float32
    )
    queries_low = (projected[:, :, :, 0] + vectors[8]).astype(jnp.bfloat16)
    keys_low = projected[:, :, :, 1].astype(jnp.bfloat16)
    values_low = (projected[:, :, :, 2] + vectors[9]).astype(jnp.bfloat16)
    ctx_projected = jnp.einsum(
        "bte,esc->btsc", context, context_low, preferred_element_type=jnp.float32
    )
    ctx_keys = context_heads(ctx_projected[:, :, 0].astype(jnp.bfloat16))
    ctx_values = context_heads((ctx_projected[:, :, 1] + vectors[11]).astype(jnp.bfloat16))
    allowed = jnp.arange(CTX, dtype=jnp.int32)[None, :] < (CLIP_TOK + text_len)[:, None]
    query_heads = to_heads(queries_low)
    ctx_scores = (
        jnp.einsum("bhqd,bhkd->bhqk", query_heads, ctx_keys, preferred_element_type=jnp.float32)
        * 0.125
    )
    ctx_scores = jnp.where(allowed[:, None, None, :], ctx_scores, -1e30)
    ctx_peak = jnp.max(ctx_scores, axis=3)
    ctx_weights = jnp.exp(ctx_scores - ctx_peak[..., None])
    initial = (
        ctx_peak,
        jnp.sum(ctx_weights, axis=3),
        jnp.einsum(
            "bhqk,bhkd->bhqd", ctx_weights, ctx_values.astype(jnp.float32), precision=highest
        ),
    )
    key_full = None
    final_state = fold_keys(
        initial,
        (
            lax.all_gather(keys_low, "rows", axis=0, tiled=True),
            lax.all_gather(values_low, "rows", axis=0, tiled=True),
        ),
        query_heads,
    )
    peak_score, weight_sum, accumulated = final_state
    attended = accumulated / weight_sum[..., None]
    log_total = peak_score + jnp.log(weight_sum)
    gathered_out = all_channels(from_heads(attended, local_rows, image_width).astype(jnp.bfloat16))
    outward = jnp.dot(gathered_out.reshape(-1, C), out_low, preferred_element_type=jnp.float32)
    activations = (
        residual + outward.reshape(local_rows, images, image_width, local_channels) + vectors[10]
    )
    grad_out = cotangent.astype(jnp.float32) * loss_weight[None, :, None, None]
    grad_low = grad_out.astype(jnp.bfloat16)
    out_grad = jnp.einsum(
        "hbwc,hbwd->cd", gathered_out, grad_low, preferred_element_type=jnp.float32
    )
    attended_grad = channel_total(
        jnp.einsum("hbwd,cd->hbwc", grad_low, out_low, preferred_element_type=jnp.float32)
    )
    grad_heads = to_heads(attended_grad.astype(jnp.bfloat16))
    grad_wide = grad_heads.astype(jnp.float32)
    row_delta = jnp.sum(grad_wide * attended, axis=3)
    ctx_probs = jnp.exp(ctx_scores - log_total[..., None])
    ctx_dprob = jnp.einsum(
        "bhqd,bhkd->bhqk", grad_heads, ctx_values, preferred_element_type=jnp.float32
    )
    ctx_dscore = (ctx_probs * (ctx_dprob - row_delta[..., None])).astype(jnp.bfloat16)
    query_accum = jnp.einsum(
        "bhqk,bhkd->bhqd", ctx_dscore, ctx_keys, preferred_element_type=jnp.float32
    )
    ctx_key_grad = (
        jnp.einsum("bhqk,bhqd->bhkd", ctx_dscore, query_heads, preferred_element_type=jnp.float32)
        * 0.125
    )
    ctx_value_grad = jnp.einsum("bhqk,bhqd->bhkd", ctx_probs, grad_wide, precision=highest)
    key_full = gather_keys(keys_low, values_low)

    def back_piece(carry_grad, pieces):
        return key_block(
            carry_grad, pieces, query_heads, grad_heads, grad_wide, log_total, row_delta
        )

    query_accum, key_terms = lax.scan(back_piece, query_accum, split_blocks(key_full))
    key_terms = key_terms.reshape(IMG_H, images, image_width, 2 * local_channels)
    key_sums = lax.psum_scatter(key_terms, "rows", scatter_dimension=0, tiled=True)
    key_low = key_sums[:, :, :, :local_channels].astype(jnp.bfloat16)
    value_low = key_sums[:, :, :, local_channels:].astype(jnp.bfloat16)
    query_low = from_heads(query_accum * 0.125, local_rows, image_width).astype(jnp.bfloat16)
    projected_grad = jnp.stack((query_low, key_low, value_low), axis=3)
    normed_grad = channel_total(
        jnp.einsum("hbwsd,csd->hbwc", projected_grad, qkv_low, preferred_element_type=jnp.float32)
    )
    qkv_grad = jnp.einsum(
        "hbwc,hbwsd->csd", gathered_three, projected_grad, preferred_element_type=jnp.float32
    )
    query_bias = jnp.sum(query_low.astype(jnp.float32), axis=(0, 1, 2))
    value_bias = jnp.sum(value_low.astype(jnp.float32), axis=(0, 1, 2))
    residual_part, gain_three, bias_three = normalize_back(
        normed_grad, centered_three, inverse_three, vectors[6], groups_here, group_count
    )
    residual_grad = grad_out + residual_part
    conv_two_bias = jnp.sum(residual_grad, axis=(0, 1, 2))
    conv_two_grad, active_two_grad = conv_backward(
        residual_grad.astype(jnp.bfloat16), conv_two_low, gathered_two, local_rows, image_width
    )
    shaped_grad = active_two_grad * silu_slope(shaped)
    scale_grad = jnp.sum(shaped_grad * normed_two, axis=(0, 2))
    shift_grad = jnp.sum(shaped_grad, axis=(0, 2))
    normed_two_grad = shaped_grad * (1.0 + scale_rows[None, :, None, :])
    hidden_grad, gain_two, bias_two = normalize_back(
        normed_two_grad, centered_two, inverse_two, vectors[3], groups_here, group_count
    )
    conv_one_bias = jnp.sum(hidden_grad, axis=(0, 1, 2))
    conv_one_grad, active_one_grad = conv_backward(
        hidden_grad.astype(jnp.bfloat16), conv_one_low, gathered_one, local_rows, image_width
    )
    normed_one_grad = active_one_grad * silu_slope(normed_one)
    pixel_part, gain_one, bias_one = normalize_back(
        normed_one_grad, centered_one, inverse_one, vectors[0], groups_here, group_count
    )
    pixel_grad = residual_grad + pixel_part
    embed_grad = jnp.einsum(
        "be,bsc->esc",
        embedding.astype(jnp.float32),
        jnp.stack((scale_grad, shift_grad), axis=1),
        precision=highest,
    )
    zeros_row = jnp.zeros((local_channels,), jnp.float32)
    vector_grad = jnp.stack(
        (
            gain_one,
            bias_one,
            conv_one_bias,
            gain_two,
            bias_two,
            conv_two_bias,
            gain_three,
            bias_three,
            query_bias,
            value_bias,
            jnp.sum(grad_out, axis=(0, 1, 2)),
            zeros_row,
            jnp.sum(scale_grad, axis=0),
            jnp.sum(shift_grad, axis=0),
        )
    )
    ctx_grad = jnp.concatenate((context_flat(ctx_key_grad), context_flat(ctx_value_grad)), axis=2)
    ctx_total, vector_total = lax.psum((ctx_grad, vector_grad), "rows")
    ctx_key_low = ctx_total[:, :, :local_channels].astype(jnp.bfloat16)
    ctx_value_low = ctx_total[:, :, local_channels:].astype(jnp.bfloat16)
    vector_total = vector_total.at[11].set(jnp.sum(ctx_value_low.astype(jnp.float32), axis=(0, 1)))
    row_share = DCTX // row_count
    context_rows = lax.dynamic_slice_in_dim(
        context, lax.axis_index("rows") * row_share, row_share, 2
    )
    context_grad = jnp.einsum(
        "bte,btsc->esc",
        context_rows,
        jnp.stack((ctx_key_low, ctx_value_low), axis=2),
        preferred_element_type=jnp.float32,
    )
    conv_one_sum, conv_two_sum, qkv_sum, out_sum, embed_sum = (
        lax.psum_scatter(conv_one_grad, "rows", scatter_dimension=1, tiled=True),
        lax.psum_scatter(conv_two_grad, "rows", scatter_dimension=1, tiled=True),
        lax.psum_scatter(qkv_grad, "rows", scatter_dimension=0, tiled=True),
        lax.psum_scatter(out_grad, "rows", scatter_dimension=0, tiled=True),
        lax.psum_scatter(embed_grad, "rows", scatter_dimension=0, tiled=True),
    )
    squared_local = jnp.zeros((), jnp.float32)
    for member in (conv_one_sum, conv_two_sum, qkv_sum, out_sum, embed_sum, context_grad):
        squared_local = squared_local + jnp.sum(member * member)
    squared_local = squared_local + jnp.where(
        lax.axis_index("rows") == 0, jnp.sum(vector_total * vector_total), 0.0
    )
    squared = lax.psum(squared_local, ("rows", "chan"))
    grad_norm = jnp.sqrt(squared)
    factor = jnp.minimum(1.0, clip_limit / grad_norm)
    conv_one = adamw(
        conv_first, conv_first_moment, conv_first_square, conv_one_sum * factor, 0.02, 0.01
    )
    conv_two = adamw(
        conv_second, conv_second_moment, conv_second_square, conv_two_sum * factor, 0.02, 0.01
    )
    qkv_new = adamw(qkv_weight, qkv_weight_moment, qkv_weight_square, qkv_sum * factor, 0.08, 0.01)
    out_new = adamw(out_weight, out_weight_moment, out_weight_square, out_sum * factor, 1.0, 0.01)
    embed_new = adamw(
        embed_weight, embed_weight_moment, embed_weight_square, embed_sum * factor, 0.02, 0.01
    )
    context_new = adamw(
        context_weight,
        context_weight_moment,
        context_weight_square,
        context_grad * factor,
        0.04,
        0.01,
    )
    vector_new = adamw(vectors, vectors_moment, vectors_square, vector_total * factor, 1.0, 0.0)
    return (
        activations.astype(jnp.bfloat16),
        pixel_grad,
        grad_norm,
        conv_one[0],
        conv_one[1],
        conv_one[2],
        conv_one[0].astype(jnp.bfloat16),
        conv_two[0],
        conv_two[1],
        conv_two[2],
        conv_two[0].astype(jnp.bfloat16),
        qkv_new[0],
        qkv_new[1],
        qkv_new[2],
        qkv_new[0].astype(jnp.bfloat16),
        out_new[0],
        out_new[1],
        out_new[2],
        out_new[0].astype(jnp.bfloat16),
        embed_new[0],
        embed_new[1],
        embed_new[2],
        embed_new[0].astype(jnp.bfloat16),
        context_new[0],
        context_new[1],
        context_new[2],
        context_new[0].astype(jnp.bfloat16),
        vector_new[0],
        vector_new[1],
        vector_new[2],
    )


def solution(mesh):
    in_specs = (
        P("rows", None, None, "chan"),
        P("rows", None, None, "chan"),
        P(),
        P(),
        P(),
        P(),
        P(),
        P(None, "rows", "chan"),
        P(None, "rows", "chan"),
        P(None, "rows", "chan"),
        P(None, "rows", "chan"),
        P(None, "rows", "chan"),
        P(None, "rows", "chan"),
        P("rows", None, "chan"),
        P("rows", None, "chan"),
        P("rows", None, "chan"),
        P("rows", "chan"),
        P("rows", "chan"),
        P("rows", "chan"),
        P("rows", None, "chan"),
        P("rows", None, "chan"),
        P("rows", None, "chan"),
        P("rows", None, "chan"),
        P("rows", None, "chan"),
        P("rows", None, "chan"),
        P(None, "chan"),
        P(None, "chan"),
        P(None, "chan"),
    )
    out_specs = (
        P("rows", None, None, "chan"),
        P("rows", None, None, "chan"),
        P(),
        P(None, "rows", "chan"),
        P(None, "rows", "chan"),
        P(None, "rows", "chan"),
        P(None, "rows", "chan"),
        P(None, "rows", "chan"),
        P(None, "rows", "chan"),
        P(None, "rows", "chan"),
        P(None, "rows", "chan"),
        P("rows", None, "chan"),
        P("rows", None, "chan"),
        P("rows", None, "chan"),
        P("rows", None, "chan"),
        P("rows", "chan"),
        P("rows", "chan"),
        P("rows", "chan"),
        P("rows", "chan"),
        P("rows", None, "chan"),
        P("rows", None, "chan"),
        P("rows", None, "chan"),
        P("rows", None, "chan"),
        P("rows", None, "chan"),
        P("rows", None, "chan"),
        P("rows", None, "chan"),
        P("rows", None, "chan"),
        P(None, "chan"),
        P(None, "chan"),
        P(None, "chan"),
    )
    return jax.shard_map(body, mesh=mesh, in_specs=in_specs, out_specs=out_specs, check_vma=False)
```

profile of v0, /device:TPU:0, one launch (start us, length us, event | category | flops | bytes accessed | tf_op | source)
XLA Modules:
  0.0 1240.3 jit_solution(17999396603047437280)
XLA Ops:
  10.5 15.2 %all-reduce.9 = (f32[2,8]{1,0:T(2,128)S(1)}, f32[2,8]{1,0:T(2,128)S(1)}) all-reduce(f32[2,8]{1,0:T(2,128)S(1)} %reduce_sum.431, f32[2,8]{1,0:T(2,128)S(1)} %reduce_sum.428), channel_id=1, replica_groups=mesh['rows'=8,'chan'=4] {'rows'}, use_global_device_ids=true, to_apply=%region_5.6 | all-reduce | flops 32 | bytes 256 | tf_op jit(solution)/shard_map/psum | solution.py:70
  38.9 33.8 %all-gather.12.cloned.1.call-done = bf16[10,2,64,512]{3,2,1,0:T(8,128)(2,1)} async-done(((bf16[10,2,64,128]{3,2,1,0:T(8,128)(2,1)}), bf16[10,2,64,512]{3,2,1,0:T(8,128)(2,1)}) %all-gather.12.cloned.1.call-update) | async-done | bytes 1310736 | tf_op jit(solution)/shard_map/all_gather | solution.py:114
  85.8 12.0 all-gather.14.cloned.1.call-done
  97.9 5.6 fusion.87
  103.8 13.1 %all-reduce.8 = (f32[2,8]{1,0:T(2,128)S(1)}, f32[2,8]{1,0:T(2,128)S(1)}) all-reduce(f32[2,8]{1,0:T(2,128)S(1)} %reduce_sum.437, f32[2,8]{1,0:T(2,128)S(1)} %reduce_sum.434), channel_id=1, replica_groups=mesh['rows'=8,'chan'=4] {'rows'}, use_global_device_ids=true, to_apply=%region_11.12 | all-reduce | flops 32 | bytes 256 | tf_op jit(solution)/shard_map/psum | solution.py:70
  123.5 37.7 %all-gather.18.cloned.1.call-done = bf16[10,2,64,512]{3,2,1,0:T(8,128)(2,1)} async-done(((bf16[10,2,64,128]{3,2,1,0:T(8,128)(2,1)}), bf16[10,2,64,512]{3,2,1,0:T(8,128)(2,1)}) %all-gather.18.cloned.1.call-update) | async-done | bytes 1310736 | tf_op jit(solution)/shard_map/all_gather | solution.py:114
  174.3 11.9 all-gather.20.cloned.1.call-done
  186.2 5.6 fusion.86
  192.1 13.1 %all-reduce.7 = (f32[2,8]{1,0:T(2,128)S(1)}, f32[2,8]{1,0:T(2,128)S(1)}) all-reduce(f32[2,8]{1,0:T(2,128)S(1)} %reduce_sum.443, f32[2,8]{1,0:T(2,128)S(1)} %reduce_sum.440), channel_id=1, replica_groups=mesh['rows'=8,'chan'=4] {'rows'}, use_global_device_ids=true, to_apply=%region_17.18 | all-reduce | flops 32 | bytes 256 | tf_op jit(solution)/shard_map/psum | solution.py:70
  207.3 9.3 all_gather.49
  218.5 9.1 all_gather.44
  227.6 9.2 all-gather.22.cloned.1.call-done
  241.2 19.9 %all-gather.24.cloned.1.call-done = bf16[2048,2,128]{2,0,1:T(8,128)(2,1)} async-done(((bf16[256,2,128]{2,0,1:T(8,128)(2,1)}), bf16[2048,2,128]{2,0,1:T(8,128)(2,1)}) %all-gather.24.cloned.1.call-update) | async-done | bytes 1048592 | tf_op jit(solution)/shard_map/all_gather | solution.py:292
  263.1 44.2 %reduce-scatter.11.cloned.1.call-done = f32[8,2,64,128]{3,2,1,0:T(8,128)} async-done(((f32[8,2,64,512]{3,2,1,0:T(8,128)}), f32[8,2,64,128]{3,2,1,0:T(8,128)}) %reduce-scatter.11.cloned.1.call-update) | async-done | bytes 524304 | tf_op jit(solution)/shard_map/reduce_scatter | solution.py:118
  312.4 24.8 %all-gather.30.cloned.1.call-done = bf16[64,2,64,1,128]{4,2,3,1,0:T(8,128)(2,1)} async-done(((bf16[8,2,64,1,128]{4,2,3,1,0:T(8,128)(2,1)}), bf16[64,2,64,1,128]{4,2,3,1,0:T(8,128)(2,1)}) %all-gather.30.cloned.1.call-update) | async-done | bytes 2097168 | tf_op jit(solution)/shard_map/all_gather | solution.py:353
  337.2 7.5 copy.239
  344.7 6.6 reshape.384
  351.3 15.1 %multiply_reduce_fusion = (f32[2,2,512]{2,1,0:T(2,128)S(1)}, f32[2,2,512,4096]{3,2,1,0:T(8,128)}) fusion(bf16[2,2,512,64]{2,3,1,0:T(8,128)(2,1)S(1)} %reshape.382, bf16[2,2,4096,64]{2,3,1,0:T(8,128)(2,1)} %reshape.384), kind=kOutput, calls=%fused_computation.13 | convolution fusion | flops 1090516992 | bytes 35921920 | tf_op jit(solution)/shard_map/bhqd,bhkd->bhqk/dot_general | solution.py:187
  367.6 7.5 copy.240
  375.1 6.6 reshape.386
  381.7 14.0 %fusion.4 = f32[2,2,512]{2,1,0:T(2,128)S(1)} fusion(f32[2,2,512,4096]{3,2,1,0:T(8,128)} %get-tuple-element.399, f32[2,2,512]{2,1,0:T(2,128)S(1)} %max.16), kind=kLoop, calls=%fused_computation.14 | loop fusion | flops 25163776 | bytes 33570816 | tf_op jit(solution)/shard_map/reduce_sum | solution.py:193
  395.7 25.6 %fusion.5 = f32[2,2,512,64]{2,3,1,0:T(8,128)S(1)} fusion(bf16[2,2,4096,64]{2,3,1,0:T(8,128)(2,1)} %reshape.386, f32[2,2,512,4096]{3,2,1,0:T(8,128)} %get-tuple-element.399, f32[2,2,512]{2,1,0:T(2,128)S(1)} %max.16), kind=kOutput, calls=%fused_computation.15 | convolution fusion | flops 6459228160 | bytes 36184064 | tf_op jit(solution)/shard_map/bhqk,bhkd->bhqd/dot_general | solution.py:194
  424.1 237.8 %while.13 = (s32[]{:T(128)}, f32[2,2,512,64]{2,3,1,0:T(8,128)}, f32[8,8,2,64,256]{4,3,2,1,0:T(8,128)}, bf16[8,8,2,64,128]{4,3,2,1,0:T(8,128)(2,1)}, bf16[2,2,512...) while((s32[]{:T(128)}, f32[2,2,512,64]{2,3,1,0:T(8,128)}, ...), condition=%wide.region_25.26_spmd, body=%wide.region_24.25_spmd.sunk | while | flops 1350041600 | bytes 38822624 | solution.py:397
  426.0 2.7 fusion.174
  429.3 3.4 multiply_convert_fusion.6
  435.5 7.8 fusion.175
  459.0 3.4 multiply_convert_fusion.6
  465.2 7.8 fusion.175
  485.5 2.7 fusion.174
  488.8 3.4 multiply_convert_fusion.6
  495.0 7.8 fusion.175
  515.2 2.7 fusion.174
  518.5 3.4 multiply_convert_fusion.6
  524.7 7.8 fusion.175
  544.9 2.7 fusion.174
  548.2 3.4 multiply_convert_fusion.6
  554.4 7.8 fusion.175
  574.6 2.7 fusion.174
  577.9 3.4 multiply_convert_fusion.6
  584.1 7.8 fusion.175
  607.7 3.4 multiply_convert_fusion.6
  613.8 7.8 fusion.175
  637.4 3.4 multiply_convert_fusion.6
  643.6 7.8 fusion.175
  664.8 68.6 %reduce-scatter.13.cloned.1.call-done = f32[8,2,64,256]{3,2,1,0:T(8,128)} async-done(((f32[64,2,64,256]{3,2,1,0:T(8,128)}), f32[8,2,64,256]{3,2,1,0:T(8,128)}) %reduce-scatter.13.cloned.1.call-update) | async-done | bytes 1048592 | tf_op jit(solution)/shard_map/reduce_scatter | solution.py:399
  737.1 43.9 %reduce-scatter.15.cloned.1.call-done = f32[8,2,64,128]{3,2,1,0:T(8,128)} async-done(((f32[8,2,64,512]{3,2,1,0:T(8,128)}), f32[8,2,64,128]{3,2,1,0:T(8,128)}) %reduce-scatter.15.cloned.1.call-update) | async-done | bytes 524304 | tf_op jit(solution)/shard_map/reduce_scatter | solution.py:118
  782.6 13.4 %all-reduce.6 = (f32[2,8]{1,0:T(2,128)S(1)}, f32[2,8]{1,0:T(2,128)S(1)}) all-reduce(f32[2,8]{1,0:T(2,128)S(1)} %reduce_sum.452, f32[2,8]{1,0:T(2,128)S(1)} %reduce_sum.449), channel_id=1, replica_groups=mesh['rows'=8,'chan'=4] {'rows'}, use_global_device_ids=true, to_apply=%region_33.34 | all-reduce | flops 32 | bytes 256 | tf_op jit(solution)/shard_map/psum | solution.py:70
  806.6 3.0 fusion.112
  809.6 26.9 %all-gather.28.cloned.1.call-done = bf16[8,2,64,512]{3,2,1,0:T(8,128)(2,1)} async-done(((bf16[8,2,64,128]{3,2,1,0:T(8,128)(2,1)}), bf16[8,2,64,512]{3,2,1,0:T(8,128)(2,1)}) %all-gather.28.cloned.1.call-update) | async-done | bytes 1048592 | tf_op jit(solution)/shard_map/all_gather | solution.py:114
  839.2 2.7 convolution_bitcast_fusion.1
  841.9 12.8 %copy.201 = bf16[4608,1024]{1,0:T(8,128)(2,1)} copy(bf16[4608,1024]{0,1:T(8,128)(2,1)} %bitcast.78) | data formatting | bytes 18874368 | tf_op jit(solution)/shard_map/ti,to->io/dot_general | solution.py:163
  854.7 7.7 fusion.115
  862.6 18.4 %reduce-scatter.17.cloned.1.call-done = f32[8,2,64,128]{3,2,1,0:T(8,128)} async-done(((f32[8,2,64,512]{3,2,1,0:T(8,128)}), f32[8,2,64,128]{3,2,1,0:T(8,128)}) %reduce-scatter.17.cloned.1.call-update) | async-done | bytes 524304 | tf_op jit(solution)/shard_map/reduce_scatter | solution.py:118
  882.8 13.4 %all-reduce.5 = (f32[2,8]{1,0:T(2,128)S(1)}, f32[2,8]{1,0:T(2,128)S(1)}) all-reduce(f32[2,8]{1,0:T(2,128)S(1)} %reduce_sum.458, f32[2,8]{1,0:T(2,128)S(1)} %reduce_sum.455), channel_id=1, replica_groups=mesh['rows'=8,'chan'=4] {'rows'}, use_global_device_ids=true, to_apply=%region_40.41 | all-reduce | flops 32 | bytes 256 | tf_op jit(solution)/shard_map/psum | solution.py:70
  899.5 12.7 %copy.200 = bf16[4608,1024]{1,0:T(8,128)(2,1)} copy(bf16[4608,1024]{0,1:T(8,128)(2,1)} %bitcast.73) | data formatting | bytes 18874368 | tf_op jit(solution)/shard_map/ti,to->io/dot_general | solution.py:163
  912.2 7.8 fusion.114
  926.0 2.9 fusion.113
  935.4 20.5 %reduce-scatter.25.cloned.1.call-done = f32[64,3,128]{2,0,1:T(8,128)} async-done(((f32[512,3,128]{2,0,1:T(8,128)}), f32[64,3,128]{2,0,1:T(8,128)}) %reduce-scatter.25.cloned.1.call-update) | async-done | bytes 98320 | tf_op jit(solution)/shard_map/reduce_scatter | solution.py:479
  957.4 44.5 %reduce-scatter.23.cloned.1.call-done = f32[9,64,128]{2,1,0:T(8,128)} async-done(((f32[9,512,128]{2,1,0:T(8,128)}), f32[9,64,128]{2,1,0:T(8,128)}) %reduce-scatter.23.cloned.1.call-update) | async-done | bytes 294928 | tf_op jit(solution)/shard_map/reduce_scatter | solution.py:478
  1003.6 42.7 %reduce-scatter.29.cloned.1.call-done = f32[256,2,128]{2,0,1:T(8,128)} async-done(((f32[2048,2,128]{2,0,1:T(8,128)}), f32[256,2,128]{2,0,1:T(8,128)}) %reduce-scatter.29.cloned.1.call-update) | async-done | bytes 262160 | tf_op jit(solution)/shard_map/reduce_scatter | solution.py:481
  1047.9 44.6 %reduce-scatter.21.cloned.1.call-done = f32[9,64,128]{2,1,0:T(8,128)} async-done(((f32[9,512,128]{2,1,0:T(8,128)}), f32[9,64,128]{2,1,0:T(8,128)}) %reduce-scatter.21.cloned.1.call-update) | async-done | bytes 294928 | tf_op jit(solution)/shard_map/reduce_scatter | solution.py:477
  1096.8 41.7 %reduce-scatter.19.cloned.1.call-done = f32[8,2,64,128]{3,2,1,0:T(8,128)} async-done(((f32[8,2,64,512]{3,2,1,0:T(8,128)}), f32[8,2,64,128]{3,2,1,0:T(8,128)}) %reduce-scatter.19.cloned.1.call-update) | async-done | bytes 524304 | tf_op jit(solution)/shard_map/reduce_scatter | solution.py:118
  1141.0 25.9 %all-reduce.11 = (f32[2,8]{1,0:T(2,128)}, f32[2,8]{1,0:T(2,128)}, bf16[2,81,256]{2,1,0:T(8,128)(2,1)S(1)}, f32[14,128]{1,0:T(8,128)S(1)}) all-reduce(f32[2,8]{1,0:T(2,128)S(1)} %reduce_sum.464, f32[2,8]{1,0:T(2,128)S(1)} %reduce_sum.461, f32[2,81,256]{2,1,0:T(8,128)S(1)} %pad_maximum_fusion.9, ...), channel_id=1, replica_groups=mesh['rows'=8,'chan'=4] {'rows'}, use_global_device_ids=true, to_apply=%region_47.48 | all-reduce | flops 43296 | bytes 263424 | tf_op jit(solution)/shard_map/psum | solution.py:70
  1172.9 38.9 %psum.119 = f32[]{:T(128)} all-reduce(f32[]{:T(128)S(6)} %add.442), channel_id=1, replica_groups=mesh['rows'=8,'chan'=4] {'rows','chan'}, use_global_device_ids=true, to_apply=%region_78.79 | all-reduce | flops 1 | bytes 8 | tf_op jit(solution)/shard_map/psum | solution.py:489
  (600 shorter events, 274.2 us)
Async XLA Ops:
  7.2 30.2 %all-gather.16.cloned.1.call-start = ((), (), s32[]{:S(2)}) async-start(), calls=%async_computation.12 | async-start | bytes 1179648 | tf_op jit(solution)/shard_map/all_gather | solution.py:291
  9.0 63.8 %all-gather.12.cloned.1.call-start = ((), (), s32[]{:S(2)}) async-start(), calls=%async_computation.10 | async-start | bytes 1638400 | tf_op jit(solution)/shard_map/all_gather | solution.py:114
  25.9 49.5 %copy-start.54 = (f32[2,128]{1,0:T(2,128)}, f32[2,128]{1,0:T(2,128)S(1)}, u32[]{:S(2)}) copy-start(f32[2,128]{1,0:T(2,128)S(1)} %mul.559) | copy-start | bytes 3076
  26.1 49.4 %copy-start.56 = (f32[2,128]{1,0:T(2,128)}, f32[2,128]{1,0:T(2,128)S(1)}, u32[]{:S(2)}) copy-start(f32[2,128]{1,0:T(2,128)S(1)} %sub.168) | copy-start | bytes 3076
  27.6 47.9 %copy-start.79 = (f32[128]{0:T(128)}, f32[128]{0:T(128)S(1)}, u32[]{:S(2)}) copy-start(f32[128]{0:T(128)S(1)} %get-tuple-element.382) | copy-start | bytes 1540
  27.6 89.7 %copy-start.73 = (f32[128]{0:T(128)}, f32[128]{0:T(128)S(1)}, u32[]{:S(2)}) copy-start(f32[128]{0:T(128)S(1)} %get-tuple-element.379) | copy-start | bytes 1540
  27.6 89.7 %copy-start.75 = (f32[128]{0:T(128)}, f32[128]{0:T(128)S(1)}, u32[]{:S(2)}) copy-start(f32[128]{0:T(128)S(1)} %get-tuple-element.380) | copy-start | bytes 1540
  27.6 178.0 %copy-start.77 = (f32[128]{0:T(128)}, f32[128]{0:T(128)S(1)}, u32[]{:S(2)}) copy-start(f32[128]{0:T(128)S(1)} %get-tuple-element.375) | copy-start | bytes 1540
  28.8 2.6 collective-permute-start
  30.1 3.1 collective-permute-start.1
  34.0 63.8 %all-gather.14.cloned.1.call-start = ((), (), s32[]{:S(2)}) async-start(), calls=%async_computation.11 | async-start | bytes 1327104 | tf_op jit(solution)/shard_map/all_gather | solution.py:287
  34.8 126.4 %all-gather.18.cloned.1.call-start = ((), (), s32[]{:S(2)}) async-start(), calls=%async_computation.13 | async-start | bytes 1638400 | tf_op jit(solution)/shard_map/all_gather | solution.py:114
  35.1 41.4 %copy-start.46 = (f32[2,1024]{1,0:T(2,128)}, f32[2,1024]{1,0:T(2,128)S(1)}, u32[]{:S(2)}) copy-start(f32[2,1024]{1,0:T(2,128)S(1)} %get-tuple-element.384) | copy-start | bytes 24580
  35.1 41.4 %copy-start.48 = (f32[2,1024]{1,0:T(2,128)}, f32[2,1024]{1,0:T(2,128)S(1)}, u32[]{:S(2)}) copy-start(f32[2,1024]{1,0:T(2,128)S(1)} %get-tuple-element.385) | copy-start | bytes 24580
  103.4 60.4 %copy-start.12 = (f32[8,2,64,128]{3,2,1,0:T(8,128)}, f32[8,2,64,128]{3,2,1,0:T(8,128)S(1)}, u32[]{:S(2)}) copy-start(f32[8,2,64,128]{3,2,1,0:T(8,128)S(1)} %get-tuple-element.394) | copy-start | bytes 1572868
  103.8 60.0 %copy-start.62 = (f32[2,128]{1,0:T(2,128)}, f32[2,128]{1,0:T(2,128)S(1)}, u32[]{:S(2)}) copy-start(f32[2,128]{1,0:T(2,128)S(1)} %get-tuple-element.386) | copy-start | bytes 3076
  103.8 60.0 %copy-start.69 = (f32[2,128]{1,0:T(2,128)}, f32[2,128]{1,0:T(2,128)S(1)}, u32[]{:S(2)}) copy-start(f32[2,128]{1,0:T(2,128)S(1)} %get-tuple-element.387) | copy-start | bytes 3076
  117.1 46.7 %copy-start.64 = (f32[2,128]{1,0:T(2,128)}, f32[2,128]{1,0:T(2,128)S(1)}, u32[]{:S(2)}) copy-start(f32[2,128]{1,0:T(2,128)S(1)} %mul.568) | copy-start | bytes 3076
  117.3 46.6 %copy-start.66 = (f32[2,128]{1,0:T(2,128)}, f32[2,128]{1,0:T(2,128)S(1)}, u32[]{:S(2)}) copy-start(f32[2,128]{1,0:T(2,128)S(1)} %sub.172) | copy-start | bytes 3076
  117.5 2.6 collective-permute-start.2
  118.8 3.1 collective-permute-start.3
  122.7 63.4 %all-gather.20.cloned.1.call-start = ((), (), s32[]{:S(2)}) async-start(), calls=%async_computation.14 | async-start | bytes 1327104 | tf_op jit(solution)/shard_map/all_gather | solution.py:288
  123.5 113.3 %all-gather.22.cloned.1.call-start = ((), (), s32[]{:S(2)}) async-start(), calls=%async_computation.15 | async-start | bytes 1310720 | tf_op jit(solution)/shard_map/all_gather | solution.py:114
  206.4 54.7 %all-gather.24.cloned.1.call-start = ((), (), s32[]{:S(2)}) async-start(), calls=%async_computation.16 | async-start | bytes 1179648 | tf_op jit(solution)/shard_map/all_gather | solution.py:292
  207.2 100.1 %reduce-scatter.11.cloned.1.call-start = ((), (), s32[]{:S(2)}) async-start(), calls=%async_computation.19 | async-start | bytes 2621440 | tf_op jit(solution)/shard_map/reduce_scatter | solution.py:118
  218.4 118.8 %all-gather.30.cloned.1.call-start = ((), (), s32[]{:S(2)}) async-start(), calls=%async_computation.29 | async-start | bytes 2359296 | tf_op jit(solution)/shard_map/all_gather | solution.py:353
  239.5 128.1 %all-gather.26.cloned.1.call-start = ((), (), s32[]{:S(2)}) async-start(), calls=%async_computation.17 | async-start | bytes 2359296 | tf_op jit(solution)/shard_map/all_gather | solution.py:354
  240.3 493.0 %reduce-scatter.13.cloned.1.call-start = ((), (), s32[]{:S(2)}) async-start(), calls=%async_computation.20 | async-start | bytes 9437184 | tf_op jit(solution)/shard_map/reduce_scatter | solution.py:399
  312.2 110.4 %copy-start.6 = (f32[2,2,512,81]{2,3,1,0:T(8,128)}, f32[2,2,512,81]{2,3,1,0:T(8,128)S(1)}, u32[]{:S(2)}) copy-start(f32[2,2,512,81]{2,3,1,0:T(8,128)S(1)} %get-tuple-element.397) | copy-start | bytes 1990660
  661.9 119.1 %reduce-scatter.15.cloned.1.call-start = ((), (), s32[]{:S(2)}) async-start(), calls=%async_computation.21 | async-start | bytes 2621440 | tf_op jit(solution)/shard_map/reduce_scatter | solution.py:118
  664.0 70.9 %copy-start.15 = (bf16[512,3,128]{2,0,1:T(8,128)(2,1)S(1)}, bf16[512,3,128]{2,0,1:T(8,128)(2,1)}, u32[]{:S(2)}) copy-start(bf16[512,3,128]{2,0,1:T(8,128)(2,1)} %copy-done.14) | copy-start | bytes 1179652
  734.8 46.2 %copy-start.11 = (f32[8,2,64,128]{3,2,1,0:T(8,128)S(1)}, f32[8,2,64,128]{3,2,1,0:T(8,128)}, u32[]{:S(2)}) copy-start(f32[8,2,64,128]{3,2,1,0:T(8,128)} %copy-done.10) | copy-start | bytes 1572868
  734.9 46.2 %copy-start.59 = (f32[2,128]{1,0:T(2,128)S(1)}, f32[2,128]{1,0:T(2,128)}, u32[]{:S(2)}) copy-start(f32[2,128]{1,0:T(2,128)} %copy-done.58) | copy-start | bytes 3076
  734.9 46.2 %copy-start.61 = (f32[2,128]{1,0:T(2,128)S(1)}, f32[2,128]{1,0:T(2,128)}, u32[]{:S(2)}) copy-start(f32[2,128]{1,0:T(2,128)} %copy-done.60) | copy-start | bytes 3076
  734.9 46.2 %copy-start.78 = (f32[128]{0:T(128)S(1)}, f32[128]{0:T(128)}, u32[]{:S(2)}) copy-start(f32[128]{0:T(128)} %copy-done.77) | copy-start | bytes 1540
  737.0 59.4 %copy-start.85 = (f32[2]{0:T(128)S(1)}, f32[2]{0:T(128)}, u32[]{:S(2)}) copy-start(f32[2]{0:T(128)} %param.34) | copy-start | bytes 28
  737.0 99.5 %all-gather.28.cloned.1.call-start = ((), (), s32[]{:S(2)}) async-start(), calls=%async_computation.18 | async-start | bytes 1310720 | tf_op jit(solution)/shard_map/all_gather | solution.py:114
  737.1 63.8 %copy-start.25 = (bf16[9,512,128]{2,1,0:T(8,128)(2,1)S(1)}, bf16[9,512,128]{2,1,0:T(8,128)(2,1)}, u32[]{:S(2)}) copy-start(bf16[9,512,128]{2,1,0:T(8,128)(2,1)} %all-gather.20.cloned.1.call-done) | copy-start | bytes 3538948
  798.3 6.8 collective-permute-start.4
  799.6 5.5 collective-permute-start.5
  804.6 76.4 %reduce-scatter.17.cloned.1.call-start = ((), (), s32[]{:S(2)}) async-start(), calls=%async_computation.22 | async-start | bytes 2621440 | tf_op jit(solution)/shard_map/reduce_scatter | solution.py:118
  809.6 123.3 %reduce-scatter.27.cloned.1.call-start = ((), (), s32[]{:S(2)}) async-start(), calls=%async_computation.27 | async-start | bytes 294912 | tf_op jit(solution)/shard_map/reduce_scatter | solution.py:480
  839.1 116.8 %reduce-scatter.25.cloned.1.call-start = ((), (), s32[]{:S(2)}) async-start(), calls=%async_computation.26 | async-start | bytes 884736 | tf_op jit(solution)/shard_map/reduce_scatter | solution.py:479
  841.9 160.1 %reduce-scatter.23.cloned.1.call-start = ((), (), s32[]{:S(2)}) async-start(), calls=%async_computation.25 | async-start | bytes 2654208 | tf_op jit(solution)/shard_map/reduce_scatter | solution.py:478
  862.5 34.5 %copy-start.47 = (f32[2,1024]{1,0:T(2,128)S(1)}, f32[2,1024]{1,0:T(2,128)}, u32[]{:S(2)}) copy-start(f32[2,1024]{1,0:T(2,128)} %copy-done.46) | copy-start | bytes 24580
  862.5 34.5 %copy-start.49 = (f32[2,1024]{1,0:T(2,128)S(1)}, f32[2,1024]{1,0:T(2,128)}, u32[]{:S(2)}) copy-start(f32[2,1024]{1,0:T(2,128)} %copy-done.48) | copy-start | bytes 24580
  862.5 34.5 %copy-start.51 = (f32[2,2048]{1,0:T(2,128)S(1)}, f32[2,2048]{1,0:T(2,128)}, u32[]{:S(2)}) copy-start(f32[2,2048]{1,0:T(2,128)} %param.36) | copy-start | bytes 49156
  862.6 183.7 %reduce-scatter.29.cloned.1.call-start = ((), (), s32[]{:S(2)}) async-start(), calls=%async_computation.28 | async-start | bytes 2359296 | tf_op jit(solution)/shard_map/reduce_scatter | solution.py:481
  899.4 193.1 %reduce-scatter.21.cloned.1.call-start = ((), (), s32[]{:S(2)}) async-start(), calls=%async_computation.24 | async-start | bytes 2654208 | tf_op jit(solution)/shard_map/reduce_scatter | solution.py:477
  920.0 218.5 %reduce-scatter.19.cloned.1.call-start = ((), (), s32[]{:S(2)}) async-start(), calls=%async_computation.23 | async-start | bytes 2621440 | tf_op jit(solution)/shard_map/reduce_scatter | solution.py:118
  920.1 4.4 collective-permute-start.6
  921.5 3.1 collective-permute-start.7
  928.9 209.6 %copy-start.9 = (f32[8,2,64,128]{3,2,1,0:T(8,128)S(1)}, f32[8,2,64,128]{3,2,1,0:T(8,128)}, u32[]{:S(2)}) copy-start(f32[8,2,64,128]{3,2,1,0:T(8,128)} %param.32) | copy-start | bytes 1572868
  928.9 209.6 %copy-start.55 = (f32[2,128]{1,0:T(2,128)S(1)}, f32[2,128]{1,0:T(2,128)}, u32[]{:S(2)}) copy-start(f32[2,128]{1,0:T(2,128)} %copy-done.54) | copy-start | bytes 3076
  928.9 209.6 %copy-start.57 = (f32[2,128]{1,0:T(2,128)S(1)}, f32[2,128]{1,0:T(2,128)}, u32[]{:S(2)}) copy-start(f32[2,128]{1,0:T(2,128)} %copy-done.56) | copy-start | bytes 3076
  928.9 209.6 %copy-start.72 = (f32[128]{0:T(128)S(1)}, f32[128]{0:T(128)}, u32[]{:S(2)}) copy-start(f32[128]{0:T(128)} %copy-done.71) | copy-start | bytes 1540
  929.0 209.6 %copy-start.80 = (f32[128]{0:T(128)S(1)}, f32[128]{0:T(128)}, u32[]{:S(2)}) copy-start(f32[128]{0:T(128)} %copy-done.79) | copy-start | bytes 1540
  932.1 208.2 %copy-start.82 = (f32[128]{0:T(128)S(1)}, f32[128]{0:T(128)}, u32[]{:S(2)}) copy-start(f32[128]{0:T(128)} %get-tuple-element.347) | copy-start | bytes 1540
  932.1 208.2 %copy-start.83 = (f32[128]{0:T(128)S(1)}, f32[128]{0:T(128)}, u32[]{:S(2)}) copy-start(f32[128]{0:T(128)} %get-tuple-element.361) | copy-start | bytes 1540
  932.1 236.2 %copy-start.45 = (bf16[2,81,256]{2,0,1:T(2,128)(2,1)S(1)}, bf16[2,81,256]{2,0,1:T(2,128)(2,1)}, u32[]{:S(2)}) copy-start(bf16[2,81,256]{2,0,1:T(2,128)(2,1)} %constant_dynamic-slice_fusion.2) | copy-start | bytes 248836
  932.7 237.8 %copy-start.81 = (f32[128]{0:T(128)S(1)}, f32[128]{0:T(128)}, u32[]{:S(2)}) copy-start(f32[128]{0:T(128)} %get-tuple-element.372) | copy-start | bytes 1540
  1094.2 118.4 %copy-start.30 = (f32[256,2,128]{2,1,0:T(2,128)S(1)}, f32[256,2,128]{2,1,0:T(2,128)}, u32[]{:S(2)}) copy-start(f32[256,2,128]{2,1,0:T(2,128)} %param.54) | copy-start | bytes 786436
  1172.9 44.5 %copy-start.31 = (f32[256,2,128]{2,1,0:T(2,128)S(1)}, f32[256,2,128]{2,1,0:T(2,128)}, u32[]{:S(2)}) copy-start(f32[256,2,128]{2,1,0:T(2,128)} %param.51) | copy-start | bytes 786436
  1172.9 44.5 %copy-start.32 = (f32[256,2,128]{2,0,1:T(8,128)S(1)}, f32[256,2,128]{2,0,1:T(8,128)}, u32[]{:S(2)}) copy-start(f32[256,2,128]{2,0,1:T(8,128)} %reduce-scatter.29.cloned.1.call-done) | copy-start | bytes 786436
  (84 other events, 853.2 us)
Sparse Core Ops, SparseCore 0:
  10.5 26.8 all-gather.15
  39.6 33.0 all-gather.11
  75.2 22.5 all-gather.13
  122.9 38.3 all-gather.17
  163.5 22.5 all-gather.19
  206.5 30.1 all-gather.21
  239.3 21.8 all-gather.23
  263.4 43.8 reduce-scatter.10
  309.9 27.2 all-gather.29
  339.6 27.8 all-gather.25
  662.0 71.2 reduce-scatter.12
  737.1 43.8 reduce-scatter.14
  804.8 31.7 all-gather.27
  838.8 42.1 reduce-scatter.16
  884.5 32.9 reduce-scatter.26
  920.8 35.0 reduce-scatter.24
  959.4 42.4 reduce-scatter.22
  1005.1 41.1 reduce-scatter.28
  1050.0 42.4 reduce-scatter.20
  1094.7 43.8 reduce-scatter.18
where the time goes:
time: 1250 us; the launch traced here: 1240 us
  waiting for transfers between devices  553 us (44%)
  matrix products  240 us (19%)
  local copies, waits for them, and re-layouts  183 us (15%)
  blocking collectives  152 us (12%)
  other arithmetic  77.8 us (6%)
  between operations  22.4 us (2%)
    reduce_scatter x4, waiting for transfers between devices, channel_total(): lax.psum_scatter(partial_value, 'chan', scatter_dimension=3, tiled=True)  148 us
    all_gather x4, waiting for transfers between devices, all_channels(): return lax.all_gather(values, 'chan', axis=3, tiled=True)  108 us
    psum x6, blocking collectives, group_totals(): lax.psum((jnp.sum(left_grouped, axis=(0, 2, 4)), jnp.sum(left_grouped * r...  94.3 us
    reduce_scatter x1, waiting for transfers between devices, body(): lax.psum_scatter(key_terms, 'rows', scatter_dimension=0, tiled=True)  68.6 us
    dot_general x8, matrix products, key_block(): jnp.einsum('bhqk,bhqd->bhkd', probs, grad_wide, precision=highest)  62 us
    reduce_scatter x1, waiting for transfers between devices, body(): lax.psum_scatter(conv_one_grad, 'rows', scatter_dimension=1, tiled=True)  44.6 us
    reduce_scatter x1, waiting for transfers between devices, body(): lax.psum_scatter(conv_two_grad, 'rows', scatter_dimension=1, tiled=True)  44.5 us
    reduce_scatter x1, waiting for transfers between devices, body(): lax.psum_scatter(embed_grad, 'rows', scatter_dimension=0, tiled=True)  42.7 us
  transfers between devices with their start and end apart: 28, of which 22 were waited for; matrix products, arithmetic and copies ran while one was open for 13% of the time, Pallas kernels for 0%

commit v1 on v0

v1 whole, which is shorter than its diff:
```python
import functools
import math

import jax
import jax.numpy as jnp
from jax import lax
from jax.experimental import pallas as pl
from jax.experimental.pallas import tpu as pltpu
from jax.sharding import PartitionSpec as P

C = 512
GROUPS = 32
HEAD_DIM = 64
EMB = 2048
DCTX = 2048
IMG_H = 64
IMG_W = 64
CLIP_TOK = 4
STEP = 10
CTX = 81
CTX_PAD = 128
GROUP_SIZE = C // GROUPS
GROUP_COUNT = IMG_H * IMG_W * GROUP_SIZE
LOG2E = 1.4426950408889634
BF = jnp.bfloat16
F32 = jnp.float32
ORDER = (0, 1, 3, 2)

clip_limit = 1.0


def swap(x, axis, distance):
    size = lax.axis_size(axis)
    return lax.ppermute(x, axis, [(i, i ^ distance) for i in range(size)])


def rows_sum(x):
    size = lax.axis_size("rows")
    x = x + swap(x, "rows", 1)
    step = 2
    while step < size:
        if step * 4 <= size:
            one, two, three = (swap(x, "rows", step * k) for k in (1, 2, 3))
            x = (x + one) + (two + three)
            step *= 4
        else:
            x = x + swap(x, "rows", step)
            step *= 2
    return x


def chan_sum(x):
    one, two, three = (swap(x, "chan", k) for k in (1, 2, 3))
    return (x + one) + (two + three)


def chan_blocks(x):
    far = swap(x, "chan", 3)
    near = swap(x, "chan", 1)
    return (x, near, far, swap(far, "chan", 1))


def rims(x):
    size = lax.axis_size("rows")
    up = [(i, i + 1) for i in range(size - 1)]
    down = [(j, i) for i, j in up]
    before = lax.ppermute(x[-1:], "rows", up)
    after = lax.ppermute(x[:1], "rows", down)
    return jnp.concatenate([before, after], axis=0)


def chan_blocks_with_rims(x):
    edge = rims(x)
    return chan_blocks(x) + chan_blocks(edge)


def chan_scatter(parts):
    got = swap(parts[2:4], "chan", 1)
    middle = (parts[1].astype(F32) + got[1].astype(F32)).astype(BF)
    return parts[0], got[0], swap(middle, "chan", 3)


def pick(x, index, axis=0):
    return lax.dynamic_index_in_dim(x, index, axis, keepdims=False)


def pair_exchange(x, pair):
    count = x.shape[0]
    return [pick(x, pair)] + [swap(pick(x, pair ^ k), "rows", 2 * k) for k in range(1, count)]


def weight_scatter(x):
    size = lax.axis_size("rows")
    taps, height, width = x.shape
    share = height // size
    row = lax.axis_index("rows")
    core, pair = row % 2, row // 2
    count = size // 2
    split = x.reshape(taps, count, 2, share, width)
    mine = pick(split, core, 2)
    other = swap(pick(split, 1 - core, 2), "rows", 1)
    both = mine.astype(F32) + other.astype(F32)
    low = both.astype(BF)
    total = pick(both, pair, 1)
    for k in range(1, count):
        total = total + swap(pick(low, pair ^ k, 1), "rows", 2 * k).astype(F32)
    return total


def local_call(kernel, outs, *args, scratch=(), flops=0):
    def spec(a):
        return pl.BlockSpec(memory_space=pltpu.SMEM if a.dtype == jnp.int32 else pltpu.VMEM)

    size = sum(math.prod(a.shape) * a.dtype.itemsize for a in (*args, *outs))
    return pl.pallas_call(
        kernel,
        out_shape=tuple(outs),
        in_specs=[spec(a) for a in args],
        out_specs=tuple(pl.BlockSpec(memory_space=pltpu.VMEM) for _ in outs),
        scratch_shapes=list(scratch),
        compiler_params=pltpu.CompilerParams(vmem_limit_bytes=50 * 1024 * 1024),
        cost_estimate=pl.CostEstimate(flops=flops, bytes_accessed=size, transcendentals=0),
    )(*args)


def out(shape, dtype):
    return jax.ShapeDtypeStruct(shape, dtype)


def nn(a, b):
    return lax.dot_general(a, b, (((1,), (0,)), ((), ())), preferred_element_type=F32)


def nt(a, b):
    return lax.dot_general(a, b, (((1,), (1,)), ((), ())), preferred_element_type=F32)


def group_mean(x):
    width = x.shape[1]
    left = lax.broadcasted_iota(jnp.int32, (width, width), 0) // GROUP_SIZE
    right = lax.broadcasted_iota(jnp.int32, (width, width), 1) // GROUP_SIZE
    same = (left == right).astype(F32)
    total = lax.dot_general(
        x, same, (((1,), (0,)), ((), ())), precision=lax.Precision.HIGHEST, preferred_element_type=F32
    )
    return total * (1.0 / GROUP_COUNT)


def moments(sums, images):
    means = group_mean(sums)
    average = means[:images]
    return average, lax.rsqrt(means[images:] - average * average + 1e-05)


def image_of(ref, b):
    rows, _, width, channels = ref.shape
    return ref[:, b].reshape(rows * width, channels)


def put_image(ref, b, value):
    rows, _, width, channels = ref.shape
    ref[:, b] = value.reshape(rows, width, channels).astype(ref.dtype)


def column_sum(x):
    return jnp.sum(x, axis=0, keepdims=True)


def silu(z):
    return z * jax.nn.sigmoid(z)


def silu_slope(z):
    s = jax.nn.sigmoid(z)
    return s * (1.0 + z * (1.0 - s))


def norm_kernel(x, sums, vec, o, *, gain, offset, active):
    images = x.shape[1]
    average, inverse = moments(sums[...], images)
    for b in range(images):
        z = (image_of(x, b) - average[b : b + 1]) * inverse[b : b + 1]
        z = z * vec[gain : gain + 1] + vec[offset : offset + 1]
        put_image(o, b, silu(z) if active else z)


def modulated(x, average, inverse, mod, vec, b, images):
    xhat = (x - average[b : b + 1]) * inverse[b : b + 1]
    scale = mod[b : b + 1] + vec[12:13]
    shift = mod[images + b : images + b + 1] + vec[13:14]
    return xhat, (xhat * vec[3:4] + vec[4:5]) * (1.0 + scale) + shift


def act_two_kernel(x, sums, mod, vec, o):
    images = x.shape[1]
    average, inverse = moments(sums[...], images)
    for b in range(images):
        _, shaped = modulated(image_of(x, b), average, inverse, mod, vec, b, images)
        put_image(o, b, silu(shaped))


def fill(xs, blocks, edges):
    rows, images, width, channels = blocks[0].shape
    span = images * width
    for j in range(4):
        lanes = slice(j * channels, (j + 1) * channels)
        if edges is None:
            xs[:, lanes] = blocks[j][...].reshape(rows * span, channels)
        else:
            xs[0:span, lanes] = edges[j][0].reshape(span, channels)
            xs[span : span + rows * span, lanes] = blocks[j][...].reshape(rows * span, channels)
            xs[span + rows * span :, lanes] = edges[j][1].reshape(span, channels)


def rows_of(z, j, width):
    return pl.ds(pl.multiple_of((z ^ ORDER[j]) * width, width), width)


def shifted(x, by, width):
    length = x.shape[0]
    column = lax.broadcasted_iota(jnp.int32, x.shape, 0) % width
    moved = pltpu.roll(x, by % length, 0)
    return jnp.where(column == (0 if by == 1 else width - 1), 0.0, moved)


def conv_taps(xs, w, z, rows, span, width, flipped):
    channels = w.shape[2]
    parts = []
    for dx in range(3):
        total = None
        for dy in range(3):
            at = (2 - dy if flipped else dy) * span
            a = xs[at : at + rows * span, :]
            taps = [w[3 * dy + dx, rows_of(z, j, channels), :] for j in range(4)]
            if flipped:
                term = nt(a, jnp.concatenate(taps, axis=1))
            else:
                term = nn(a, jnp.concatenate(taps, axis=0))
            total = term if total is None else total + term
        parts.append(total)
    if flipped:
        parts = parts[::-1]
    return parts[1] + shifted(parts[0], 1, width) + shifted(parts[2], -1, width)


def conv_one_kernel(zi, x0, x1, x2, x3, e0, e1, e2, e3, w, vec, hidden, sums, xs):
    rows, images, width, channels = x0.shape
    fill(xs, (x0, x1, x2, x3), (e0, e1, e2, e3))
    result = conv_taps(xs, w, zi[0], rows, images * width, width, False) + vec[2:3]
    hidden[...] = result.reshape(hidden.shape)
    for b in range(images):
        v = image_of(hidden, b)
        sums[b : b + 1] = column_sum(v)
        sums[images + b : images + b + 1] = column_sum(v * v)


def conv_two_kernel(zi, x0, x1, x2, x3, e0, e1, e2, e3, w, vec, pixels, residual, sums, xs):
    rows, images, width, channels = x0.shape
    fill(xs, (x0, x1, x2, x3), (e0, e1, e2, e3))
    result = conv_taps(xs, w, zi[0], rows, images * width, width, False) + vec[5:6]
    residual[...] = pixels[...] + result.reshape(residual.shape)
    for b in range(images):
        v = image_of(residual, b)
        sums[b : b + 1] = column_sum(v)
        sums[images + b : images + b + 1] = column_sum(v * v)


def conv_two_back_kernel(
    zi, x0, x1, x2, x3, e0, e1, e2, e3, w, vec, hidden, stats, mod, shaped_grad, sums, xs
):
    rows, images, width, channels = x0.shape
    fill(xs, (x0, x1, x2, x3), (e0, e1, e2, e3))
    result = conv_taps(xs, w, zi[0], rows, images * width, width, True)
    shaped_grad[...] = result.reshape(shaped_grad.shape)
    average, inverse = moments(stats[...], images)
    for b in range(images):
        xhat, shaped = modulated(image_of(hidden, b), average, inverse, mod, vec, b, images)
        g = image_of(shaped_grad, b) * silu_slope(shaped)
        put_image(shaped_grad, b, g)
        sums[b : b + 1] = column_sum(g)
        sums[images + b : images + b + 1] = column_sum(g * xhat)


def conv_one_back_kernel(
    zi, x0, x1, x2, x3, e0, e1, e2, e3, w, vec, pixels, stats, normed_grad, sums, xs
):
    rows, images, width, channels = x0.shape
    fill(xs, (x0, x1, x2, x3), (e0, e1, e2, e3))
    result = conv_taps(xs, w, zi[0], rows, images * width, width, True)
    normed_grad[...] = result.reshape(normed_grad.shape)
    average, inverse = moments(stats[...], images)
    for b in range(images):
        xhat = (image_of(pixels, b) - average[b : b + 1]) * inverse[b : b + 1]
        g = image_of(normed_grad, b) * silu_slope(xhat * vec[0:1] + vec[1:2])
        put_image(normed_grad, b, g)
        sums[b : b + 1] = column_sum(g)
        sums[images + b : images + b + 1] = column_sum(g * xhat)


def conv_weight_kernel(zi, x0, x1, x2, x3, e0, e1, e2, e3, r, o, xs):
    rows, images, width, channels = x0.shape
    span = images * width
    fill(xs, (x0, x1, x2, x3), (e0, e1, e2, e3))
    turned = xs[...].T
    wide = r[...].reshape(rows * span, channels).astype(F32)
    three = jnp.concatenate(
        [shifted(wide, -1, width).astype(BF), wide.astype(BF), shifted(wide, 1, width).astype(BF)],
        axis=1,
    )
    for dy in range(3):
        grad = nn(turned[:, dy * span : (dy + rows) * span], three)
        for dx in range(3):
            for j in range(4):
                o[3 * dy + dx, rows_of(zi[0], j, channels), :] = grad[
                    j * channels : (j + 1) * channels, dx * channels : (dx + 1) * channels
                ].astype(BF)


def heads_out(o, leading, value, b, heads):
    turned = value.T.astype(o.dtype)
    for h in range(heads):
        o[b * heads + h, leading] = turned[h * HEAD_DIM : (h + 1) * HEAD_DIM]


def project_kernel(zi, x0, x1, x2, x3, w, vec, o, *, base):
    rows, images, width, channels = x0.shape
    heads = channels // HEAD_DIM
    pixels = rows * images * width
    a = jnp.concatenate([x[...].reshape(pixels, channels) for x in (x0, x1, x2, x3)], axis=1)
    for s in range(3):
        taps = [w[base + s, rows_of(zi[0], j, channels), :] for j in range(4)]
        value = nn(a, jnp.concatenate(taps, axis=0))
        if s != 1:
            at = 8 if s == 0 else 9
            value = value + vec[at : at + 1]
        split = value.reshape(rows, images, width, channels)
        for b in range(images):
            heads_out(o, s, split[:, b].reshape(rows * width, channels), b, heads)


def output_grad_kernel(zi, x0, x1, x2, x3, w, o, *, tap):
    rows, images, width, channels = x0.shape
    heads = channels // HEAD_DIM
    pixels = rows * images * width
    a = jnp.concatenate([x[...].reshape(pixels, channels) for x in (x0, x1, x2, x3)], axis=1)
    taps = [w[tap, rows_of(zi[0], j, channels), :] for j in range(4)]
    split = nt(a, jnp.concatenate(taps, axis=1)).reshape(rows, images, width, channels)
    for b in range(images):
        turned = split[:, b].reshape(rows * width, channels).T.astype(BF)
        for h in range(heads):
            o[b * heads + h] = turned[h * HEAD_DIM : (h + 1) * HEAD_DIM]


def attention_kernel(
    live, q_ref, do_ref, kv_ref, sib_ref, ctx_ref, oq_ref, own_ref, other_ref, ctx_grad_ref, kt_s, k_s, v_s, s_s, p_s, acc_s, *, chunk
):
    step = pl.program_id(0)
    last = pl.num_programs(0) - 1
    depth, queries = q_ref.shape
    half = kv_ref.shape[2]
    keys = 2 * half
    extra = ctx_ref.shape[2]

    @pl.when(step == 0)
    def _():
        kt_s[:, :, 0:half] = kv_ref[...]
        kt_s[:, :, half:keys] = sib_ref[...]
        kt_s[:, :, keys:] = ctx_ref[...]
        k_s[...] = kt_s[0].T
        v_s[...] = kt_s[1].T
        acc_s[...] = jnp.zeros_like(acc_s)

    q = q_ref[...]
    do = do_ref[...]
    spans = [(i * chunk, chunk) for i in range(keys // chunk)] + [(keys, extra)]
    highest = None
    for at, size in spans:
        s = nn(k_s[at : at + size], q)
        if at == keys:
            position = lax.broadcasted_iota(jnp.int32, s.shape, 0)
            s = jnp.where(position < live[0], s, -1e30)
        s_s[at : at + size] = s
        top = jnp.max(s.reshape(size // 8, 8, queries), axis=0)
        highest = top if highest is None else jnp.maximum(highest, top)
    factor = 0.125 * LOG2E
    peak = jnp.max(highest, axis=0, keepdims=True) * factor
    weight_sum = jnp.zeros((8, queries), F32)
    mixture = jnp.zeros((depth, queries), F32)
    for at, size in spans:
        p = jnp.exp2(s_s[at : at + size] * factor - peak)
        weight_sum = weight_sum + jnp.sum(p.reshape(size // 8, 8, queries), axis=0)
        low = p.astype(BF)
        p_s[at : at + size] = low
        mixture = mixture + nn(kt_s[1, :, at : at + size], low)
    inverse = 1.0 / jnp.sum(weight_sum, axis=0, keepdims=True)
    attended = mixture * inverse
    oq_ref[0] = attended.astype(BF)
    delta = jnp.sum(do.astype(F32) * attended, axis=0, keepdims=True)
    do_scaled = (do.astype(F32) * inverse).astype(BF)
    q_scaled = (q.astype(F32) * (inverse * 0.125)).astype(BF)
    query_grad = jnp.zeros((depth, queries), F32)
    for at, size in spans:
        dprob = nn(v_s[at : at + size], do)
        low = p_s[at : at + size]
        dscore = (low.astype(F32) * (dprob - delta)).astype(BF)
        query_grad = query_grad + nn(kt_s[0, :, at : at + size], dscore)
        acc_s[0, :, at : at + size] += nt(q_scaled, dscore)
        acc_s[1, :, at : at + size] += nt(do_scaled, low)
    oq_ref[1] = (query_grad * (inverse * 0.125)).astype(BF)

    @pl.when(step == last)
    def _():
        own_ref[...] = acc_s[:, :, 0:half]
        other_ref[...] = acc_s[:, :, half:keys].astype(BF)
        ctx_grad_ref[...] = acc_s[:, :, keys:]


def attention(live, q, do, kv, sib, ctx):
    depth, queries = q.shape
    half = kv.shape[2]
    total = 2 * half + ctx.shape[2]
    block = min(512, queries)
    chunk = min(1024, 2 * half)

    def whole(a):
        return pl.BlockSpec(a.shape, lambda i: (0,) * len(a.shape))

    columns = pl.BlockSpec((depth, block), lambda i: (0, i))
    outs = (
        out((2, depth, queries), BF),
        out((2, depth, half), F32),
        out((2, depth, half), BF),
        out(ctx.shape, F32),
    )
    return pl.pallas_call(
        functools.partial(attention_kernel, chunk=chunk),
        grid=(queries // block,),
        in_specs=[pl.BlockSpec(memory_space=pltpu.SMEM), columns, columns, whole(kv), whole(sib), whole(ctx)],
        out_specs=(
            pl.BlockSpec((2, depth, block), lambda i: (0, 0, i)),
            whole(outs[1]),
            whole(outs[2]),
            whole(outs[3]),
        ),
        out_shape=outs,
        scratch_shapes=[
            pltpu.VMEM((2, depth, total), BF),
            pltpu.VMEM((total, depth), BF),
            pltpu.VMEM((total, depth), BF),
            pltpu.VMEM((total, block), F32),
            pltpu.VMEM((total, block), BF),
            pltpu.VMEM((2, depth, total), F32),
        ],
        compiler_params=pltpu.CompilerParams(
            vmem_limit_bytes=56 * 1024 * 1024, dimension_semantics=("arbitrary",)
        ),
        cost_estimate=pl.CostEstimate(
            flops=12 * depth * queries * total, bytes_accessed=8 * depth * total, transcendentals=queries * total
        ),
    )(live, q, do, kv, sib, ctx)


def back_project_kernel(zi, rec, w, attended, grads, parts, biases, *, base):
    rows, images, width, channels = attended.shape
    heads = channels // HEAD_DIM
    for b in range(images):
        for s in range(4):
            blocks = [rec[(b * heads + h) ^ zi[1], s] for h in range(heads)]
            value = jnp.concatenate(blocks, axis=0).T.reshape(rows, width, channels)
            if s == 0:
                attended[:, b] = value
            else:
                grads[:, b, :, (s - 1) * channels : s * channels] = value
    flat = grads[...].reshape(rows * images * width, 3 * channels)
    for place, j in enumerate((0, 2, 1, 3)):
        at = rows_of(zi[0], j, channels)
        taps = jnp.concatenate([w[base + s, at, :] for s in range(3)], axis=1)
        parts[place] = nt(flat, taps).astype(BF).reshape(parts.shape[1:])
    wide = flat.astype(F32)
    biases[0:1] = column_sum(wide[:, 0:channels])
    biases[1:2] = column_sum(wide[:, 2 * channels :])


def product_weight_kernel(zi, x0, x1, x2, x3, g, o):
    rows, images, width, channels = x0.shape
    pixels = rows * images * width
    a = jnp.concatenate([x[...].reshape(pixels, channels) for x in (x0, x1, x2, x3)], axis=1)
    columns = g.shape[3]
    grad = nn(a.T, g[...].reshape(pixels, columns))
    for s in range(columns // channels):
        for j in range(4):
            o[s, rows_of(zi[0], j, channels), :] = grad[
                j * channels : (j + 1) * channels, s * channels : (s + 1) * channels
            ].astype(BF)


def out_project_kernel(zi, x0, x1, x2, x3, w, vec, residual, o, *, tap):
    rows, images, width, channels = x0.shape
    pixels = rows * images * width
    a = jnp.concatenate([x[...].reshape(pixels, channels) for x in (x0, x1, x2, x3)], axis=1)
    taps = [w[tap, rows_of(zi[0], j, channels), :] for j in range(4)]
    value = nn(a, jnp.concatenate(taps, axis=0)) + vec[10:11]
    o[...] = (residual[...] + value.reshape(o.shape)).astype(BF)


def back_three_sum_kernel(t0, t1, t2, residual, stats, g_out, sums):
    images = residual.shape[1]
    average, inverse = moments(stats[...], images)
    for b in range(images):
        g = image_of(t0, b).astype(F32) + image_of(t1, b).astype(F32) + image_of(t2, b).astype(F32)
        xhat = (image_of(residual, b) - average[b : b + 1]) * inverse[b : b + 1]
        put_image(g_out, b, g)
        sums[b : b + 1] = column_sum(g)
        sums[images + b : images + b + 1] = column_sum(g * xhat)


def back_three_kernel(g_in, residual, stats, sums, vec, grad_out, residual_grad, low, bias):
    images = residual.shape[1]
    average, inverse = moments(stats[...], images)
    means = group_mean(sums[...] * vec[6:7])
    total = None
    for b in range(images):
        xhat = (image_of(residual, b) - average[b : b + 1]) * inverse[b : b + 1]
        scaled = image_of(g_in, b) * vec[6:7]
        g = inverse[b : b + 1] * (scaled - means[b : b + 1] - xhat * means[images + b : images + b + 1])
        g = image_of(grad_out, b) + g
        put_image(residual_grad, b, g)
        put_image(low, b, g)
        part = column_sum(g)
        total = part if total is None else total + part
    bias[...] = total


def back_two_kernel(g_in, hidden, stats, sums, mod, vec, low, bias):
    images = hidden.shape[1]
    average, inverse = moments(stats[...], images)
    scale = 1.0 + (mod[0:images] + vec[12:13])
    both = jnp.concatenate([scale, scale], axis=0)
    means = group_mean(sums[...] * both * vec[3:4])
    total = None
    for b in range(images):
        xhat = (image_of(hidden, b) - average[b : b + 1]) * inverse[b : b + 1]
        scaled = image_of(g_in, b) * scale[b : b + 1] * vec[3:4]
        g = inverse[b : b + 1] * (scaled - means[b : b + 1] - xhat * means[images + b : images + b + 1])
        put_image(low, b, g)
        part = column_sum(g)
        total = part if total is None else total + part
    bias[...] = total


def back_one_kernel(g_in, pixels, stats, sums, vec, residual_grad, pixel_grad):
    images = pixels.shape[1]
    average, inverse = moments(stats[...], images)
    means = group_mean(sums[...] * vec[0:1])
    for b in range(images):
        xhat = (image_of(pixels, b) - average[b : b + 1]) * inverse[b : b + 1]
        scaled = image_of(g_in, b) * vec[0:1]
        g = inverse[b : b + 1] * (scaled - means[b : b + 1] - xhat * means[images + b : images + b + 1])
        put_image(pixel_grad, b, image_of(residual_grad, b) + g)


def adamw(weight, moment, square, gradient, step_rate, weight_decay):
    moment_new = 0.9 * moment + 0.1 * gradient
    square_new = 0.999 * square + 0.001 * gradient * gradient
    corrected = moment_new / (1.0 - 0.9**STEP)
    scaled = square_new / (1.0 - 0.999**STEP)
    weight_new = weight - step_rate * (
        corrected / (jnp.sqrt(scaled) + 1e-08) + weight_decay * weight
    )
    return (weight_new, moment_new, square_new)


def turn_weights(x, row_count, chan_count):
    share = row_count // chan_count
    moves = []
    for r in range(row_count):
        for z in range(chan_count):
            moves.append((r * chan_count + z, (z * share + r % share) * chan_count + r // share))
    return lax.ppermute(x, ("rows", "chan"), moves)


def body(
    pixels,
    cotangent,
    loss_weight,
    timesteps,
    clip_embed,
    context,
    text_len,
    conv_first,
    conv_first_moment,
    conv_first_square,
    conv_second,
    conv_second_moment,
    conv_second_square,
    qkv_weight,
    qkv_weight_moment,
    qkv_weight_square,
    out_weight,
    out_weight_moment,
    out_weight_square,
    embed_weight,
    embed_weight_moment,
    embed_weight_square,
    context_weight,
    context_weight_moment,
    context_weight_square,
    vectors,
    vectors_moment,
    vectors_square,
):
    row_count = lax.axis_size("rows")
    chan_count = lax.axis_size("chan")
    row = lax.axis_index("rows")
    chan = lax.axis_index("chan")
    local_rows, images, width, channels = pixels.shape
    heads = channels // HEAD_DIM
    pairs = images * heads
    assert chan_count == 4 and row_count == 2 * pairs
    pair = row // 2
    zi = jnp.stack([chan, pair]).astype(jnp.int32)
    act = (local_rows, images, width, channels)
    edge_rows = (local_rows + 2) * images * width
    xs = pltpu.VMEM((edge_rows, C), BF)
    conv_flops = 2 * local_rows * images * width * 9 * C * channels

    one_low = conv_first.astype(BF)
    two_low = conv_second.astype(BF)
    qkv_low = jnp.transpose(qkv_weight, (1, 0, 2)).astype(BF)
    out_low = out_weight.astype(BF)[None]
    one_full = lax.all_gather(one_low, "rows", axis=1, tiled=True)
    out_turned = turn_weights(out_low, row_count, chan_count)
    two_full = lax.all_gather(
        jnp.concatenate([two_low, qkv_low, out_low, out_turned], axis=0), "rows", axis=1, tiled=True
    )
    ctx_full = lax.all_gather(context_weight.astype(BF), "rows", axis=0, tiled=True)
    back_full = lax.all_gather(
        turn_weights(jnp.concatenate([two_low, one_low], axis=0), row_count, chan_count),
        "rows",
        axis=1,
        tiled=True,
    )

    share = EMB // row_count
    index = row * share + jnp.arange(share, dtype=jnp.int32)
    half_width = EMB // 2
    frequency = jnp.exp(-math.log(10000.0) * (index % half_width).astype(F32) / half_width)
    phases = timesteps.astype(F32)[:, None] * frequency[None, :]
    features = jnp.where(index[None, :] < half_width, jnp.cos(phases), jnp.sin(phases))
    clip_share = lax.dynamic_slice_in_dim(clip_embed, row * share, share, 1)
    embedding = jax.nn.silu(features + clip_share).astype(BF)
    modulation = jnp.einsum(
        "be,esc->sbc", embedding, embed_weight.astype(BF), preferred_element_type=F32
    ).reshape(2 * images, channels)

    first = jnp.concatenate(
        [jnp.sum(pixels, axis=(0, 2)), jnp.sum(pixels * pixels, axis=(0, 2)), modulation], axis=0
    )
    first = rows_sum(first)
    stats_one, mod = first[: 2 * images], first[2 * images :]
    (active_one,) = local_call(
        functools.partial(norm_kernel, gain=0, offset=1, active=True),
        [out(act, BF)],
        pixels,
        stats_one,
        vectors,
    )
    blocks_one = chan_blocks_with_rims(active_one)
    sums_shape = out((2 * images, channels), F32)
    hidden, stats_two = local_call(
        conv_one_kernel,
        [out(act, F32), sums_shape],
        zi,
        *blocks_one,
        one_full,
        vectors,
        scratch=[xs],
        flops=conv_flops,
    )
    stats_two = rows_sum(stats_two)
    (active_two,) = local_call(act_two_kernel, [out(act, BF)], hidden, stats_two, mod, vectors)
    blocks_two = chan_blocks_with_rims(active_two)
    residual, stats_three = local_call(
        conv_two_kernel,
        [out(act, F32), sums_shape],
        zi,
        *blocks_two,
        two_full,
        vectors,
        pixels,
        scratch=[xs],
        flops=conv_flops,
    )
    stats_three = rows_sum(stats_three)
    (normed,) = local_call(
        functools.partial(norm_kernel, gain=6, offset=7, active=False),
        [out(act, BF)],
        residual,
        stats_three,
        vectors,
    )
    blocks_three = chan_blocks(normed)
    tokens = local_rows * width
    (projected,) = local_call(
        functools.partial(project_kernel, base=9),
        [out((pairs, 3, HEAD_DIM, tokens), BF)],
        zi,
        *blocks_three,
        two_full,
        vectors,
        flops=conv_flops // 3,
    )
    mine = jnp.concatenate(pair_exchange(projected, pair), axis=2)
    query, key_value = mine[0], mine[1:]
    sibling = swap(key_value, "rows", 1)

    grad_out = cotangent.astype(F32) * loss_weight[None, :, None, None]
    grad_low = grad_out.astype(BF)
    out_bias = jnp.sum(grad_out, axis=(0, 1, 2))[None]
    (attended_grad,) = local_call(
        functools.partial(output_grad_kernel, tap=13),
        [out((pairs, HEAD_DIM, tokens), BF)],
        zi,
        *chan_blocks(grad_low),
        two_full,
    )
    attended_grad = jnp.concatenate(pair_exchange(attended_grad, pair), axis=1)

    image, head = pair // heads, pair % heads
    ctx_low = pick(context, image)
    ctx_projected = jnp.einsum("te,esc->sct", ctx_low, ctx_full, preferred_element_type=F32)
    ctx_bias = jnp.stack([jnp.zeros_like(vectors[11]), vectors[11]])[:, :, None]
    ctx_heads = lax.dynamic_slice_in_dim(ctx_projected + ctx_bias, head * HEAD_DIM, HEAD_DIM, 1)
    ctx_heads = jnp.pad(ctx_heads.astype(BF), ((0, 0), (0, 0), (0, CTX_PAD - CTX)))
    live = (CLIP_TOK + pick(text_len, image))[None].astype(jnp.int32)

    out_query, own, other, ctx_grad = attention(
        live, query, attended_grad, key_value, sibling, ctx_heads
    )
    own = (own + swap(other, "rows", 1).astype(F32)).astype(BF)
    back = jnp.concatenate([out_query, own], axis=0)
    returned = [back[:, :, k * tokens : (k + 1) * tokens] for k in range(pairs)]
    received = jnp.stack(
        [returned[0]] + [swap(returned[k], "rows", 2 * k) for k in range(1, pairs)]
    )
    ctx_low_grad = (ctx_grad + swap(ctx_grad, "rows", 1)).astype(BF)
    ctx_all = jnp.stack(
        [ctx_low_grad] + [swap(ctx_low_grad, "rows", 2 * k) for k in range(1, pairs)]
    )

    attended, grads, parts, qv_bias = local_call(
        functools.partial(back_project_kernel, base=9),
        [
            out(act, BF),
            out((local_rows, images, width, 3 * channels), BF),
            out((4,) + act, BF),
            out((2, channels), F32),
        ],
        zi,
        received,
        two_full,
        flops=conv_flops // 3,
    )
    terms = chan_scatter(parts)
    normed_grad, sums_three = local_call(
        back_three_sum_kernel, [out(act, F32), sums_shape], *terms, residual, stats_three
    )
    sums_three = rows_sum(sums_three)
    residual_grad, residual_low, conv_two_bias = local_call(
        back_three_kernel,
        [out(act, F32), out(act, BF), out((1, channels), F32)],
        normed_grad,
        residual,
        stats_three,
        sums_three,
        vectors,
        grad_out,
    )
    shaped_grad, sums_two = local_call(
        conv_two_back_kernel,
        [out(act, F32), sums_shape],
        zi,
        *chan_blocks_with_rims(residual_low),
        back_full[:9],
        vectors,
        hidden,
        stats_two,
        mod,
        scratch=[xs],
        flops=conv_flops,
    )
    second = rows_sum(jnp.concatenate([sums_two, conv_two_bias, qv_bias, out_bias], axis=0))
    sums_two = second[: 2 * images]
    hidden_low, conv_one_bias = local_call(
        back_two_kernel,
        [out(act, BF), out((1, channels), F32)],
        shaped_grad,
        hidden,
        stats_two,
        sums_two,
        mod,
        vectors,
    )
    normed_one_grad, sums_one = local_call(
        conv_one_back_kernel,
        [out(act, F32), sums_shape],
        zi,
        *chan_blocks_with_rims(hidden_low),
        back_full[9:],
        vectors,
        pixels,
        stats_one,
        scratch=[xs],
        flops=conv_flops,
    )
    third = rows_sum(jnp.concatenate([sums_one, conv_one_bias], axis=0))
    sums_one = third[: 2 * images]
    (pixel_grad,) = local_call(
        back_one_kernel,
        [out(act, F32)],
        normed_one_grad,
        pixels,
        stats_one,
        sums_one,
        vectors,
        residual_grad,
    )

    attended_blocks = chan_blocks(attended)
    (activations,) = local_call(
        functools.partial(out_project_kernel, tap=12),
        [out(act, BF)],
        zi,
        *attended_blocks,
        two_full,
        vectors,
        residual,
    )

    taps = (9, C, channels)
    (two_grad,) = local_call(
        conv_weight_kernel,
        [out(taps, BF)],
        zi,
        *blocks_two,
        residual_low,
        scratch=[xs],
        flops=conv_flops,
    )
    (qkv_grad,) = local_call(
        product_weight_kernel, [out((3, C, channels), BF)], zi, *blocks_three, grads
    )
    (out_grad,) = local_call(
        product_weight_kernel, [out((1, C, channels), BF)], zi, *attended_blocks, grad_low
    )
    two_sum = weight_scatter(jnp.concatenate([two_grad, qkv_grad, out_grad], axis=0))
    qkv_sum = jnp.transpose(two_sum[9:12], (1, 0, 2))
    out_sum = two_sum[12]
    two_sum = two_sum[:9]
    (one_grad,) = local_call(
        conv_weight_kernel,
        [out(taps, BF)],
        zi,
        *blocks_one,
        hidden_low,
        scratch=[xs],
        flops=conv_flops,
    )
    one_sum = weight_scatter(one_grad)

    shift_grad, crossed = sums_two[:images], sums_two[images:]
    scale_grad = crossed * vectors[3] + shift_grad * vectors[4]
    embed_grad = jnp.einsum(
        "be,sbc->esc",
        embedding.astype(F32),
        jnp.stack((scale_grad, shift_grad)),
        precision=lax.Precision.HIGHEST,
    )
    order = jnp.arange(pairs, dtype=jnp.int32) ^ pair
    ctx_all = jnp.take(ctx_all, order, axis=0)[:, :, :, :CTX]
    ctx_all = ctx_all.reshape(images, heads, 2, HEAD_DIM, CTX)
    ctx_share = DCTX // row_count
    ctx_rows = lax.dynamic_slice_in_dim(context, row * ctx_share, ctx_share, 2)
    context_grad = jnp.einsum(
        "bte,bhsdt->eshd", ctx_rows, ctx_all, preferred_element_type=F32
    ).reshape(ctx_share, 2, channels)
    ctx_value_bias = jnp.sum(ctx_all[:, :, 1].astype(F32), axis=(0, 3)).reshape(1, channels)

    modulated_scale = 1.0 + mod[:images] + vectors[12]
    vector_grad = jnp.concatenate(
        (
            jnp.sum(sums_one[images:], axis=0, keepdims=True),
            jnp.sum(sums_one[:images], axis=0, keepdims=True),
            third[2 * images :],
            jnp.sum(modulated_scale * crossed, axis=0, keepdims=True),
            jnp.sum(modulated_scale * shift_grad, axis=0, keepdims=True),
            second[2 * images : 2 * images + 1],
            jnp.sum(sums_three[images:], axis=0, keepdims=True),
            jnp.sum(sums_three[:images], axis=0, keepdims=True),
            second[2 * images + 1 : 2 * images + 4],
            ctx_value_bias,
            jnp.sum(scale_grad, axis=0, keepdims=True),
            jnp.sum(shift_grad, axis=0, keepdims=True),
        ),
        axis=0,
    )

    squared = jnp.zeros((), F32)
    for member in (two_sum, qkv_sum, out_sum, embed_grad, context_grad, one_sum):
        squared = squared + jnp.sum(member * member)
    squared = squared + jnp.where(row == 0, jnp.sum(vector_grad * vector_grad), 0.0)
    squared = chan_sum(rows_sum(jnp.broadcast_to(squared, (8, 128))))[0, 0]
    grad_norm = jnp.sqrt(squared)
    factor = jnp.minimum(1.0, clip_limit / grad_norm)
    conv_one = adamw(
        conv_first, conv_first_moment, conv_first_square, one_sum * factor, 0.02, 0.01
    )
    conv_two = adamw(
        conv_second, conv_second_moment, conv_second_square, two_sum * factor, 0.02, 0.01
    )
    qkv_new = adamw(qkv_weight, qkv_weight_moment, qkv_weight_square, qkv_sum * factor, 0.08, 0.01)
    out_new = adamw(out_weight, out_weight_moment, out_weight_square, out_sum * factor, 1.0, 0.01)
    embed_new = adamw(
        embed_weight, embed_weight_moment, embed_weight_square, embed_grad * factor, 0.02, 0.01
    )
    context_new = adamw(
        context_weight,
        context_weight_moment,
        context_weight_square,
        context_grad * factor,
        0.04,
        0.01,
    )
    vector_new = adamw(vectors, vectors_moment, vectors_square, vector_grad * factor, 1.0, 0.0)
    result = [activations, pixel_grad, grad_norm]
    for new in (conv_one, conv_two, qkv_new, out_new, embed_new, context_new):
        result += [new[0], new[1], new[2], new[0].astype(BF)]
    return (*result, *vector_new)


def solution(mesh):
    act = P("rows", None, None, "chan")
    conv = P(None, "rows", "chan")
    wide = P("rows", None, "chan")
    flat = P("rows", "chan")
    vec = P(None, "chan")
    weights = (conv, conv, wide, flat, wide, wide)
    in_specs = (act, act) + (P(),) * 5 + tuple(s for w in weights for s in (w,) * 3) + (vec,) * 3
    out_specs = (act, act, P()) + tuple(s for w in weights for s in (w,) * 4) + (vec,) * 3
    return jax.shard_map(body, mesh=mesh, in_specs=in_specs, out_specs=out_specs, check_vma=False)
```

time: 1250 us -> 448 us (0.36)
  waiting for transfers between devices: 553 us -> 115 us
  matrix products: 240 us -> 5.54 us
  blocking collectives: 152 us -> 0 us
  local copies, waits for them, and re-layouts: 183 us -> 38.8 us
  starting transfers between devices: 11.9 us -> 148 us
  Pallas kernels: 0 us -> 76.2 us
  other arithmetic: 77.8 us -> 33.7 us
    reduce_scatter x10 -> x0, waiting for transfers between devices: 369 us -> none  [the longest x4 148 us: channel_total(): lax.psum_scatter(partial_value, 'chan', scatter_dimension=3, tiled=True)]
    dot_general x64 -> x3, matrix products: 240 us -> 3.58 us  [the longest x1 2.42 us: body(): jnp.einsum('be,sbc->esc', embedding.astype(F32), jnp.stack((scale_grad, s...]
    all_gather x10 -> x4, waiting for transfers between devices: 180 us -> 0.04 us  [the longest x1 0.02 us: body(): one_full = lax.all_gather(one_low, 'rows', axis=1, tiled=True)]
    ppermute x8 -> x99, starting transfers between devices: 10.6 us -> 148 us  [the longest x89 135 us: swap(): return lax.ppermute(x, axis, [(i, i ^ distance) for i in range(size)])]
    psum x7 -> x0, blocking collectives: 133 us -> none  [the longest x6 94.3 us: group_totals(): lax.psum((jnp.sum(left_grouped, axis=(0, 2, 4)), jnp.sum(left_grouped * r...]
    ppermute x8 -> x99, waiting for transfers between devices: 3.75 us -> 115 us  [the longest x89 114 us: swap(): return lax.ppermute(x, axis, [(i, i ^ distance) for i in range(size)])]
    pallas_call x0 -> x20, Pallas kernels: none -> 76.2 us  [the longest x19 39.6 us: local_call(): pl.pallas_call(kernel, out_shape=tuple(outs), in_specs=[spec(a) for a in...]
    reshape x41 -> x1, local copies, waits for them, and re-layouts: 62.4 us -> 0.6 us  [body(): jnp.sum(ctx_all[:, :, 1].astype(F32), axis=(0, 3)).reshape(1, channels)]
  transfers between devices with their start and end apart: 28 -> 103, of which waited for: 22 -> 46; matrix products, arithmetic and copies ran while one was open for 13% -> 11% of each run, Pallas kernels for 0% -> 16%
where the time goes in v1:
time: 448 us; the launch traced here: 441 us
  starting transfers between devices  148 us (33%)
  waiting for transfers between devices  115 us (26%)
  Pallas kernels  76.2 us (17%)
  local copies, waits for them, and re-layouts  38.8 us (9%)
  other arithmetic  33.7 us (8%)
  between operations  23.2 us (5%)
  matrix products  5.54 us (1%)
    ppermute x89, starting transfers between devices, swap(): return lax.ppermute(x, axis, [(i, i ^ distance) for i in range(size)])  135 us
    ppermute x89, waiting for transfers between devices, swap(): return lax.ppermute(x, axis, [(i, i ^ distance) for i in range(size)])  114 us
    pallas_call x19, Pallas kernels, local_call(): pl.pallas_call(kernel, out_shape=tuple(outs), in_specs=[spec(a) for a in...  39.6 us
    pallas_call x1, Pallas kernels, attention(): pl.pallas_call(functools.partial(attention_kernel, chunk=chunk), grid=(qu...  36.6 us
    unnamed x259, local copies, waits for them, and re-layouts  18.4 us
  transfers between devices with their start and end apart: 103, of which 46 were waited for; matrix products, arithmetic and copies ran while one was open for 11% of the time, Pallas kernels for 16%

profile of v1, /device:TPU:0, one launch (start us, length us, event | category | flops | bytes accessed | tf_op | source)
XLA Modules:
  0.0 441.3 jit_solution(13376606239754689738)
XLA Ops:
  15.9 7.7 %collective-permute-start.2 = (f32[8,128]{1,0:T(8,128)S(1)}, f32[8,128]{1,0:T(8,128)S(1)}, u32[]{:S(2)}, u32[]{:S(2)}) collective-permute-start(f32[8,128]{1,0:T(8,128)S(1)} %fusion.46), channel_id=1, source_target_pairs={{0,16},{4,20},{8,24},{12,28},{16,0},{20,4},{24,8},{28,12},{1,17},{... | collective-permute-start | bytes 12296 | tf_op jit(solution)/shard_map/ppermute | solution.py:34
  23.6 2.8 collective-permute-start.3
  31.0 2.6 collective-permute-start.5
  36.3 4.1 collective-permute-done.5.x2
  40.4 3.2 collective-permute-start.6
  43.6 2.7 collective-permute-start.10
  47.3 6.0 %collective-permute-done.10.e2 = bf16[2,2,64,128]{3,2,1,0:T(8,128)(2,1)S(1)} collective-permute-done((bf16[2,2,64,128]{3,2,1,0:T(8,128)(2,1)S(1)}, bf16[2,2,64,128]{3,2,1,0:T(8,128)(2,1)S(1)}, u32[]{:S(2)}, u32[]{:S(2)}) %collective-permute-start.10) | collective-permute-done | bytes 65568 | tf_op jit(solution)/shard_map/ppermute | solution.py:34
  53.7 3.9 collective-permute-done.11.e3
  59.1 3.2 shard_map.500
  67.2 2.6 collective-permute-done.15
  71.5 2.6 collective-permute-start.17
  76.8 4.5 %collective-permute-done.17.x2 = bf16[8,2,64,128]{3,2,1,0:T(8,128)(2,1)S(1)} collective-permute-done((bf16[8,2,64,128]{3,2,1,0:T(8,128)(2,1)S(1)}, bf16[8,2,64,128]{3,2,1,0:T(8,128)(2,1)S(1)}, u32[]{:S(2)}, u32[]{:S(2)}) %collective-permute-start.17) | collective-permute-done | bytes 262176 | tf_op jit(solution)/shard_map/ppermute | solution.py:34
  81.3 2.5 collective-permute-start.18
  83.8 2.7 collective-permute-start.22
  86.5 6.9 %collective-permute-done.22.e2 = bf16[2,2,64,128]{3,2,1,0:T(8,128)(2,1)S(1)} collective-permute-done((bf16[2,2,64,128]{3,2,1,0:T(8,128)(2,1)S(1)}, bf16[2,2,64,128]{3,2,1,0:T(8,128)(2,1)S(1)}, u32[]{:S(2)}, u32[]{:S(2)}) %collective-permute-start.22) | collective-permute-done | bytes 65568 | tf_op jit(solution)/shard_map/ppermute | solution.py:34
  93.9 3.9 collective-permute-done.23.e3
  97.8 4.3 shard_map.502
  110.7 4.9 %collective-permute-start.30 = (bf16[8,2,64,128]{3,2,1,0:T(8,128)(2,1)}, bf16[8,2,64,128]{3,2,1,0:T(8,128)(2,1)}, u32[]{:S(2)}, u32[]{:S(2)}) collective-permute-start(bf16[8,2,64,128]{3,2,1,0:T(8,128)(2,1)} %shard_map.503.x0), channel_id=1, source_target_pairs={{0,3},{1,2},{2,1},{3,0},{4,7},{5,6},{6,5},{7,4},{8,11},{9,10},{10,... | collective-permute-start | bytes 786440 | tf_op jit(solution)/shard_map/ppermute | solution.py:34
  115.7 2.5 fusion.50
  118.9 23.4 %collective-permute-start.29 = (bf16[8,2,64,128]{3,2,1,0:T(8,128)(2,1)}, bf16[8,2,64,128]{3,2,1,0:T(8,128)(2,1)}, u32[]{:S(2)}, u32[]{:S(2)}) collective-permute-start(bf16[8,2,64,128]{3,2,1,0:T(8,128)(2,1)} %shard_map.503.x0), channel_id=1, source_target_pairs={{0,1},{1,0},{2,3},{3,2},{4,5},{5,4},{6,7},{7,6},{8,9},{9,8},{10,11... | collective-permute-start | bytes 786440 | tf_op jit(solution)/shard_map/ppermute | solution.py:34
  149.1 4.4 %collective-permute-done.29.x1 = bf16[8,2,64,128]{3,2,1,0:T(8,128)(2,1)} collective-permute-done((bf16[8,2,64,128]{3,2,1,0:T(8,128)(2,1)}, bf16[8,2,64,128]{3,2,1,0:T(8,128)(2,1)}, u32[]{:S(2)}, u32[]{:S(2)}) %collective-permute-start.29) | collective-permute-done | bytes 262176 | tf_op jit(solution)/shard_map/ppermute | solution.py:34
  153.5 5.6 %collective-permute-done.31.x3 = bf16[8,2,64,128]{3,2,1,0:T(8,128)(2,1)} collective-permute-done((bf16[8,2,64,128]{3,2,1,0:T(8,128)(2,1)}, bf16[8,2,64,128]{3,2,1,0:T(8,128)(2,1)}, u32[]{:S(2)}, u32[]{:S(2)}) %collective-permute-start.31) | collective-permute-done | bytes 262176 | tf_op jit(solution)/shard_map/ppermute | solution.py:34
  159.8 2.3 shard_map.504
  164.5 1.9 collective-permute-start.32
  166.5 2.0 fusion.2
  172.5 3.5 collective-permute-done.34
  176.0 3.1 collective-permute-done.33
  184.3 36.6 %shard_map.506 = (bf16[2,64,2048]{2,1,0:T(8,128)(2,1)}, f32[2,64,2048]{2,1,0:T(8,128)}, bf16[2,64,2048]{2,1,0:T(8,128)(2,1)}, f32[2,64,128]{2,1,0:T(8,128)}) custom-call(s32[1]{0:T(128)S(6)} %add_shard_map.4.live, bf16[64,2048]{1,0:T(8,128)(2,1)} %maximum_bitcast_fusion.q_ref, bf16[64,2048]{1,0:T(8,128)(2,1)} %pad_maximum_fusion.7.do_ref, ...), custom_call_target="tpu_custom_call" | custom-call | flops 6643777536 | bytes 2162688 | tf_op jit(solution)/shard_map/pallas_call | solution.py:435
  224.6 2.7 collective-permute-start.45
  228.2 2.6 collective-permute-start.87
  230.9 3.9 collective-permute-done.45
  235.1 5.1 %collective-permute-done.44 = bf16[4,64,512]{2,1,0:T(8,128)(2,1)S(1)} collective-permute-done((bf16[4,64,512]{2,1,0:T(8,128)(2,1)S(1)}, bf16[4,64,512]{2,1,0:T(8,128)(2,1)S(1)}, u32[]{:S(2)}, u32[]{:S(2)}) %collective-permute-start.44) | collective-permute-done | bytes 262176 | tf_op jit(solution)/shard_map/ppermute | solution.py:34
  240.7 3.6 shard_map.507
  251.2 2.1 gather_fusion
  254.3 7.1 %collective-permute-done.49 = bf16[2,8,2,64,128]{4,3,2,1,0:T(8,128)(2,1)} collective-permute-done((bf16[2,8,2,64,128]{4,3,2,1,0:T(8,128)(2,1)}, bf16[2,8,2,64,128]{4,3,2,1,0:T(8,128)(2,1)}, u32[]{:S(2)}, u32[]{:S(2)}) %collective-permute-start.49) | collective-permute-done | bytes 524320 | tf_op jit(solution)/shard_map/ppermute | solution.py:34
  262.5 3.5 collective-permute-start.50
  268.4 4.3 collective-permute-done.50.t2
  274.3 2.7 collective-permute-start.53
  279.2 10.1 %collective-permute-start.46 = (bf16[8,2,64,128]{3,2,1,0:T(8,128)(2,1)}, bf16[8,2,64,128]{3,2,1,0:T(8,128)(2,1)}, u32[]{:S(2)}, u32[]{:S(2)}) collective-permute-start(bf16[8,2,64,128]{3,2,1,0:T(8,128)(2,1)} %get-tuple-element.60.x0), channel_id=1, source_target_pairs={{0,1},{1,0},{2,3},{3,2},{4,5},{5,4},{6,7},{7,6},{8,9},{9,8},{10,11... | collective-permute-start | bytes 786440 | tf_op jit(solution)/shard_map/ppermute | solution.py:34
  291.8 3.3 collective-permute-start.56
  296.5 2.3 collective-permute-start.58
  300.7 2.0 shard_map.516
  309.4 3.3 collective-permute-start.61
  312.8 2.9 shard_map.515
  315.7 2.1 collective-permute-start.60
  318.1 6.0 %collective-permute-done.60.e1 = bf16[2,2,64,128]{3,2,1,0:T(8,128)(2,1)S(1)} collective-permute-done((bf16[2,2,64,128]{3,2,1,0:T(8,128)(2,1)S(1)}, bf16[2,2,64,128]{3,2,1,0:T(8,128)(2,1)S(1)}, u32[]{:S(2)}, u32[]{:S(2)}) %collective-permute-start.60) | collective-permute-done | bytes 65568 | tf_op jit(solution)/shard_map/ppermute | solution.py:34
  325.2 4.2 shard_map.511
  334.9 2.2 collective-permute-done.67
  337.8 2.3 collective-permute-start.69
  342.7 2.4 multiply_reduce_fusion.3
  347.7 3.1 collective-permute-done.69.x2
  354.1 2.5 shard_map.518
  356.7 3.5 collective-permute-done.74.e2
  361.7 2.7 collective-permute-done.75.e3
  364.5 3.6 shard_map.513
  374.4 2.9 collective-permute-start.83
  379.5 4.1 collective-permute-done.83
  383.6 3.5 collective-permute-done.82
  389.0 2.4 fusion.72
  400.1 2.2 collective-permute-done.90
  402.3 2.6 multiply_reduce_fusion.1
  410.4 2.3 collective-permute-done.95
  413.8 2.0 collective-permute-start.98
  416.9 2.3 shard_map.508
  (532 shorter events, 140.8 us)
Async XLA Ops:
  7.3 50.3 %all-gather.5.cloned.1.call-start = ((), (), s32[]{:S(2)}) async-start(), calls=%async_computation | async-start | bytes 1327104 | tf_op jit(solution)/shard_map/all_gather | solution.py:631
  9.1 88.7 %all-gather.7.cloned.1.call-start = ((), (), s32[]{:S(2)}) async-start(), calls=%async_computation.1 | async-start | bytes 2064384 | tf_op jit(solution)/shard_map/all_gather | solution.py:633
  13.3 153.2 %all-gather.9.cloned.1.call-start = ((), (), s32[]{:S(2)}) async-start(), calls=%async_computation.2 | async-start | bytes 1179648 | tf_op jit(solution)/shard_map/all_gather | solution.py:636
  15.9 11.0 %collective-permute-start.2 = (f32[8,128]{1,0:T(8,128)S(1)}, f32[8,128]{1,0:T(8,128)S(1)}, u32[]{:S(2)}, u32[]{:S(2)}) collective-permute-start(f32[8,128]{1,0:T(8,128)S(1)} %fusion.46), channel_id=1, source_target_pairs={{0,16},{4,20},{8,24},{12,28},{16,0},{20,4},{24,8},{28,12},{1,17},{... | collective-permute-start | bytes 12296 | tf_op jit(solution)/shard_map/ppermute | solution.py:34
  31.0 9.4 %collective-permute-start.5 = (bf16[8,2,64,128]{3,2,1,0:T(8,128)(2,1)S(1)}, bf16[8,2,64,128]{3,2,1,0:T(8,128)(2,1)S(1)}, u32[]{:S(2)}, u32[]{:S(2)}) collective-permute-start(bf16[8,2,64,128]{3,2,1,0:T(8,128)(2,1)S(1)} %shard_map.499.x0), channel_id=1, source_target_pairs={{0,3},{1,2},{2,1},{3,0},{4,7},{5,6},{6,5},{7,4},{8,11},{9,10},{10,... | collective-permute-start | bytes 786440 | tf_op jit(solution)/shard_map/ppermute | solution.py:34
  34.9 22.6 %collective-permute-start.4 = (bf16[8,2,64,128]{3,2,1,0:T(8,128)(2,1)S(1)}, bf16[8,2,64,128]{3,2,1,0:T(8,128)(2,1)S(1)}, u32[]{:S(2)}, u32[]{:S(2)}) collective-permute-start(bf16[8,2,64,128]{3,2,1,0:T(8,128)(2,1)S(1)} %shard_map.499.x0), channel_id=1, source_target_pairs={{0,1},{1,0},{2,3},{3,2},{4,5},{5,4},{6,7},{7,6},{8,9},{9,8},{10,11... | collective-permute-start | bytes 786440 | tf_op jit(solution)/shard_map/ppermute | solution.py:34
  35.0 8.6 %collective-permute-start.8 = (bf16[1,2,64,128]{3,2,1,0:T(8,128)(2,1)S(1)}, bf16[1,2,64,128]{3,2,1,0:T(8,128)(2,1)S(1)}, u32[]{:S(2)}, u32[]{:S(2)}) collective-permute-start(bf16[1,2,64,128]{3,2,1,0:T(8,128)(2,1)S(1)} %get-tuple-element.209), channel_id=1, source_target_pairs={{4,0},{8,4},{12,8},{16,12},{20,16},{24,20},{28,24},{5,1},{9,5},{13... | collective-permute-start | bytes 98312 | tf_op jit(solution)/shard_map/ppermute | solution.py:68
  40.4 17.2 %collective-permute-start.6 = (bf16[8,2,64,128]{3,2,1,0:T(8,128)(2,1)S(1)}, bf16[8,2,64,128]{3,2,1,0:T(8,128)(2,1)S(1)}, u32[]{:S(2)}, u32[]{:S(2)}) collective-permute-start(bf16[8,2,64,128]{3,2,1,0:T(8,128)(2,1)S(1)} %collective-permute-done.5.x2), channel_id=1, source_target_pairs={{0,1},{1,0},{2,3},{3,2},{4,5},{5,4},{6,7},{7,6},{8,9},{9,8},{10,11... | collective-permute-start | bytes 786440 | tf_op jit(solution)/shard_map/ppermute | solution.py:34
  43.6 9.7 %collective-permute-start.10 = (bf16[2,2,64,128]{3,2,1,0:T(8,128)(2,1)S(1)}, bf16[2,2,64,128]{3,2,1,0:T(8,128)(2,1)S(1)}, u32[]{:S(2)}, u32[]{:S(2)}) collective-permute-start(bf16[2,2,64,128]{3,2,1,0:T(8,128)(2,1)S(1)} %constant_dynamic-update-slice_fusion.e0), channel_id=1, source_target_pairs={{0,3},{1,2},{2,1},{3,0},{4,7},{5,6},{6,5},{7,4},{8,11},{9,10},{10,... | collective-permute-start | bytes 196616 | tf_op jit(solution)/shard_map/ppermute | solution.py:34
  47.1 200.7 %all-gather.11.cloned.1.call-start = ((), (), s32[]{:S(2)}) async-start(), calls=%async_computation.3 | async-start | bytes 2654208 | tf_op jit(solution)/shard_map/all_gather | solution.py:637
  71.5 9.8 %collective-permute-start.17 = (bf16[8,2,64,128]{3,2,1,0:T(8,128)(2,1)S(1)}, bf16[8,2,64,128]{3,2,1,0:T(8,128)(2,1)S(1)}, u32[]{:S(2)}, u32[]{:S(2)}) collective-permute-start(bf16[8,2,64,128]{3,2,1,0:T(8,128)(2,1)S(1)} %shard_map.501.x0), channel_id=1, source_target_pairs={{0,3},{1,2},{2,1},{3,0},{4,7},{5,6},{6,5},{7,4},{8,11},{9,10},{10,... | collective-permute-start | bytes 786440 | tf_op jit(solution)/shard_map/ppermute | solution.py:34
  74.1 9.7 %collective-permute-start.19 = (bf16[1,2,64,128]{3,2,1,0:T(8,128)(2,1)S(1)}, bf16[1,2,64,128]{3,2,1,0:T(8,128)(2,1)S(1)}, u32[]{:S(2)}, u32[]{:S(2)}) collective-permute-start(bf16[1,2,64,128]{3,2,1,0:T(8,128)(2,1)S(1)} %get-tuple-element.208), channel_id=1, source_target_pairs={{0,4},{4,8},{8,12},{12,16},{16,20},{20,24},{24,28},{1,5},{5,9},{9,... | collective-permute-start | bytes 98312 | tf_op jit(solution)/shard_map/ppermute | solution.py:67
  75.4 22.3 %collective-permute-start.16 = (bf16[8,2,64,128]{3,2,1,0:T(8,128)(2,1)S(1)}, bf16[8,2,64,128]{3,2,1,0:T(8,128)(2,1)S(1)}, u32[]{:S(2)}, u32[]{:S(2)}) collective-permute-start(bf16[8,2,64,128]{3,2,1,0:T(8,128)(2,1)S(1)} %shard_map.501.x0), channel_id=1, source_target_pairs={{0,1},{1,0},{2,3},{3,2},{4,5},{5,4},{6,7},{7,6},{8,9},{9,8},{10,11... | collective-permute-start | bytes 786440 | tf_op jit(solution)/shard_map/ppermute | solution.py:34
  75.5 8.3 %collective-permute-start.20 = (bf16[1,2,64,128]{3,2,1,0:T(8,128)(2,1)S(1)}, bf16[1,2,64,128]{3,2,1,0:T(8,128)(2,1)S(1)}, u32[]{:S(2)}, u32[]{:S(2)}) collective-permute-start(bf16[1,2,64,128]{3,2,1,0:T(8,128)(2,1)S(1)} %get-tuple-element.207), channel_id=1, source_target_pairs={{4,0},{8,4},{12,8},{16,12},{20,16},{24,20},{28,24},{5,1},{9,5},{13... | collective-permute-start | bytes 98312 | tf_op jit(solution)/shard_map/ppermute | solution.py:68
  81.3 16.5 %collective-permute-start.18 = (bf16[8,2,64,128]{3,2,1,0:T(8,128)(2,1)S(1)}, bf16[8,2,64,128]{3,2,1,0:T(8,128)(2,1)S(1)}, u32[]{:S(2)}, u32[]{:S(2)}) collective-permute-start(bf16[8,2,64,128]{3,2,1,0:T(8,128)(2,1)S(1)} %collective-permute-done.17.x2), channel_id=1, source_target_pairs={{0,1},{1,0},{2,3},{3,2},{4,5},{5,4},{6,7},{7,6},{8,9},{9,8},{10,11... | collective-permute-start | bytes 786440 | tf_op jit(solution)/shard_map/ppermute | solution.py:34
  83.8 9.7 %collective-permute-start.22 = (bf16[2,2,64,128]{3,2,1,0:T(8,128)(2,1)S(1)}, bf16[2,2,64,128]{3,2,1,0:T(8,128)(2,1)S(1)}, u32[]{:S(2)}, u32[]{:S(2)}) collective-permute-start(bf16[2,2,64,128]{3,2,1,0:T(8,128)(2,1)S(1)} %constant_dynamic-update-slice_fusion.2.e0), channel_id=1, source_target_pairs={{0,3},{1,2},{2,1},{3,0},{4,7},{5,6},{6,5},{7,4},{8,11},{9,10},{10,... | collective-permute-start | bytes 196616 | tf_op jit(solution)/shard_map/ppermute | solution.py:34
  86.5 7.3 %collective-permute-start.21 = (bf16[2,2,64,128]{3,2,1,0:T(8,128)(2,1)S(1)}, bf16[2,2,64,128]{3,2,1,0:T(8,128)(2,1)S(1)}, u32[]{:S(2)}, u32[]{:S(2)}) collective-permute-start(bf16[2,2,64,128]{3,2,1,0:T(8,128)(2,1)S(1)} %constant_dynamic-update-slice_fusion.2.e0), channel_id=1, source_target_pairs={{0,1},{1,0},{2,3},{3,2},{4,5},{5,4},{6,7},{7,6},{8,9},{9,8},{10,11... | collective-permute-start | bytes 196616 | tf_op jit(solution)/shard_map/ppermute | solution.py:34
  107.0 11.4 %collective-permute-start.63 = (bf16[18,64,128]{2,1,0:T(8,128)(2,1)S(1)}, bf16[18,64,128]{2,1,0:T(8,128)(2,1)}, u32[]{:S(2)}, u32[]{:S(2)}) collective-permute-start(bf16[18,64,128]{2,1,0:T(8,128)(2,1)S(1)} %pad_maximum_fusion.5), channel_id=1, source_target_pairs={{0,0},{1,8},{2,16},{3,24},{4,4},{5,12},{6,20},{7,28},{8,1},{9,9},{... | collective-permute-start | bytes 884744 | tf_op jit(solution)/shard_map/ppermute | solution.py:579
  110.7 31.6 %collective-permute-start.30 = (bf16[8,2,64,128]{3,2,1,0:T(8,128)(2,1)}, bf16[8,2,64,128]{3,2,1,0:T(8,128)(2,1)}, u32[]{:S(2)}, u32[]{:S(2)}) collective-permute-start(bf16[8,2,64,128]{3,2,1,0:T(8,128)(2,1)} %shard_map.503.x0), channel_id=1, source_target_pairs={{0,3},{1,2},{2,1},{3,0},{4,7},{5,6},{6,5},{7,4},{8,11},{9,10},{10,... | collective-permute-start | bytes 786440 | tf_op jit(solution)/shard_map/ppermute | solution.py:34
  118.2 50.3 %collective-permute-start.35 = (bf16[8,2,64,128]{3,2,1,0:T(8,128)(2,1)}, bf16[8,2,64,128]{3,2,1,0:T(8,128)(2,1)}, u32[]{:S(2)}, u32[]{:S(2)}) collective-permute-start(bf16[8,2,64,128]{3,2,1,0:T(8,128)(2,1)} %get-tuple-element.197.x0.g), channel_id=1, source_target_pairs={{0,1},{1,0},{2,3},{3,2},{4,5},{5,4},{6,7},{7,6},{8,9},{9,8},{10,11... | collective-permute-start | bytes 786440 | tf_op jit(solution)/shard_map/ppermute | solution.py:34
  118.2 30.2 %collective-permute-start.36 = (bf16[8,2,64,128]{3,2,1,0:T(8,128)(2,1)}, bf16[8,2,64,128]{3,2,1,0:T(8,128)(2,1)}, u32[]{:S(2)}, u32[]{:S(2)}) collective-permute-start(bf16[8,2,64,128]{3,2,1,0:T(8,128)(2,1)} %get-tuple-element.197.x0.g), channel_id=1, source_target_pairs={{0,3},{1,2},{2,1},{3,0},{4,7},{5,6},{6,5},{7,4},{8,11},{9,10},{10,... | collective-permute-start | bytes 786440 | tf_op jit(solution)/shard_map/ppermute | solution.py:34
  118.9 34.6 %collective-permute-start.29 = (bf16[8,2,64,128]{3,2,1,0:T(8,128)(2,1)}, bf16[8,2,64,128]{3,2,1,0:T(8,128)(2,1)}, u32[]{:S(2)}, u32[]{:S(2)}) collective-permute-start(bf16[8,2,64,128]{3,2,1,0:T(8,128)(2,1)} %shard_map.503.x0), channel_id=1, source_target_pairs={{0,1},{1,0},{2,3},{3,2},{4,5},{5,4},{6,7},{7,6},{8,9},{9,8},{10,11... | collective-permute-start | bytes 786440 | tf_op jit(solution)/shard_map/ppermute | solution.py:34
  142.3 16.8 %collective-permute-start.31 = (bf16[8,2,64,128]{3,2,1,0:T(8,128)(2,1)}, bf16[8,2,64,128]{3,2,1,0:T(8,128)(2,1)}, u32[]{:S(2)}, u32[]{:S(2)}) collective-permute-start(bf16[8,2,64,128]{3,2,1,0:T(8,128)(2,1)} %collective-permute-done.30.x2), channel_id=1, source_target_pairs={{0,1},{1,0},{2,3},{3,2},{4,5},{5,4},{6,7},{7,6},{8,9},{9,8},{10,11... | collective-permute-start | bytes 786440 | tf_op jit(solution)/shard_map/ppermute | solution.py:34
  148.4 20.1 %collective-permute-start.37 = (bf16[8,2,64,128]{3,2,1,0:T(8,128)(2,1)}, bf16[8,2,64,128]{3,2,1,0:T(8,128)(2,1)}, u32[]{:S(2)}, u32[]{:S(2)}) collective-permute-start(bf16[8,2,64,128]{3,2,1,0:T(8,128)(2,1)} %collective-permute-done.36.x2), channel_id=1, source_target_pairs={{0,1},{1,0},{2,3},{3,2},{4,5},{5,4},{6,7},{7,6},{8,9},{9,8},{10,11... | collective-permute-start | bytes 786440 | tf_op jit(solution)/shard_map/ppermute | solution.py:34
  163.0 13.0 %collective-permute-start.34 = (bf16[3,64,512]{2,1,0:T(8,128)(2,1)}, bf16[3,64,512]{2,1,0:T(8,128)(2,1)}, u32[]{:S(2)}, u32[]{:S(2)}) collective-permute-start(bf16[3,64,512]{2,1,0:T(8,128)(2,1)} %get-tuple-element.190), channel_id=1, source_target_pairs={{0,24},{4,28},{8,16},{12,20},{16,8},{20,12},{24,0},{28,4},{1,25},{... | collective-permute-start | bytes 589832 | tf_op jit(solution)/shard_map/ppermute | solution.py:34
  163.0 16.1 %collective-permute-start.33 = (bf16[3,64,512]{2,1,0:T(8,128)(2,1)}, bf16[3,64,512]{2,1,0:T(8,128)(2,1)}, u32[]{:S(2)}, u32[]{:S(2)}) collective-permute-start(bf16[3,64,512]{2,1,0:T(8,128)(2,1)} %get-tuple-element.191), channel_id=1, source_target_pairs={{0,16},{4,20},{8,24},{12,28},{16,0},{20,4},{24,8},{28,12},{1,17},{... | collective-permute-start | bytes 589832 | tf_op jit(solution)/shard_map/ppermute | solution.py:34
  164.5 14.6 %collective-permute-start.32 = (bf16[3,64,512]{2,1,0:T(8,128)(2,1)}, bf16[3,64,512]{2,1,0:T(8,128)(2,1)}, u32[]{:S(2)}, u32[]{:S(2)}) collective-permute-start(bf16[3,64,512]{2,1,0:T(8,128)(2,1)} %get-tuple-element.192), channel_id=1, source_target_pairs={{0,8},{4,12},{8,0},{12,4},{16,24},{20,28},{24,16},{28,20},{1,9},{5... | collective-permute-start | bytes 589832 | tf_op jit(solution)/shard_map/ppermute | solution.py:34
  170.9 10.2 %collective-permute-start.40 = (bf16[64,512]{1,0:T(8,128)(2,1)S(1)}, bf16[64,512]{1,0:T(8,128)(2,1)S(1)}, u32[]{:S(2)}, u32[]{:S(2)}) collective-permute-start(bf16[64,512]{1,0:T(8,128)(2,1)S(1)} %get-tuple-element.204), channel_id=1, source_target_pairs={{0,24},{4,28},{8,16},{12,20},{16,8},{20,12},{24,0},{28,4},{1,25},{... | collective-permute-start | bytes 196616 | tf_op jit(solution)/shard_map/ppermute | solution.py:34
  171.0 10.2 %collective-permute-start.39 = (bf16[64,512]{1,0:T(8,128)(2,1)S(1)}, bf16[64,512]{1,0:T(8,128)(2,1)S(1)}, u32[]{:S(2)}, u32[]{:S(2)}) collective-permute-start(bf16[64,512]{1,0:T(8,128)(2,1)S(1)} %get-tuple-element.205), channel_id=1, source_target_pairs={{0,16},{4,20},{8,24},{12,28},{16,0},{20,4},{24,8},{28,12},{1,17},{... | collective-permute-start | bytes 196616 | tf_op jit(solution)/shard_map/ppermute | solution.py:34
  224.6 10.1 %collective-permute-start.45 = (bf16[4,64,512]{2,1,0:T(8,128)(2,1)S(1)}, bf16[4,64,512]{2,1,0:T(8,128)(2,1)S(1)}, u32[]{:S(2)}, u32[]{:S(2)}) collective-permute-start(bf16[4,64,512]{2,1,0:T(8,128)(2,1)S(1)} %get-tuple-element.184), channel_id=1, source_target_pairs={{0,24},{4,28},{8,16},{12,20},{16,8},{20,12},{24,0},{28,4},{1,25},{... | collective-permute-start | bytes 786440 | tf_op jit(solution)/shard_map/ppermute | solution.py:34
  227.3 12.9 %collective-permute-start.44 = (bf16[4,64,512]{2,1,0:T(8,128)(2,1)S(1)}, bf16[4,64,512]{2,1,0:T(8,128)(2,1)S(1)}, u32[]{:S(2)}, u32[]{:S(2)}) collective-permute-start(bf16[4,64,512]{2,1,0:T(8,128)(2,1)S(1)} %get-tuple-element.185), channel_id=1, source_target_pairs={{0,16},{4,20},{8,24},{12,28},{16,0},{20,4},{24,8},{28,12},{1,17},{... | collective-permute-start | bytes 786440 | tf_op jit(solution)/shard_map/ppermute | solution.py:34
  227.3 13.3 %collective-permute-start.43 = (bf16[4,64,512]{2,1,0:T(8,128)(2,1)S(1)}, bf16[4,64,512]{2,1,0:T(8,128)(2,1)S(1)}, u32[]{:S(2)}, u32[]{:S(2)}) collective-permute-start(bf16[4,64,512]{2,1,0:T(8,128)(2,1)S(1)} %get-tuple-element.183), channel_id=1, source_target_pairs={{0,8},{4,12},{8,0},{12,4},{16,24},{20,28},{24,16},{28,20},{1,9},{5... | collective-permute-start | bytes 786440 | tf_op jit(solution)/shard_map/ppermute | solution.py:34
  228.2 21.4 %collective-permute-start.87 = (bf16[2,64,128]{2,1,0:T(8,128)(2,1)S(1)}, bf16[2,64,128]{2,1,0:T(8,128)(2,1)}, u32[]{:S(2)}, u32[]{:S(2)}) collective-permute-start(bf16[2,64,128]{2,1,0:T(8,128)(2,1)S(1)} %add_convert_fusion.2), channel_id=1, source_target_pairs={{0,24},{4,28},{8,16},{12,20},{16,8},{20,12},{24,0},{28,4},{1,25},{... | collective-permute-start | bytes 98312 | tf_op jit(solution)/shard_map/ppermute | solution.py:34
  230.9 18.8 %collective-permute-start.86 = (bf16[2,64,128]{2,1,0:T(8,128)(2,1)S(1)}, bf16[2,64,128]{2,1,0:T(8,128)(2,1)}, u32[]{:S(2)}, u32[]{:S(2)}) collective-permute-start(bf16[2,64,128]{2,1,0:T(8,128)(2,1)S(1)} %add_convert_fusion.2), channel_id=1, source_target_pairs={{0,16},{4,20},{8,24},{12,28},{16,0},{20,4},{24,8},{28,12},{1,17},{... | collective-permute-start | bytes 98312 | tf_op jit(solution)/shard_map/ppermute | solution.py:34
  234.8 14.9 %collective-permute-start.85 = (bf16[2,64,128]{2,1,0:T(8,128)(2,1)S(1)}, bf16[2,64,128]{2,1,0:T(8,128)(2,1)}, u32[]{:S(2)}, u32[]{:S(2)}) collective-permute-start(bf16[2,64,128]{2,1,0:T(8,128)(2,1)S(1)} %add_convert_fusion.2), channel_id=1, source_target_pairs={{0,8},{4,12},{8,0},{12,4},{16,24},{20,28},{24,16},{28,20},{1,9},{5... | collective-permute-start | bytes 98312 | tf_op jit(solution)/shard_map/ppermute | solution.py:34
  247.6 13.8 %collective-permute-start.49 = (bf16[2,8,2,64,128]{4,3,2,1,0:T(8,128)(2,1)}, bf16[2,8,2,64,128]{4,3,2,1,0:T(8,128)(2,1)}, u32[]{:S(2)}, u32[]{:S(2)}) collective-permute-start(bf16[2,8,2,64,128]{4,3,2,1,0:T(8,128)(2,1)} %slice.154), channel_id=1, source_target_pairs={{0,1},{1,0},{2,3},{3,2},{4,5},{5,4},{6,7},{7,6},{8,9},{9,8},{10,11... | collective-permute-start | bytes 1572872 | tf_op jit(solution)/shard_map/ppermute | solution.py:34
  262.5 10.2 %collective-permute-start.50 = (bf16[8,2,64,128]{3,2,1,0:T(8,128)(2,1)S(1)}, bf16[8,2,64,128]{3,2,1,0:T(8,128)(2,1)S(1)}, u32[]{:S(2)}, u32[]{:S(2)}) collective-permute-start(bf16[8,2,64,128]{3,2,1,0:T(8,128)(2,1)S(1)} %fusion.9), channel_id=1, source_target_pairs={{0,3},{1,2},{2,1},{3,0},{4,7},{5,6},{6,5},{7,4},{8,11},{9,10},{10,... | collective-permute-start | bytes 786440 | tf_op jit(solution)/shard_map/ppermute | solution.py:34
  266.9 22.3 %collective-permute-start.47 = (bf16[8,2,64,128]{3,2,1,0:T(8,128)(2,1)}, bf16[8,2,64,128]{3,2,1,0:T(8,128)(2,1)}, u32[]{:S(2)}, u32[]{:S(2)}) collective-permute-start(bf16[8,2,64,128]{3,2,1,0:T(8,128)(2,1)} %get-tuple-element.60.x0), channel_id=1, source_target_pairs={{0,3},{1,2},{2,1},{3,0},{4,7},{5,6},{6,5},{7,4},{8,11},{9,10},{10,... | collective-permute-start | bytes 786440 | tf_op jit(solution)/shard_map/ppermute | solution.py:34
  274.3 14.9 %collective-permute-start.53 = (f32[4,128]{1,0:T(4,128)S(1)}, f32[4,128]{1,0:T(4,128)S(1)}, u32[]{:S(2)}, u32[]{:S(2)}) collective-permute-start(f32[4,128]{1,0:T(4,128)S(1)} %add.408), channel_id=1, source_target_pairs={{0,16},{4,20},{8,24},{12,28},{16,0},{20,4},{24,8},{28,12},{1,17},{... | collective-permute-start | bytes 6152 | tf_op jit(solution)/shard_map/ppermute | solution.py:34
  277.0 12.3 %collective-permute-start.54 = (f32[4,128]{1,0:T(4,128)S(1)}, f32[4,128]{1,0:T(4,128)S(1)}, u32[]{:S(2)}, u32[]{:S(2)}) collective-permute-start(f32[4,128]{1,0:T(4,128)S(1)} %add.408), channel_id=1, source_target_pairs={{0,24},{4,28},{8,16},{12,20},{16,8},{20,12},{24,0},{28,4},{1,25},{... | collective-permute-start | bytes 6152 | tf_op jit(solution)/shard_map/ppermute | solution.py:34
  277.0 12.3 %collective-permute-start.52 = (f32[4,128]{1,0:T(4,128)S(1)}, f32[4,128]{1,0:T(4,128)S(1)}, u32[]{:S(2)}, u32[]{:S(2)}) collective-permute-start(f32[4,128]{1,0:T(4,128)S(1)} %add.408), channel_id=1, source_target_pairs={{0,8},{4,12},{8,0},{12,4},{16,24},{20,28},{24,16},{28,20},{1,9},{5... | collective-permute-start | bytes 6152 | tf_op jit(solution)/shard_map/ppermute | solution.py:34
  279.2 23.6 %collective-permute-start.46 = (bf16[8,2,64,128]{3,2,1,0:T(8,128)(2,1)}, bf16[8,2,64,128]{3,2,1,0:T(8,128)(2,1)}, u32[]{:S(2)}, u32[]{:S(2)}) collective-permute-start(bf16[8,2,64,128]{3,2,1,0:T(8,128)(2,1)} %get-tuple-element.60.x0), channel_id=1, source_target_pairs={{0,1},{1,0},{2,3},{3,2},{4,5},{5,4},{6,7},{7,6},{8,9},{9,8},{10,11... | collective-permute-start | bytes 786440 | tf_op jit(solution)/shard_map/ppermute | solution.py:34
  289.2 13.6 %collective-permute-start.48 = (bf16[8,2,64,128]{3,2,1,0:T(8,128)(2,1)}, bf16[8,2,64,128]{3,2,1,0:T(8,128)(2,1)}, u32[]{:S(2)}, u32[]{:S(2)}) collective-permute-start(bf16[8,2,64,128]{3,2,1,0:T(8,128)(2,1)} %collective-permute-done.47.x2), channel_id=1, source_target_pairs={{0,1},{1,0},{2,3},{3,2},{4,5},{5,4},{6,7},{7,6},{8,9},{9,8},{10,11... | collective-permute-start | bytes 786440 | tf_op jit(solution)/shard_map/ppermute | solution.py:34
  291.8 20.9 %collective-permute-start.56 = (bf16[8,2,64,128]{3,2,1,0:T(8,128)(2,1)}, bf16[8,2,64,128]{3,2,1,0:T(8,128)(2,1)}, u32[]{:S(2)}, u32[]{:S(2)}) collective-permute-start(bf16[8,2,64,128]{3,2,1,0:T(8,128)(2,1)} %get-tuple-element.64.x0.r), channel_id=1, source_target_pairs={{0,3},{1,2},{2,1},{3,0},{4,7},{5,6},{6,5},{7,4},{8,11},{9,10},{10,... | collective-permute-start | bytes 786440 | tf_op jit(solution)/shard_map/ppermute | solution.py:34
  296.5 11.0 %collective-permute-start.58 = (bf16[1,2,64,128]{3,2,1,0:T(8,128)(2,1)}, bf16[1,2,64,128]{3,2,1,0:T(8,128)(2,1)}, u32[]{:S(2)}, u32[]{:S(2)}) collective-permute-start(bf16[1,2,64,128]{3,2,1,0:T(8,128)(2,1)} %get-tuple-element.202), channel_id=1, source_target_pairs={{0,4},{4,8},{8,12},{12,16},{16,20},{20,24},{24,28},{1,5},{5,9},{9,... | collective-permute-start | bytes 98312 | tf_op jit(solution)/shard_map/ppermute | solution.py:67
  304.6 20.6 %collective-permute-start.55 = (bf16[8,2,64,128]{3,2,1,0:T(8,128)(2,1)}, bf16[8,2,64,128]{3,2,1,0:T(8,128)(2,1)S(1)}, u32[]{:S(2)}, u32[]{:S(2)}) collective-permute-start(bf16[8,2,64,128]{3,2,1,0:T(8,128)(2,1)} %get-tuple-element.64.x0.r), channel_id=1, source_target_pairs={{0,1},{1,0},{2,3},{3,2},{4,5},{5,4},{6,7},{7,6},{8,9},{9,8},{10,11... | collective-permute-start | bytes 786440 | tf_op jit(solution)/shard_map/ppermute | solution.py:34
  309.4 8.5 %collective-permute-start.61 = (bf16[2,2,64,128]{3,2,1,0:T(8,128)(2,1)S(1)}, bf16[2,2,64,128]{3,2,1,0:T(8,128)(2,1)S(1)}, u32[]{:S(2)}, u32[]{:S(2)}) collective-permute-start(bf16[2,2,64,128]{3,2,1,0:T(8,128)(2,1)S(1)} %constant_dynamic-update-slice_fusion.4.e0), channel_id=1, source_target_pairs={{0,3},{1,2},{2,1},{3,0},{4,7},{5,6},{6,5},{7,4},{8,11},{9,10},{10,... | collective-permute-start | bytes 196616 | tf_op jit(solution)/shard_map/ppermute | solution.py:34
  312.7 12.5 %collective-permute-start.57 = (bf16[8,2,64,128]{3,2,1,0:T(8,128)(2,1)}, bf16[8,2,64,128]{3,2,1,0:T(8,128)(2,1)S(1)}, u32[]{:S(2)}, u32[]{:S(2)}) collective-permute-start(bf16[8,2,64,128]{3,2,1,0:T(8,128)(2,1)} %collective-permute-done.56.x2), channel_id=1, source_target_pairs={{0,1},{1,0},{2,3},{3,2},{4,5},{5,4},{6,7},{7,6},{8,9},{9,8},{10,11... | collective-permute-start | bytes 786440 | tf_op jit(solution)/shard_map/ppermute | solution.py:34
  315.7 8.4 %collective-permute-start.60 = (bf16[2,2,64,128]{3,2,1,0:T(8,128)(2,1)S(1)}, bf16[2,2,64,128]{3,2,1,0:T(8,128)(2,1)S(1)}, u32[]{:S(2)}, u32[]{:S(2)}) collective-permute-start(bf16[2,2,64,128]{3,2,1,0:T(8,128)(2,1)S(1)} %constant_dynamic-update-slice_fusion.4.e0), channel_id=1, source_target_pairs={{0,1},{1,0},{2,3},{3,2},{4,5},{5,4},{6,7},{7,6},{8,9},{9,8},{10,11... | collective-permute-start | bytes 196616 | tf_op jit(solution)/shard_map/ppermute | solution.py:34
  317.8 7.3 %collective-permute-start.62 = (bf16[2,2,64,128]{3,2,1,0:T(8,128)(2,1)S(1)}, bf16[2,2,64,128]{3,2,1,0:T(8,128)(2,1)S(1)}, u32[]{:S(2)}, u32[]{:S(2)}) collective-permute-start(bf16[2,2,64,128]{3,2,1,0:T(8,128)(2,1)S(1)} %collective-permute-done.61.e2), channel_id=1, source_target_pairs={{0,1},{1,0},{2,3},{3,2},{4,5},{5,4},{6,7},{7,6},{8,9},{9,8},{10,11... | collective-permute-start | bytes 196616 | tf_op jit(solution)/shard_map/ppermute | solution.py:34
  334.9 33.4 %collective-permute-start.80 = (bf16[13,4,64,128]{3,2,1,0:T(8,128)(2,1)S(1)}, bf16[13,4,64,128]{3,2,1,0:T(8,128)(2,1)S(1)}, u32[]{:S(2)}, u32[]{:S(2)}) collective-permute-start(bf16[13,4,64,128]{3,2,1,0:T(8,128)(2,1)S(1)} %dynamic-slice_bitcast_fusion), channel_id=1, source_target_pairs={{0,4},{4,0},{8,12},{12,8},{16,20},{20,16},{24,28},{28,24},{1,5},{5... | collective-permute-start | bytes 2555912 | tf_op jit(solution)/shard_map/ppermute | solution.py:34
  337.7 26.8 %collective-permute-start.68 = (bf16[8,2,64,128]{3,2,1,0:T(8,128)(2,1)S(1)}, bf16[8,2,64,128]{3,2,1,0:T(8,128)(2,1)S(1)}, u32[]{:S(2)}, u32[]{:S(2)}) collective-permute-start(bf16[8,2,64,128]{3,2,1,0:T(8,128)(2,1)S(1)} %get-tuple-element.69.x0.r), channel_id=1, source_target_pairs={{0,1},{1,0},{2,3},{3,2},{4,5},{5,4},{6,7},{7,6},{8,9},{9,8},{10,11... | collective-permute-start | bytes 786440 | tf_op jit(solution)/shard_map/ppermute | solution.py:34
  337.8 13.0 %collective-permute-start.69 = (bf16[8,2,64,128]{3,2,1,0:T(8,128)(2,1)S(1)}, bf16[8,2,64,128]{3,2,1,0:T(8,128)(2,1)S(1)}, u32[]{:S(2)}, u32[]{:S(2)}) collective-permute-start(bf16[8,2,64,128]{3,2,1,0:T(8,128)(2,1)S(1)} %get-tuple-element.69.x0.r), channel_id=1, source_target_pairs={{0,3},{1,2},{2,1},{3,0},{4,7},{5,6},{6,5},{7,4},{8,11},{9,10},{10,... | collective-permute-start | bytes 786440 | tf_op jit(solution)/shard_map/ppermute | solution.py:34
  340.2 7.5 %collective-permute-start.71 = (bf16[1,2,64,128]{3,2,1,0:T(8,128)(2,1)S(1)}, bf16[1,2,64,128]{3,2,1,0:T(8,128)(2,1)S(1)}, u32[]{:S(2)}, u32[]{:S(2)}) collective-permute-start(bf16[1,2,64,128]{3,2,1,0:T(8,128)(2,1)S(1)} %get-tuple-element.200), channel_id=1, source_target_pairs={{0,4},{4,8},{8,12},{12,16},{16,20},{20,24},{24,28},{1,5},{5,9},{9,... | collective-permute-start | bytes 98312 | tf_op jit(solution)/shard_map/ppermute | solution.py:67
  350.8 13.7 %collective-permute-start.70 = (bf16[8,2,64,128]{3,2,1,0:T(8,128)(2,1)S(1)}, bf16[8,2,64,128]{3,2,1,0:T(8,128)(2,1)S(1)}, u32[]{:S(2)}, u32[]{:S(2)}) collective-permute-start(bf16[8,2,64,128]{3,2,1,0:T(8,128)(2,1)S(1)} %collective-permute-done.69.x2), channel_id=1, source_target_pairs={{0,1},{1,0},{2,3},{3,2},{4,5},{5,4},{6,7},{7,6},{8,9},{9,8},{10,11... | collective-permute-start | bytes 786440 | tf_op jit(solution)/shard_map/ppermute | solution.py:34
  352.1 8.1 %collective-permute-start.74 = (bf16[2,2,64,128]{3,2,1,0:T(8,128)(2,1)S(1)}, bf16[2,2,64,128]{3,2,1,0:T(8,128)(2,1)S(1)}, u32[]{:S(2)}, u32[]{:S(2)}) collective-permute-start(bf16[2,2,64,128]{3,2,1,0:T(8,128)(2,1)S(1)} %constant_dynamic-update-slice_fusion.6.e0), channel_id=1, source_target_pairs={{0,3},{1,2},{2,1},{3,0},{4,7},{5,6},{6,5},{7,4},{8,11},{9,10},{10,... | collective-permute-start | bytes 196616 | tf_op jit(solution)/shard_map/ppermute | solution.py:34
  361.6 27.4 %collective-permute-start.88 = (bf16[9,4,64,128]{3,2,1,0:T(8,128)(2,1)}, bf16[9,4,64,128]{3,2,1,0:T(8,128)(2,1)}, u32[]{:S(2)}, u32[]{:S(2)}) collective-permute-start(bf16[9,4,64,128]{3,2,1,0:T(8,128)(2,1)} %dynamic-slice_bitcast_fusion.1), channel_id=1, source_target_pairs={{0,4},{4,0},{8,12},{12,8},{16,20},{20,16},{24,28},{28,24},{1,5},{5... | collective-permute-start | bytes 1769480 | tf_op jit(solution)/shard_map/ppermute | solution.py:34
  369.9 7.4 %collective-permute-start.78 = (f32[5,128]{1,0:T(8,128)S(1)}, f32[5,128]{1,0:T(8,128)S(1)}, u32[]{:S(2)}, u32[]{:S(2)}) collective-permute-start(f32[5,128]{1,0:T(8,128)S(1)} %fusion.44), channel_id=1, source_target_pairs={{0,16},{4,20},{8,24},{12,28},{16,0},{20,4},{24,8},{28,12},{1,17},{... | collective-permute-start | bytes 7688 | tf_op jit(solution)/shard_map/ppermute | solution.py:34
  374.4 9.3 %collective-permute-start.83 = (bf16[13,64,128]{2,1,0:T(8,128)(2,1)}, bf16[13,64,128]{2,1,0:T(8,128)(2,1)S(1)}, u32[]{:S(2)}, u32[]{:S(2)}) collective-permute-start(bf16[13,64,128]{2,1,0:T(8,128)(2,1)} %get-tuple-element.187), channel_id=1, source_target_pairs={{0,24},{4,28},{8,16},{12,20},{16,8},{20,12},{24,0},{28,4},{1,25},{... | collective-permute-start | bytes 638984 | tf_op jit(solution)/shard_map/ppermute | solution.py:34
  377.3 9.9 %collective-permute-start.82 = (bf16[13,64,128]{2,1,0:T(8,128)(2,1)}, bf16[13,64,128]{2,1,0:T(8,128)(2,1)S(1)}, u32[]{:S(2)}, u32[]{:S(2)}) collective-permute-start(bf16[13,64,128]{2,1,0:T(8,128)(2,1)} %get-tuple-element.188), channel_id=1, source_target_pairs={{0,16},{4,20},{8,24},{12,28},{16,0},{20,4},{24,8},{28,12},{1,17},{... | collective-permute-start | bytes 638984 | tf_op jit(solution)/shard_map/ppermute | solution.py:34
  377.4 9.8 %collective-permute-start.81 = (bf16[13,64,128]{2,1,0:T(8,128)(2,1)S(1)}, bf16[13,64,128]{2,1,0:T(8,128)(2,1)S(1)}, u32[]{:S(2)}, u32[]{:S(2)}) collective-permute-start(bf16[13,64,128]{2,1,0:T(8,128)(2,1)S(1)} %get-tuple-element.186), channel_id=1, source_target_pairs={{0,8},{4,12},{8,0},{12,4},{16,24},{20,28},{24,16},{28,20},{1,9},{5... | collective-permute-start | bytes 638984 | tf_op jit(solution)/shard_map/ppermute | solution.py:34
  392.1 8.0 %collective-permute-start.91 = (bf16[9,64,128]{2,1,0:T(8,128)(2,1)}, bf16[9,64,128]{2,1,0:T(8,128)(2,1)}, u32[]{:S(2)}, u32[]{:S(2)}) collective-permute-start(bf16[9,64,128]{2,1,0:T(8,128)(2,1)} %get-tuple-element.194), channel_id=1, source_target_pairs={{0,24},{4,28},{8,16},{12,20},{16,8},{20,12},{24,0},{28,4},{1,25},{... | collective-permute-start | bytes 442376 | tf_op jit(solution)/shard_map/ppermute | solution.py:34
  393.9 8.4 %collective-permute-start.90 = (bf16[9,64,128]{2,1,0:T(8,128)(2,1)}, bf16[9,64,128]{2,1,0:T(8,128)(2,1)}, u32[]{:S(2)}, u32[]{:S(2)}) collective-permute-start(bf16[9,64,128]{2,1,0:T(8,128)(2,1)} %get-tuple-element.195), channel_id=1, source_target_pairs={{0,16},{4,20},{8,24},{12,28},{16,0},{20,4},{24,8},{28,12},{1,17},{... | collective-permute-start | bytes 442376 | tf_op jit(solution)/shard_map/ppermute | solution.py:34
  413.3 7.2 %collective-permute-start.97 = (f32[8,128]{1,0:T(8,128)S(1)}, f32[8,128]{1,0:T(8,128)S(1)}, u32[]{:S(2)}, u32[]{:S(2)}) collective-permute-start(f32[8,128]{1,0:T(8,128)S(1)} %add_add_fusion.1), channel_id=1, source_target_pairs={{0,2},{1,3},{2,0},{3,1},{4,6},{5,7},{6,4},{7,5},{8,10},{9,11},{10,... | collective-permute-start | bytes 12296 | tf_op jit(solution)/shard_map/ppermute | solution.py:34
  (162 other events, 1766.7 us)
Sparse Core Ops, SparseCore 0:
  10.6 26.7 all-gather.4
  39.9 26.7 all-gather.6
  69.1 23.9 all-gather.8
  118.5 62.8 all-gather.10

commit v2 on v1

v2 whole, which is shorter than its diff:
```python
import functools
import math

import jax
import jax.numpy as jnp
from jax import lax
from jax.experimental import pallas as pl
from jax.experimental.pallas import tpu as pltpu
from jax.sharding import PartitionSpec as P

C = 512
GROUPS = 32
HEAD_DIM = 64
EMB = 2048
DCTX = 2048
IMG_H = 64
IMG_W = 64
CLIP_TOK = 4
STEP = 10
CTX = 81
CTX_PAD = 128
GROUP_SIZE = C // GROUPS
GROUP_COUNT = IMG_H * IMG_W * GROUP_SIZE
LOG2E = 1.4426950408889634
BF = jnp.bfloat16
F32 = jnp.float32
ORDER = (0, 1, 3, 2)

clip_limit = 1.0


def swap(x, axis, distance):
    size = lax.axis_size(axis)
    return lax.ppermute(x, axis, [(i, i ^ distance) for i in range(size)])


def rows_sum(x, first=None):
    size = lax.axis_size("rows")
    x = x + swap(x, "rows", 1) if first is None else first
    step = 2
    while step < size:
        if step * 4 <= size:
            one, two, three = (swap(x, "rows", step * k) for k in (1, 2, 3))
            x = (x + one) + (two + three)
            step *= 4
        else:
            x = x + swap(x, "rows", step)
            step *= 2
    return x


def chan_blocks(x, *beside):
    far = swap(x, "chan", 3)
    near = swap(x, "chan", 1)
    return (x, near, far, swap(after(far, *beside), "chan", 1))


def rims(top, bottom):
    size = lax.axis_size("rows")
    up = [(i, i + 1) for i in range(size - 1)]
    down = [(j, i) for i, j in up]
    return lax.ppermute(bottom, "rows", up), lax.ppermute(top, "rows", down)


def after(x, *earlier):
    return lax.optimization_barrier((x, *earlier))[0]


def pick(x, index, axis=0):
    return lax.dynamic_index_in_dim(x, index, axis, keepdims=False)


def weight_scatter(mine, other):
    count, _, *rest = mine[0].shape
    shape = (sum(a.shape[1] for a in mine), *rest)
    total, *low = local_call(
        scatter_kernel,
        [out(shape, F32)] + [out(shape, BF)] * (count - 1),
        *mine,
        *other,
    )
    return [total] + [swap(low[k - 1], "rows", 2 * k) for k in range(1, count)]


class Far:
    def __init__(self, array):
        self.array = array


def near_rows(*arrays):
    return tuple(a.reshape(math.prod(a.shape[:-1]), a.shape[-1]) for a in arrays)


def far_rows(*arrays):
    return tuple(Far(a.reshape(math.prod(a.shape[:-1]), a.shape[-1])) for a in arrays)


def local_call(kernel, outs, *args, scratch=(), copies=0, flops=0, limit=50):
    arrays = [a.array if isinstance(a, Far) else a for a in args]

    def spec(a):
        if isinstance(a, Far):
            return pl.BlockSpec(memory_space=pl.ANY)
        return pl.BlockSpec(memory_space=pltpu.SMEM if a.dtype == jnp.int32 else pltpu.VMEM)

    size = sum(math.prod(a.shape) * a.dtype.itemsize for a in (*arrays, *outs))
    scratch = list(scratch)
    if copies:
        scratch.append(pltpu.SemaphoreType.DMA((copies,)))
    return pl.pallas_call(
        kernel,
        out_shape=tuple(outs),
        in_specs=[spec(a) for a in args],
        out_specs=tuple(pl.BlockSpec(memory_space=pltpu.VMEM) for _ in outs),
        scratch_shapes=scratch,
        compiler_params=pltpu.CompilerParams(vmem_limit_bytes=(56 if copies else limit) * 1024 * 1024),
        cost_estimate=pl.CostEstimate(flops=1, bytes_accessed=1, transcendentals=0),
    )(*arrays)


def begin(sems, *moves):
    started = []
    for i, (source, place) in enumerate(moves):
        copy = pltpu.make_async_copy(source, place, sems.at[i])
        copy.start()
        started.append(copy)
    return started


def fetch(sems, *moves):
    for copy in begin(sems, *moves):
        copy.wait()


def lanes_of(xs, j):
    width = xs.shape[1] // 4
    return xs.at[:, j * width : (j + 1) * width]


def block_moves(xs, blocks):
    return [(x, lanes_of(xs, j)) for j, x in enumerate(blocks)]


def out(shape, dtype):
    return jax.ShapeDtypeStruct(shape, dtype)


def nn(a, b):
    return lax.dot_general(a, b, (((1,), (0,)), ((), ())), preferred_element_type=F32)


def nt(a, b):
    return lax.dot_general(a, b, (((1,), (1,)), ((), ())), preferred_element_type=F32)


def group_mean(x):
    width = x.shape[1]
    left = lax.broadcasted_iota(jnp.int32, (width, width), 0) // GROUP_SIZE
    right = lax.broadcasted_iota(jnp.int32, (width, width), 1) // GROUP_SIZE
    same = (left == right).astype(F32)
    total = lax.dot_general(
        x, same, (((1,), (0,)), ((), ())), precision=lax.Precision.HIGHEST, preferred_element_type=F32
    )
    return total * (1.0 / GROUP_COUNT)


def moments(sums, images):
    means = group_mean(sums)
    average = means[:images]
    return average, lax.rsqrt(means[images:] - average * average + 1e-05)


def image_of(ref, b):
    rows, _, width, channels = ref.shape
    return ref[:, b].reshape(rows * width, channels)


def put_image(ref, b, value):
    rows, _, width, channels = ref.shape
    ref[:, b] = value.reshape(rows, width, channels).astype(ref.dtype)


def column_sum(x):
    return jnp.sum(x, axis=0, keepdims=True)


def silu(z):
    return z * jax.nn.sigmoid(z)


def silu_slope(z):
    s = jax.nn.sigmoid(z)
    return s * (1.0 + z * (1.0 - s))


def put_sums(sums, b, images, v, w):
    sums[b : b + 1] = column_sum(v)
    sums[images + b : images + b + 1] = column_sum(v * w)


def start_kernel(pixels, sums):
    images = pixels.shape[1]
    for b in range(images):
        v = image_of(pixels, b)
        put_sums(sums, b, images, v, v)


def edge_of(ref, b):
    return ref[0, b]


def put_wide(o, b, zi, before, value, behind):
    rows, _, width, channels = o.shape
    top = (zi[2] > 0).astype(F32)
    bottom = (zi[3] > 0).astype(F32)
    o[0, b] = (before * top).astype(o.dtype)
    o[1 : rows - 1, b] = value.reshape(rows - 2, width, channels).astype(o.dtype)
    o[rows - 1, b] = (behind * bottom).astype(o.dtype)


def act_one_kernel(zi, x, before, behind, sums, vec, o):
    images = x.shape[1]
    average, inverse = moments(sums[0 : 2 * images], images)
    for b in range(images):

        def active(v):
            xhat = (v - average[b : b + 1]) * inverse[b : b + 1]
            return silu(xhat * vec[0:1] + vec[1:2])

        put_wide(
            o, b, zi, active(edge_of(before, b)), active(image_of(x, b)), active(edge_of(behind, b))
        )


def shaped_of(xhat, mod, vec, b, images):
    scale = 1.0 + (mod[b : b + 1] + vec[12:13])
    shift = mod[images + b : images + b + 1] + vec[13:14]
    return (xhat * vec[3:4] + vec[4:5]) * scale + shift


def act_two_kernel(zi, x, before, behind, sums, mod, vec, o):
    images = x.shape[1]
    average, inverse = moments(sums[...], images)
    for b in range(images):

        def active(v):
            xhat = (v - average[b : b + 1]) * inverse[b : b + 1]
            return silu(shaped_of(xhat, mod, vec, b, images))

        put_wide(
            o, b, zi, active(edge_of(before, b)), active(image_of(x, b)), active(edge_of(behind, b))
        )


def norm_three_kernel(x, sums, vec, o):
    images = x.shape[1]
    average, inverse = moments(sums[...], images)
    for b in range(images):
        xhat = (image_of(x, b) - average[b : b + 1]) * inverse[b : b + 1]
        put_image(o, b, xhat * vec[6:7] + vec[7:8])


def rows_of(z, j, width):
    return pl.ds(pl.multiple_of((z ^ ORDER[j]) * width, width), width)


def shifted(x, by, width):
    length = x.shape[0]
    column = lax.broadcasted_iota(jnp.int32, x.shape, 0) % width
    moved = pltpu.roll(x, by % length, 0)
    return jnp.where(column == (0 if by == 1 else width - 1), 0.0, moved)


def conv_taps(blocks, w, extra, zi, xs, rows, span, width, flipped):
    z = zi[0]
    if extra:
        w_far, (w, sems) = w, extra
        fetch(sems, (w_far.at[0:9], w), *block_moves(xs, blocks))
    else:
        for j, x in enumerate(blocks):
            lanes_of(xs, j)[...] = x[...]
    channels = w.shape[2]
    parts = []
    for dx in range(3):
        total = None
        for dy in range(3):
            at = (2 - dy if flipped else dy) * span
            a = xs[at : at + rows * span, :]
            taps = [w[3 * dy + dx, rows_of(z, j, channels), :] for j in range(4)]
            if flipped:
                term = nt(a, jnp.concatenate(taps, axis=1))
            else:
                term = nn(a, jnp.concatenate(taps, axis=0))
            total = term if total is None else total + term
        parts.append(total)
    if flipped:
        parts = parts[::-1]
    return parts[1] + shifted(parts[0], 1, width) + shifted(parts[2], -1, width)


def conv_one_kernel(zi, x0, x1, x2, x3, w_far, vec, hidden, sums, top, bottom, xs, *extra):
    rows, images, width, channels = hidden.shape
    blocks = (x0, x1, x2, x3)
    result = conv_taps(
        blocks, w_far, extra, zi, xs, rows, images * width, width, False
    ) + vec[2:3]
    hidden[...] = result.reshape(hidden.shape)
    for b in range(images):
        v = image_of(hidden, b)
        put_sums(sums, b, images, v, v)
    top[...] = hidden[0:1]
    bottom[...] = hidden[rows - 1 : rows]


def conv_two_kernel(zi, x0, x1, x2, x3, w_far, vec, pixels, residual, sums, xs, *extra):
    rows, images, width, channels = residual.shape
    blocks = (x0, x1, x2, x3)
    result = conv_taps(
        blocks, w_far, extra, zi, xs, rows, images * width, width, False
    ) + vec[5:6]
    residual[...] = pixels[...] + result.reshape(residual.shape)
    for b in range(images):
        v = image_of(residual, b)
        put_sums(sums, b, images, v, v)


def conv_two_back_kernel(
    zi, x0, x1, x2, x3, w_far, vec, hidden, stats, mod, shaped_grad, sums, top, bottom, xs, *extra
):
    rows, images, width, channels = hidden.shape
    blocks = (x0, x1, x2, x3)
    result = conv_taps(
        blocks, w_far, extra, zi, xs, rows, images * width, width, True
    )
    shaped_grad[...] = result.reshape(shaped_grad.shape)
    average, inverse = moments(stats[...], images)
    for b in range(images):
        xhat = (image_of(hidden, b) - average[b : b + 1]) * inverse[b : b + 1]
        g = image_of(shaped_grad, b) * silu_slope(shaped_of(xhat, mod, vec, b, images))
        put_image(shaped_grad, b, g)
        put_sums(sums, b, images, g, xhat)
    top[...] = shaped_grad[0:1]
    bottom[...] = shaped_grad[rows - 1 : rows]


def conv_one_back_kernel(
    zi, x0, x1, x2, x3, w_far, vec, pixels, stats, normed_grad, sums, xs, *extra
):
    rows, images, width, channels = pixels.shape
    blocks = (x0, x1, x2, x3)
    result = conv_taps(
        blocks, w_far, extra, zi, xs, rows, images * width, width, True
    )
    normed_grad[...] = result.reshape(normed_grad.shape)
    average, inverse = moments(stats[0 : 2 * images], images)
    for b in range(images):
        xhat = (image_of(pixels, b) - average[b : b + 1]) * inverse[b : b + 1]
        g = image_of(normed_grad, b) * silu_slope(xhat * vec[0:1] + vec[1:2])
        put_image(normed_grad, b, g)
        put_sums(sums, b, images, g, xhat)


def put_shares(box, zi, tap, grad):
    share, channels = box.shape[3:]
    each = channels // share
    for j in range(4):
        for i in range(each):
            at = j * channels + i * share
            row = (zi[0] ^ ORDER[j]) * each + i
            box[(row & 1) ^ zi[4], (row >> 1) ^ zi[1], tap] = grad[at : at + share].astype(box.dtype)


def conv_weights(zi, xs, r, box):
    rows, images, width, channels = r.shape
    rows = rows - 2
    span = images * width
    turned = xs[...].T
    wide = r[1 : rows + 1].reshape(rows * span, channels).astype(F32)
    three = jnp.concatenate(
        [shifted(wide, -1, width).astype(BF), wide.astype(BF), shifted(wide, 1, width).astype(BF)],
        axis=1,
    )
    for dy in range(3):
        grad = nn(turned[:, dy * span : (dy + rows) * span], three)
        for dx in range(3):
            put_shares(box, zi, 3 * dy + dx, grad[:, dx * channels : (dx + 1) * channels])


def weights_two_kernel(
    zi, x0, x1, x2, x3, r, n0, n1, n2, n3, grads, att, c0, c1, c2, c3, loss, mine, other, xs, ns, cs, box, sems
):
    blocks = begin(
        sems,
        *block_moves(xs, (x0, x1, x2, x3)),
        *block_moves(ns, (n0, n1, n2, n3)),
        *block_moves(cs, (c0, c1, c2, c3)),
    )
    for copy in blocks[:4]:
        copy.wait()
    conv_weights(zi, xs, r, box)
    for copy in blocks[4:]:
        copy.wait()
    rows, images, width, columns = grads.shape
    channels = att.shape[3]
    pixels = rows * images * width
    grad = nn(ns[...].T, grads[...].reshape(pixels, columns))
    for s in range(3):
        put_shares(box, zi, 9 + s, grad[:, s * channels : (s + 1) * channels])
    scale = jnp.concatenate([loss[b : b + 1] for b in range(images)], axis=0)
    scale = jnp.concatenate([scale] * 4, axis=1)[None, :, None, :]
    low = (cs[...].reshape(rows, images, width, 4 * channels).astype(F32) * scale).astype(BF)
    grad = nn(att[...].reshape(pixels, channels).T, low.reshape(pixels, 4 * channels))
    by_output = [grad[:, j * channels : (j + 1) * channels] for j in range(4)]
    put_shares(box, zi, 12, jnp.concatenate(by_output, axis=0))
    mine[...] = box[0]
    other[...] = box[1]


def weights_one_kernel(zi, x0, x1, x2, x3, r, mine, other, xs, box, sems):
    fetch(sems, *block_moves(xs, (x0, x1, x2, x3)))
    conv_weights(zi, xs, r, box)
    mine[...] = box[0]
    other[...] = box[1]


def scatter_kernel(mine_two, mine_one, other_two, other_one, total, *low):
    at = 0
    for mine, other in ((mine_two, other_two), (mine_one, other_one)):
        taps = slice(at, at + mine.shape[1])
        at += mine.shape[1]
        total[taps] = mine[0].astype(F32) + other[0].astype(F32)
        for k, o in enumerate(low):
            o[taps] = (mine[k + 1].astype(F32) + other[k + 1].astype(F32)).astype(BF)


def put_heads(scratch, leading, value, b, heads):
    turned = value.T.astype(scratch.dtype)
    for h in range(heads):
        scratch[b * heads + h, leading] = turned[h * HEAD_DIM : (h + 1) * HEAD_DIM]


def project_kernel(*refs, base):
    zi, w_far, vec, blocks = refs[0], refs[1], refs[2], refs[3:7]
    outs, (xs, w, scratch, sems) = refs[7:-4], refs[-4:]
    fetch(sems, (w_far.at[base : base + 3], w), *block_moves(xs, blocks))
    tokens = outs[0].shape[2]
    channels = w.shape[2]
    heads = channels // HEAD_DIM
    images = len(outs) // heads
    rows = xs.shape[0] // (images * IMG_W)
    a = xs[...]
    for s in range(3):
        rows_in = [w[s, rows_of(zi[0], j, channels), :] for j in range(4)]
        value = nn(a, jnp.concatenate(rows_in, axis=0))
        if s != 1:
            at = 8 if s == 0 else 9
            value = value + vec[at : at + 1]
        split = value.reshape(rows, images, IMG_W, channels)
        for b in range(images):
            put_heads(scratch, s, split[:, b].reshape(tokens, channels), b, heads)
    for k, o in enumerate(outs):
        o[...] = scratch[zi[1] ^ k]


def output_grad_kernel(*refs, tap):
    zi, w_far, cots, loss = refs[0], refs[1], refs[2:6], refs[6]
    outs, (xs, w, scratch, sems) = refs[7:-4], refs[-4:]
    fetch(sems, (w_far.at[tap : tap + 1], w), *block_moves(xs, cots))
    tokens = outs[0].shape[1]
    channels = w.shape[2]
    heads = channels // HEAD_DIM
    images = len(outs) // heads
    rows = xs.shape[0] // (images * IMG_W)
    lanes = [w[0, rows_of(zi[0], j, channels), :] for j in range(4)]
    turned = jnp.concatenate(lanes, axis=1)
    wide = xs[...].reshape(rows, images, IMG_W, 4 * channels)
    for b in range(images):
        scale = jnp.concatenate([loss[b : b + 1]] * 4, axis=1)
        low = (wide[:, b].reshape(tokens, 4 * channels).astype(F32) * scale).astype(BF)
        put_heads(scratch, 0, nt(low, turned), b, heads)
    for k, o in enumerate(outs):
        o[...] = scratch[zi[1] ^ k, 0]


def attention_kernel(*refs, chunk, count, block):
    live, ctx_ref = refs[0], refs[1]
    mine, grads, sibs = (refs[2 + i * count : 2 + (i + 1) * count] for i in range(3))
    oq_ref, own_ref, other_ref = refs[2 + 3 * count : 5 + 3 * count]
    q_s, do_s, kt_s, k_s, v_s, s_s, p_s, acc_s = refs[5 + 3 * count :]
    step = pl.program_id(0)
    last = pl.num_programs(0) - 1
    tokens = mine[0].shape[2]
    depth = HEAD_DIM
    queries = block
    half = count * tokens
    keys = 2 * half
    extra = ctx_ref.shape[2]

    @pl.when(step == 0)
    def _():
        for k in range(count):
            lanes = slice(k * tokens, (k + 1) * tokens)
            q_s[:, lanes] = mine[k][0]
            do_s[:, lanes] = grads[k][...]
            kt_s[:, :, lanes] = mine[k][1:3]
            kt_s[:, :, half + k * tokens : half + (k + 1) * tokens] = sibs[k][1:3]
        kt_s[:, :, keys:] = ctx_ref[...]
        k_s[...] = kt_s[0].T
        v_s[...] = kt_s[1].T
        acc_s[...] = jnp.zeros_like(acc_s)

    here = pl.ds(pl.multiple_of(step * block, block), block)
    q = q_s[:, here]
    do = do_s[:, here]
    spans = [(i * chunk, chunk) for i in range(keys // chunk)] + [(keys, extra)]
    highest = None
    for at, size in spans:
        s = nn(k_s[at : at + size], q)
        if at == keys:
            position = lax.broadcasted_iota(jnp.int32, s.shape, 0)
            s = jnp.where(position < live[0], s, -1e30)
        s_s[at : at + size] = s
        top = jnp.max(s.reshape(size // 8, 8, queries), axis=0)
        highest = top if highest is None else jnp.maximum(highest, top)
    factor = 0.125 * LOG2E
    peak = jnp.max(highest, axis=0, keepdims=True) * factor
    weight_sum = jnp.zeros((8, queries), F32)
    mixture = jnp.zeros((depth, queries), F32)
    for at, size in spans:
        p = jnp.exp2(s_s[at : at + size] * factor - peak)
        weight_sum = weight_sum + jnp.sum(p.reshape(size // 8, 8, queries), axis=0)
        low = p.astype(BF)
        p_s[at : at + size] = low
        mixture = mixture + nn(kt_s[1, :, at : at + size], low)
    inverse = 1.0 / jnp.sum(weight_sum, axis=0, keepdims=True)
    attended = mixture * inverse
    oq_ref[0] = attended.astype(BF)
    delta = jnp.sum(do.astype(F32) * attended, axis=0, keepdims=True)
    do_scaled = (do.astype(F32) * inverse).astype(BF)
    q_scaled = (q.astype(F32) * (inverse * 0.125)).astype(BF)
    query_grad = jnp.zeros((depth, queries), F32)
    for at, size in spans:
        dprob = nn(v_s[at : at + size], do)
        low = p_s[at : at + size]
        dscore = (low.astype(F32) * (dprob - delta)).astype(BF)
        query_grad = query_grad + nn(kt_s[0, :, at : at + size], dscore)
        acc_s[0, :, at : at + size] += nt(q_scaled, dscore)
        acc_s[1, :, at : at + size] += nt(do_scaled, low)
    oq_ref[1] = (query_grad * (inverse * 0.125)).astype(BF)

    @pl.when(step == last)
    def _():
        own_ref[:, :, 0:half] = acc_s[:, :, 0:half].astype(BF)
        own_ref[:, :, half:] = acc_s[:, :, keys:].astype(BF)
        other_ref[...] = acc_s[:, :, half:].astype(BF)


def attention(live, ctx, mine, grads, sibs):
    count = len(mine)
    depth, tokens = grads[0].shape
    queries = count * tokens
    total = 2 * queries + ctx.shape[2]
    block = min(512, queries)
    chunk = min(1024, 2 * queries)

    def whole(a):
        return pl.BlockSpec(a.shape, lambda i: (0,) * len(a.shape))

    outs = (
        out((2, depth, queries), BF),
        out((2, depth, queries + ctx.shape[2]), BF),
        out((2, depth, queries + ctx.shape[2]), BF),
    )
    arrays = (ctx, *mine, *grads, *sibs)
    return pl.pallas_call(
        functools.partial(attention_kernel, chunk=chunk, count=count, block=block),
        grid=(queries // block,),
        in_specs=[pl.BlockSpec(memory_space=pltpu.SMEM)] + [whole(a) for a in arrays],
        out_specs=(
            pl.BlockSpec((2, depth, block), lambda i: (0, 0, i)),
            whole(outs[1]),
            whole(outs[2]),
        ),
        out_shape=outs,
        scratch_shapes=[
            pltpu.VMEM((depth, queries), BF),
            pltpu.VMEM((depth, queries), BF),
            pltpu.VMEM((2, depth, total), BF),
            pltpu.VMEM((total, depth), BF),
            pltpu.VMEM((total, depth), BF),
            pltpu.VMEM((total, block), F32),
            pltpu.VMEM((total, block), BF),
            pltpu.VMEM((2, depth, total), F32),
        ],
        compiler_params=pltpu.CompilerParams(
            vmem_limit_bytes=56 * 1024 * 1024, dimension_semantics=("arbitrary",)
        ),
        cost_estimate=pl.CostEstimate(
            flops=12 * depth * queries * total, bytes_accessed=8 * depth * total, transcendentals=queries * total
        ),
    )(live, *arrays)


def merge_kernel(oq_far, own_far, other_far, *refs):
    oq, own, other, sems = refs[-4:]
    outs = refs[:-4]
    count = len(outs) // 2
    fetch(sems, (oq_far, oq), (own_far, own), (other_far, other))
    tokens = oq.shape[2] // count
    both = (own[...].astype(F32) + other[...].astype(F32)).astype(BF)
    for k in range(count):
        lanes = slice(k * tokens, (k + 1) * tokens)
        outs[k][0] = oq[1, :, lanes]
        outs[k][1:3] = both[:, :, lanes]
        outs[count + k][:, 0:tokens] = oq[0, :, lanes]
        for s in range(2):
            at = tokens + s * CTX_PAD
            outs[count + k][:, at : at + CTX_PAD] = both[s, :, count * tokens :]


def back_project_kernel(*refs, base, count):
    zi, w_far, pieces = refs[0], refs[1], refs[2 : 2 + count]
    grads, part_own, part_near, part_cross, part_far, biases = refs[2 + count : -3]
    rec, w, sems = refs[-3:]
    fetch(sems, (w_far.at[base : base + 3], w))
    rows, images, width, channels = part_own.shape
    heads = channels // HEAD_DIM
    for k in range(count):
        rec[zi[1] ^ k] = pieces[k][...]
    for b in range(images):
        for s in range(3):
            blocks = [rec[b * heads + h, s] for h in range(heads)]
            value = jnp.concatenate(blocks, axis=0).T.reshape(rows, width, channels)
            grads[:, b, :, s * channels : (s + 1) * channels] = value
    flat = grads[...].reshape(rows * images * width, 3 * channels)
    for j, part in enumerate((part_own, part_near, part_far, part_cross)):
        at = rows_of(zi[0], j, channels)
        taps = jnp.concatenate([w[s, at, :] for s in range(3)], axis=1)
        part[...] = nt(flat, taps).astype(part.dtype).reshape(part.shape)
    wide = flat.astype(F32)
    biases[0:1] = column_sum(wide[:, 0:channels])
    biases[1:2] = column_sum(wide[:, 2 * channels :])


def attended_kernel(*refs):
    zi, pieces = refs[0], refs[1:-3]
    attended, ctx, rec = refs[-3:]
    rows, images, width, channels = attended.shape
    heads = channels // HEAD_DIM
    tokens = rows * width
    for k, piece in enumerate(pieces):
        rec[zi[1] ^ k] = piece[...]
    for b in range(images):
        blocks = [rec[b * heads + h, :, 0:tokens] for h in range(heads)]
        attended[:, b] = jnp.concatenate(blocks, axis=0).T.reshape(rows, width, channels)
    for q in range(len(pieces)):
        for s in range(2):
            at = tokens + s * CTX_PAD
            ctx[q, s] = rec[q, :, at : at + CTX_PAD]


def out_project_kernel(zi, x0, x1, x2, x3, w_far, vec, residual, o, xs, w, sems, *, tap):
    fetch(sems, (w_far.at[tap : tap + 1], w), *block_moves(xs, (x0, x1, x2, x3)))
    channels = w.shape[2]
    rows_in = [w[0, rows_of(zi[0], j, channels), :] for j in range(4)]
    value = nn(xs[...], jnp.concatenate(rows_in, axis=0)) + vec[10:11]
    o[...] = (residual[...] + value.reshape(o.shape)).astype(BF)


def back_three_sum_kernel(t0, t1, t2, residual, cotangent, loss, stats, g_out, sums, top, bottom):
    rows, images, width, channels = residual.shape
    average, inverse = moments(stats[...], images)
    for b in range(images):
        g = image_of(t0, b).astype(F32) + image_of(t1, b).astype(F32) + image_of(t2, b).astype(F32)
        xhat = (image_of(residual, b) - average[b : b + 1]) * inverse[b : b + 1]
        put_image(g_out, b, g)
        put_sums(sums, b, images, g, xhat)
        for edge, at in ((top, 0), (bottom, rows - 1)):
            edge[0, b, :, 0:channels] = g_out[at, b]
            edge[0, b, :, channels : 2 * channels] = residual[at, b]
            edge[0, b, :, 2 * channels :] = cotangent[at, b].astype(F32) * loss[b : b + 1]


def back_three_kernel(
    zi, g0, x0, c0, before, behind, stats, sums, vec, loss, residual_grad, low, bias
):
    images, channels = x0.shape[1], x0.shape[3]
    average, inverse = moments(stats[...], images)
    means = group_mean(sums[...] * vec[6:7])
    total = None
    for b in range(images):

        def back(g, x, c):
            xhat = (x - average[b : b + 1]) * inverse[b : b + 1]
            part = g * vec[6:7] - means[b : b + 1] - xhat * means[images + b : images + b + 1]
            return c + inverse[b : b + 1] * part

        def back_edge(edge):
            return back(*(edge[0, b, :, i * channels : (i + 1) * channels] for i in range(3)))

        cot = image_of(c0, b).astype(F32) * loss[b : b + 1]
        g = back(image_of(g0, b), image_of(x0, b), cot)
        put_image(residual_grad, b, g)
        put_wide(low, b, zi, back_edge(before), g, back_edge(behind))
        part = column_sum(g)
        total = part if total is None else total + part
    bias[...] = total


def back_two_kernel(zi, g0, g1, g2, x0, x1, x2, stats, sums, mod, vec, low, bias):
    images = x0.shape[1]
    average, inverse = moments(stats[...], images)
    gains = [vec[3:4] * (1.0 + (mod[b : b + 1] + vec[12:13])) for b in range(images)]
    means = group_mean(sums[0 : 2 * images] * jnp.concatenate(gains + gains, axis=0))
    total = None
    for b in range(images):

        def back(g, x):
            xhat = (x - average[b : b + 1]) * inverse[b : b + 1]
            part = g * gains[b] - means[b : b + 1] - xhat * means[images + b : images + b + 1]
            return inverse[b : b + 1] * part

        g = back(image_of(g0, b), image_of(x0, b))
        before = back(edge_of(g1, b), edge_of(x1, b))
        behind = back(edge_of(g2, b), edge_of(x2, b))
        put_wide(low, b, zi, before, g, behind)
        part = column_sum(g)
        total = part if total is None else total + part
    bias[...] = total


def back_one_kernel(g_in, pixels, stats, sums, vec, residual_grad, pixel_grad):
    images = pixels.shape[1]
    average, inverse = moments(stats[0 : 2 * images], images)
    means = group_mean(sums[0 : 2 * images] * vec[0:1])
    for b in range(images):
        xhat = (image_of(pixels, b) - average[b : b + 1]) * inverse[b : b + 1]
        scaled = image_of(g_in, b) * vec[0:1]
        g = inverse[b : b + 1] * (scaled - means[b : b + 1] - xhat * means[images + b : images + b + 1])
        put_image(pixel_grad, b, image_of(residual_grad, b) + g)


RATES = (0.02, 0.02, 0.08, 1.0, 0.02, 0.04, 1.0)


def finish_kernel(*refs):
    terms, (squares, sums, bias, two_sum, qkv_sum, out_sum, one_sum, payload) = refs[:-8], refs[-8:]
    squared = squares[...]
    at = 0
    for o in (two_sum, qkv_sum, out_sum, one_sum):
        taps = slice(at, at + o.shape[0])
        at += o.shape[0]
        total = terms[0][taps]
        for term in terms[1:]:
            total = total + term[taps].astype(F32)
        o[...] = total
        squared = squared + column_sum((total * total).reshape(-1, total.shape[-1]))
    count = sums.shape[0]
    payload[0:count] = sums[...]
    payload[count : count + 1] = bias[...]
    payload[count + 1 : count + 2] = squared
    payload[count + 2 :] = jnp.zeros((payload.shape[0] - count - 2, payload.shape[1]), F32)


def vector_kernel(third, second, sums_three, mod, vec, ctx, grad, squares):
    images = sums_three.shape[0] // 2

    def total(ref, at):
        return column_sum(ref[at : at + images])

    scale = 1.0 + (mod[0:images] + vec[12:13])
    shift_grad = second[0:images]
    crossed = second[images : 2 * images]
    scale_grad = crossed * vec[3:4] + shift_grad * vec[4:5]
    at = 2 * images
    rows = (
        total(third, images),
        total(third, 0),
        third[at : at + 1],
        column_sum(scale * crossed),
        column_sum(scale * shift_grad),
        second[at : at + 1],
        total(sums_three, images),
        total(sums_three, 0),
        second[at + 1 : at + 2],
        second[at + 2 : at + 3],
        second[at + 3 : at + 4],
        ctx[...],
        column_sum(scale_grad),
        column_sum(shift_grad),
    )
    squared = third[at + 1 : at + 2]
    for i, row in enumerate(rows):
        grad[i : i + 1] = row
        squared = squared + row * row
    squares[...] = jnp.broadcast_to(squared, squares.shape)


def update_kernel(*refs):
    count = len(RATES)
    squares, given = refs[0:4], refs[4 : 4 + 4 * count]
    made, held, sems = refs[4 + 4 * count : -4 * count - 1], refs[-4 * count - 1 : -1], refs[-1]
    arriving = begin(sems, *zip(given, held))
    near = squares[0][0:1] + squares[1][0:1]
    total = jnp.sum(near + (squares[2][0:1] + squares[3][0:1]), axis=1, keepdims=True)
    norm = jnp.sqrt(total)
    made[0][...] = jnp.broadcast_to(norm, made[0].shape)
    factor = jnp.minimum(1.0, clip_limit / norm)
    at = 1
    for i, rate in enumerate(RATES):
        for copy in arriving[4 * i : 4 * i + 4]:
            copy.wait()
        weight, moment, square, gradient = held[4 * i : 4 * i + 4]
        decay = 0.0 if i == count - 1 else 0.01
        scale = factor.reshape((1,) * (len(weight.shape) - 2) + factor.shape)
        new = adamw(weight[...], moment[...], square[...], gradient[...] * scale, rate, decay)
        for value in new:
            made[at][...] = value
            at += 1
        if i < count - 1:
            made[at][...] = new[0].astype(BF)
            at += 1


def adamw(weight, moment, square, gradient, step_rate, weight_decay):
    moment_new = 0.9 * moment + 0.1 * gradient
    square_new = 0.999 * square + 0.001 * gradient * gradient
    corrected = moment_new / (1.0 - 0.9**STEP)
    scaled = square_new / (1.0 - 0.999**STEP)
    weight_new = weight - step_rate * (
        corrected / (jnp.sqrt(scaled) + 1e-08) + weight_decay * weight
    )
    return (weight_new, moment_new, square_new)


def turn_moves(row_count, chan_count):
    share = row_count // chan_count
    return [
        (r * chan_count + z, (z * share + r % share) * chan_count + r // share)
        for r in range(row_count)
        for z in range(chan_count)
    ]


def turn_weights(x, row_count, chan_count):
    return lax.ppermute(x, ("rows", "chan"), turn_moves(row_count, chan_count))


def turn_back(x, row_count, chan_count):
    moves = [(j, i) for i, j in turn_moves(row_count, chan_count)]
    return lax.ppermute(x, ("rows", "chan"), moves)


def body(
    pixels,
    cotangent,
    loss_weight,
    timesteps,
    clip_embed,
    context,
    text_len,
    conv_first,
    conv_first_moment,
    conv_first_square,
    conv_second,
    conv_second_moment,
    conv_second_square,
    qkv_weight,
    qkv_weight_moment,
    qkv_weight_square,
    out_weight,
    out_weight_moment,
    out_weight_square,
    embed_weight,
    embed_weight_moment,
    embed_weight_square,
    context_weight,
    context_weight_moment,
    context_weight_square,
    vectors,
    vectors_moment,
    vectors_square,
):
    row_count = lax.axis_size("rows")
    chan_count = lax.axis_size("chan")
    row = lax.axis_index("rows")
    chan = lax.axis_index("chan")
    local_rows, images, width, channels = pixels.shape
    heads = channels // HEAD_DIM
    pairs = images * heads
    assert chan_count == 4 and row_count == 2 * pairs
    pair = row // 2
    zi = jnp.stack(
        [chan, pair, row, row_count - 1 - row, row % 2]
    ).astype(jnp.int32)
    act = (local_rows, images, width, channels)
    edge_rows = (local_rows + 2) * images * width
    xs = pltpu.VMEM((edge_rows, C), BF)
    flat = pltpu.VMEM((local_rows * images * width, C), BF)
    taps = pltpu.VMEM((9, C, channels), BF)
    conv_flops = 2 * local_rows * images * width * 9 * C * channels

    (sums,) = local_call(start_kernel, [out((2 * images, channels), F32)], pixels)
    loss = jnp.broadcast_to(loss_weight[:, None], (images, channels))
    cot = after(cotangent, sums)
    cot_near, cot_far = swap(cot, "chan", 1), swap(cot, "chan", 3)

    sums_shape = out((2 * images, channels), F32)
    tall = (local_rows + 2, images, width, channels)
    by_chip = sums + swap(sums, "rows", 1)
    stats_one = rows_sum(sums, by_chip)

    one_full = lax.all_gather(after(conv_first, by_chip).astype(BF), "rows", axis=1, tiled=True)
    two_low = after(conv_second, by_chip).astype(BF)
    qkv_low = jnp.transpose(after(qkv_weight, by_chip), (1, 0, 2)).astype(BF)
    out_low = out_weight.astype(BF)[None]
    pixel_rims = rims(pixels[:1], pixels[-1:])
    (active_one,) = local_call(
        act_one_kernel, [out(tall, BF)], zi, pixels, *pixel_rims, after(stats_one, cot_near, cot_far), vectors
    )
    out_turned = turn_weights(after(out_low, active_one), row_count, chan_count)
    blocks_one = chan_blocks(active_one)
    ctx_full = lax.all_gather(
        after(context_weight, blocks_one[2]).astype(BF), "rows", axis=0, tiled=True
    )

    share = EMB // row_count
    index = row * share + jnp.arange(share, dtype=jnp.int32)
    half_width = EMB // 2
    frequency = jnp.exp(-math.log(10000.0) * (index % half_width).astype(F32) / half_width)
    phases = after(timesteps, active_one).astype(F32)[:, None] * frequency[None, :]
    features = jnp.where(index[None, :] < half_width, jnp.cos(phases), jnp.sin(phases))
    clip_share = lax.dynamic_slice_in_dim(clip_embed, row * share, share, 1)
    embedding = jax.nn.silu(features + clip_share).astype(BF)
    both = jnp.eye(2, dtype=F32)[None, :, :, None]
    embed_rows = (embedding.astype(F32).T[:, None, None, :] * both).reshape(2 * share, 2 * images)
    modulation = jnp.einsum(
        "be,esc->sbc",
        embedding,
        after(embed_weight, active_one).astype(BF),
        preferred_element_type=F32,
    ).reshape(2 * images, channels)

    two_full = lax.all_gather(
        jnp.concatenate([two_low, qkv_low, out_low, after(out_turned, blocks_one[2])], axis=0),
        "rows",
        axis=1,
        tiled=True,
    )
    cot_cross = swap(after(cot_far, *blocks_one), "chan", 1)
    edge = out((1,) + act[1:], F32)
    hidden, sums, *edges = local_call(
        conv_one_kernel,
        [out(act, F32), sums_shape, edge, edge],
        zi,
        *near_rows(*blocks_one),
        one_full,
        vectors,
        scratch=[xs],
        flops=conv_flops,
    )
    hidden_rims = rims(*edges)
    stats_two = rows_sum(jnp.concatenate([after(sums, cot_cross), modulation], axis=0))
    stats_two, mod = stats_two[: 2 * images], stats_two[2 * images :]
    (active_two,) = local_call(
        act_two_kernel, [out(tall, BF)], zi, hidden, *hidden_rims, stats_two, mod, vectors
    )

    tokens = local_rows * width
    cots = (cotangent, cot_near, cot_far, after(cot_cross, active_two))
    grad_pieces = local_call(
        functools.partial(output_grad_kernel, tap=13),
        [out((HEAD_DIM, tokens), BF)] * pairs,
        zi,
        Far(two_full),
        *far_rows(*cots),
        loss,
        scratch=[
            flat,
            pltpu.VMEM((1, C, channels), BF),
            pltpu.VMEM((pairs, 1, HEAD_DIM, tokens), BF),
        ],
        copies=5,
    )
    blocks_two = chan_blocks(active_two, *grad_pieces)
    grad_pieces = [grad_pieces[0]] + [
        swap(grad_pieces[k], "rows", 2 * k) for k in range(1, pairs)
    ]

    residual, sums = local_call(
        conv_two_kernel,
        [out(act, F32), sums_shape],
        zi,
        *far_rows(*blocks_two),
        Far(two_full),
        after(vectors, *grad_pieces),
        pixels,
        scratch=[xs, taps],
        copies=5,
        flops=conv_flops,
    )
    stats_three = rows_sum(sums)
    (normed,) = local_call(norm_three_kernel, [out(act, BF)], residual, stats_three, vectors)
    blocks_three = chan_blocks(normed)

    image, head = pair // heads, pair % heads
    ctx_low = pick(context, image)
    ctx_projected = jnp.einsum("te,esc->sct", ctx_low, ctx_full, preferred_element_type=F32)
    ctx_bias = jnp.stack([jnp.zeros_like(vectors[11]), vectors[11]])[:, :, None]
    ctx_heads = lax.dynamic_slice_in_dim(ctx_projected + ctx_bias, head * HEAD_DIM, HEAD_DIM, 1)
    ctx_heads = jnp.pad(ctx_heads.astype(BF), ((0, 0), (0, 0), (0, CTX_PAD - CTX)))
    live = (CLIP_TOK + pick(text_len, image))[None].astype(jnp.int32)

    pieces = local_call(
        functools.partial(project_kernel, base=9),
        [out((3, HEAD_DIM, tokens), BF)] * pairs,
        zi,
        Far(two_full),
        after(vectors, ctx_heads),
        *far_rows(*blocks_three),
        scratch=[
            flat,
            pltpu.VMEM((3, C, channels), BF),
            pltpu.VMEM((pairs, 3, HEAD_DIM, tokens), BF),
        ],
        copies=5,
        flops=conv_flops // 3,
    )
    pieces = [pieces[0]] + [swap(pieces[k], "rows", 2 * k) for k in range(1, pairs)]
    siblings = [swap(piece, "rows", 1) for piece in pieces]

    turned = turn_weights(
        after(jnp.concatenate([two_low, conv_first.astype(BF)], axis=0), *siblings),
        row_count,
        chan_count,
    )

    out_query, own, other = attention(
        live, ctx_heads, pieces, grad_pieces, siblings
    )
    merged = local_call(
        merge_kernel,
        [out((3, HEAD_DIM, tokens), BF)] * pairs
        + [out((HEAD_DIM, tokens + 2 * CTX_PAD), BF)] * pairs,
        Far(out_query),
        Far(own),
        Far(swap(after(other, turned), "rows", 1)),
        scratch=[
            pltpu.VMEM(out_query.shape, BF),
            pltpu.VMEM(own.shape, BF),
            pltpu.VMEM(own.shape, BF),
        ],
        copies=3,
    )
    received = [merged[0]] + [swap(merged[k], "rows", 2 * k) for k in range(1, pairs)]

    grads, part_own, part_near, part_cross, part_far, qv_bias = local_call(
        functools.partial(back_project_kernel, base=9, count=pairs),
        [
            out((local_rows, images, width, 3 * channels), BF),
            out(act, F32),
            out(act, BF),
            out(act, BF),
            out(act, F32),
            out((2, channels), F32),
        ],
        zi,
        Far(two_full),
        *received,
        scratch=[
            pltpu.VMEM((pairs, 3, HEAD_DIM, tokens), BF),
            pltpu.VMEM((3, C, channels), BF),
        ],
        copies=1,
        flops=conv_flops // 3,
    )
    turned = after(turned, part_cross)
    two_turned = lax.all_gather(turned[:9], "rows", axis=1, tiled=True)
    one_turned = lax.all_gather(after(turned[9:], two_turned), "rows", axis=1, tiled=True)
    cross = swap(part_cross, "chan", 1)
    near = swap(part_near, "chan", 1)
    far = swap((part_far + cross.astype(F32)).astype(BF), "chan", 3)
    long_edge = out((1, images, width, 3 * channels), F32)
    late = [after(piece, part_cross) for piece in merged[pairs:]]
    late = [late[0]] + [swap(late[k], "rows", 2 * k) for k in range(1, pairs)]
    normed_grad, sums, *edges = local_call(
        back_three_sum_kernel,
        [out(act, F32), sums_shape, long_edge, long_edge],
        part_own,
        near,
        far,
        residual,
        cotangent,
        after(loss, *late),
        stats_three,
    )
    normed_rims = rims(*edges)
    sums_three = rows_sum(sums)
    residual_grad, residual_low, conv_two_bias = local_call(
        back_three_kernel,
        [out(act, F32), out(tall, BF), out((1, channels), F32)],
        zi,
        normed_grad,
        residual,
        cotangent,
        *normed_rims,
        stats_three,
        sums_three,
        vectors,
        loss,
    )
    attended, ctx_all = local_call(
        attended_kernel,
        [out(act, BF), out((pairs, 2, HEAD_DIM, CTX_PAD), BF)],
        zi,
        *late,
        scratch=[pltpu.VMEM((pairs, HEAD_DIM, tokens + 2 * CTX_PAD), BF)],
    )
    weights_scratch = [
        xs,
        flat,
        flat,
        pltpu.VMEM((2, pairs, 13, C // row_count, channels), BF),
    ]
    two_grads = local_call(
        weights_two_kernel,
        [out((pairs, 13, C // row_count, channels), BF)] * 2,
        zi,
        *far_rows(*blocks_two),
        residual_low,
        *far_rows(*blocks_three),
        grads,
        attended,
        *far_rows(*cots),
        loss,
        scratch=weights_scratch,
        copies=12,
        flops=conv_flops,
    )
    blocks = chan_blocks(residual_low, *two_grads)
    two_other = swap(two_grads[1], "rows", 1)
    shaped_grad, sums, *edges = local_call(
        conv_two_back_kernel,
        [out(act, F32), sums_shape, edge, edge],
        zi,
        *far_rows(*blocks),
        Far(two_turned),
        vectors,
        hidden,
        stats_two,
        mod,
        scratch=[xs, taps],
        copies=5,
        flops=conv_flops,
    )
    shaped_rims = rims(*edges)
    out_bias = jnp.sum(
        cotangent.astype(F32) * loss_weight[None, :, None, None], axis=(0, 1, 2)
    )[None]
    second = rows_sum(jnp.concatenate([sums, conv_two_bias, qv_bias, out_bias], axis=0))
    sums_two = second[: 2 * images]
    hidden_low, conv_one_bias = local_call(
        back_two_kernel,
        [out(tall, BF), out((1, channels), F32)],
        zi,
        shaped_grad,
        *shaped_rims,
        hidden,
        *hidden_rims,
        stats_two,
        sums_two,
        mod,
        vectors,
    )
    one_grads = local_call(
        weights_one_kernel,
        [out((pairs, 9, C // row_count, channels), BF)] * 2,
        zi,
        *far_rows(*blocks_one),
        hidden_low,
        scratch=[xs, pltpu.VMEM((2, pairs, 9, C // row_count, channels), BF)],
        copies=4,
        flops=conv_flops,
    )
    blocks = chan_blocks(hidden_low, *one_grads)
    terms = weight_scatter(
        (two_grads[0], one_grads[0]), (two_other, swap(one_grads[1], "rows", 1))
    )
    normed_one_grad, sums = local_call(
        conv_one_back_kernel,
        [out(act, F32), sums_shape],
        zi,
        *far_rows(*blocks),
        Far(one_turned),
        vectors,
        pixels,
        stats_one,
        scratch=[xs, taps],
        copies=5,
        flops=conv_flops,
    )
    attended_blocks = chan_blocks(after(attended, sums))
    (activations,) = local_call(
        functools.partial(out_project_kernel, tap=12),
        [out(act, BF)],
        zi,
        *far_rows(*attended_blocks),
        Far(two_full),
        vectors,
        residual,
        scratch=[flat, pltpu.VMEM((1, C, channels), BF)],
        copies=5,
    )

    shift_grad, crossed = sums_two[:images], sums_two[images : 2 * images]
    scale_grad = crossed * vectors[3] + shift_grad * vectors[4]
    embed_grad = jnp.dot(
        embed_rows,
        jnp.concatenate((scale_grad, shift_grad), axis=0),
        precision=lax.Precision.HIGHEST,
    )
    ctx_all = ctx_all[:, :, :, :CTX].reshape(images, heads, 2, HEAD_DIM, CTX)
    ctx_share = DCTX // row_count
    ctx_rows = lax.dynamic_slice_in_dim(context, row * ctx_share, ctx_share, 2)
    context_grad = jnp.einsum(
        "bte,bhsdt->eshd", ctx_rows, ctx_all, preferred_element_type=F32
    ).reshape(2 * ctx_share, channels)
    ctx_value_bias = jnp.sum(ctx_all[:, :, 1].astype(F32), axis=(0, 3)).reshape(1, channels)

    squared = jnp.zeros((1, channels), F32)
    for member in (embed_grad, context_grad):
        squared = squared + jnp.sum((member * member).reshape(-1, channels), axis=0)[None]
    conv_share = (9, C // row_count, channels)
    two_sum, qkv_sum, out_sum, one_sum, payload = local_call(
        finish_kernel,
        [
            out(conv_share, F32),
            out((3,) + conv_share[1:], F32),
            out((1,) + conv_share[1:], F32),
            out(conv_share, F32),
            out((-(-(2 * images + 2) // 8) * 8, channels), F32),
        ],
        *terms,
        squared,
        sums,
        conv_one_bias,
    )
    out_sum = turn_back(out_sum, row_count, chan_count)[0]
    third = rows_sum(payload)
    (pixel_grad,) = local_call(
        back_one_kernel,
        [out(act, F32)],
        normed_one_grad,
        pixels,
        stats_one,
        third,
        vectors,
        residual_grad,
    )
    vector_grad, squares = local_call(
        vector_kernel,
        [out((14, channels), F32), out((8, channels), F32)],
        third,
        second,
        sums_three,
        mod,
        vectors,
        ctx_value_bias,
    )
    squares = [squares] + [swap(squares, "chan", k) for k in (1, 2, 3)]
    squares[0] = after(squares[0], activations, pixel_grad)

    def turn(x):
        return jnp.transpose(x, (1, 0, 2))

    def flat_rows(x):
        return x.reshape(-1, x.shape[2])

    weights = (
        (conv_first, conv_first_moment, conv_first_square, one_sum),
        (conv_second, conv_second_moment, conv_second_square, two_sum),
        (turn(qkv_weight), turn(qkv_weight_moment), turn(qkv_weight_square), qkv_sum),
        (out_weight, out_weight_moment, out_weight_square, out_sum),
        (flat_rows(embed_weight), flat_rows(embed_weight_moment), flat_rows(embed_weight_square), embed_grad),
        (
            flat_rows(context_weight),
            flat_rows(context_weight_moment),
            flat_rows(context_weight_square),
            context_grad,
        ),
        (vectors, vectors_moment, vectors_square, vector_grad),
    )
    outs = [out((1, channels), F32)]
    for weight, *_ in weights:
        outs += [out(weight.shape, F32)] * 3 + [out(weight.shape, BF)]
    operands = [a for group in weights for a in group]
    norm, *updated = local_call(
        update_kernel,
        outs[:-1],
        *squares,
        *(Far(a) for a in operands),
        scratch=[pltpu.VMEM(a.shape, F32) for a in operands],
        copies=len(operands),
    )
    for i in (8, 9, 10, 11):
        updated[i] = turn(updated[i])
    for i in range(16, 24):
        updated[i] = updated[i].reshape(-1, 2, channels)
    return (activations, pixel_grad, norm[0, 0], *updated)


def solution(mesh):
    act = P("rows", None, None, "chan")
    conv = P(None, "rows", "chan")
    wide = P("rows", None, "chan")
    flat = P("rows", "chan")
    vec = P(None, "chan")
    weights = (conv, conv, wide, flat, wide, wide)
    in_specs = (act, act) + (P(),) * 5 + tuple(s for w in weights for s in (w,) * 3) + (vec,) * 3
    out_specs = (act, act, P()) + tuple(s for w in weights for s in (w,) * 4) + (vec,) * 3
    return jax.shard_map(body, mesh=mesh, in_specs=in_specs, out_specs=out_specs, check_vma=False)
```

time: 448 us -> 407 us (0.908)
  Pallas kernels: 76.2 us -> 105 us
  other arithmetic: 33.7 us -> 9.19 us
  starting transfers between devices: 148 us -> 130 us
  local copies, waits for them, and re-layouts: 38.8 us -> 24.1 us
  between operations: 23.2 us -> 16.2 us
    pallas_call x19 -> x24, Pallas kernels: 39.6 us -> 68 us  [local_call(): pl.pallas_call(kernel, out_shape=tuple(outs), in_specs=[spec(a) for a in...]
    ppermute x89 -> x73, starting transfers between devices: 135 us -> 114 us  [swap(): return lax.ppermute(x, axis, [(i, i ^ distance) for i in range(size)])]
    convert_element_type x15 -> x8, other arithmetic: 13.6 us -> 3.57 us  [the longest x1 1.65 us: body(): after(conv_first, by_chip).astype(BF)]
    reduce_sum x11 -> x2, other arithmetic: 10.1 us -> 0.36 us  [the longest x1 0.25 us: body(): jnp.sum(cotangent.astype(F32) * loss_weight[None, :, None, None], axis=(0...]
    ppermute x89 -> x73, waiting for transfers between devices: 114 us -> 105 us  [swap(): return lax.ppermute(x, axis, [(i, i ^ distance) for i in range(size)])]
    ppermute x10 -> x11, waiting for transfers between devices: 1.05 us -> 7.91 us  [the longest x8 7.9 us: rims(): return (lax.ppermute(bottom, 'rows', up), lax.ppermute(top, 'rows', down))]
    slice x12 -> x3, local copies, waits for them, and re-layouts: 6.72 us -> 0.74 us  [the longest x1 0.73 us: body(): turned[9:]]
    squeeze x8 -> x0, local copies, waits for them, and re-layouts: 5.43 us -> none  [the longest x6 3.5 us: pick(): return lax.dynamic_index_in_dim(x, index, axis, keepdims=False)]
  transfers between devices with their start and end apart: 103 -> 89, of which waited for: 46 -> 38; matrix products, arithmetic and copies ran while one was open for 11% -> 5% of each run, Pallas kernels for 16% -> 22%
where the time goes in v2:
time: 407 us; the launch traced here: 401 us
  starting transfers between devices  130 us (32%)
  waiting for transfers between devices  113 us (28%)
  Pallas kernels  105 us (26%)
  local copies, waits for them, and re-layouts  24.1 us (6%)
  between operations  16.2 us (4%)
  other arithmetic  9.19 us (2%)
    ppermute x73, starting transfers between devices, swap(): return lax.ppermute(x, axis, [(i, i ^ distance) for i in range(size)])  114 us
    ppermute x73, waiting for transfers between devices, swap(): return lax.ppermute(x, axis, [(i, i ^ distance) for i in range(size)])  105 us
    pallas_call x24, Pallas kernels, local_call(): pl.pallas_call(kernel, out_shape=tuple(outs), in_specs=[spec(a) for a in...  68 us
    pallas_call x1, Pallas kernels, attention(): pl.pallas_call(functools.partial(attention_kernel, chunk=chunk, count=cou...  36.9 us
    unnamed x214, local copies, waits for them, and re-layouts  14.6 us
    ppermute x8, starting transfers between devices, rims(): return (lax.ppermute(bottom, 'rows', up), lax.ppermute(top, 'rows', down))  13 us
  transfers between devices with their start and end apart: 89, of which 38 were waited for; matrix products, arithmetic and copies ran while one was open for 5% of the time, Pallas kernels for 22%

profile of v2, /device:TPU:0, one launch (start us, length us, event | category | flops | bytes accessed | tf_op | source)
XLA Modules:
  0.0 400.7 jit_solution(998118675891214745)
XLA Ops:
  11.5 3.0 collective-permute-start.6
  14.5 2.5 collective-permute-start.7
  24.4 5.0 %collective-permute-done.7 = bf16[8,2,64,128]{3,2,1,0:T(8,128)(2,1)} collective-permute-done((bf16[8,2,64,128]{3,2,1,0:T(8,128)(2,1)}, bf16[8,2,64,128]{3,2,1,0:T(8,128)(2,1)}, u32[]{:S(2)}, u32[]{:S(2)}) %collective-permute-start.7) | collective-permute-done | bytes 262176 | tf_op jit(solution)/shard_map/ppermute | solution.py:34
  32.5 10.1 %collective-permute-done.8 = bf16[10,2,64,128]{3,2,1,0:T(8,128)(2,1)S(1)} collective-permute-done((bf16[10,2,64,128]{3,2,1,0:T(8,128)(2,1)S(1)}, bf16[10,2,64,128]{3,2,1,0:T(8,128)(2,1)S(1)}, u32[]{:S(2)}, u32[]{:S(2)}) %collective-permute-start.8) | collective-permute-done | bytes 327712 | tf_op jit(solution)/shard_map/ppermute | solution.py:34
  43.5 6.1 %collective-permute-start.10 = (bf16[10,2,64,128]{3,2,1,0:T(8,128)(2,1)S(1)}, bf16[10,2,64,128]{3,2,1,0:T(8,128)(2,1)S(1)}, u32[]{:S(2)}, u32[]{:S(2)}) collective-permute-start(bf16[10,2,64,128]{3,2,1,0:T(8,128)(2,1)S(1)} %shard_map.500), channel_id=1, source_target_pairs={{0,1},{1,0},{2,3},{3,2},{4,5},{5,4},{6,7},{7,6},{8,9},{9,8},{10,11... | collective-permute-start | bytes 983048 | tf_op jit(solution)/shard_map/ppermute | solution.py:34
  50.4 7.8 %collective-permute-done.10 = bf16[10,2,64,128]{3,2,1,0:T(8,128)(2,1)S(1)} collective-permute-done((bf16[10,2,64,128]{3,2,1,0:T(8,128)(2,1)S(1)}, bf16[10,2,64,128]{3,2,1,0:T(8,128)(2,1)S(1)}, u32[]{:S(2)}, u32[]{:S(2)}) %collective-permute-start.10) | collective-permute-done | bytes 327712 | tf_op jit(solution)/shard_map/ppermute | solution.py:34
  58.2 6.0 %collective-permute-done.11 = bf16[10,2,64,128]{3,2,1,0:T(8,128)(2,1)S(1)} collective-permute-done((bf16[10,2,64,128]{3,2,1,0:T(8,128)(2,1)S(1)}, bf16[10,2,64,128]{3,2,1,0:T(8,128)(2,1)S(1)}, u32[]{:S(2)}, u32[]{:S(2)}) %collective-permute-start.11) | collective-permute-done | bytes 327712 | tf_op jit(solution)/shard_map/ppermute | solution.py:34
  64.2 1.7 collective-permute-start.14
  68.9 3.2 shard_map.501
  73.4 3.2 collective-permute-start.17
  80.5 1.8 collective-permute-start.13
  82.4 2.5 collective-permute-done.13.behind.x2
  88.2 3.3 shard_map.503
  91.5 4.8 %collective-permute-done.20 = bf16[10,2,64,128]{3,2,1,0:T(8,128)(2,1)S(1)} collective-permute-done((bf16[10,2,64,128]{3,2,1,0:T(8,128)(2,1)S(1)}, bf16[10,2,64,128]{3,2,1,0:T(8,128)(2,1)S(1)}, u32[]{:S(2)}, u32[]{:S(2)}) %collective-permute-start.20) | collective-permute-done | bytes 327712 | tf_op jit(solution)/shard_map/ppermute | solution.py:34
  96.3 7.8 %collective-permute-start.21 = (bf16[10,2,64,128]{3,2,1,0:T(8,128)(2,1)S(1)}, bf16[10,2,64,128]{3,2,1,0:T(8,128)(2,1)S(1)}, u32[]{:S(2)}, u32[]{:S(2)}) collective-permute-start(bf16[10,2,64,128]{3,2,1,0:T(8,128)(2,1)S(1)} %collective-permute-done.20), channel_id=1, source_target_pairs={{0,1},{1,0},{2,3},{3,2},{4,5},{5,4},{6,7},{7,6},{8,9},{9,8},{10,11... | collective-permute-start | bytes 983048 | tf_op jit(solution)/shard_map/ppermute | solution.py:34
  104.1 3.0 collective-permute-start.22
  110.0 2.3 collective-permute-done.23.refs_8_
  114.2 6.2 %shard_map.504 = (f32[8,2,64,128]{3,2,1,0:T(8,128)}, f32[4,128]{1,0:T(4,128)}) custom-call(s32[5]{0:T(128)} %copy-done.34, bf16[1280,128]{1,0:T(8,128)(2,1)} %bitcast.102, bf16[1280,128]{1,0:T(8,128)(2,1)} %bitcast.121, bf16[1280,128]{1,0:T(8,128)(2,1)} %bitcast.119, bf16[1280,128]{1,0:T(8,128)(2,1)} %bitcast.123, ...), custom_call_target="tpu_custom_call" | custom-call | flops 1 | bytes 1 | tf_op jit(solution)/shard_map/pallas_call | solution.py:110
  123.7 2.5 collective-permute-start.28
  133.8 8.5 %collective-permute-done.30 = bf16[8,2,64,128]{3,2,1,0:T(8,128)(2,1)S(1)} collective-permute-done((bf16[8,2,64,128]{3,2,1,0:T(8,128)(2,1)S(1)}, bf16[8,2,64,128]{3,2,1,0:T(8,128)(2,1)S(1)}, u32[]{:S(2)}, u32[]{:S(2)}) %collective-permute-start.30) | collective-permute-done | bytes 262176 | tf_op jit(solution)/shard_map/ppermute | solution.py:34
  142.3 3.0 collective-permute-start.31
  145.3 1.7 fusion
  147.8 3.2 collective-permute-done.31
  151.8 4.2 %shard_map.506 = (bf16[3,64,512]{2,1,0:T(8,128)(2,1)}, bf16[3,64,512]{2,1,0:T(8,128)(2,1)}, bf16[3,64,512]{2,1,0:T(8,128)(2,1)}, bf16[3,64,512]{2,1,0:T(8,128)(2,1)}) custom-call(s32[5]{0:T(128)} %copy-done.34, bf16[14,512,128]{2,1,0:T(8,128)(2,1)} %all-gather.8.cloned.1.call-done.refs_1_.w_far, f32[14,128]{1,0:T(8,128)} %refs_28_.1, ...), custom_call_target="tpu_custom_call" | custom-call | flops 1 | bytes 1 | tf_op jit(solution)/shard_map/pallas_call | solution.py:110
  157.8 1.7 collective-permute-start.34
  159.5 4.3 %collective-permute-done.32.refs_3_ = bf16[3,64,512]{2,1,0:T(8,128)(2,1)S(1)} collective-permute-done((bf16[3,64,512]{2,1,0:T(8,128)(2,1)}, bf16[3,64,512]{2,1,0:T(8,128)(2,1)S(1)}, u32[]{:S(2)}, u32[]{:S(2)}) %collective-permute-start.32) | collective-permute-done | bytes 196640 | tf_op jit(solution)/shard_map/ppermute | solution.py:34
  163.8 2.3 collective-permute-done.33.refs_4_
  169.0 36.9 %shard_map.507 = (bf16[2,64,2048]{2,1,0:T(8,128)(2,1)}, bf16[2,64,2176]{2,1,0:T(8,128)(2,1)}, bf16[2,64,2176]{2,1,0:T(8,128)(2,1)}) custom-call(s32[1]{0:T(128)S(6)} %add_shard_map.4.refs_0_, bf16[2,64,128]{2,1,0:T(8,128)(2,1)} %pad.5.refs_1_, bf16[3,64,512]{2,1,0:T(8,128)(2,1)} %get-tuple-element.176.refs_2_, bf16[3,64,512]{2,1,0:T(8,128)(2,1)} %copy-done.92, ...), custom_call_target="tpu_custom_call" | custom-call | flops 6643777536 | bytes 2162688 | tf_op jit(solution)/shard_map/pallas_call | solution.py:575
  206.0 2.1 collective-permute-done.40.other_far
  209.0 2.5 shard_map.508
  211.4 4.4 %collective-permute-start.41 = (bf16[3,64,512]{2,1,0:T(8,128)(2,1)}, bf16[3,64,512]{2,1,0:T(8,128)(2,1)S(1)}, u32[]{:S(2)}, u32[]{:S(2)}) collective-permute-start(bf16[3,64,512]{2,1,0:T(8,128)(2,1)} %get-tuple-element.187), channel_id=1, source_target_pairs={{0,8},{4,12},{8,0},{12,4},{16,24},{20,28},{24,16},{28,20},{1,9},{5... | collective-permute-start | bytes 589832 | tf_op jit(solution)/shard_map/ppermute | solution.py:34
  217.4 4.4 %collective-permute-done.41.refs_3_ = bf16[3,64,512]{2,1,0:T(8,128)(2,1)S(1)} collective-permute-done((bf16[3,64,512]{2,1,0:T(8,128)(2,1)}, bf16[3,64,512]{2,1,0:T(8,128)(2,1)S(1)}, u32[]{:S(2)}, u32[]{:S(2)}) %collective-permute-start.41) | collective-permute-done | bytes 196640 | tf_op jit(solution)/shard_map/ppermute | solution.py:34
  221.7 5.2 %collective-permute-done.42.refs_4_ = bf16[3,64,512]{2,1,0:T(8,128)(2,1)S(1)} collective-permute-done((bf16[3,64,512]{2,1,0:T(8,128)(2,1)}, bf16[3,64,512]{2,1,0:T(8,128)(2,1)S(1)}, u32[]{:S(2)}, u32[]{:S(2)}) %collective-permute-start.42) | collective-permute-done | bytes 196640 | tf_op jit(solution)/shard_map/ppermute | solution.py:34
  227.6 4.2 %shard_map.509 = (bf16[8,2,64,384]{3,2,1,0:T(8,128)(2,1)}, f32[8,2,64,128]{3,2,1,0:T(8,128)}, bf16[8,2,64,128]{3,2,1,0:T(8,128)(2,1)}, bf16[8,2,64,128]{3,2,1,0:...) custom-call(s32[5]{0:T(128)} %copy-done.34, ...), custom_call_target="tpu_custom_call" | custom-call | flops 1 | bytes 1 | tf_op jit(solution)/shard_map/pallas_call | solution.py:110
  234.9 7.4 %collective-permute-done.48 = bf16[8,2,64,128]{3,2,1,0:T(8,128)(2,1)S(1)} collective-permute-done((bf16[8,2,64,128]{3,2,1,0:T(8,128)(2,1)}, bf16[8,2,64,128]{3,2,1,0:T(8,128)(2,1)S(1)}, u32[]{:S(2)}, u32[]{:S(2)}) %collective-permute-start.48) | collective-permute-done | bytes 262176 | tf_op jit(solution)/shard_map/ppermute | solution.py:34
  243.4 2.4 collective-permute-start.49
  247.5 1.8 collective-permute-start.46
  251.8 2.0 collective-permute-done.46.refs_4_
  255.4 2.9 collective-permute-start.54
  263.1 3.3 collective-permute-done.51.behind
  270.9 6.8 %shard_map.513 = (bf16[4,13,64,128]{3,2,1,0:T(8,128)(2,1)}, bf16[4,13,64,128]{3,2,1,0:T(8,128)(2,1)}) custom-call(s32[5]{0:T(128)} %copy-done.34, bf16[1280,128]{1,0:T(8,128)(2,1)} %bitcast.103, bf16[1280,128]{1,0:T(8,128)(2,1)} %bitcast.122, bf16[1280,128]{1,0:T(8,128)(2,1)} %bitcast.120, bf16[1280,128]{1,0:T(8,128)(2,1)} %bitcast.124, ...), custom_call_target="tpu_custom_call" | custom-call | flops 1 | bytes 1 | tf_op jit(solution)/shard_map/pallas_call | solution.py:110
  277.7 6.3 %collective-permute-start.58 = (bf16[10,2,64,128]{3,2,1,0:T(8,128)(2,1)S(1)}, bf16[10,2,64,128]{3,2,1,0:T(8,128)(2,1)S(1)}, u32[]{:S(2)}, u32[]{:S(2)}) collective-permute-start(bf16[10,2,64,128]{3,2,1,0:T(8,128)(2,1)S(1)} %collective-permute-done.57), channel_id=1, source_target_pairs={{0,1},{1,0},{2,3},{3,2},{4,5},{5,4},{6,7},{7,6},{8,9},{9,8},{10,11... | collective-permute-start | bytes 983048 | tf_op jit(solution)/shard_map/ppermute | solution.py:34
  284.2 2.6 collective-permute-done.56
  286.9 7.0 %collective-permute-done.58 = bf16[10,2,64,128]{3,2,1,0:T(8,128)(2,1)S(1)} collective-permute-done((bf16[10,2,64,128]{3,2,1,0:T(8,128)(2,1)S(1)}, bf16[10,2,64,128]{3,2,1,0:T(8,128)(2,1)S(1)}, u32[]{:S(2)}, u32[]{:S(2)}) %collective-permute-start.58) | collective-permute-done | bytes 327712 | tf_op jit(solution)/shard_map/ppermute | solution.py:34
  294.7 6.7 %shard_map.514 = (f32[8,2,64,128]{3,2,1,0:T(8,128)}, f32[4,128]{1,0:T(4,128)}, f32[1,2,64,128]{3,2,1,0:T(8,128)}, f32[1,2,64,128]{3,2,1,0:T(8,128)}) custom-call(s32[5]{0:T(128)} %copy-done.34, bf16[1280,128]{1,0:T(8,128)(2,1)} %bitcast.108, bf16[1280,128]{1,0:T(8,128)(2,1)} %bitcast.139, bf16[1280,128]{1,0:T(8,128)(2,1)} %bitcast.138, ...), custom_call_target="tpu_custom_call" | custom-call | flops 1 | bytes 1 | tf_op jit(solution)/shard_map/pallas_call | solution.py:110
  304.4 4.1 %collective-permute-start.63 = (f32[8,128]{1,0:T(8,128)S(1)}, f32[8,128]{1,0:T(8,128)S(1)}, u32[]{:S(2)}, u32[]{:S(2)}) collective-permute-start(f32[8,128]{1,0:T(8,128)S(1)} %fusion.22), channel_id=1, source_target_pairs={{0,16},{4,20},{8,24},{12,28},{16,0},{20,4},{24,8},{28,12},{1,17},{... | collective-permute-start | bytes 12296 | tf_op jit(solution)/shard_map/ppermute | solution.py:34
  310.1 2.4 collective-permute-start.59
  314.1 2.1 collective-permute-done.60.g2
  317.3 1.7 shard_map.515
  319.5 2.0 collective-permute-start.66
  321.5 5.3 %shard_map.516 = (bf16[4,9,64,128]{3,2,1,0:T(8,128)(2,1)}, bf16[4,9,64,128]{3,2,1,0:T(8,128)(2,1)}) custom-call(s32[5]{0:T(128)} %copy-done.34, bf16[1280,128]{1,0:T(8,128)(2,1)} %bitcast.105, bf16[1280,128]{1,0:T(8,128)(2,1)} %bitcast.112, bf16[1280,128]{1,0:T(8,128)(2,1)} %bitcast.110, bf16[1280,128]{1,0:T(8,128)(2,1)} %bitcast.114, ...), custom_call_target="tpu_custom_call" | custom-call | flops 1 | bytes 1 | tf_op jit(solution)/shard_map/pallas_call | solution.py:110
  326.9 2.7 collective-permute-start.72
  331.9 5.8 %collective-permute-start.67 = (bf16[10,2,64,128]{3,2,1,0:T(8,128)(2,1)}, bf16[10,2,64,128]{3,2,1,0:T(8,128)(2,1)}, u32[]{:S(2)}, u32[]{:S(2)}) collective-permute-start(bf16[10,2,64,128]{3,2,1,0:T(8,128)(2,1)} %collective-permute-done.66), channel_id=1, source_target_pairs={{0,1},{1,0},{2,3},{3,2},{4,5},{5,4},{6,7},{7,6},{8,9},{9,8},{10,11... | collective-permute-start | bytes 983048 | tf_op jit(solution)/shard_map/ppermute | solution.py:34
  339.0 2.3 shard_map.519
  341.2 2.3 collective-permute-start.73
  343.5 2.3 collective-permute-start.74
  348.0 6.5 %shard_map.517 = (f32[8,2,64,128]{3,2,1,0:T(8,128)}, f32[4,128]{1,0:T(4,128)}) custom-call(s32[5]{0:T(128)} %copy-done.34, bf16[1280,128]{1,0:T(8,128)(2,1)} %bitcast.33.x0, bf16[1280,128]{1,0:T(8,128)(2,1)} %bitcast.34.x1, bf16[1280,128]{1,0:T(8,128)(2,1)} %bitcast.35.x2, bf16[1280,128]{1,0:T(8,128)(2,1)} %bitcast.36.x3, ...), custom_call_target="tpu_custom_call" | custom-call | flops 1 | bytes 1 | tf_op jit(solution)/shard_map/pallas_call | solution.py:110
  354.6 1.9 collective-permute-start.69
  357.8 4.9 %collective-permute-done.74.refs_2_ = bf16[22,64,128]{2,1,0:T(8,128)(2,1)S(1)} collective-permute-done((bf16[22,64,128]{2,1,0:T(8,128)(2,1)}, bf16[22,64,128]{2,1,0:T(8,128)(2,1)S(1)}, u32[]{:S(2)}, u32[]{:S(2)}) %collective-permute-start.74) | collective-permute-done | bytes 360480 | tf_op jit(solution)/shard_map/ppermute | solution.py:34
  373.1 3.3 collective-permute-start.80
  376.4 3.2 collective-permute-start.81
  380.7 2.0 reshape.311.refs_27_
  384.0 3.5 shard_map.518
  388.2 5.7 %shard_map.523 = (f32[1,128]{1,0:T(1,128)}, f32[9,64,128]{2,1,0:T(8,128)}, f32[9,64,128]{2,1,0:T(8,128)}, f32[9,64,128]{2,1,0:T(8,128)}, bf16[9,64,128]{2,1,0:T(...) custom-call(f32[8,128]{1,0:T(8,128)} %copy-done.51, ...), custom_call_target="tpu_custom_call" | custom-call | flops 1 | bytes 1 | tf_op jit(solution)/shard_map/pallas_call | solution.py:110
  (415 shorter events, 99.8 us)
Async XLA Ops:
  7.2 60.4 %all-gather.10.cloned.1.call-start = ((), (), s32[]{:S(2)}) async-start(), calls=%async_computation.2 | async-start | bytes 1327104 | tf_op jit(solution)/shard_map/all_gather | solution.py:913
  11.5 76.1 %all-gather.8.cloned.1.call-start = ((), (), s32[]{:S(2)}) async-start(), calls=%async_computation.1 | async-start | bytes 2064384 | tf_op jit(solution)/shard_map/all_gather | solution.py:944
  11.5 12.9 %collective-permute-start.6 = (bf16[8,2,64,128]{3,2,1,0:T(8,128)(2,1)}, bf16[8,2,64,128]{3,2,1,0:T(8,128)(2,1)S(1)}, u32[]{:S(2)}, u32[]{:S(2)}) collective-permute-start(bf16[8,2,64,128]{3,2,1,0:T(8,128)(2,1)} %c0.1), channel_id=1, source_target_pairs={{0,1},{1,0},{2,3},{3,2},{4,5},{5,4},{6,7},{7,6},{8,9},{9,8},{10,11... | collective-permute-start | bytes 786440 | tf_op jit(solution)/shard_map/ppermute | solution.py:34
  14.5 14.9 %collective-permute-start.7 = (bf16[8,2,64,128]{3,2,1,0:T(8,128)(2,1)}, bf16[8,2,64,128]{3,2,1,0:T(8,128)(2,1)}, u32[]{:S(2)}, u32[]{:S(2)}) collective-permute-start(bf16[8,2,64,128]{3,2,1,0:T(8,128)(2,1)} %c0.1), channel_id=1, source_target_pairs={{0,3},{1,2},{2,1},{3,0},{4,7},{5,6},{6,5},{7,4},{8,11},{9,10},{10,... | collective-permute-start | bytes 786440 | tf_op jit(solution)/shard_map/ppermute | solution.py:34
  20.7 8.7 %collective-permute-start = (f32[1,2,64,128]{3,2,1,0:T(8,128)S(1)}, f32[1,2,64,128]{3,2,1,0:T(8,128)S(1)}, u32[]{:S(2)}, u32[]{:S(2)}) collective-permute-start(f32[1,2,64,128]{3,2,1,0:T(8,128)S(1)} %get-tuple-element.273), channel_id=1, source_target_pairs={{0,4},{4,8},{8,12},{12,16},{16,20},{20,24},{24,28},{1,5},{5,9},{9,... | collective-permute-start | bytes 196616 | tf_op jit(solution)/shard_map/ppermute | solution.py:62
  23.1 6.3 %collective-permute-start.1 = (f32[1,2,64,128]{3,2,1,0:T(8,128)S(1)}, f32[1,2,64,128]{3,2,1,0:T(8,128)S(1)}, u32[]{:S(2)}, u32[]{:S(2)}) collective-permute-start(f32[1,2,64,128]{3,2,1,0:T(8,128)S(1)} %get-tuple-element.272), channel_id=1, source_target_pairs={{4,0},{8,4},{12,8},{16,12},{20,16},{24,20},{28,24},{5,1},{9,5},{13... | collective-permute-start | bytes 196616 | tf_op jit(solution)/shard_map/ppermute | solution.py:62
  30.3 12.4 %collective-permute-start.8 = (bf16[10,2,64,128]{3,2,1,0:T(8,128)(2,1)S(1)}, bf16[10,2,64,128]{3,2,1,0:T(8,128)(2,1)S(1)}, u32[]{:S(2)}, u32[]{:S(2)}) collective-permute-start(bf16[10,2,64,128]{3,2,1,0:T(8,128)(2,1)S(1)} %shard_map.500), channel_id=1, source_target_pairs={{0,3},{1,2},{2,1},{3,0},{4,7},{5,6},{6,5},{7,4},{8,11},{9,10},{10,... | collective-permute-start | bytes 983048 | tf_op jit(solution)/shard_map/ppermute | solution.py:34
  43.5 101.8 %all-gather.6.cloned.1.call-start = ((), (), s32[]{:S(2)}) async-start(), calls=%async_computation | async-start | bytes 1179648 | tf_op jit(solution)/shard_map/all_gather | solution.py:923
  43.5 14.7 %collective-permute-start.10 = (bf16[10,2,64,128]{3,2,1,0:T(8,128)(2,1)S(1)}, bf16[10,2,64,128]{3,2,1,0:T(8,128)(2,1)S(1)}, u32[]{:S(2)}, u32[]{:S(2)}) collective-permute-start(bf16[10,2,64,128]{3,2,1,0:T(8,128)(2,1)S(1)} %shard_map.500), channel_id=1, source_target_pairs={{0,1},{1,0},{2,3},{3,2},{4,5},{5,4},{6,7},{7,6},{8,9},{9,8},{10,11... | collective-permute-start | bytes 983048 | tf_op jit(solution)/shard_map/ppermute | solution.py:34
  49.7 14.5 %collective-permute-start.11 = (bf16[10,2,64,128]{3,2,1,0:T(8,128)(2,1)S(1)}, bf16[10,2,64,128]{3,2,1,0:T(8,128)(2,1)S(1)}, u32[]{:S(2)}, u32[]{:S(2)}) collective-permute-start(bf16[10,2,64,128]{3,2,1,0:T(8,128)(2,1)S(1)} %collective-permute-done.8), channel_id=1, source_target_pairs={{0,1},{1,0},{2,3},{3,2},{4,5},{5,4},{6,7},{7,6},{8,9},{9,8},{10,11... | collective-permute-start | bytes 983048 | tf_op jit(solution)/shard_map/ppermute | solution.py:34
  64.2 7.9 %collective-permute-start.14 = (bf16[8,2,64,128]{3,2,1,0:T(8,128)(2,1)}, bf16[8,2,64,128]{3,2,1,0:T(8,128)(2,1)S(1)}, u32[]{:S(2)}, u32[]{:S(2)}) collective-permute-start(bf16[8,2,64,128]{3,2,1,0:T(8,128)(2,1)} %collective-permute-done.7), channel_id=1, source_target_pairs={{0,1},{1,0},{2,3},{3,2},{4,5},{5,4},{6,7},{7,6},{8,9},{9,8},{10,11... | collective-permute-start | bytes 786440 | tf_op jit(solution)/shard_map/ppermute | solution.py:34
  73.4 8.9 %collective-permute-start.17 = (f32[8,128]{1,0:T(8,128)S(1)}, f32[8,128]{1,0:T(8,128)S(1)}, u32[]{:S(2)}, u32[]{:S(2)}) collective-permute-start(f32[8,128]{1,0:T(8,128)S(1)} %fusion.21), channel_id=1, source_target_pairs={{0,16},{4,20},{8,24},{12,28},{16,0},{20,4},{24,8},{28,12},{1,17},{... | collective-permute-start | bytes 12296 | tf_op jit(solution)/shard_map/ppermute | solution.py:34
  76.6 5.7 %collective-permute-start.18 = (f32[8,128]{1,0:T(8,128)S(1)}, f32[8,128]{1,0:T(8,128)S(1)}, u32[]{:S(2)}, u32[]{:S(2)}) collective-permute-start(f32[8,128]{1,0:T(8,128)S(1)} %fusion.21), channel_id=1, source_target_pairs={{0,24},{4,28},{8,16},{12,20},{16,8},{20,12},{24,0},{28,4},{1,25},{... | collective-permute-start | bytes 12296 | tf_op jit(solution)/shard_map/ppermute | solution.py:34
  77.3 5.0 %collective-permute-start.16 = (f32[8,128]{1,0:T(8,128)S(1)}, f32[8,128]{1,0:T(8,128)S(1)}, u32[]{:S(2)}, u32[]{:S(2)}) collective-permute-start(f32[8,128]{1,0:T(8,128)S(1)} %fusion.21), channel_id=1, source_target_pairs={{0,8},{4,12},{8,0},{12,4},{16,24},{20,28},{24,16},{28,20},{1,9},{5... | collective-permute-start | bytes 12296 | tf_op jit(solution)/shard_map/ppermute | solution.py:34
  79.0 189.4 %all-gather.12.cloned.1.call-start = ((), (), s32[]{:S(2)}) async-start(), calls=%async_computation.3 | async-start | bytes 1327104 | tf_op jit(solution)/shard_map/all_gather | solution.py:1078
  85.9 10.5 %collective-permute-start.20 = (bf16[10,2,64,128]{3,2,1,0:T(8,128)(2,1)S(1)}, bf16[10,2,64,128]{3,2,1,0:T(8,128)(2,1)S(1)}, u32[]{:S(2)}, u32[]{:S(2)}) collective-permute-start(bf16[10,2,64,128]{3,2,1,0:T(8,128)(2,1)S(1)} %shard_map.502), channel_id=1, source_target_pairs={{0,3},{1,2},{2,1},{3,0},{4,7},{5,6},{6,5},{7,4},{8,11},{9,10},{10,... | collective-permute-start | bytes 983048 | tf_op jit(solution)/shard_map/ppermute | solution.py:34
  86.8 26.5 %collective-permute-start.19 = (bf16[10,2,64,128]{3,2,1,0:T(8,128)(2,1)S(1)}, bf16[10,2,64,128]{3,2,1,0:T(8,128)(2,1)S(1)}, u32[]{:S(2)}, u32[]{:S(2)}) collective-permute-start(bf16[10,2,64,128]{3,2,1,0:T(8,128)(2,1)S(1)} %shard_map.502), channel_id=1, source_target_pairs={{0,1},{1,0},{2,3},{3,2},{4,5},{5,4},{6,7},{7,6},{8,9},{9,8},{10,11... | collective-permute-start | bytes 983048 | tf_op jit(solution)/shard_map/ppermute | solution.py:34
  96.3 17.0 %collective-permute-start.21 = (bf16[10,2,64,128]{3,2,1,0:T(8,128)(2,1)S(1)}, bf16[10,2,64,128]{3,2,1,0:T(8,128)(2,1)S(1)}, u32[]{:S(2)}, u32[]{:S(2)}) collective-permute-start(bf16[10,2,64,128]{3,2,1,0:T(8,128)(2,1)S(1)} %collective-permute-done.20), channel_id=1, source_target_pairs={{0,1},{1,0},{2,3},{3,2},{4,5},{5,4},{6,7},{7,6},{8,9},{9,8},{10,11... | collective-permute-start | bytes 983048 | tf_op jit(solution)/shard_map/ppermute | solution.py:34
  104.1 5.8 %collective-permute-start.22 = (bf16[64,512]{1,0:T(8,128)(2,1)}, bf16[64,512]{1,0:T(8,128)(2,1)S(1)}, u32[]{:S(2)}, u32[]{:S(2)}) collective-permute-start(bf16[64,512]{1,0:T(8,128)(2,1)} %get-tuple-element.169), channel_id=1, source_target_pairs={{0,8},{4,12},{8,0},{12,4},{16,24},{20,28},{24,16},{28,20},{1,9},{5... | collective-permute-start | bytes 196616 | tf_op jit(solution)/shard_map/ppermute | solution.py:34
  107.1 5.2 %collective-permute-start.23 = (bf16[64,512]{1,0:T(8,128)(2,1)}, bf16[64,512]{1,0:T(8,128)(2,1)S(1)}, u32[]{:S(2)}, u32[]{:S(2)}) collective-permute-start(bf16[64,512]{1,0:T(8,128)(2,1)} %get-tuple-element.170), channel_id=1, source_target_pairs={{0,16},{4,20},{8,24},{12,28},{16,0},{20,4},{24,8},{28,12},{1,17},{... | collective-permute-start | bytes 196616 | tf_op jit(solution)/shard_map/ppermute | solution.py:34
  107.9 5.4 %collective-permute-start.24 = (bf16[64,512]{1,0:T(8,128)(2,1)}, bf16[64,512]{1,0:T(8,128)(2,1)S(1)}, u32[]{:S(2)}, u32[]{:S(2)}) collective-permute-start(bf16[64,512]{1,0:T(8,128)(2,1)} %get-tuple-element.171), channel_id=1, source_target_pairs={{0,24},{4,28},{8,16},{12,20},{16,8},{20,12},{24,0},{28,4},{1,25},{... | collective-permute-start | bytes 196616 | tf_op jit(solution)/shard_map/ppermute | solution.py:34
  131.2 11.1 %collective-permute-start.30 = (bf16[8,2,64,128]{3,2,1,0:T(8,128)(2,1)S(1)}, bf16[8,2,64,128]{3,2,1,0:T(8,128)(2,1)S(1)}, u32[]{:S(2)}, u32[]{:S(2)}) collective-permute-start(bf16[8,2,64,128]{3,2,1,0:T(8,128)(2,1)S(1)} %shard_map.505), channel_id=1, source_target_pairs={{0,3},{1,2},{2,1},{3,0},{4,7},{5,6},{6,5},{7,4},{8,11},{9,10},{10,... | collective-permute-start | bytes 786440 | tf_op jit(solution)/shard_map/ppermute | solution.py:34
  133.0 14.9 %collective-permute-start.29 = (bf16[8,2,64,128]{3,2,1,0:T(8,128)(2,1)S(1)}, bf16[8,2,64,128]{3,2,1,0:T(8,128)(2,1)S(1)}, u32[]{:S(2)}, u32[]{:S(2)}) collective-permute-start(bf16[8,2,64,128]{3,2,1,0:T(8,128)(2,1)S(1)} %shard_map.505), channel_id=1, source_target_pairs={{0,1},{1,0},{2,3},{3,2},{4,5},{5,4},{6,7},{7,6},{8,9},{9,8},{10,11... | collective-permute-start | bytes 786440 | tf_op jit(solution)/shard_map/ppermute | solution.py:34
  142.3 8.8 %collective-permute-start.31 = (bf16[8,2,64,128]{3,2,1,0:T(8,128)(2,1)S(1)}, bf16[8,2,64,128]{3,2,1,0:T(8,128)(2,1)S(1)}, u32[]{:S(2)}, u32[]{:S(2)}) collective-permute-start(bf16[8,2,64,128]{3,2,1,0:T(8,128)(2,1)S(1)} %collective-permute-done.30), channel_id=1, source_target_pairs={{0,1},{1,0},{2,3},{3,2},{4,5},{5,4},{6,7},{7,6},{8,9},{9,8},{10,11... | collective-permute-start | bytes 786440 | tf_op jit(solution)/shard_map/ppermute | solution.py:34
  155.9 7.9 %collective-permute-start.32 = (bf16[3,64,512]{2,1,0:T(8,128)(2,1)}, bf16[3,64,512]{2,1,0:T(8,128)(2,1)S(1)}, u32[]{:S(2)}, u32[]{:S(2)}) collective-permute-start(bf16[3,64,512]{2,1,0:T(8,128)(2,1)} %get-tuple-element.177), channel_id=1, source_target_pairs={{0,8},{4,12},{8,0},{12,4},{16,24},{20,28},{24,16},{28,20},{1,9},{5... | collective-permute-start | bytes 589832 | tf_op jit(solution)/shard_map/ppermute | solution.py:34
  156.3 9.8 %collective-permute-start.33 = (bf16[3,64,512]{2,1,0:T(8,128)(2,1)}, bf16[3,64,512]{2,1,0:T(8,128)(2,1)S(1)}, u32[]{:S(2)}, u32[]{:S(2)}) collective-permute-start(bf16[3,64,512]{2,1,0:T(8,128)(2,1)} %get-tuple-element.178), channel_id=1, source_target_pairs={{0,16},{4,20},{8,24},{12,28},{16,0},{20,4},{24,8},{28,12},{1,17},{... | collective-permute-start | bytes 589832 | tf_op jit(solution)/shard_map/ppermute | solution.py:34
  157.8 8.4 %collective-permute-start.34 = (bf16[3,64,512]{2,1,0:T(8,128)(2,1)}, bf16[3,64,512]{2,1,0:T(8,128)(2,1)S(1)}, u32[]{:S(2)}, u32[]{:S(2)}) collective-permute-start(bf16[3,64,512]{2,1,0:T(8,128)(2,1)} %get-tuple-element.179), channel_id=1, source_target_pairs={{0,24},{4,28},{8,16},{12,20},{16,8},{20,12},{24,0},{28,4},{1,25},{... | collective-permute-start | bytes 589832 | tf_op jit(solution)/shard_map/ppermute | solution.py:34
  159.5 8.5 %collective-permute-start.35 = (bf16[3,64,512]{2,1,0:T(8,128)(2,1)}, bf16[3,64,512]{2,1,0:T(8,128)(2,1)S(1)}, u32[]{:S(2)}, u32[]{:S(2)}) collective-permute-start(bf16[3,64,512]{2,1,0:T(8,128)(2,1)} %get-tuple-element.176.refs_2_), channel_id=1, source_target_pairs={{0,4},{4,0},{8,12},{12,8},{16,20},{20,16},{24,28},{28,24},{1,5},{5... | collective-permute-start | bytes 589832 | tf_op jit(solution)/shard_map/ppermute | solution.py:34
  168.0 37.8 %collective-permute-start.39 = (bf16[18,64,128]{2,1,0:T(8,128)(2,1)S(1)}, bf16[18,64,128]{2,1,0:T(8,128)(2,1)S(1)}, u32[]{:S(2)}, u32[]{:S(2)}) collective-permute-start(bf16[18,64,128]{2,1,0:T(8,128)(2,1)S(1)} %pad_maximum_fusion), channel_id=1, source_target_pairs={{0,0},{1,8},{2,16},{3,24},{4,4},{5,12},{6,20},{7,28},{8,1},{9,9},{... | collective-permute-start | bytes 884744 | tf_op jit(solution)/shard_map/ppermute | solution.py:846
  211.4 10.3 %collective-permute-start.41 = (bf16[3,64,512]{2,1,0:T(8,128)(2,1)}, bf16[3,64,512]{2,1,0:T(8,128)(2,1)S(1)}, u32[]{:S(2)}, u32[]{:S(2)}) collective-permute-start(bf16[3,64,512]{2,1,0:T(8,128)(2,1)} %get-tuple-element.187), channel_id=1, source_target_pairs={{0,8},{4,12},{8,0},{12,4},{16,24},{20,28},{24,16},{28,20},{1,9},{5... | collective-permute-start | bytes 589832 | tf_op jit(solution)/shard_map/ppermute | solution.py:34
  215.8 11.1 %collective-permute-start.42 = (bf16[3,64,512]{2,1,0:T(8,128)(2,1)}, bf16[3,64,512]{2,1,0:T(8,128)(2,1)S(1)}, u32[]{:S(2)}, u32[]{:S(2)}) collective-permute-start(bf16[3,64,512]{2,1,0:T(8,128)(2,1)} %get-tuple-element.188), channel_id=1, source_target_pairs={{0,16},{4,20},{8,24},{12,28},{16,0},{20,4},{24,8},{28,12},{1,17},{... | collective-permute-start | bytes 589832 | tf_op jit(solution)/shard_map/ppermute | solution.py:34
  217.3 9.6 %collective-permute-start.43 = (bf16[3,64,512]{2,1,0:T(8,128)(2,1)}, bf16[3,64,512]{2,1,0:T(8,128)(2,1)S(1)}, u32[]{:S(2)}, u32[]{:S(2)}) collective-permute-start(bf16[3,64,512]{2,1,0:T(8,128)(2,1)} %get-tuple-element.189), channel_id=1, source_target_pairs={{0,24},{4,28},{8,16},{12,20},{16,8},{20,12},{24,0},{28,4},{1,25},{... | collective-permute-start | bytes 589832 | tf_op jit(solution)/shard_map/ppermute | solution.py:34
  232.7 115.2 %all-gather.14.cloned.1.call-start = ((), (), s32[]{:S(2)}) async-start(), calls=%async_computation.4 | async-start | bytes 1327104 | tf_op jit(solution)/shard_map/all_gather | solution.py:1079
  232.8 9.5 %collective-permute-start.48 = (bf16[8,2,64,128]{3,2,1,0:T(8,128)(2,1)}, bf16[8,2,64,128]{3,2,1,0:T(8,128)(2,1)S(1)}, u32[]{:S(2)}, u32[]{:S(2)}) collective-permute-start(bf16[8,2,64,128]{3,2,1,0:T(8,128)(2,1)} %get-tuple-element.190), channel_id=1, source_target_pairs={{0,1},{1,0},{2,3},{3,2},{4,5},{5,4},{6,7},{7,6},{8,9},{9,8},{10,11... | collective-permute-start | bytes 786440 | tf_op jit(solution)/shard_map/ppermute | solution.py:34
  234.1 19.6 %collective-permute-start.47 = (bf16[8,2,64,128]{3,2,1,0:T(8,128)(2,1)}, bf16[8,2,64,128]{3,2,1,0:T(8,128)(2,1)S(1)}, u32[]{:S(2)}, u32[]{:S(2)}) collective-permute-start(bf16[8,2,64,128]{3,2,1,0:T(8,128)(2,1)} %get-tuple-element.200), channel_id=1, source_target_pairs={{0,1},{1,0},{2,3},{3,2},{4,5},{5,4},{6,7},{7,6},{8,9},{9,8},{10,11... | collective-permute-start | bytes 786440 | tf_op jit(solution)/shard_map/ppermute | solution.py:34
  243.4 10.3 %collective-permute-start.49 = (bf16[8,2,64,128]{3,2,1,0:T(8,128)(2,1)S(1)}, bf16[8,2,64,128]{3,2,1,0:T(8,128)(2,1)S(1)}, u32[]{:S(2)}, u32[]{:S(2)}) collective-permute-start(bf16[8,2,64,128]{3,2,1,0:T(8,128)(2,1)S(1)} %add_convert_fusion), channel_id=1, source_target_pairs={{0,3},{1,2},{2,1},{3,0},{4,7},{5,6},{6,5},{7,4},{8,11},{9,10},{10,... | collective-permute-start | bytes 786440 | tf_op jit(solution)/shard_map/ppermute | solution.py:34
  245.9 4.6 %collective-permute-start.44 = (bf16[64,768]{1,0:T(8,128)(2,1)S(1)}, bf16[64,768]{1,0:T(8,128)(2,1)S(1)}, u32[]{:S(2)}, u32[]{:S(2)}) collective-permute-start(bf16[64,768]{1,0:T(8,128)(2,1)S(1)} %copy-done.101), channel_id=1, source_target_pairs={{0,8},{4,12},{8,0},{12,4},{16,24},{20,28},{24,16},{28,20},{1,9},{5... | collective-permute-start | bytes 294920 | tf_op jit(solution)/shard_map/ppermute | solution.py:34
  247.2 4.6 %collective-permute-start.45 = (bf16[64,768]{1,0:T(8,128)(2,1)S(1)}, bf16[64,768]{1,0:T(8,128)(2,1)S(1)}, u32[]{:S(2)}, u32[]{:S(2)}) collective-permute-start(bf16[64,768]{1,0:T(8,128)(2,1)S(1)} %copy-done.100), channel_id=1, source_target_pairs={{0,16},{4,20},{8,24},{12,28},{16,0},{20,4},{24,8},{28,12},{1,17},{... | collective-permute-start | bytes 294920 | tf_op jit(solution)/shard_map/ppermute | solution.py:34
  247.5 6.2 %collective-permute-start.46 = (bf16[64,768]{1,0:T(8,128)(2,1)S(1)}, bf16[64,768]{1,0:T(8,128)(2,1)S(1)}, u32[]{:S(2)}, u32[]{:S(2)}) collective-permute-start(bf16[64,768]{1,0:T(8,128)(2,1)S(1)} %copy-done.99), channel_id=1, source_target_pairs={{0,24},{4,28},{8,16},{12,20},{16,8},{20,12},{24,0},{28,4},{1,25},{... | collective-permute-start | bytes 294920 | tf_op jit(solution)/shard_map/ppermute | solution.py:34
  255.4 7.4 %collective-permute-start.54 = (f32[4,128]{1,0:T(4,128)S(1)}, f32[4,128]{1,0:T(4,128)S(1)}, u32[]{:S(2)}, u32[]{:S(2)}) collective-permute-start(f32[4,128]{1,0:T(4,128)S(1)} %add.170), channel_id=1, source_target_pairs={{0,16},{4,20},{8,24},{12,28},{16,0},{20,4},{24,8},{28,12},{1,17},{... | collective-permute-start | bytes 6152 | tf_op jit(solution)/shard_map/ppermute | solution.py:34
  261.3 5.1 %collective-permute-start.51 = (f32[1,2,64,384]{3,2,1,0:T(8,128)S(1)}, f32[1,2,64,384]{3,2,1,0:T(8,128)S(1)}, u32[]{:S(2)}, u32[]{:S(2)}) collective-permute-start(f32[1,2,64,384]{3,2,1,0:T(8,128)S(1)} %get-tuple-element.205), channel_id=1, source_target_pairs={{4,0},{8,4},{12,8},{16,12},{20,16},{24,20},{28,24},{5,1},{9,5},{13... | collective-permute-start | bytes 589832 | tf_op jit(solution)/shard_map/ppermute | solution.py:62
  268.4 9.3 %collective-permute-start.57 = (bf16[10,2,64,128]{3,2,1,0:T(8,128)(2,1)S(1)}, bf16[10,2,64,128]{3,2,1,0:T(8,128)(2,1)S(1)}, u32[]{:S(2)}, u32[]{:S(2)}) collective-permute-start(bf16[10,2,64,128]{3,2,1,0:T(8,128)(2,1)S(1)} %get-tuple-element.207.r), channel_id=1, source_target_pairs={{0,3},{1,2},{2,1},{3,0},{4,7},{5,6},{6,5},{7,4},{8,11},{9,10},{10,... | collective-permute-start | bytes 983048 | tf_op jit(solution)/shard_map/ppermute | solution.py:34
  269.8 17.0 %collective-permute-start.56 = (bf16[10,2,64,128]{3,2,1,0:T(8,128)(2,1)S(1)}, bf16[10,2,64,128]{3,2,1,0:T(8,128)(2,1)S(1)}, u32[]{:S(2)}, u32[]{:S(2)}) collective-permute-start(bf16[10,2,64,128]{3,2,1,0:T(8,128)(2,1)S(1)} %get-tuple-element.207.r), channel_id=1, source_target_pairs={{0,1},{1,0},{2,3},{3,2},{4,5},{5,4},{6,7},{7,6},{8,9},{9,8},{10,11... | collective-permute-start | bytes 983048 | tf_op jit(solution)/shard_map/ppermute | solution.py:34
  277.7 16.2 %collective-permute-start.58 = (bf16[10,2,64,128]{3,2,1,0:T(8,128)(2,1)S(1)}, bf16[10,2,64,128]{3,2,1,0:T(8,128)(2,1)S(1)}, u32[]{:S(2)}, u32[]{:S(2)}) collective-permute-start(bf16[10,2,64,128]{3,2,1,0:T(8,128)(2,1)S(1)} %collective-permute-done.57), channel_id=1, source_target_pairs={{0,1},{1,0},{2,3},{3,2},{4,5},{5,4},{6,7},{7,6},{8,9},{9,8},{10,11... | collective-permute-start | bytes 983048 | tf_op jit(solution)/shard_map/ppermute | solution.py:34
  304.4 8.1 %collective-permute-start.63 = (f32[8,128]{1,0:T(8,128)S(1)}, f32[8,128]{1,0:T(8,128)S(1)}, u32[]{:S(2)}, u32[]{:S(2)}) collective-permute-start(f32[8,128]{1,0:T(8,128)S(1)} %fusion.22), channel_id=1, source_target_pairs={{0,16},{4,20},{8,24},{12,28},{16,0},{20,4},{24,8},{28,12},{1,17},{... | collective-permute-start | bytes 12296 | tf_op jit(solution)/shard_map/ppermute | solution.py:34
  308.5 5.5 %collective-permute-start.64 = (f32[8,128]{1,0:T(8,128)S(1)}, f32[8,128]{1,0:T(8,128)S(1)}, u32[]{:S(2)}, u32[]{:S(2)}) collective-permute-start(f32[8,128]{1,0:T(8,128)S(1)} %fusion.22), channel_id=1, source_target_pairs={{0,24},{4,28},{8,16},{12,20},{16,8},{20,12},{24,0},{28,4},{1,25},{... | collective-permute-start | bytes 12296 | tf_op jit(solution)/shard_map/ppermute | solution.py:34
  309.3 4.7 %collective-permute-start.62 = (f32[8,128]{1,0:T(8,128)S(1)}, f32[8,128]{1,0:T(8,128)S(1)}, u32[]{:S(2)}, u32[]{:S(2)}) collective-permute-start(f32[8,128]{1,0:T(8,128)S(1)} %fusion.22), channel_id=1, source_target_pairs={{0,8},{4,12},{8,0},{12,4},{16,24},{20,28},{24,16},{28,20},{1,9},{5... | collective-permute-start | bytes 12296 | tf_op jit(solution)/shard_map/ppermute | solution.py:34
  310.0 28.9 %collective-permute-start.71 = (bf16[4,13,64,128]{3,2,1,0:T(8,128)(2,1)}, bf16[4,13,64,128]{3,2,1,0:T(8,128)(2,1)}, u32[]{:S(2)}, u32[]{:S(2)}) collective-permute-start(bf16[4,13,64,128]{3,2,1,0:T(8,128)(2,1)} %get-tuple-element.210), channel_id=1, source_target_pairs={{0,4},{4,0},{8,12},{12,8},{16,20},{20,16},{24,28},{28,24},{1,5},{5... | collective-permute-start | bytes 2555912 | tf_op jit(solution)/shard_map/ppermute | solution.py:34
  319.5 12.3 %collective-permute-start.66 = (bf16[10,2,64,128]{3,2,1,0:T(8,128)(2,1)}, bf16[10,2,64,128]{3,2,1,0:T(8,128)(2,1)}, u32[]{:S(2)}, u32[]{:S(2)}) collective-permute-start(bf16[10,2,64,128]{3,2,1,0:T(8,128)(2,1)} %get-tuple-element.219.r), channel_id=1, source_target_pairs={{0,3},{1,2},{2,1},{3,0},{4,7},{5,6},{6,5},{7,4},{8,11},{9,10},{10,... | collective-permute-start | bytes 983048 | tf_op jit(solution)/shard_map/ppermute | solution.py:34
  326.9 12.0 %collective-permute-start.72 = (bf16[4,9,64,128]{3,2,1,0:T(8,128)(2,1)}, bf16[4,9,64,128]{3,2,1,0:T(8,128)(2,1)S(1)}, u32[]{:S(2)}, u32[]{:S(2)}) collective-permute-start(bf16[4,9,64,128]{3,2,1,0:T(8,128)(2,1)} %get-tuple-element.221), channel_id=1, source_target_pairs={{0,4},{4,0},{8,12},{12,8},{16,20},{20,16},{24,28},{28,24},{1,5},{5... | collective-permute-start | bytes 1769480 | tf_op jit(solution)/shard_map/ppermute | solution.py:34
  330.9 16.4 %collective-permute-start.65 = (bf16[10,2,64,128]{3,2,1,0:T(8,128)(2,1)}, bf16[10,2,64,128]{3,2,1,0:T(8,128)(2,1)}, u32[]{:S(2)}, u32[]{:S(2)}) collective-permute-start(bf16[10,2,64,128]{3,2,1,0:T(8,128)(2,1)} %get-tuple-element.219.r), channel_id=1, source_target_pairs={{0,1},{1,0},{2,3},{3,2},{4,5},{5,4},{6,7},{7,6},{8,9},{9,8},{10,11... | collective-permute-start | bytes 983048 | tf_op jit(solution)/shard_map/ppermute | solution.py:34
  331.9 16.1 %collective-permute-start.67 = (bf16[10,2,64,128]{3,2,1,0:T(8,128)(2,1)}, bf16[10,2,64,128]{3,2,1,0:T(8,128)(2,1)}, u32[]{:S(2)}, u32[]{:S(2)}) collective-permute-start(bf16[10,2,64,128]{3,2,1,0:T(8,128)(2,1)} %collective-permute-done.66), channel_id=1, source_target_pairs={{0,1},{1,0},{2,3},{3,2},{4,5},{5,4},{6,7},{7,6},{8,9},{9,8},{10,11... | collective-permute-start | bytes 983048 | tf_op jit(solution)/shard_map/ppermute | solution.py:34
  341.2 16.6 %collective-permute-start.73 = (bf16[22,64,128]{2,1,0:T(8,128)(2,1)}, bf16[22,64,128]{2,1,0:T(8,128)(2,1)S(1)}, u32[]{:S(2)}, u32[]{:S(2)}) collective-permute-start(bf16[22,64,128]{2,1,0:T(8,128)(2,1)} %get-tuple-element.228), channel_id=1, source_target_pairs={{0,8},{4,12},{8,0},{12,4},{16,24},{20,28},{24,16},{28,20},{1,9},{5... | collective-permute-start | bytes 1081352 | tf_op jit(solution)/shard_map/ppermute | solution.py:34
  343.5 19.2 %collective-permute-start.74 = (bf16[22,64,128]{2,1,0:T(8,128)(2,1)}, bf16[22,64,128]{2,1,0:T(8,128)(2,1)S(1)}, u32[]{:S(2)}, u32[]{:S(2)}) collective-permute-start(bf16[22,64,128]{2,1,0:T(8,128)(2,1)} %get-tuple-element.229), channel_id=1, source_target_pairs={{0,16},{4,20},{8,24},{12,28},{16,0},{20,4},{24,8},{28,12},{1,17},{... | collective-permute-start | bytes 1081352 | tf_op jit(solution)/shard_map/ppermute | solution.py:34
  345.8 16.9 %collective-permute-start.75 = (bf16[22,64,128]{2,1,0:T(8,128)(2,1)}, bf16[22,64,128]{2,1,0:T(8,128)(2,1)S(1)}, u32[]{:S(2)}, u32[]{:S(2)}) collective-permute-start(bf16[22,64,128]{2,1,0:T(8,128)(2,1)} %get-tuple-element.230), channel_id=1, source_target_pairs={{0,24},{4,28},{8,16},{12,20},{16,8},{20,12},{24,0},{28,4},{1,25},{... | collective-permute-start | bytes 1081352 | tf_op jit(solution)/shard_map/ppermute | solution.py:34
  354.6 15.8 %collective-permute-start.69 = (bf16[8,2,64,128]{3,2,1,0:T(8,128)(2,1)S(1)}, bf16[8,2,64,128]{3,2,1,0:T(8,128)(2,1)}, u32[]{:S(2)}, u32[]{:S(2)}) collective-permute-start(bf16[8,2,64,128]{3,2,1,0:T(8,128)(2,1)S(1)} %copy-done.24), channel_id=1, source_target_pairs={{0,3},{1,2},{2,1},{3,0},{4,7},{5,6},{6,5},{7,4},{8,11},{9,10},{10,... | collective-permute-start | bytes 786440 | tf_op jit(solution)/shard_map/ppermute | solution.py:34
  365.8 13.8 %collective-permute-start.68 = (bf16[8,2,64,128]{3,2,1,0:T(8,128)(2,1)S(1)}, bf16[8,2,64,128]{3,2,1,0:T(8,128)(2,1)S(1)}, u32[]{:S(2)}, u32[]{:S(2)}) collective-permute-start(bf16[8,2,64,128]{3,2,1,0:T(8,128)(2,1)S(1)} %copy-done.24), channel_id=1, source_target_pairs={{0,1},{1,0},{2,3},{3,2},{4,5},{5,4},{6,7},{7,6},{8,9},{9,8},{10,11... | collective-permute-start | bytes 786440 | tf_op jit(solution)/shard_map/ppermute | solution.py:34
  367.0 4.6 %collective-permute-start.78 = (f32[8,128]{1,0:T(8,128)S(1)}, f32[8,128]{1,0:T(8,128)S(1)}, u32[]{:S(2)}, u32[]{:S(2)}) collective-permute-start(f32[8,128]{1,0:T(8,128)S(1)} %add.180), channel_id=1, source_target_pairs={{0,16},{4,20},{8,24},{12,28},{16,0},{20,4},{24,8},{28,12},{1,17},{... | collective-permute-start | bytes 12296 | tf_op jit(solution)/shard_map/ppermute | solution.py:34
  367.4 4.9 %collective-permute-start.79 = (f32[8,128]{1,0:T(8,128)S(1)}, f32[8,128]{1,0:T(8,128)S(1)}, u32[]{:S(2)}, u32[]{:S(2)}) collective-permute-start(f32[8,128]{1,0:T(8,128)S(1)} %add.180), channel_id=1, source_target_pairs={{0,24},{4,28},{8,16},{12,20},{16,8},{20,12},{24,0},{28,4},{1,25},{... | collective-permute-start | bytes 12296 | tf_op jit(solution)/shard_map/ppermute | solution.py:34
  370.4 13.5 %collective-permute-start.70 = (bf16[8,2,64,128]{3,2,1,0:T(8,128)(2,1)}, bf16[8,2,64,128]{3,2,1,0:T(8,128)(2,1)}, u32[]{:S(2)}, u32[]{:S(2)}) collective-permute-start(bf16[8,2,64,128]{3,2,1,0:T(8,128)(2,1)} %collective-permute-done.69), channel_id=1, source_target_pairs={{0,1},{1,0},{2,3},{3,2},{4,5},{5,4},{6,7},{7,6},{8,9},{9,8},{10,11... | collective-permute-start | bytes 786440 | tf_op jit(solution)/shard_map/ppermute | solution.py:34
  371.6 16.0 %collective-permute-start.83 = (f32[1,64,128]{2,1,0:T(8,128)S(1)}, f32[1,64,128]{2,1,0:T(8,128)S(1)}, u32[]{:S(2)}, u32[]{:S(2)}) collective-permute-start(f32[1,64,128]{2,1,0:T(8,128)S(1)} %get-tuple-element.240), channel_id=1, source_target_pairs={{0,0},{8,1},{16,2},{24,3},{4,4},{12,5},{20,6},{28,7},{1,8},{9,9},{... | collective-permute-start | bytes 98312 | tf_op jit(solution)/shard_map/ppermute | solution.py:851
  373.1 14.4 %collective-permute-start.80 = (f32[8,128]{1,0:T(8,128)S(1)}, f32[8,128]{1,0:T(8,128)S(1)}, u32[]{:S(2)}, u32[]{:S(2)}) collective-permute-start(f32[8,128]{1,0:T(8,128)S(1)} %get-tuple-element.236.refs_0_), channel_id=1, source_target_pairs={{0,1},{1,0},{2,3},{3,2},{4,5},{5,4},{6,7},{7,6},{8,9},{9,8},{10,11... | collective-permute-start | bytes 12296 | tf_op jit(solution)/shard_map/ppermute | solution.py:34
  376.4 11.1 %collective-permute-start.81 = (f32[8,128]{1,0:T(8,128)S(1)}, f32[8,128]{1,0:T(8,128)S(1)}, u32[]{:S(2)}, u32[]{:S(2)}) collective-permute-start(f32[8,128]{1,0:T(8,128)S(1)} %get-tuple-element.236.refs_0_), channel_id=1, source_target_pairs={{0,2},{1,3},{2,0},{3,1},{4,6},{5,7},{6,4},{7,5},{8,10},{9,11},{10,... | collective-permute-start | bytes 12296 | tf_op jit(solution)/shard_map/ppermute | solution.py:34
  379.6 7.9 %collective-permute-start.82 = (f32[8,128]{1,0:T(8,128)S(1)}, f32[8,128]{1,0:T(8,128)S(1)}, u32[]{:S(2)}, u32[]{:S(2)}) collective-permute-start(f32[8,128]{1,0:T(8,128)S(1)} %get-tuple-element.236.refs_0_), channel_id=1, source_target_pairs={{0,3},{1,2},{2,1},{3,0},{4,7},{5,6},{6,5},{7,4},{8,11},{9,10},{10,... | collective-permute-start | bytes 12296 | tf_op jit(solution)/shard_map/ppermute | solution.py:34
  (132 other events, 1543.1 us)
Sparse Core Ops, SparseCore 0:
  11.6 27.2 all-gather.9
  43.6 31.1 all-gather.7
  79.1 22.3 all-gather.5
  232.9 24.6 all-gather.11
  268.6 29.1 all-gather.13

commit v3 on v2

--- a/solution.py
+++ b/solution.py
@@ -55,11 +55,23 @@
     return (x, near, far, swap(after(far, *beside), "chan", 1))
 
 
-def rims(top, bottom):
+def chan_scatter(own, near, cross, far):
+    cross = swap(cross, "chan", 1)
+    near = swap(near, "chan", 1)
+    return own, near, swap((far + cross.astype(F32)).astype(BF), "chan", 3)
+
+
+def rims(blocks):
     size = lax.axis_size("rows")
-    up = [(i, i + 1) for i in range(size - 1)]
-    down = [(j, i) for i, j in up]
-    return lax.ppermute(bottom, "rows", up), lax.ppermute(top, "rows", down)
+    even = lax.axis_index("rows") % 2 == 0
+    top = jnp.stack([x[0] for x in blocks])
+    bottom = jnp.stack([x[-1] for x in blocks])
+    inside = swap(jnp.where(even, bottom, top), "rows", 1)
+    pairs = [(i, i + 1) for i in range(1, size - 1, 2)]
+    outside = jnp.where(even, top, bottom)
+    outside = lax.ppermute(outside, "rows", pairs + [(j, i) for i, j in pairs])
+    shape = (len(blocks), -1, inside.shape[-1])
+    return inside.reshape(shape), outside.reshape(shape)
 
 
 def after(x, *earlier):
@@ -71,13 +83,10 @@
 
 
 def weight_scatter(mine, other):
-    count, _, *rest = mine[0].shape
-    shape = (sum(a.shape[1] for a in mine), *rest)
+    count = mine.shape[0]
+    shape = mine.shape[1:]
     total, *low = local_call(
-        scatter_kernel,
-        [out(shape, F32)] + [out(shape, BF)] * (count - 1),
-        *mine,
-        *other,
+        scatter_kernel, [out(shape, F32)] + [out(shape, BF)] * (count - 1), mine, other
     )
     return [total] + [swap(low[k - 1], "rows", 2 * k) for k in range(1, count)]
 
@@ -95,7 +104,7 @@
     return tuple(Far(a.reshape(math.prod(a.shape[:-1]), a.shape[-1])) for a in arrays)
 
 
-def local_call(kernel, outs, *args, scratch=(), copies=0, flops=0, limit=50):
+def local_call(kernel, outs, *args, scratch=(), copies=0, flops=0, limit=0):
     arrays = [a.array if isinstance(a, Far) else a for a in args]
 
     def spec(a):
@@ -113,7 +122,7 @@
         in_specs=[spec(a) for a in args],
         out_specs=tuple(pl.BlockSpec(memory_space=pltpu.VMEM) for _ in outs),
         scratch_shapes=scratch,
-        compiler_params=pltpu.CompilerParams(vmem_limit_bytes=(56 if copies else limit) * 1024 * 1024),
+        compiler_params=pltpu.CompilerParams(vmem_limit_bytes=(limit or (56 if copies else 50)) * 1024 * 1024),
         cost_estimate=pl.CostEstimate(flops=1, bytes_accessed=1, transcendentals=0),
     )(*arrays)
 
@@ -132,13 +141,23 @@
         copy.wait()
 
 
-def lanes_of(xs, j):
+def lanes_of(xs, j, start=0, size=None):
     width = xs.shape[1] // 4
-    return xs.at[:, j * width : (j + 1) * width]
-
-
-def block_moves(xs, blocks):
-    return [(x, lanes_of(xs, j)) for j, x in enumerate(blocks)]
+    size = xs.shape[0] if size is None else size
+    return xs.at[start : start + size, j * width : (j + 1) * width]
+
+
+def block_moves(xs, blocks, start=0):
+    return [(x, lanes_of(xs, j, start, x.shape[0])) for j, x in enumerate(blocks)]
+
+
+def put_rims(xs, zi, inside, outside):
+    count, span, width = inside.shape
+    last = xs.shape[0] - span
+    for j in range(count):
+        lanes = slice(j * width, (j + 1) * width)
+        xs[pl.ds(pl.multiple_of((1 - zi[4]) * last, span), span), lanes] = inside[j]
+        xs[pl.ds(pl.multiple_of(zi[4] * last, span), span), lanes] = outside[j]
 
 
 def out(shape, dtype):
@@ -205,31 +224,12 @@
         put_sums(sums, b, images, v, v)
 
 
-def edge_of(ref, b):
-    return ref[0, b]
-
-
-def put_wide(o, b, zi, before, value, behind):
-    rows, _, width, channels = o.shape
-    top = (zi[2] > 0).astype(F32)
-    bottom = (zi[3] > 0).astype(F32)
-    o[0, b] = (before * top).astype(o.dtype)
-    o[1 : rows - 1, b] = value.reshape(rows - 2, width, channels).astype(o.dtype)
-    o[rows - 1, b] = (behind * bottom).astype(o.dtype)
-
-
-def act_one_kernel(zi, x, before, behind, sums, vec, o):
+def act_one_kernel(x, sums, vec, o):
     images = x.shape[1]
-    average, inverse = moments(sums[0 : 2 * images], images)
-    for b in range(images):
-
-        def active(v):
-            xhat = (v - average[b : b + 1]) * inverse[b : b + 1]
-            return silu(xhat * vec[0:1] + vec[1:2])
-
-        put_wide(
-            o, b, zi, active(edge_of(before, b)), active(image_of(x, b)), active(edge_of(behind, b))
-        )
+    average, inverse = moments(sums[...], images)
+    for b in range(images):
+        xhat = (image_of(x, b) - average[b : b + 1]) * inverse[b : b + 1]
+        put_image(o, b, silu(xhat * vec[0:1] + vec[1:2]))
 
 
 def shaped_of(xhat, mod, vec, b, images):
@@ -238,18 +238,12 @@
     return (xhat * vec[3:4] + vec[4:5]) * scale + shift
 
 
-def act_two_kernel(zi, x, before, behind, sums, mod, vec, o):
+def act_two_kernel(x, sums, mod, vec, o):
     images = x.shape[1]
     average, inverse = moments(sums[...], images)
     for b in range(images):
-
-        def active(v):
-            xhat = (v - average[b : b + 1]) * inverse[b : b + 1]
-            return silu(shaped_of(xhat, mod, vec, b, images))
-
-        put_wide(
-            o, b, zi, active(edge_of(before, b)), active(image_of(x, b)), active(edge_of(behind, b))
-        )
+        xhat = (image_of(x, b) - average[b : b + 1]) * inverse[b : b + 1]
+        put_image(o, b, silu(shaped_of(xhat, mod, vec, b, images)))
 
 
 def norm_three_kernel(x, sums, vec, o):
@@ -271,52 +265,49 @@
     return jnp.where(column == (0 if by == 1 else width - 1), 0.0, moved)
 
 
-def conv_taps(blocks, w, extra, zi, xs, rows, span, width, flipped):
+def conv_taps(blocks, edges, w, extra, zi, xs, rows, span, width):
     z = zi[0]
     if extra:
         w_far, (w, sems) = w, extra
-        fetch(sems, (w_far.at[0:9], w), *block_moves(xs, blocks))
+        copies = begin(sems, (w_far.at[0:9], w), *block_moves(xs, blocks, span))
+        put_rims(xs, zi, *edges)
+        for copy in copies:
+            copy.wait()
     else:
+        put_rims(xs, zi, *edges)
         for j, x in enumerate(blocks):
-            lanes_of(xs, j)[...] = x[...]
+            lanes_of(xs, j, span, x.shape[0])[...] = x[...]
     channels = w.shape[2]
     parts = []
     for dx in range(3):
         total = None
         for dy in range(3):
-            at = (2 - dy if flipped else dy) * span
+            at = dy * span
             a = xs[at : at + rows * span, :]
             taps = [w[3 * dy + dx, rows_of(z, j, channels), :] for j in range(4)]
-            if flipped:
-                term = nt(a, jnp.concatenate(taps, axis=1))
-            else:
-                term = nn(a, jnp.concatenate(taps, axis=0))
+            term = nn(a, jnp.concatenate(taps, axis=0))
             total = term if total is None else total + term
         parts.append(total)
-    if flipped:
-        parts = parts[::-1]
     return parts[1] + shifted(parts[0], 1, width) + shifted(parts[2], -1, width)
 
 
-def conv_one_kernel(zi, x0, x1, x2, x3, w_far, vec, hidden, sums, top, bottom, xs, *extra):
+def conv_one_kernel(zi, x0, x1, x2, x3, e0, e1, w_far, vec, hidden, sums, xs, *extra):
     rows, images, width, channels = hidden.shape
     blocks = (x0, x1, x2, x3)
     result = conv_taps(
-        blocks, w_far, extra, zi, xs, rows, images * width, width, False
+        blocks, (e0, e1), w_far, extra, zi, xs, rows, images * width, width
     ) + vec[2:3]
     hidden[...] = result.reshape(hidden.shape)
     for b in range(images):
         v = image_of(hidden, b)
         put_sums(sums, b, images, v, v)
-    top[...] = hidden[0:1]
-    bottom[...] = hidden[rows - 1 : rows]
-
-
-def conv_two_kernel(zi, x0, x1, x2, x3, w_far, vec, pixels, residual, sums, xs, *extra):
+
+
+def conv_two_kernel(zi, x0, x1, x2, x3, e0, e1, w_far, vec, pixels, residual, sums, xs, *extra):
     rows, images, width, channels = residual.shape
     blocks = (x0, x1, x2, x3)
     result = conv_taps(
-        blocks, w_far, extra, zi, xs, rows, images * width, width, False
+        blocks, (e0, e1), w_far, extra, zi, xs, rows, images * width, width
     ) + vec[5:6]
     residual[...] = pixels[...] + result.reshape(residual.shape)
     for b in range(images):
@@ -324,58 +315,65 @@
         put_sums(sums, b, images, v, v)
 
 
-def conv_two_back_kernel(
-    zi, x0, x1, x2, x3, w_far, vec, hidden, stats, mod, shaped_grad, sums, top, bottom, xs, *extra
-):
-    rows, images, width, channels = hidden.shape
-    blocks = (x0, x1, x2, x3)
-    result = conv_taps(
-        blocks, w_far, extra, zi, xs, rows, images * width, width, True
-    )
-    shaped_grad[...] = result.reshape(shaped_grad.shape)
+def conv_back_kernel(zi, r, e0, e1, w, own, near, cross, far, xs, *, first):
+    rows, images, width, channels = r.shape
+    span = images * width
+    put_rims(xs, zi, e0, e1)
+    xs[span : span + rows * span] = r[...].reshape(rows * span, channels)
+    wide = xs[...].astype(F32)
+    turned = [shifted(wide, -1, width).astype(BF), xs[...], shifted(wide, 1, width).astype(BF)]
+    taps = [(dy, dx) for dy in range(3) for dx in range(3)]
+    a = jnp.concatenate(
+        [turned[dx][(2 - dy) * span : (2 - dy + rows) * span] for dy, dx in taps], axis=1
+    )
+    for j, part in enumerate((own, near, far, cross)):
+        at = rows_of(zi[0], j, channels)
+        b = jnp.concatenate([w[first + 3 * dy + dx, at, :] for dy, dx in taps], axis=1)
+        part[...] = nt(a, b).astype(part.dtype).reshape(part.shape)
+
+
+def total_image(terms, b):
+    total = image_of(terms[0], b)
+    for term in terms[1:]:
+        total = total + image_of(term, b).astype(F32)
+    return total
+
+
+def back_two_sum_kernel(t0, t1, t2, vec, hidden, stats, mod, shaped_grad, sums):
+    images = hidden.shape[1]
     average, inverse = moments(stats[...], images)
     for b in range(images):
         xhat = (image_of(hidden, b) - average[b : b + 1]) * inverse[b : b + 1]
-        g = image_of(shaped_grad, b) * silu_slope(shaped_of(xhat, mod, vec, b, images))
+        g = total_image((t0, t1, t2), b) * silu_slope(shaped_of(xhat, mod, vec, b, images))
         put_image(shaped_grad, b, g)
         put_sums(sums, b, images, g, xhat)
-    top[...] = shaped_grad[0:1]
-    bottom[...] = shaped_grad[rows - 1 : rows]
-
-
-def conv_one_back_kernel(
-    zi, x0, x1, x2, x3, w_far, vec, pixels, stats, normed_grad, sums, xs, *extra
-):
-    rows, images, width, channels = pixels.shape
-    blocks = (x0, x1, x2, x3)
-    result = conv_taps(
-        blocks, w_far, extra, zi, xs, rows, images * width, width, True
-    )
-    normed_grad[...] = result.reshape(normed_grad.shape)
+
+
+def back_one_sum_kernel(t0, t1, t2, vec, pixels, stats, residual_grad, partial, sums):
+    images = pixels.shape[1]
     average, inverse = moments(stats[0 : 2 * images], images)
     for b in range(images):
         xhat = (image_of(pixels, b) - average[b : b + 1]) * inverse[b : b + 1]
-        g = image_of(normed_grad, b) * silu_slope(xhat * vec[0:1] + vec[1:2])
-        put_image(normed_grad, b, g)
+        g = total_image((t0, t1, t2), b) * silu_slope(xhat * vec[0:1] + vec[1:2])
+        put_image(partial, b, image_of(residual_grad, b) + g * (inverse[b : b + 1] * vec[0:1]))
         put_sums(sums, b, images, g, xhat)
 
 
-def put_shares(box, zi, tap, grad):
+def put_shares(box, zi, tap, grad, base=0):
     share, channels = box.shape[3:]
     each = channels // share
     for j in range(4):
         for i in range(each):
             at = j * channels + i * share
             row = (zi[0] ^ ORDER[j]) * each + i
-            box[(row & 1) ^ zi[4], (row >> 1) ^ zi[1], tap] = grad[at : at + share].astype(box.dtype)
-
-
-def conv_weights(zi, xs, r, box):
+            box[(row & 1) ^ zi[4], (row >> 1) ^ base, tap] = grad[at : at + share].astype(box.dtype)
+
+
+def conv_weights(zi, xs, r, box, base=0):
     rows, images, width, channels = r.shape
-    rows = rows - 2
     span = images * width
     turned = xs[...].T
-    wide = r[1 : rows + 1].reshape(rows * span, channels).astype(F32)
+    wide = r[...].reshape(rows * span, channels).astype(F32)
     three = jnp.concatenate(
         [shifted(wide, -1, width).astype(BF), wide.astype(BF), shifted(wide, 1, width).astype(BF)],
         axis=1,
@@ -383,18 +381,19 @@
     for dy in range(3):
         grad = nn(turned[:, dy * span : (dy + rows) * span], three)
         for dx in range(3):
-            put_shares(box, zi, 3 * dy + dx, grad[:, dx * channels : (dx + 1) * channels])
+            put_shares(box, zi, 3 * dy + dx, grad[:, dx * channels : (dx + 1) * channels], base)
 
 
 def weights_two_kernel(
-    zi, x0, x1, x2, x3, r, n0, n1, n2, n3, grads, att, c0, c1, c2, c3, loss, mine, other, xs, ns, cs, box, sems
+    zi, x0, x1, x2, x3, e0, e1, r, n0, n1, n2, n3, grads, att, c0, c1, c2, c3, loss, mine, other, xs, ns, cs, box, sems
 ):
     blocks = begin(
         sems,
-        *block_moves(xs, (x0, x1, x2, x3)),
+        *block_moves(xs, (x0, x1, x2, x3), e0.shape[1]),
         *block_moves(ns, (n0, n1, n2, n3)),
         *block_moves(cs, (c0, c1, c2, c3)),
     )
+    put_rims(xs, zi, e0, e1)
     for copy in blocks[:4]:
         copy.wait()
     conv_weights(zi, xs, r, box)
@@ -416,21 +415,24 @@
     other[...] = box[1]
 
 
-def weights_one_kernel(zi, x0, x1, x2, x3, r, mine, other, xs, box, sems):
-    fetch(sems, *block_moves(xs, (x0, x1, x2, x3)))
-    conv_weights(zi, xs, r, box)
+def weights_one_kernel(zi, x0, x1, x2, x3, e0, e1, r, mine, other, xs, box, sems):
+    copies = begin(sems, *block_moves(xs, (x0, x1, x2, x3), e0.shape[1]))
+    put_rims(xs, zi, e0, e1)
+    for copy in copies:
+        copy.wait()
+    conv_weights(zi, xs, r, box, zi[1])
     mine[...] = box[0]
     other[...] = box[1]
 
 
-def scatter_kernel(mine_two, mine_one, other_two, other_one, total, *low):
-    at = 0
-    for mine, other in ((mine_two, other_two), (mine_one, other_one)):
-        taps = slice(at, at + mine.shape[1])
-        at += mine.shape[1]
-        total[taps] = mine[0].astype(F32) + other[0].astype(F32)
-        for k, o in enumerate(low):
-            o[taps] = (mine[k + 1].astype(F32) + other[k + 1].astype(F32)).astype(BF)
+def pair_sum_kernel(mine, other, o):
+    o[...] = (mine[...].astype(F32) + other[...].astype(F32)).astype(BF)
+
+
+def scatter_kernel(mine, other, total, *low):
+    total[...] = mine[0].astype(F32) + other[0].astype(F32)
+    for k, o in enumerate(low):
+        o[...] = (mine[k + 1].astype(F32) + other[k + 1].astype(F32)).astype(BF)
 
 
 def put_heads(scratch, leading, value, b, heads):
@@ -440,8 +442,8 @@
 
 
 def project_kernel(*refs, base):
-    zi, w_far, vec, blocks = refs[0], refs[1], refs[2], refs[3:7]
-    outs, (xs, w, scratch, sems) = refs[7:-4], refs[-4:]
+    zi, w_far, vec, grads, blocks = refs[0], refs[1], refs[2], refs[3], refs[4:8]
+    outs, (xs, w, scratch, sems) = refs[8:-4], refs[-4:]
     fetch(sems, (w_far.at[base : base + 3], w), *block_moves(xs, blocks))
     tokens = outs[0].shape[2]
     channels = w.shape[2]
@@ -459,34 +461,28 @@
         for b in range(images):
             put_heads(scratch, s, split[:, b].reshape(tokens, channels), b, heads)
     for k, o in enumerate(outs):
-        o[...] = scratch[zi[1] ^ k]
-
-
-def output_grad_kernel(*refs, tap):
-    zi, w_far, cots, loss = refs[0], refs[1], refs[2:6], refs[6]
-    outs, (xs, w, scratch, sems) = refs[7:-4], refs[-4:]
-    fetch(sems, (w_far.at[tap : tap + 1], w), *block_moves(xs, cots))
-    tokens = outs[0].shape[1]
-    channels = w.shape[2]
+        o[0:3] = scratch[zi[1] ^ k]
+        o[3] = grads[zi[1] ^ k, 0]
+
+
+def output_grad_kernel(c0, c1, c2, c3, w0, w1, w2, w3, loss, o, xs, sems):
+    fetch(sems, *block_moves(xs, (c0, c1, c2, c3)))
+    images, channels = loss.shape
     heads = channels // HEAD_DIM
-    images = len(outs) // heads
-    rows = xs.shape[0] // (images * IMG_W)
-    lanes = [w[0, rows_of(zi[0], j, channels), :] for j in range(4)]
-    turned = jnp.concatenate(lanes, axis=1)
-    wide = xs[...].reshape(rows, images, IMG_W, 4 * channels)
+    tokens = o.shape[3]
+    turned = jnp.concatenate([w[...] for w in (w0, w1, w2, w3)], axis=1)
+    wide = xs[...].reshape(tokens // IMG_W, images, IMG_W, 4 * channels)
     for b in range(images):
         scale = jnp.concatenate([loss[b : b + 1]] * 4, axis=1)
         low = (wide[:, b].reshape(tokens, 4 * channels).astype(F32) * scale).astype(BF)
-        put_heads(scratch, 0, nt(low, turned), b, heads)
-    for k, o in enumerate(outs):
-        o[...] = scratch[zi[1] ^ k, 0]
+        put_heads(o, 0, nt(low, turned), b, heads)
 
 
 def attention_kernel(*refs, chunk, count, block):
     live, ctx_ref = refs[0], refs[1]
-    mine, grads, sibs = (refs[2 + i * count : 2 + (i + 1) * count] for i in range(3))
-    oq_ref, own_ref, other_ref = refs[2 + 3 * count : 5 + 3 * count]
-    q_s, do_s, kt_s, k_s, v_s, s_s, p_s, acc_s = refs[5 + 3 * count :]
+    mine, sibs = (refs[2 + i * count : 2 + (i + 1) * count] for i in range(2))
+    oq_ref, own_ref, other_ref = refs[2 + 2 * count : 5 + 2 * count]
+    q_s, do_s, kt_s, k_s, v_s, s_s, p_s, acc_s = refs[5 + 2 * count :]
     step = pl.program_id(0)
     last = pl.num_programs(0) - 1
     tokens = mine[0].shape[2]
@@ -501,7 +497,7 @@
         for k in range(count):
             lanes = slice(k * tokens, (k + 1) * tokens)
             q_s[:, lanes] = mine[k][0]
-            do_s[:, lanes] = grads[k][...]
+            do_s[:, lanes] = mine[k][3]
             kt_s[:, :, lanes] = mine[k][1:3]
             kt_s[:, :, half + k * tokens : half + (k + 1) * tokens] = sibs[k][1:3]
         kt_s[:, :, keys:] = ctx_ref[...]
@@ -555,9 +551,9 @@
         other_ref[...] = acc_s[:, :, half:].astype(BF)
 
 
-def attention(live, ctx, mine, grads, sibs):
+def attention(live, ctx, mine, sibs):
     count = len(mine)
-    depth, tokens = grads[0].shape
+    _, depth, tokens = mine[0].shape
     queries = count * tokens
     total = 2 * queries + ctx.shape[2]
     block = min(512, queries)
@@ -571,7 +567,7 @@
         out((2, depth, queries + ctx.shape[2]), BF),
         out((2, depth, queries + ctx.shape[2]), BF),
     )
-    arrays = (ctx, *mine, *grads, *sibs)
+    arrays = (ctx, *mine, *sibs)
     return pl.pallas_call(
         functools.partial(attention_kernel, chunk=chunk, count=count, block=block),
         grid=(queries // block,),
@@ -667,77 +663,57 @@
     o[...] = (residual[...] + value.reshape(o.shape)).astype(BF)
 
 
-def back_three_sum_kernel(t0, t1, t2, residual, cotangent, loss, stats, g_out, sums, top, bottom):
-    rows, images, width, channels = residual.shape
+def back_three_sum_kernel(t0, t1, t2, residual, stats, g_out, sums):
+    images = residual.shape[1]
     average, inverse = moments(stats[...], images)
     for b in range(images):
         g = image_of(t0, b).astype(F32) + image_of(t1, b).astype(F32) + image_of(t2, b).astype(F32)
         xhat = (image_of(residual, b) - average[b : b + 1]) * inverse[b : b + 1]
         put_image(g_out, b, g)
         put_sums(sums, b, images, g, xhat)
-        for edge, at in ((top, 0), (bottom, rows - 1)):
-            edge[0, b, :, 0:channels] = g_out[at, b]
-            edge[0, b, :, channels : 2 * channels] = residual[at, b]
-            edge[0, b, :, 2 * channels :] = cotangent[at, b].astype(F32) * loss[b : b + 1]
-
-
-def back_three_kernel(
-    zi, g0, x0, c0, before, behind, stats, sums, vec, loss, residual_grad, low, bias
-):
-    images, channels = x0.shape[1], x0.shape[3]
+
+
+def back_three_kernel(g0, x0, c0, stats, sums, vec, loss, residual_grad, low, bias):
+    images = x0.shape[1]
     average, inverse = moments(stats[...], images)
     means = group_mean(sums[...] * vec[6:7])
     total = None
     for b in range(images):
-
-        def back(g, x, c):
-            xhat = (x - average[b : b + 1]) * inverse[b : b + 1]
-            part = g * vec[6:7] - means[b : b + 1] - xhat * means[images + b : images + b + 1]
-            return c + inverse[b : b + 1] * part
-
-        def back_edge(edge):
-            return back(*(edge[0, b, :, i * channels : (i + 1) * channels] for i in range(3)))
-
-        cot = image_of(c0, b).astype(F32) * loss[b : b + 1]
-        g = back(image_of(g0, b), image_of(x0, b), cot)
+        xhat = (image_of(x0, b) - average[b : b + 1]) * inverse[b : b + 1]
+        g = image_of(g0, b) * vec[6:7] - means[b : b + 1] - xhat * means[images + b : images + b + 1]
+        g = image_of(c0, b).astype(F32) * loss[b : b + 1] + inverse[b : b + 1] * g
         put_image(residual_grad, b, g)
-        put_wide(low, b, zi, back_edge(before), g, back_edge(behind))
+        put_image(low, b, g)
         part = column_sum(g)
         total = part if total is None else total + part
     bias[...] = total
 
 
-def back_two_kernel(zi, g0, g1, g2, x0, x1, x2, stats, sums, mod, vec, low, bias):
+def back_two_kernel(g0, x0, stats, sums, mod, vec, low, bias):
     images = x0.shape[1]
     average, inverse = moments(stats[...], images)
     gains = [vec[3:4] * (1.0 + (mod[b : b + 1] + vec[12:13])) for b in range(images)]
     means = group_mean(sums[0 : 2 * images] * jnp.concatenate(gains + gains, axis=0))
     total = None
     for b in range(images):
-
-        def back(g, x):
-            xhat = (x - average[b : b + 1]) * inverse[b : b + 1]
-            part = g * gains[b] - means[b : b + 1] - xhat * means[images + b : images + b + 1]
-            return inverse[b : b + 1] * part
-
-        g = back(image_of(g0, b), image_of(x0, b))
-        before = back(edge_of(g1, b), edge_of(x1, b))
-        behind = back(edge_of(g2, b), edge_of(x2, b))
-        put_wide(low, b, zi, before, g, behind)
+        xhat = (image_of(x0, b) - average[b : b + 1]) * inverse[b : b + 1]
+        g = image_of(g0, b) * gains[b]
+        g = g - means[b : b + 1] - xhat * means[images + b : images + b + 1]
+        g = inverse[b : b + 1] * g
+        put_image(low, b, g)
         part = column_sum(g)
         total = part if total is None else total + part
     bias[...] = total
 
 
-def back_one_kernel(g_in, pixels, stats, sums, vec, residual_grad, pixel_grad):
+def back_one_kernel(partial, pixels, stats, sums, vec, pixel_grad):
     images = pixels.shape[1]
     average, inverse = moments(stats[0 : 2 * images], images)
     means = group_mean(sums[0 : 2 * images] * vec[0:1])
     for b in range(images):
-        xhat = (image_of(pixels, b) - average[b : b + 1]) * inverse[b : b + 1]
-        scaled = image_of(g_in, b) * vec[0:1]
-        g = inverse[b : b + 1] * (scaled - means[b : b + 1] - xhat * means[images + b : images + b + 1])
-        put_image(pixel_grad, b, image_of(residual_grad, b) + g)
+        slope = inverse[b : b + 1] * inverse[b : b + 1] * means[images + b : images + b + 1]
+        level = inverse[b : b + 1] * means[b : b + 1] - average[b : b + 1] * slope
+        put_image(pixel_grad, b, image_of(partial, b) - (image_of(pixels, b) * slope + level))
 
 
 RATES = (0.02, 0.02, 0.08, 1.0, 0.02, 0.04, 1.0)
@@ -748,11 +724,13 @@
     squared = squares[...]
     at = 0
     for o in (two_sum, qkv_sum, out_sum, one_sum):
-        taps = slice(at, at + o.shape[0])
-        at += o.shape[0]
-        total = terms[0][taps]
-        for term in terms[1:]:
-            total = total + term[taps].astype(F32)
+        if o is one_sum:
+            total = terms[1][...]
+            for term in terms[2:]:
+                total = total + term[...].astype(F32)
+        else:
+            total = terms[0][at : at + o.shape[0]].astype(F32)
+            at += o.shape[0]
         o[...] = total
         squared = squared + column_sum((total * total).reshape(-1, total.shape[-1]))
     count = sums.shape[0]
@@ -799,8 +777,9 @@
 def update_kernel(*refs):
     count = len(RATES)
     squares, given = refs[0:4], refs[4 : 4 + 4 * count]
-    made, held, sems = refs[4 + 4 * count : -4 * count - 1], refs[-4 * count - 1 : -1], refs[-1]
-    arriving = begin(sems, *zip(given, held))
+    made, held, sems = refs[4 + 4 * count : -3 * count - 1], refs[-3 * count - 1 : -1], refs[-1]
+    far = [a for i, a in enumerate(given) if i % 4 < 3]
+    arriving = begin(sems, *zip(far, held))
     near = squares[0][0:1] + squares[1][0:1]
     total = jnp.sum(near + (squares[2][0:1] + squares[3][0:1]), axis=1, keepdims=True)
     norm = jnp.sqrt(total)
@@ -808,9 +787,10 @@
     factor = jnp.minimum(1.0, clip_limit / norm)
     at = 1
     for i, rate in enumerate(RATES):
-        for copy in arriving[4 * i : 4 * i + 4]:
+        for copy in arriving[3 * i : 3 * i + 3]:
             copy.wait()
-        weight, moment, square, gradient = held[4 * i : 4 * i + 4]
+        weight, moment, square = held[3 * i : 3 * i + 3]
+        gradient = given[4 * i + 3]
         decay = 0.0 if i == count - 1 else 0.01
         scale = factor.reshape((1,) * (len(weight.shape) - 2) + factor.shape)
         new = adamw(weight[...], moment[...], square[...], gradient[...] * scale, rate, decay)
@@ -840,10 +820,6 @@
         for r in range(row_count)
         for z in range(chan_count)
     ]
-
-
-def turn_weights(x, row_count, chan_count):
-    return lax.ppermute(x, ("rows", "chan"), turn_moves(row_count, chan_count))
 
 
 def turn_back(x, row_count, chan_count):
@@ -906,22 +882,23 @@
     cot_near, cot_far = swap(cot, "chan", 1), swap(cot, "chan", 3)
 
     sums_shape = out((2 * images, channels), F32)
-    tall = (local_rows + 2, images, width, channels)
     by_chip = sums + swap(sums, "rows", 1)
     stats_one = rows_sum(sums, by_chip)
 
     one_full = lax.all_gather(after(conv_first, by_chip).astype(BF), "rows", axis=1, tiled=True)
-    two_low = after(conv_second, by_chip).astype(BF)
-    qkv_low = jnp.transpose(after(qkv_weight, by_chip), (1, 0, 2)).astype(BF)
-    out_low = out_weight.astype(BF)[None]
-    pixel_rims = rims(pixels[:1], pixels[-1:])
     (active_one,) = local_call(
-        act_one_kernel, [out(tall, BF)], zi, pixels, *pixel_rims, after(stats_one, cot_near, cot_far), vectors
-    )
-    out_turned = turn_weights(after(out_low, active_one), row_count, chan_count)
+        act_one_kernel, [out(act, BF)], pixels, after(stats_one, cot_near, cot_far), vectors
+    )
     blocks_one = chan_blocks(active_one)
+    arrived = blocks_one[1:3]
+    two_low = after(conv_second, *arrived).astype(BF)
+    qkv_low = jnp.transpose(after(qkv_weight, *arrived), (1, 0, 2)).astype(BF)
+    out_low = after(out_weight, *arrived).astype(BF)[None]
+    two_full = lax.all_gather(
+        jnp.concatenate([two_low, qkv_low, out_low], axis=0), "rows", axis=1, tiled=True
+    )
     ctx_full = lax.all_gather(
-        after(context_weight, blocks_one[2]).astype(BF), "rows", axis=0, tiled=True
+        after(context_weight, *arrived).astype(BF), "rows", axis=0, tiled=True
     )
 
     share = EMB // row_count
@@ -941,59 +918,55 @@
         preferred_element_type=F32,
     ).reshape(2 * images, channels)
 
-    two_full = lax.all_gather(
-        jnp.concatenate([two_low, qkv_low, out_low, after(out_turned, blocks_one[2])], axis=0),
-        "rows",
-        axis=1,
-        tiled=True,
-    )
     cot_cross = swap(after(cot_far, *blocks_one), "chan", 1)
-    edge = out((1,) + act[1:], F32)
-    hidden, sums, *edges = local_call(
+    rims_one = rims(blocks_one)
+    hidden, sums = local_call(
         conv_one_kernel,
-        [out(act, F32), sums_shape, edge, edge],
+        [out(act, F32), sums_shape],
         zi,
         *near_rows(*blocks_one),
+        *rims_one,
         one_full,
         vectors,
         scratch=[xs],
         flops=conv_flops,
     )
-    hidden_rims = rims(*edges)
     stats_two = rows_sum(jnp.concatenate([after(sums, cot_cross), modulation], axis=0))
     stats_two, mod = stats_two[: 2 * images], stats_two[2 * images :]
     (active_two,) = local_call(
-        act_two_kernel, [out(tall, BF)], zi, hidden, *hidden_rims, stats_two, mod, vectors
-    )
-
+        act_two_kernel, [out(act, BF)], hidden, stats_two, mod, vectors
+    )
+
+    blocks_two = chan_blocks(active_two)
+
+    def out_rows(owner):
+        return lax.dynamic_slice_in_dim(two_full[12], owner * channels, channels, 0)
+
+    out_part = [out_rows(chan)] + [swap(out_rows(chan ^ k), "chan", k) for k in ORDER[1:]]
     tokens = local_rows * width
-    cots = (cotangent, cot_near, cot_far, after(cot_cross, active_two))
-    grad_pieces = local_call(
-        functools.partial(output_grad_kernel, tap=13),
-        [out((HEAD_DIM, tokens), BF)] * pairs,
-        zi,
-        Far(two_full),
-        *far_rows(*cots),
+    cots = (cotangent, cot_near, cot_far, cot_cross)
+    (attended_grad,) = local_call(
+        output_grad_kernel,
+        [out((pairs, 1, HEAD_DIM, tokens), BF)],
+        *far_rows(*(after(a, active_two) for a in cots)),
+        *out_part,
         loss,
-        scratch=[
-            flat,
-            pltpu.VMEM((1, C, channels), BF),
-            pltpu.VMEM((pairs, 1, HEAD_DIM, tokens), BF),
-        ],
-        copies=5,
-    )
-    blocks_two = chan_blocks(active_two, *grad_pieces)
-    grad_pieces = [grad_pieces[0]] + [
-        swap(grad_pieces[k], "rows", 2 * k) for k in range(1, pairs)
-    ]
-
+        scratch=[flat],
+        copies=4,
+    )
+    ctx_share = DCTX // row_count
+    ctx_rows = lax.dynamic_slice_in_dim(context, row * ctx_share, ctx_share, 2)
+    ctx_rows = jnp.transpose(ctx_rows, (2, 0, 1)).reshape(ctx_share, 1, 1, -1)
+    ctx_rows = (ctx_rows * jnp.eye(2, dtype=BF)[None, :, :, None]).reshape(2 * ctx_share, -1)
+    rims_two = rims((after(blocks_two[0], attended_grad), *blocks_two[1:]))
     residual, sums = local_call(
         conv_two_kernel,
         [out(act, F32), sums_shape],
         zi,
         *far_rows(*blocks_two),
+        *rims_two,
         Far(two_full),
-        after(vectors, *grad_pieces),
+        after(vectors, ctx_rows, embed_rows),
         pixels,
         scratch=[xs, taps],
         copies=5,
@@ -1013,10 +986,11 @@
 
     pieces = local_call(
         functools.partial(project_kernel, base=9),
-        [out((3, HEAD_DIM, tokens), BF)] * pairs,
+        [out((4, HEAD_DIM, tokens), BF)] * pairs,
         zi,
         Far(two_full),
         after(vectors, ctx_heads),
+        attended_grad,
         *far_rows(*blocks_three),
         scratch=[
             flat,
@@ -1029,22 +1003,14 @@
     pieces = [pieces[0]] + [swap(pieces[k], "rows", 2 * k) for k in range(1, pairs)]
     siblings = [swap(piece, "rows", 1) for piece in pieces]
 
-    turned = turn_weights(
-        after(jnp.concatenate([two_low, conv_first.astype(BF)], axis=0), *siblings),
-        row_count,
-        chan_count,
-    )
-
-    out_query, own, other = attention(
-        live, ctx_heads, pieces, grad_pieces, siblings
-    )
+    out_query, own, other = attention(live, ctx_heads, pieces, siblings)
     merged = local_call(
         merge_kernel,
         [out((3, HEAD_DIM, tokens), BF)] * pairs
         + [out((HEAD_DIM, tokens + 2 * CTX_PAD), BF)] * pairs,
         Far(out_query),
         Far(own),
-        Far(swap(after(other, turned), "rows", 1)),
+        Far(swap(other, "rows", 1)),
         scratch=[
             pltpu.VMEM(out_query.shape, BF),
             pltpu.VMEM(own.shape, BF),
@@ -1074,36 +1040,23 @@
         copies=1,
         flops=conv_flops // 3,
     )
-    turned = after(turned, part_cross)
-    two_turned = lax.all_gather(turned[:9], "rows", axis=1, tiled=True)
-    one_turned = lax.all_gather(after(turned[9:], two_turned), "rows", axis=1, tiled=True)
-    cross = swap(part_cross, "chan", 1)
-    near = swap(part_near, "chan", 1)
-    far = swap((part_far + cross.astype(F32)).astype(BF), "chan", 3)
-    long_edge = out((1, images, width, 3 * channels), F32)
+    normed_terms = chan_scatter(part_own, part_near, part_cross, part_far)
     late = [after(piece, part_cross) for piece in merged[pairs:]]
     late = [late[0]] + [swap(late[k], "rows", 2 * k) for k in range(1, pairs)]
-    normed_grad, sums, *edges = local_call(
+    normed_grad, sums = local_call(
         back_three_sum_kernel,
-        [out(act, F32), sums_shape, long_edge, long_edge],
-        part_own,
-        near,
-        far,
+        [out(act, F32), sums_shape],
+        *normed_terms,
         residual,
-        cotangent,
-        after(loss, *late),
-        stats_three,
-    )
-    normed_rims = rims(*edges)
+        after(stats_three, *late),
+    )
     sums_three = rows_sum(sums)
     residual_grad, residual_low, conv_two_bias = local_call(
         back_three_kernel,
-        [out(act, F32), out(tall, BF), out((1, channels), F32)],
-        zi,
+        [out(act, F32), out(act, BF), out((1, channels), F32)],
         normed_grad,
         residual,
         cotangent,
-        *normed_rims,
         stats_three,
         sums_three,
         vectors,
@@ -1127,6 +1080,7 @@
         [out((pairs, 13, C // row_count, channels), BF)] * 2,
         zi,
         *far_rows(*blocks_two),
+        *rims_two,
         residual_low,
         *far_rows(*blocks_three),
         grads,
@@ -1137,23 +1091,34 @@
         copies=12,
         flops=conv_flops,
     )
-    blocks = chan_blocks(residual_low, *two_grads)
-    two_other = swap(two_grads[1], "rows", 1)
-    shaped_grad, sums, *edges = local_call(
-        conv_two_back_kernel,
-        [out(act, F32), sums_shape, edge, edge],
+    one_edge = pltpu.VMEM((edge_rows, channels), BF)
+    back_parts = [out(act, F32), out(act, BF), out(act, BF), out(act, F32)]
+    (two_pairs,) = local_call(
+        pair_sum_kernel,
+        [out((pairs, 13, C // row_count, channels), BF)],
+        two_grads[0],
+        swap(two_grads[1], "rows", 1),
+    )
+    groups = [[2 * p + c for p in range(pairs)] for c in range(2)]
+    two_total = lax.psum_scatter(two_pairs, "rows", axis_index_groups=groups)
+    parts = local_call(
+        functools.partial(conv_back_kernel, first=0),
+        back_parts,
         zi,
-        *far_rows(*blocks),
-        Far(two_turned),
+        residual_low,
+        *rims((residual_low,)),
+        two_full,
+        scratch=[one_edge],
+    )
+    shaped_grad, sums = local_call(
+        back_two_sum_kernel,
+        [out(act, F32), sums_shape],
+        *chan_scatter(*parts),
         vectors,
         hidden,
         stats_two,
         mod,
-        scratch=[xs, taps],
-        copies=5,
-        flops=conv_flops,
-    )
-    shaped_rims = rims(*edges)
+    )
     out_bias = jnp.sum(
         cotangent.astype(F32) * loss_weight[None, :, None, None], axis=(0, 1, 2)
     )[None]
@@ -1161,13 +1126,10 @@
     sums_two = second[: 2 * images]
     hidden_low, conv_one_bias = local_call(
         back_two_kernel,
-        [out(tall, BF), out((1, channels), F32)],
-        zi,
+        [out(act, BF), out((1, channels), F32)],
         shaped_grad,
-        *shaped_rims,
         hidden,
-        *hidden_rims,
-        stats_two,
+        after(stats_two, two_pairs),
         sums_two,
         mod,
         vectors,
@@ -1177,28 +1139,32 @@
         [out((pairs, 9, C // row_count, channels), BF)] * 2,
         zi,
         *far_rows(*blocks_one),
+        *rims_one,
         hidden_low,
         scratch=[xs, pltpu.VMEM((2, pairs, 9, C // row_count, channels), BF)],
         copies=4,
         flops=conv_flops,
     )
-    blocks = chan_blocks(hidden_low, *one_grads)
-    terms = weight_scatter(
-        (two_grads[0], one_grads[0]), (two_other, swap(one_grads[1], "rows", 1))
-    )
-    normed_one_grad, sums = local_call(
-        conv_one_back_kernel,
+    one_terms = weight_scatter(one_grads[0], swap(one_grads[1], "rows", 1))
+    parts = local_call(
+        functools.partial(conv_back_kernel, first=0),
+        back_parts,
+        zi,
+        hidden_low,
+        *rims((hidden_low,)),
+        one_full,
+        scratch=[one_edge],
+    )
+    partial, sums = local_call(
+        back_one_sum_kernel,
         [out(act, F32), sums_shape],
-        zi,
-        *far_rows(*blocks),
-        Far(one_turned),
-        vectors,
+        *chan_scatter(*parts),
+        after(vectors, *one_terms),
         pixels,
         stats_one,
-        scratch=[xs, taps],
-        copies=5,
-        flops=conv_flops,
-    )
+        residual_grad,
+    )
+
     attended_blocks = chan_blocks(after(attended, sums))
     (activations,) = local_call(
         functools.partial(out_project_kernel, tap=12),
@@ -1220,11 +1186,11 @@
         precision=lax.Precision.HIGHEST,
     )
     ctx_all = ctx_all[:, :, :, :CTX].reshape(images, heads, 2, HEAD_DIM, CTX)
-    ctx_share = DCTX // row_count
-    ctx_rows = lax.dynamic_slice_in_dim(context, row * ctx_share, ctx_share, 2)
-    context_grad = jnp.einsum(
-        "bte,bhsdt->eshd", ctx_rows, ctx_all, preferred_element_type=F32
-    ).reshape(2 * ctx_share, channels)
+    context_grad = jnp.dot(
+        ctx_rows,
+        jnp.transpose(ctx_all, (2, 0, 4, 1, 3)).reshape(-1, channels),
+        preferred_element_type=F32,
+    )
     ctx_value_bias = jnp.sum(ctx_all[:, :, 1].astype(F32), axis=(0, 3)).reshape(1, channels)
 
     squared = jnp.zeros((1, channels), F32)
@@ -1240,7 +1206,8 @@
             out(conv_share, F32),
             out((-(-(2 * images + 2) // 8) * 8, channels), F32),
         ],
-        *terms,
+        two_total,
+        *one_terms,
         squared,
         sums,
         conv_one_bias,
@@ -1250,12 +1217,11 @@
     (pixel_grad,) = local_call(
         back_one_kernel,
         [out(act, F32)],
-        normed_one_grad,
+        partial,
         pixels,
         stats_one,
         third,
         vectors,
-        residual_grad,
     )
     vector_grad, squares = local_call(
         vector_kernel,
@@ -1298,9 +1264,10 @@
         update_kernel,
         outs[:-1],
         *squares,
-        *(Far(a) for a in operands),
-        scratch=[pltpu.VMEM(a.shape, F32) for a in operands],
-        copies=len(operands),
+        *(a if i % 4 == 3 else Far(a) for i, a in enumerate(operands)),
+        scratch=[pltpu.VMEM(a.shape, F32) for i, a in enumerate(operands) if i % 4 < 3],
+        copies=3 * len(weights),
+        limit=24,
     )
     for i in (8, 9, 10, 11):
         updated[i] = turn(updated[i])

time: 407 us -> 394 us (0.968)
  starting transfers between devices: 130 us -> 107 us
  waiting for transfers between devices: 113 us -> 125 us
  Pallas kernels: 105 us -> 95.4 us
  local copies, waits for them, and re-layouts: 24.1 us -> 32.4 us
    ppermute x73 -> x77, waiting for transfers between devices: 105 us -> 124 us  [swap(): return lax.ppermute(x, axis, [(i, i ^ distance) for i in range(size)])]
    ppermute x73 -> x77, starting transfers between devices: 114 us -> 102 us  [swap(): return lax.ppermute(x, axis, [(i, i ^ distance) for i in range(size)])]
    ppermute x10 -> x4, starting transfers between devices: 14.5 us -> 3.65 us  [rims(): outside = lax.ppermute(outside, 'rows', pairs + [(j, i) for i, j in pairs])]
    pallas_call x24 -> x27, Pallas kernels: 68 us -> 58.5 us  [local_call(): pl.pallas_call(kernel, out_shape=tuple(outs), in_specs=[spec(a) for a in...]
    unnamed x214 -> x264, local copies, waits for them, and re-layouts: 14.6 us -> 24 us
    ppermute x10 -> x4, waiting for transfers between devices: 7.9 us -> 0.01 us  [rims(): outside = lax.ppermute(outside, 'rows', pairs + [(j, i) for i, j in pairs])]
  transfers between devices with their start and end apart: 89 -> 86, of which waited for: 38 -> 53; matrix products, arithmetic and copies ran while one was open for 5% -> 5% of each run, Pallas kernels for 22% -> 10%
where the time goes in v3:
time: 394 us; the launch traced here: 387 us
  waiting for transfers between devices  125 us (32%)
  starting transfers between devices  107 us (27%)
  Pallas kernels  95.4 us (24%)
  local copies, waits for them, and re-layouts  32.4 us (8%)
  between operations  16.4 us (4%)
  other arithmetic  8.06 us (2%)
    ppermute x77, waiting for transfers between devices, swap(): return lax.ppermute(x, axis, [(i, i ^ distance) for i in range(size)])  124 us
    ppermute x77, starting transfers between devices, swap(): return lax.ppermute(x, axis, [(i, i ^ distance) for i in range(size)])  102 us
    pallas_call x27, Pallas kernels, local_call(): pl.pallas_call(kernel, out_shape=tuple(outs), in_specs=[spec(a) for a in...  58.5 us
    pallas_call x1, Pallas kernels, attention(): pl.pallas_call(functools.partial(attention_kernel, chunk=chunk, count=cou...  36.9 us
    unnamed x264, local copies, waits for them, and re-layouts  24 us
  transfers between devices with their start and end apart: 86, of which 53 were waited for; matrix products, arithmetic and copies ran while one was open for 5% of the time, Pallas kernels for 10%

profile of v3, /device:TPU:0, one launch (start us, length us, event | category | flops | bytes accessed | tf_op | source)
XLA Modules:
  0.0 387.4 jit_solution(17293359983674465449)
XLA Ops:
  9.8 1.6 convert_element_type.85
  11.5 5.0 %collective-permute-start.5 = (bf16[8,2,64,128]{3,2,1,0:T(8,128)(2,1)}, bf16[8,2,64,128]{3,2,1,0:T(8,128)(2,1)S(1)}, u32[]{:S(2)}, u32[]{:S(2)}) collective-permute-start(bf16[8,2,64,128]{3,2,1,0:T(8,128)(2,1)} %c0.1), channel_id=1, source_target_pairs={{0,3},{1,2},{2,1},{3,0},{4,7},{5,6},{6,5},{7,4},{8,11},{9,10},{10,... | collective-permute-start | bytes 786440 | tf_op jit(solution)/shard_map/ppermute | solution.py:34
  16.5 2.4 collective-permute-start.3
  23.9 5.2 %collective-permute-done.4 = bf16[8,2,64,128]{3,2,1,0:T(8,128)(2,1)S(1)} collective-permute-done((bf16[8,2,64,128]{3,2,1,0:T(8,128)(2,1)}, bf16[8,2,64,128]{3,2,1,0:T(8,128)(2,1)S(1)}, u32[]{:S(2)}, u32[]{:S(2)}) %collective-permute-start.4) | collective-permute-done | bytes 262176 | tf_op jit(solution)/shard_map/ppermute | solution.py:34
  31.8 1.7 collective-permute-start.7
  33.5 9.3 %collective-permute-done.7 = bf16[8,2,64,128]{3,2,1,0:T(8,128)(2,1)S(1)} collective-permute-done((bf16[8,2,64,128]{3,2,1,0:T(8,128)(2,1)S(1)}, bf16[8,2,64,128]{3,2,1,0:T(8,128)(2,1)S(1)}, u32[]{:S(2)}, u32[]{:S(2)}) %collective-permute-start.7) | collective-permute-done | bytes 262176 | tf_op jit(solution)/shard_map/ppermute | solution.py:34
  42.8 3.6 collective-permute-done.6
  49.3 6.7 %collective-permute-done.8 = bf16[8,2,64,128]{3,2,1,0:T(8,128)(2,1)S(1)} collective-permute-done((bf16[8,2,64,128]{3,2,1,0:T(8,128)(2,1)S(1)}, bf16[8,2,64,128]{3,2,1,0:T(8,128)(2,1)S(1)}, u32[]{:S(2)}, u32[]{:S(2)}) %collective-permute-start.8) | collective-permute-done | bytes 262176 | tf_op jit(solution)/shard_map/ppermute | solution.py:34
  57.1 2.7 collective-permute-start.9
  62.0 3.2 shard_map.501
  65.3 2.2 collective-permute-start.12
  68.4 3.0 collective-permute-start.15
  72.9 2.0 collective-permute-done.14
  75.4 3.5 collective-permute-start.20
  80.7 5.8 %collective-permute-done.20 = bf16[8,2,64,128]{3,2,1,0:T(8,128)(2,1)S(1)} collective-permute-done((bf16[8,2,64,128]{3,2,1,0:T(8,128)(2,1)S(1)}, bf16[8,2,64,128]{3,2,1,0:T(8,128)(2,1)S(1)}, u32[]{:S(2)}, u32[]{:S(2)}) %collective-permute-start.20) | collective-permute-done | bytes 262176 | tf_op jit(solution)/shard_map/ppermute | solution.py:34
  86.6 3.8 collective-permute-start.21
  93.5 2.0 collective-permute-start.17
  95.6 2.6 collective-permute-done.21
  98.2 2.3 collective-permute-done.17.w2
  101.1 3.3 shard_map.503.refs_3_
  105.7 2.8 collective-permute-start.22
  110.3 6.2 %shard_map.504 = (f32[8,2,64,128]{3,2,1,0:T(8,128)}, f32[4,128]{1,0:T(4,128)}) custom-call(s32[5]{0:T(128)} %copy-done.72, bf16[1024,128]{1,0:T(8,128)(2,1)} %bitcast.113, bf16[1024,128]{1,0:T(8,128)(2,1)} %bitcast.149, bf16[1024,128]{1,0:T(8,128)(2,1)} %bitcast.147, bf16[1024,128]{1,0:T(8,128)(2,1)} %bitcast.151, bf16[4,128,128]{2,1,0:T(8,128)(2,1)} %bitcast.166, ...), custom_call_target="tpu_custom_call" | custom-call | flops 1 | bytes 1 | tf_op jit(solution)/shard_map/pallas_call | solution.py:119
  119.3 4.0 %collective-permute-start.27 = (f32[4,128]{1,0:T(4,128)S(1)}, f32[4,128]{1,0:T(4,128)S(1)}, u32[]{:S(2)}, u32[]{:S(2)}) collective-permute-start(f32[4,128]{1,0:T(4,128)S(1)} %add.195), channel_id=1, source_target_pairs={{0,24},{4,28},{8,16},{12,20},{16,8},{20,12},{24,0},{28,4},{1,25},{... | collective-permute-start | bytes 6152 | tf_op jit(solution)/shard_map/ppermute | solution.py:34
  124.8 2.0 collective-permute-done.26
  128.7 1.7 collective-permute-start.29
  131.2 8.6 %collective-permute-done.29 = bf16[8,2,64,128]{3,2,1,0:T(8,128)(2,1)S(1)} collective-permute-done((bf16[8,2,64,128]{3,2,1,0:T(8,128)(2,1)S(1)}, bf16[8,2,64,128]{3,2,1,0:T(8,128)(2,1)S(1)}, u32[]{:S(2)}, u32[]{:S(2)}) %collective-permute-start.29) | collective-permute-done | bytes 262176 | tf_op jit(solution)/shard_map/ppermute | solution.py:34
  139.8 1.6 collective-permute-start.30
  141.5 1.7 fusion
  143.9 4.8 %collective-permute-done.30 = bf16[8,2,64,128]{3,2,1,0:T(8,128)(2,1)S(1)} collective-permute-done((bf16[8,2,64,128]{3,2,1,0:T(8,128)(2,1)S(1)}, bf16[8,2,64,128]{3,2,1,0:T(8,128)(2,1)S(1)}, u32[]{:S(2)}, u32[]{:S(2)}) %collective-permute-start.30) | collective-permute-done | bytes 262176 | tf_op jit(solution)/shard_map/ppermute | solution.py:34
  149.4 4.4 %shard_map.506 = (bf16[4,64,512]{2,1,0:T(8,128)(2,1)}, bf16[4,64,512]{2,1,0:T(8,128)(2,1)}, bf16[4,64,512]{2,1,0:T(8,128)(2,1)}, bf16[4,64,512]{2,1,0:T(8,128)(2,1)}) custom-call(s32[5]{0:T(128)} %copy-done.72, bf16[13,512,128]{2,1,0:T(8,128)(2,1)} %all-gather.6.cloned.1.call-done.w_far.refs_1_.w, f32[14,128]{1,0:T(8,128)} %refs_28_.1, ...), custom_call_target="tpu_custom_call" | custom-call | flops 1 | bytes 1 | tf_op jit(solution)/shard_map/pallas_call | solution.py:119
  157.4 5.9 %collective-permute-done.31.refs_3_ = bf16[4,64,512]{2,1,0:T(8,128)(2,1)S(1)} collective-permute-done((bf16[4,64,512]{2,1,0:T(8,128)(2,1)}, bf16[4,64,512]{2,1,0:T(8,128)(2,1)S(1)}, u32[]{:S(2)}, u32[]{:S(2)}) %collective-permute-start.31) | collective-permute-done | bytes 262176 | tf_op jit(solution)/shard_map/ppermute | solution.py:34
  163.4 4.2 %collective-permute-done.32.refs_4_ = bf16[4,64,512]{2,1,0:T(8,128)(2,1)S(1)} collective-permute-done((bf16[4,64,512]{2,1,0:T(8,128)(2,1)}, bf16[4,64,512]{2,1,0:T(8,128)(2,1)S(1)}, u32[]{:S(2)}, u32[]{:S(2)}) %collective-permute-start.32) | collective-permute-done | bytes 262176 | tf_op jit(solution)/shard_map/ppermute | solution.py:34
  171.5 36.9 %shard_map.507 = (bf16[2,64,2048]{2,1,0:T(8,128)(2,1)}, bf16[2,64,2176]{2,1,0:T(8,128)(2,1)}, bf16[2,64,2176]{2,1,0:T(8,128)(2,1)}) custom-call(s32[1]{0:T(128)S(6)} %add_shard_map.4.refs_0_, bf16[2,64,128]{2,1,0:T(8,128)(2,1)} %pad.5.refs_1_, bf16[4,64,512]{2,1,0:T(8,128)(2,1)} %get-tuple-element.168.refs_2_, bf16[4,64,512]{2,1,0:T(8,128)(2,1)} %copy-done.120, ...), custom_call_target="tpu_custom_call" | custom-call | flops 6643777536 | bytes 2162688 | tf_op jit(solution)/shard_map/pallas_call | solution.py:571
  208.9 1.8 collective-permute-done.38.other_far
  211.5 2.5 shard_map.508
  215.1 1.6 collective-permute-start.40
  217.5 4.4 %collective-permute-done.39.refs_3_ = bf16[3,64,512]{2,1,0:T(8,128)(2,1)S(1)} collective-permute-done((bf16[3,64,512]{2,1,0:T(8,128)(2,1)}, bf16[3,64,512]{2,1,0:T(8,128)(2,1)S(1)}, u32[]{:S(2)}, u32[]{:S(2)}) %collective-permute-start.39) | collective-permute-done | bytes 196640 | tf_op jit(solution)/shard_map/ppermute | solution.py:34
  222.0 3.5 collective-permute-done.40.refs_4_
  227.2 4.3 %shard_map.509 = (bf16[8,2,64,384]{3,2,1,0:T(8,128)(2,1)}, f32[8,2,64,128]{3,2,1,0:T(8,128)}, bf16[8,2,64,128]{3,2,1,0:T(8,128)(2,1)}, bf16[8,2,64,128]{3,2,1,0:...) custom-call(s32[5]{0:T(128)} %copy-done.72, ...), custom_call_target="tpu_custom_call" | custom-call | flops 1 | bytes 1 | tf_op jit(solution)/shard_map/pallas_call | solution.py:119
  231.7 2.0 collective-permute-start.45
  233.7 7.4 %collective-permute-done.46 = bf16[8,2,64,128]{3,2,1,0:T(8,128)(2,1)S(1)} collective-permute-done((bf16[8,2,64,128]{3,2,1,0:T(8,128)(2,1)}, bf16[8,2,64,128]{3,2,1,0:T(8,128)(2,1)S(1)}, u32[]{:S(2)}, u32[]{:S(2)}) %collective-permute-start.46) | collective-permute-done | bytes 262176 | tf_op jit(solution)/shard_map/ppermute | solution.py:34
  242.3 1.7 collective-permute-start.47
  249.5 2.4 collective-permute-done.44.refs_4_
  262.1 2.5 collective-permute-start.52
  265.5 3.2 shard_map.513
  271.6 6.8 %shard_map.515 = (bf16[4,13,64,128]{3,2,1,0:T(8,128)(2,1)}, bf16[4,13,64,128]{3,2,1,0:T(8,128)(2,1)}) custom-call(s32[5]{0:T(128)} %copy-done.72, bf16[1024,128]{1,0:T(8,128)(2,1)} %bitcast.114, bf16[1024,128]{1,0:T(8,128)(2,1)} %bitcast.150, bf16[1024,128]{1,0:T(8,128)(2,1)} %bitcast.148, bf16[1024,128]{1,0:T(8,128)(2,1)} %bitcast.152, ...), custom_call_target="tpu_custom_call" | custom-call | flops 1 | bytes 1 | tf_op jit(solution)/shard_map/pallas_call | solution.py:119
  279.4 2.2 collective-permute-start.56
  281.8 5.4 %collective-permute-done.54.t1 = bf16[8,2,64,128]{3,2,1,0:T(8,128)(2,1)S(1)} collective-permute-done((bf16[8,2,64,128]{3,2,1,0:T(8,128)(2,1)S(1)}, bf16[8,2,64,128]{3,2,1,0:T(8,128)(2,1)S(1)}, u32[]{:S(2)}, u32[]{:S(2)}) %collective-permute-start.54) | collective-permute-done | bytes 262176 | tf_op jit(solution)/shard_map/ppermute | solution.py:34
  287.3 6.4 %collective-permute-done.56.t2 = bf16[8,2,64,128]{3,2,1,0:T(8,128)(2,1)S(1)} collective-permute-done((bf16[8,2,64,128]{3,2,1,0:T(8,128)(2,1)S(1)}, bf16[8,2,64,128]{3,2,1,0:T(8,128)(2,1)S(1)}, u32[]{:S(2)}, u32[]{:S(2)}) %collective-permute-start.56) | collective-permute-done | bytes 262176 | tf_op jit(solution)/shard_map/ppermute | solution.py:34
  296.5 2.3 collective-permute-start.61
  306.9 2.0 collective-permute-start.62
  310.4 3.9 %shard_map.518 = (f32[8,2,64,128]{3,2,1,0:T(8,128)S(1)}, bf16[8,2,64,128]{3,2,1,0:T(8,128)(2,1)}, bf16[8,2,64,128]{3,2,1,0:T(8,128)(2,1)}, f32[8,2,64,128]{3,2,1,0:T(8,128)S(1)}) custom-call(s32[5]{0:T(128)S(1)} %copy-done.74, bf16[8,2,64,128]{3,2,1,0:T(8,128)(2,1)S(1)} %get-tuple-element.208.r, bf16[1,128,128]{2,1,0:T(8,128)(2,1)S(1)} %bitcast.146, ...), custom_call_target="tpu_custom_call" | custom-call | flops 1 | bytes 1 | tf_op jit(solution)/shard_map/pallas_call | solution.py:119
  316.0 5.3 %shard_map.519 = (bf16[4,9,64,128]{3,2,1,0:T(8,128)(2,1)}, bf16[4,9,64,128]{3,2,1,0:T(8,128)(2,1)}) custom-call(s32[5]{0:T(128)} %copy-done.72, bf16[1024,128]{1,0:T(8,128)(2,1)} %bitcast.116, bf16[1024,128]{1,0:T(8,128)(2,1)} %bitcast.122, bf16[1024,128]{1,0:T(8,128)(2,1)} %bitcast.120, bf16[1024,128]{1,0:T(8,128)(2,1)} %bitcast.124, ...), custom_call_target="tpu_custom_call" | custom-call | flops 1 | bytes 1 | tf_op jit(solution)/shard_map/pallas_call | solution.py:119
  325.2 1.8 collective-permute-start.66
  329.2 1.9 collective-permute-start.68
  331.1 1.9 collective-permute-start.69
  333.6 1.7 collective-permute-done.68.refs_2_
  336.0 3.2 collective-permute-done.69.refs_3_
  343.9 2.2 collective-permute-start.72
  353.2 4.3 %collective-permute-start.73 = (bf16[8,2,64,128]{3,2,1,0:T(8,128)(2,1)}, bf16[8,2,64,128]{3,2,1,0:T(8,128)(2,1)}, u32[]{:S(2)}, u32[]{:S(2)}) collective-permute-start(bf16[8,2,64,128]{3,2,1,0:T(8,128)(2,1)} %collective-permute-done.72), channel_id=1, source_target_pairs={{0,1},{1,0},{2,3},{3,2},{4,5},{5,4},{6,7},{7,6},{8,9},{9,8},{10,11... | collective-permute-start | bytes 786440 | tf_op jit(solution)/shard_map/ppermute | solution.py:34
  357.6 2.7 collective-permute-start.77
  363.9 6.2 %collective-permute-start.80 = (f32[8,128]{1,0:T(8,128)S(1)}, f32[8,128]{1,0:T(8,128)S(1)}, u32[]{:S(2)}, u32[]{:S(2)}) collective-permute-start(f32[8,128]{1,0:T(8,128)S(1)} %get-tuple-element.228.refs_0_), channel_id=1, source_target_pairs={{0,3},{1,2},{2,1},{3,0},{4,7},{5,6},{6,5},{7,4},{8,11},{9,10},{10,... | collective-permute-start | bytes 12296 | tf_op jit(solution)/shard_map/ppermute | solution.py:34
  371.0 3.7 shard_map.522
  376.0 4.6 %shard_map.526 = (f32[1,128]{1,0:T(1,128)}, f32[9,64,128]{2,1,0:T(8,128)}, f32[9,64,128]{2,1,0:T(8,128)}, f32[9,64,128]{2,1,0:T(8,128)}, bf16[9,64,128]{2,1,0:T(...) custom-call(f32[8,128]{1,0:T(8,128)S(1)} %get-tuple-element.228.refs, ...), custom_call_target="tpu_custom_call" | custom-call | flops 1 | bytes 1 | tf_op jit(solution)/shard_map/pallas_call | solution.py:119
  (477 shorter events, 108.3 us)
Async XLA Ops:
  7.2 53.5 %all-gather.8.cloned.1.call-start = ((), (), s32[]{:S(2)}) async-start(), calls=%async_computation.3 | async-start | bytes 1327104 | tf_op jit(solution)/shard_map/all_gather | solution.py:888
  11.5 79.0 %all-gather.6.cloned.1.call-start = ((), (), s32[]{:S(2)}) async-start(), calls=%async_computation.2 | async-start | bytes 1916928 | tf_op jit(solution)/shard_map/all_gather | solution.py:897
  11.5 12.4 %collective-permute-start.5 = (bf16[8,2,64,128]{3,2,1,0:T(8,128)(2,1)}, bf16[8,2,64,128]{3,2,1,0:T(8,128)(2,1)S(1)}, u32[]{:S(2)}, u32[]{:S(2)}) collective-permute-start(bf16[8,2,64,128]{3,2,1,0:T(8,128)(2,1)} %c0.1), channel_id=1, source_target_pairs={{0,3},{1,2},{2,1},{3,0},{4,7},{5,6},{6,5},{7,4},{8,11},{9,10},{10,... | collective-permute-start | bytes 786440 | tf_op jit(solution)/shard_map/ppermute | solution.py:34
  16.5 12.6 %collective-permute-start.4 = (bf16[8,2,64,128]{3,2,1,0:T(8,128)(2,1)}, bf16[8,2,64,128]{3,2,1,0:T(8,128)(2,1)S(1)}, u32[]{:S(2)}, u32[]{:S(2)}) collective-permute-start(bf16[8,2,64,128]{3,2,1,0:T(8,128)(2,1)} %c0.1), channel_id=1, source_target_pairs={{0,1},{1,0},{2,3},{3,2},{4,5},{5,4},{6,7},{7,6},{8,9},{9,8},{10,11... | collective-permute-start | bytes 786440 | tf_op jit(solution)/shard_map/ppermute | solution.py:34
  16.5 4.5 %collective-permute-start.3 = (f32[4,128]{1,0:T(4,128)S(1)}, f32[4,128]{1,0:T(4,128)S(1)}, u32[]{:S(2)}, u32[]{:S(2)}) collective-permute-start(f32[4,128]{1,0:T(4,128)S(1)} %add.173), channel_id=1, source_target_pairs={{0,24},{4,28},{8,16},{12,20},{16,8},{20,12},{24,0},{28,4},{1,25},{... | collective-permute-start | bytes 6152 | tf_op jit(solution)/shard_map/ppermute | solution.py:34
  19.5 3.6 collective-permute-start.1
  31.8 11.0 %collective-permute-start.7 = (bf16[8,2,64,128]{3,2,1,0:T(8,128)(2,1)S(1)}, bf16[8,2,64,128]{3,2,1,0:T(8,128)(2,1)S(1)}, u32[]{:S(2)}, u32[]{:S(2)}) collective-permute-start(bf16[8,2,64,128]{3,2,1,0:T(8,128)(2,1)S(1)} %shard_map.500), channel_id=1, source_target_pairs={{0,3},{1,2},{2,1},{3,0},{4,7},{5,6},{6,5},{7,4},{8,11},{9,10},{10,... | collective-permute-start | bytes 786440 | tf_op jit(solution)/shard_map/ppermute | solution.py:34
  33.5 12.9 %collective-permute-start.6 = (bf16[8,2,64,128]{3,2,1,0:T(8,128)(2,1)S(1)}, bf16[8,2,64,128]{3,2,1,0:T(8,128)(2,1)S(1)}, u32[]{:S(2)}, u32[]{:S(2)}) collective-permute-start(bf16[8,2,64,128]{3,2,1,0:T(8,128)(2,1)S(1)} %shard_map.500), channel_id=1, source_target_pairs={{0,1},{1,0},{2,3},{3,2},{4,5},{5,4},{6,7},{7,6},{8,9},{9,8},{10,11... | collective-permute-start | bytes 786440 | tf_op jit(solution)/shard_map/ppermute | solution.py:34
  47.2 94.2 %all-gather.4.cloned.1.call-start = ((), (), s32[]{:S(2)}) async-start(), calls=%async_computation.1 | async-start | bytes 1179648 | tf_op jit(solution)/shard_map/all_gather | solution.py:900
  48.9 7.1 %collective-permute-start.8 = (bf16[8,2,64,128]{3,2,1,0:T(8,128)(2,1)S(1)}, bf16[8,2,64,128]{3,2,1,0:T(8,128)(2,1)S(1)}, u32[]{:S(2)}, u32[]{:S(2)}) collective-permute-start(bf16[8,2,64,128]{3,2,1,0:T(8,128)(2,1)S(1)} %collective-permute-done.7), channel_id=1, source_target_pairs={{0,1},{1,0},{2,3},{3,2},{4,5},{5,4},{6,7},{7,6},{8,9},{9,8},{10,11... | collective-permute-start | bytes 786440 | tf_op jit(solution)/shard_map/ppermute | solution.py:34
  56.0 9.3 %collective-permute-start.11 = (bf16[8,2,64,128]{3,2,1,0:T(8,128)(2,1)S(1)}, bf16[8,2,64,128]{3,2,1,0:T(8,128)(2,1)}, u32[]{:S(2)}, u32[]{:S(2)}) collective-permute-start(bf16[8,2,64,128]{3,2,1,0:T(8,128)(2,1)S(1)} %collective-permute-done.5), channel_id=1, source_target_pairs={{0,1},{1,0},{2,3},{3,2},{4,5},{5,4},{6,7},{7,6},{8,9},{9,8},{10,11... | collective-permute-start | bytes 786440 | tf_op jit(solution)/shard_map/ppermute | solution.py:34
  57.1 3.7 collective-permute-start.9
  68.4 4.6 %collective-permute-start.15 = (f32[8,128]{1,0:T(8,128)S(1)}, f32[8,128]{1,0:T(8,128)S(1)}, u32[]{:S(2)}, u32[]{:S(2)}) collective-permute-start(f32[8,128]{1,0:T(8,128)S(1)} %fusion.20), channel_id=1, source_target_pairs={{0,24},{4,28},{8,16},{12,20},{16,8},{20,12},{24,0},{28,4},{1,25},{... | collective-permute-start | bytes 12296 | tf_op jit(solution)/shard_map/ppermute | solution.py:34
  71.4 3.6 collective-permute-start.14
  71.4 3.6 collective-permute-start.13
  75.4 11.1 %collective-permute-start.20 = (bf16[8,2,64,128]{3,2,1,0:T(8,128)(2,1)S(1)}, bf16[8,2,64,128]{3,2,1,0:T(8,128)(2,1)S(1)}, u32[]{:S(2)}, u32[]{:S(2)}) collective-permute-start(bf16[8,2,64,128]{3,2,1,0:T(8,128)(2,1)S(1)} %shard_map.502), channel_id=1, source_target_pairs={{0,3},{1,2},{2,1},{3,0},{4,7},{5,6},{6,5},{7,4},{8,11},{9,10},{10,... | collective-permute-start | bytes 786440 | tf_op jit(solution)/shard_map/ppermute | solution.py:34
  78.9 11.5 %collective-permute-start.19 = (bf16[8,2,64,128]{3,2,1,0:T(8,128)(2,1)S(1)}, bf16[8,2,64,128]{3,2,1,0:T(8,128)(2,1)S(1)}, u32[]{:S(2)}, u32[]{:S(2)}) collective-permute-start(bf16[8,2,64,128]{3,2,1,0:T(8,128)(2,1)S(1)} %shard_map.502), channel_id=1, source_target_pairs={{0,1},{1,0},{2,3},{3,2},{4,5},{5,4},{6,7},{7,6},{8,9},{9,8},{10,11... | collective-permute-start | bytes 786440 | tf_op jit(solution)/shard_map/ppermute | solution.py:34
  80.7 266.0 %reduce-scatter.4.cloned.1.call-start = ((), (), s32[]{:S(2)}) async-start(), calls=%async_computation.4 | async-start | bytes 1064960
  86.6 11.6 %collective-permute-start.21 = (bf16[8,2,64,128]{3,2,1,0:T(8,128)(2,1)S(1)}, bf16[8,2,64,128]{3,2,1,0:T(8,128)(2,1)S(1)}, u32[]{:S(2)}, u32[]{:S(2)}) collective-permute-start(bf16[8,2,64,128]{3,2,1,0:T(8,128)(2,1)S(1)} %collective-permute-done.20), channel_id=1, source_target_pairs={{0,1},{1,0},{2,3},{3,2},{4,5},{5,4},{6,7},{7,6},{8,9},{9,8},{10,11... | collective-permute-start | bytes 786440 | tf_op jit(solution)/shard_map/ppermute | solution.py:34
  92.1 6.1 %collective-permute-start.18 = (bf16[128,128]{1,0:T(8,128)(2,1)S(1)}, bf16[128,128]{1,0:T(8,128)(2,1)S(1)}, u32[]{:S(2)}, u32[]{:S(2)}) collective-permute-start(bf16[128,128]{1,0:T(8,128)(2,1)S(1)} %get-tuple-element.288), channel_id=1, source_target_pairs={{0,2},{1,3},{2,0},{3,1},{4,6},{5,7},{6,4},{7,5},{8,10},{9,11},{10,... | collective-permute-start | bytes 98312 | tf_op jit(solution)/shard_map/ppermute | solution.py:34
  93.5 7.0 %collective-permute-start.17 = (bf16[128,128]{1,0:T(8,128)(2,1)S(1)}, bf16[128,128]{1,0:T(8,128)(2,1)S(1)}, u32[]{:S(2)}, u32[]{:S(2)}) collective-permute-start(bf16[128,128]{1,0:T(8,128)(2,1)S(1)} %get-tuple-element.289), channel_id=1, source_target_pairs={{0,3},{1,2},{2,1},{3,0},{4,7},{5,6},{6,5},{7,4},{8,11},{9,10},{10,... | collective-permute-start | bytes 98312 | tf_op jit(solution)/shard_map/ppermute | solution.py:34
  95.5 4.9 %collective-permute-start.16 = (bf16[128,128]{1,0:T(8,128)(2,1)S(1)}, bf16[128,128]{1,0:T(8,128)(2,1)S(1)}, u32[]{:S(2)}, u32[]{:S(2)}) collective-permute-start(bf16[128,128]{1,0:T(8,128)(2,1)S(1)} %get-tuple-element.290), channel_id=1, source_target_pairs={{0,1},{1,0},{2,3},{3,2},{4,5},{5,4},{6,7},{7,6},{8,9},{9,8},{10,11... | collective-permute-start | bytes 98312 | tf_op jit(solution)/shard_map/ppermute | solution.py:34
  104.5 5.1 %collective-permute-start.23 = (bf16[4,2,64,128]{3,2,1,0:T(8,128)(2,1)S(1)}, bf16[4,2,64,128]{3,2,1,0:T(8,128)(2,1)S(1)}, u32[]{:S(2)}, u32[]{:S(2)}) collective-permute-start(bf16[4,2,64,128]{3,2,1,0:T(8,128)(2,1)S(1)} %get-tuple-element.268), channel_id=1, source_target_pairs={{4,8},{12,16},{20,24},{8,4},{16,12},{24,20},{5,9},{13,17},{21,25},... | collective-permute-start | bytes 393224 | tf_op jit(solution)/shard_map/ppermute | solution.py:72
  105.7 3.9 collective-permute-start.22
  119.3 5.6 %collective-permute-start.27 = (f32[4,128]{1,0:T(4,128)S(1)}, f32[4,128]{1,0:T(4,128)S(1)}, u32[]{:S(2)}, u32[]{:S(2)}) collective-permute-start(f32[4,128]{1,0:T(4,128)S(1)} %add.195), channel_id=1, source_target_pairs={{0,24},{4,28},{8,16},{12,20},{16,8},{20,12},{24,0},{28,4},{1,25},{... | collective-permute-start | bytes 6152 | tf_op jit(solution)/shard_map/ppermute | solution.py:34
  128.7 11.2 %collective-permute-start.29 = (bf16[8,2,64,128]{3,2,1,0:T(8,128)(2,1)S(1)}, bf16[8,2,64,128]{3,2,1,0:T(8,128)(2,1)S(1)}, u32[]{:S(2)}, u32[]{:S(2)}) collective-permute-start(bf16[8,2,64,128]{3,2,1,0:T(8,128)(2,1)S(1)} %shard_map.505), channel_id=1, source_target_pairs={{0,3},{1,2},{2,1},{3,0},{4,7},{5,6},{6,5},{7,4},{8,11},{9,10},{10,... | collective-permute-start | bytes 786440 | tf_op jit(solution)/shard_map/ppermute | solution.py:34
  131.2 12.8 %collective-permute-start.28 = (bf16[8,2,64,128]{3,2,1,0:T(8,128)(2,1)S(1)}, bf16[8,2,64,128]{3,2,1,0:T(8,128)(2,1)S(1)}, u32[]{:S(2)}, u32[]{:S(2)}) collective-permute-start(bf16[8,2,64,128]{3,2,1,0:T(8,128)(2,1)S(1)} %shard_map.505), channel_id=1, source_target_pairs={{0,1},{1,0},{2,3},{3,2},{4,5},{5,4},{6,7},{7,6},{8,9},{9,8},{10,11... | collective-permute-start | bytes 786440 | tf_op jit(solution)/shard_map/ppermute | solution.py:34
  139.8 8.9 %collective-permute-start.30 = (bf16[8,2,64,128]{3,2,1,0:T(8,128)(2,1)S(1)}, bf16[8,2,64,128]{3,2,1,0:T(8,128)(2,1)S(1)}, u32[]{:S(2)}, u32[]{:S(2)}) collective-permute-start(bf16[8,2,64,128]{3,2,1,0:T(8,128)(2,1)S(1)} %collective-permute-done.29), channel_id=1, source_target_pairs={{0,1},{1,0},{2,3},{3,2},{4,5},{5,4},{6,7},{7,6},{8,9},{9,8},{10,11... | collective-permute-start | bytes 786440 | tf_op jit(solution)/shard_map/ppermute | solution.py:34
  153.9 9.5 %collective-permute-start.31 = (bf16[4,64,512]{2,1,0:T(8,128)(2,1)}, bf16[4,64,512]{2,1,0:T(8,128)(2,1)S(1)}, u32[]{:S(2)}, u32[]{:S(2)}) collective-permute-start(bf16[4,64,512]{2,1,0:T(8,128)(2,1)} %get-tuple-element.169), channel_id=1, source_target_pairs={{0,8},{4,12},{8,0},{12,4},{16,24},{20,28},{24,16},{28,20},{1,9},{5... | collective-permute-start | bytes 786440 | tf_op jit(solution)/shard_map/ppermute | solution.py:34
  154.8 12.7 %collective-permute-start.32 = (bf16[4,64,512]{2,1,0:T(8,128)(2,1)}, bf16[4,64,512]{2,1,0:T(8,128)(2,1)S(1)}, u32[]{:S(2)}, u32[]{:S(2)}) collective-permute-start(bf16[4,64,512]{2,1,0:T(8,128)(2,1)} %get-tuple-element.170), channel_id=1, source_target_pairs={{0,16},{4,20},{8,24},{12,28},{16,0},{20,4},{24,8},{28,12},{1,17},{... | collective-permute-start | bytes 786440 | tf_op jit(solution)/shard_map/ppermute | solution.py:34
  156.4 12.2 %collective-permute-start.33 = (bf16[4,64,512]{2,1,0:T(8,128)(2,1)}, bf16[4,64,512]{2,1,0:T(8,128)(2,1)S(1)}, u32[]{:S(2)}, u32[]{:S(2)}) collective-permute-start(bf16[4,64,512]{2,1,0:T(8,128)(2,1)} %get-tuple-element.171), channel_id=1, source_target_pairs={{0,24},{4,28},{8,16},{12,20},{16,8},{20,12},{24,0},{28,4},{1,25},{... | collective-permute-start | bytes 786440 | tf_op jit(solution)/shard_map/ppermute | solution.py:34
  157.4 12.4 %collective-permute-start.34 = (bf16[4,64,512]{2,1,0:T(8,128)(2,1)}, bf16[4,64,512]{2,1,0:T(8,128)(2,1)S(1)}, u32[]{:S(2)}, u32[]{:S(2)}) collective-permute-start(bf16[4,64,512]{2,1,0:T(8,128)(2,1)} %get-tuple-element.168.refs_2_), channel_id=1, source_target_pairs={{0,4},{4,0},{8,12},{12,8},{16,20},{20,16},{24,28},{28,24},{1,5},{5... | collective-permute-start | bytes 786440 | tf_op jit(solution)/shard_map/ppermute | solution.py:34
  163.4 6.5 %collective-permute-start.35 = (bf16[4,64,512]{2,1,0:T(8,128)(2,1)S(1)}, bf16[4,64,512]{2,1,0:T(8,128)(2,1)S(1)}, u32[]{:S(2)}, u32[]{:S(2)}) collective-permute-start(bf16[4,64,512]{2,1,0:T(8,128)(2,1)S(1)} %collective-permute-done.31.refs_3_), channel_id=1, source_target_pairs={{0,4},{4,0},{8,12},{12,8},{16,20},{20,16},{24,28},{28,24},{1,5},{5... | collective-permute-start | bytes 786440 | tf_op jit(solution)/shard_map/ppermute | solution.py:34
  214.0 8.0 %collective-permute-start.39 = (bf16[3,64,512]{2,1,0:T(8,128)(2,1)}, bf16[3,64,512]{2,1,0:T(8,128)(2,1)S(1)}, u32[]{:S(2)}, u32[]{:S(2)}) collective-permute-start(bf16[3,64,512]{2,1,0:T(8,128)(2,1)} %get-tuple-element.177), channel_id=1, source_target_pairs={{0,8},{4,12},{8,0},{12,4},{16,24},{20,28},{24,16},{28,20},{1,9},{5... | collective-permute-start | bytes 589832 | tf_op jit(solution)/shard_map/ppermute | solution.py:34
  215.1 10.4 %collective-permute-start.40 = (bf16[3,64,512]{2,1,0:T(8,128)(2,1)}, bf16[3,64,512]{2,1,0:T(8,128)(2,1)S(1)}, u32[]{:S(2)}, u32[]{:S(2)}) collective-permute-start(bf16[3,64,512]{2,1,0:T(8,128)(2,1)} %get-tuple-element.178), channel_id=1, source_target_pairs={{0,16},{4,20},{8,24},{12,28},{16,0},{20,4},{24,8},{28,12},{1,17},{... | collective-permute-start | bytes 589832 | tf_op jit(solution)/shard_map/ppermute | solution.py:34
  216.7 9.8 %collective-permute-start.41 = (bf16[3,64,512]{2,1,0:T(8,128)(2,1)}, bf16[3,64,512]{2,1,0:T(8,128)(2,1)S(1)}, u32[]{:S(2)}, u32[]{:S(2)}) collective-permute-start(bf16[3,64,512]{2,1,0:T(8,128)(2,1)} %get-tuple-element.179), channel_id=1, source_target_pairs={{0,24},{4,28},{8,16},{12,20},{16,8},{20,12},{24,0},{28,4},{1,25},{... | collective-permute-start | bytes 589832 | tf_op jit(solution)/shard_map/ppermute | solution.py:34
  231.6 9.5 %collective-permute-start.46 = (bf16[8,2,64,128]{3,2,1,0:T(8,128)(2,1)}, bf16[8,2,64,128]{3,2,1,0:T(8,128)(2,1)S(1)}, u32[]{:S(2)}, u32[]{:S(2)}) collective-permute-start(bf16[8,2,64,128]{3,2,1,0:T(8,128)(2,1)} %get-tuple-element.180), channel_id=1, source_target_pairs={{0,1},{1,0},{2,3},{3,2},{4,5},{5,4},{6,7},{7,6},{8,9},{9,8},{10,11... | collective-permute-start | bytes 786440 | tf_op jit(solution)/shard_map/ppermute | solution.py:34
  231.7 20.2 %collective-permute-start.45 = (bf16[8,2,64,128]{3,2,1,0:T(8,128)(2,1)}, bf16[8,2,64,128]{3,2,1,0:T(8,128)(2,1)S(1)}, u32[]{:S(2)}, u32[]{:S(2)}) collective-permute-start(bf16[8,2,64,128]{3,2,1,0:T(8,128)(2,1)} %get-tuple-element.190), channel_id=1, source_target_pairs={{0,1},{1,0},{2,3},{3,2},{4,5},{5,4},{6,7},{7,6},{8,9},{9,8},{10,11... | collective-permute-start | bytes 786440 | tf_op jit(solution)/shard_map/ppermute | solution.py:34
  242.3 9.7 %collective-permute-start.47 = (bf16[8,2,64,128]{3,2,1,0:T(8,128)(2,1)S(1)}, bf16[8,2,64,128]{3,2,1,0:T(8,128)(2,1)S(1)}, u32[]{:S(2)}, u32[]{:S(2)}) collective-permute-start(bf16[8,2,64,128]{3,2,1,0:T(8,128)(2,1)S(1)} %add_convert_fusion.2), channel_id=1, source_target_pairs={{0,3},{1,2},{2,1},{3,0},{4,7},{5,6},{6,5},{7,4},{8,11},{9,10},{10,... | collective-permute-start | bytes 786440 | tf_op jit(solution)/shard_map/ppermute | solution.py:34
  244.0 4.6 %collective-permute-start.42 = (bf16[64,768]{1,0:T(8,128)(2,1)S(1)}, bf16[64,768]{1,0:T(8,128)(2,1)S(1)}, u32[]{:S(2)}, u32[]{:S(2)}) collective-permute-start(bf16[64,768]{1,0:T(8,128)(2,1)S(1)} %copy-done.129), channel_id=1, source_target_pairs={{0,8},{4,12},{8,0},{12,4},{16,24},{20,28},{24,16},{28,20},{1,9},{5... | collective-permute-start | bytes 294920 | tf_op jit(solution)/shard_map/ppermute | solution.py:34
  244.9 4.6 %collective-permute-start.43 = (bf16[64,768]{1,0:T(8,128)(2,1)S(1)}, bf16[64,768]{1,0:T(8,128)(2,1)S(1)}, u32[]{:S(2)}, u32[]{:S(2)}) collective-permute-start(bf16[64,768]{1,0:T(8,128)(2,1)S(1)} %copy-done.128), channel_id=1, source_target_pairs={{0,16},{4,20},{8,24},{12,28},{16,0},{20,4},{24,8},{28,12},{1,17},{... | collective-permute-start | bytes 294920 | tf_op jit(solution)/shard_map/ppermute | solution.py:34
  246.4 5.5 %collective-permute-start.44 = (bf16[64,768]{1,0:T(8,128)(2,1)S(1)}, bf16[64,768]{1,0:T(8,128)(2,1)S(1)}, u32[]{:S(2)}, u32[]{:S(2)}) collective-permute-start(bf16[64,768]{1,0:T(8,128)(2,1)S(1)} %copy-done.127), channel_id=1, source_target_pairs={{0,24},{4,28},{8,16},{12,20},{16,8},{20,12},{24,0},{28,4},{1,25},{... | collective-permute-start | bytes 294920 | tf_op jit(solution)/shard_map/ppermute | solution.py:34
  254.6 4.5 %collective-permute-start.51 = (f32[4,128]{1,0:T(4,128)S(1)}, f32[4,128]{1,0:T(4,128)S(1)}, u32[]{:S(2)}, u32[]{:S(2)}) collective-permute-start(f32[4,128]{1,0:T(4,128)S(1)} %add.200), channel_id=1, source_target_pairs={{0,24},{4,28},{8,16},{12,20},{16,8},{20,12},{24,0},{28,4},{1,25},{... | collective-permute-start | bytes 6152 | tf_op jit(solution)/shard_map/ppermute | solution.py:34
  268.7 10.6 %collective-permute-start.55 = (bf16[8,2,64,128]{3,2,1,0:T(8,128)(2,1)S(1)}, bf16[8,2,64,128]{3,2,1,0:T(8,128)(2,1)S(1)}, u32[]{:S(2)}, u32[]{:S(2)}) collective-permute-start(bf16[8,2,64,128]{3,2,1,0:T(8,128)(2,1)S(1)} %get-tuple-element.199), channel_id=1, source_target_pairs={{0,1},{1,0},{2,3},{3,2},{4,5},{5,4},{6,7},{7,6},{8,9},{9,8},{10,11... | collective-permute-start | bytes 786440 | tf_op jit(solution)/shard_map/ppermute | solution.py:34
  278.5 25.2 %collective-permute-start.57 = (bf16[4,13,64,128]{3,2,1,0:T(8,128)(2,1)}, bf16[4,13,64,128]{3,2,1,0:T(8,128)(2,1)S(1)}, u32[]{:S(2)}, u32[]{:S(2)}) collective-permute-start(bf16[4,13,64,128]{3,2,1,0:T(8,128)(2,1)} %get-tuple-element.203), channel_id=1, source_target_pairs={{0,4},{4,0},{8,12},{12,8},{16,20},{20,16},{24,28},{28,24},{1,5},{5... | collective-permute-start | bytes 2555912 | tf_op jit(solution)/shard_map/ppermute | solution.py:34
  278.7 8.5 %collective-permute-start.54 = (bf16[8,2,64,128]{3,2,1,0:T(8,128)(2,1)S(1)}, bf16[8,2,64,128]{3,2,1,0:T(8,128)(2,1)S(1)}, u32[]{:S(2)}, u32[]{:S(2)}) collective-permute-start(bf16[8,2,64,128]{3,2,1,0:T(8,128)(2,1)S(1)} %get-tuple-element.197), channel_id=1, source_target_pairs={{0,1},{1,0},{2,3},{3,2},{4,5},{5,4},{6,7},{7,6},{8,9},{9,8},{10,11... | collective-permute-start | bytes 786440 | tf_op jit(solution)/shard_map/ppermute | solution.py:34
  279.4 14.3 %collective-permute-start.56 = (bf16[8,2,64,128]{3,2,1,0:T(8,128)(2,1)S(1)}, bf16[8,2,64,128]{3,2,1,0:T(8,128)(2,1)S(1)}, u32[]{:S(2)}, u32[]{:S(2)}) collective-permute-start(bf16[8,2,64,128]{3,2,1,0:T(8,128)(2,1)S(1)} %add_convert_fusion.1), channel_id=1, source_target_pairs={{0,3},{1,2},{2,1},{3,0},{4,7},{5,6},{6,5},{7,4},{8,11},{9,10},{10,... | collective-permute-start | bytes 786440 | tf_op jit(solution)/shard_map/ppermute | solution.py:34
  296.5 4.6 %collective-permute-start.61 = (f32[8,128]{1,0:T(8,128)S(1)}, f32[8,128]{1,0:T(8,128)S(1)}, u32[]{:S(2)}, u32[]{:S(2)}) collective-permute-start(f32[8,128]{1,0:T(8,128)S(1)} %fusion.21), channel_id=1, source_target_pairs={{0,24},{4,28},{8,16},{12,20},{16,8},{20,12},{24,0},{28,4},{1,25},{... | collective-permute-start | bytes 12296 | tf_op jit(solution)/shard_map/ppermute | solution.py:34
  314.3 9.9 %collective-permute-start.65 = (bf16[8,2,64,128]{3,2,1,0:T(8,128)(2,1)}, bf16[8,2,64,128]{3,2,1,0:T(8,128)(2,1)}, u32[]{:S(2)}, u32[]{:S(2)}) collective-permute-start(bf16[8,2,64,128]{3,2,1,0:T(8,128)(2,1)} %get-tuple-element.212), channel_id=1, source_target_pairs={{0,1},{1,0},{2,3},{3,2},{4,5},{5,4},{6,7},{7,6},{8,9},{9,8},{10,11... | collective-permute-start | bytes 786440 | tf_op jit(solution)/shard_map/ppermute | solution.py:34
  321.3 7.0 %collective-permute-start.67 = (bf16[4,9,64,128]{3,2,1,0:T(8,128)(2,1)}, bf16[4,9,64,128]{3,2,1,0:T(8,128)(2,1)S(1)}, u32[]{:S(2)}, u32[]{:S(2)}) collective-permute-start(bf16[4,9,64,128]{3,2,1,0:T(8,128)(2,1)} %get-tuple-element.214), channel_id=1, source_target_pairs={{0,4},{4,0},{8,12},{12,8},{16,20},{20,16},{24,28},{28,24},{1,5},{5... | collective-permute-start | bytes 1769480 | tf_op jit(solution)/shard_map/ppermute | solution.py:34
  323.4 17.6 %collective-permute-start.64 = (bf16[8,2,64,128]{3,2,1,0:T(8,128)(2,1)}, bf16[8,2,64,128]{3,2,1,0:T(8,128)(2,1)S(1)}, u32[]{:S(2)}, u32[]{:S(2)}) collective-permute-start(bf16[8,2,64,128]{3,2,1,0:T(8,128)(2,1)} %get-tuple-element.210), channel_id=1, source_target_pairs={{0,1},{1,0},{2,3},{3,2},{4,5},{5,4},{6,7},{7,6},{8,9},{9,8},{10,11... | collective-permute-start | bytes 786440 | tf_op jit(solution)/shard_map/ppermute | solution.py:34
  325.2 15.8 %collective-permute-start.66 = (bf16[8,2,64,128]{3,2,1,0:T(8,128)(2,1)S(1)}, bf16[8,2,64,128]{3,2,1,0:T(8,128)(2,1)S(1)}, u32[]{:S(2)}, u32[]{:S(2)}) collective-permute-start(bf16[8,2,64,128]{3,2,1,0:T(8,128)(2,1)S(1)} %add_convert_fusion), channel_id=1, source_target_pairs={{0,3},{1,2},{2,1},{3,0},{4,7},{5,6},{6,5},{7,4},{8,11},{9,10},{10,... | collective-permute-start | bytes 786440 | tf_op jit(solution)/shard_map/ppermute | solution.py:34
  329.2 6.1 %collective-permute-start.68 = (bf16[9,64,128]{2,1,0:T(8,128)(2,1)S(1)}, bf16[9,64,128]{2,1,0:T(8,128)(2,1)S(1)}, u32[]{:S(2)}, u32[]{:S(2)}) collective-permute-start(bf16[9,64,128]{2,1,0:T(8,128)(2,1)S(1)} %get-tuple-element.216), channel_id=1, source_target_pairs={{0,8},{4,12},{8,0},{12,4},{16,24},{20,28},{24,16},{28,20},{1,9},{5... | collective-permute-start | bytes 442376 | tf_op jit(solution)/shard_map/ppermute | solution.py:34
  331.1 8.0 %collective-permute-start.69 = (bf16[9,64,128]{2,1,0:T(8,128)(2,1)S(1)}, bf16[9,64,128]{2,1,0:T(8,128)(2,1)S(1)}, u32[]{:S(2)}, u32[]{:S(2)}) collective-permute-start(bf16[9,64,128]{2,1,0:T(8,128)(2,1)S(1)} %get-tuple-element.217), channel_id=1, source_target_pairs={{0,16},{4,20},{8,24},{12,28},{16,0},{20,4},{24,8},{28,12},{1,17},{... | collective-permute-start | bytes 442376 | tf_op jit(solution)/shard_map/ppermute | solution.py:34
  333.1 7.3 %collective-permute-start.70 = (bf16[9,64,128]{2,1,0:T(8,128)(2,1)S(1)}, bf16[9,64,128]{2,1,0:T(8,128)(2,1)S(1)}, u32[]{:S(2)}, u32[]{:S(2)}) collective-permute-start(bf16[9,64,128]{2,1,0:T(8,128)(2,1)S(1)} %get-tuple-element.218), channel_id=1, source_target_pairs={{0,24},{4,28},{8,16},{12,20},{16,8},{20,12},{24,0},{28,4},{1,25},{... | collective-permute-start | bytes 442376 | tf_op jit(solution)/shard_map/ppermute | solution.py:34
  343.9 9.4 %collective-permute-start.72 = (bf16[8,2,64,128]{3,2,1,0:T(8,128)(2,1)S(1)}, bf16[8,2,64,128]{3,2,1,0:T(8,128)(2,1)}, u32[]{:S(2)}, u32[]{:S(2)}) collective-permute-start(bf16[8,2,64,128]{3,2,1,0:T(8,128)(2,1)S(1)} %copy-done.32), channel_id=1, source_target_pairs={{0,3},{1,2},{2,1},{3,0},{4,7},{5,6},{6,5},{7,4},{8,11},{9,10},{10,... | collective-permute-start | bytes 786440 | tf_op jit(solution)/shard_map/ppermute | solution.py:34
  351.8 5.8 %collective-permute-start.74 = (f32[8,128]{1,0:T(8,128)S(1)}, f32[8,128]{1,0:T(8,128)S(1)}, u32[]{:S(2)}, u32[]{:S(2)}) collective-permute-start(f32[8,128]{1,0:T(8,128)S(1)} %get-tuple-element.226), channel_id=1, source_target_pairs={{0,4},{4,0},{8,12},{12,8},{16,20},{20,16},{24,28},{28,24},{1,5},{5... | collective-permute-start | bytes 12296 | tf_op jit(solution)/shard_map/ppermute | solution.py:34
  351.8 18.3 %collective-permute-start.71 = (bf16[8,2,64,128]{3,2,1,0:T(8,128)(2,1)S(1)}, bf16[8,2,64,128]{3,2,1,0:T(8,128)(2,1)}, u32[]{:S(2)}, u32[]{:S(2)}) collective-permute-start(bf16[8,2,64,128]{3,2,1,0:T(8,128)(2,1)S(1)} %copy-done.32), channel_id=1, source_target_pairs={{0,1},{1,0},{2,3},{3,2},{4,5},{5,4},{6,7},{7,6},{8,9},{9,8},{10,11... | collective-permute-start | bytes 786440 | tf_op jit(solution)/shard_map/ppermute | solution.py:34
  353.2 17.5 %collective-permute-start.73 = (bf16[8,2,64,128]{3,2,1,0:T(8,128)(2,1)}, bf16[8,2,64,128]{3,2,1,0:T(8,128)(2,1)}, u32[]{:S(2)}, u32[]{:S(2)}) collective-permute-start(bf16[8,2,64,128]{3,2,1,0:T(8,128)(2,1)} %collective-permute-done.72), channel_id=1, source_target_pairs={{0,1},{1,0},{2,3},{3,2},{4,5},{5,4},{6,7},{7,6},{8,9},{9,8},{10,11... | collective-permute-start | bytes 786440 | tf_op jit(solution)/shard_map/ppermute | solution.py:34
  357.6 4.5 %collective-permute-start.77 = (f32[8,128]{1,0:T(8,128)S(1)}, f32[8,128]{1,0:T(8,128)S(1)}, u32[]{:S(2)}, u32[]{:S(2)}) collective-permute-start(f32[8,128]{1,0:T(8,128)S(1)} %add.213), channel_id=1, source_target_pairs={{0,24},{4,28},{8,16},{12,20},{16,8},{20,12},{24,0},{28,4},{1,25},{... | collective-permute-start | bytes 12296 | tf_op jit(solution)/shard_map/ppermute | solution.py:34
  362.1 13.7 %collective-permute-start.81 = (f32[1,64,128]{2,1,0:T(8,128)}, f32[1,64,128]{2,1,0:T(8,128)S(1)}, u32[]{:S(2)}, u32[]{:S(2)}) collective-permute-start(f32[1,64,128]{2,1,0:T(8,128)} %copy-done.95), channel_id=1, source_target_pairs={{0,0},{8,1},{16,2},{24,3},{4,4},{12,5},{20,6},{28,7},{1,8},{9,9},{... | collective-permute-start | bytes 98312 | tf_op jit(solution)/shard_map/ppermute | solution.py:827
  363.9 11.8 %collective-permute-start.80 = (f32[8,128]{1,0:T(8,128)S(1)}, f32[8,128]{1,0:T(8,128)S(1)}, u32[]{:S(2)}, u32[]{:S(2)}) collective-permute-start(f32[8,128]{1,0:T(8,128)S(1)} %get-tuple-element.228.refs_0_), channel_id=1, source_target_pairs={{0,3},{1,2},{2,1},{3,0},{4,7},{5,6},{6,5},{7,4},{8,11},{9,10},{10,... | collective-permute-start | bytes 12296 | tf_op jit(solution)/shard_map/ppermute | solution.py:34
  370.1 5.7 %collective-permute-start.79 = (f32[8,128]{1,0:T(8,128)S(1)}, f32[8,128]{1,0:T(8,128)S(1)}, u32[]{:S(2)}, u32[]{:S(2)}) collective-permute-start(f32[8,128]{1,0:T(8,128)S(1)} %get-tuple-element.228.refs_0_), channel_id=1, source_target_pairs={{0,2},{1,3},{2,0},{3,1},{4,6},{5,7},{6,4},{7,5},{8,10},{9,11},{10,... | collective-permute-start | bytes 12296 | tf_op jit(solution)/shard_map/ppermute | solution.py:34
  370.1 5.7 %collective-permute-start.78 = (f32[8,128]{1,0:T(8,128)S(1)}, f32[8,128]{1,0:T(8,128)S(1)}, u32[]{:S(2)}, u32[]{:S(2)}) collective-permute-start(f32[8,128]{1,0:T(8,128)S(1)} %get-tuple-element.228.refs_0_), channel_id=1, source_target_pairs={{0,1},{1,0},{2,3},{3,2},{4,5},{5,4},{6,7},{7,6},{8,9},{9,8},{10,11... | collective-permute-start | bytes 12296 | tf_op jit(solution)/shard_map/ppermute | solution.py:34
  (154 other events, 1633.1 us)
Sparse Core Ops, SparseCore 0:
  11.6 26.6 all-gather.7
  47.3 26.0 all-gather.5
  80.8 22.7 all-gather.3
  305.5 25.4 reduce-scatter.3

commit v4 on v3

--- a/solution.py
+++ b/solution.py
@@ -1119,6 +1119,8 @@
         stats_two,
         mod,
     )
+    att = after(attended, sums)
+    att_near, att_far = swap(att, "chan", 1), swap(att, "chan", 3)
     out_bias = jnp.sum(
         cotangent.astype(F32) * loss_weight[None, :, None, None], axis=(0, 1, 2)
     )[None]
@@ -1150,7 +1152,7 @@
         functools.partial(conv_back_kernel, first=0),
         back_parts,
         zi,
-        hidden_low,
+        after(hidden_low, att_near, att_far),
         *rims((hidden_low,)),
         one_full,
         scratch=[one_edge],
@@ -1165,7 +1167,8 @@
         residual_grad,
     )
 
-    attended_blocks = chan_blocks(after(attended, sums))
+    att_far = after(att_far, sums)
+    attended_blocks = (attended, att_near, att_far, swap(att_far, "chan", 1))
     (activations,) = local_call(
         functools.partial(out_project_kernel, tap=12),
         [out(act, BF)],

time: 394 us -> 384 us (0.975)
  starting transfers between devices: 107 us -> 100 us
    ppermute x77, starting transfers between devices: 102 us -> 95.9 us  [swap(): return lax.ppermute(x, axis, [(i, i ^ distance) for i in range(size)])]
    unnamed x264 -> x246, local copies, waits for them, and re-layouts: 24 us -> 25 us
  transfers between devices with their start and end apart: 86 -> 86, of which waited for: 53 -> 49; matrix products, arithmetic and copies ran while one was open for 5% -> 4% of each run, Pallas kernels for 10% -> 10%
where the time goes in v4:
time: 384 us; the launch traced here: 377 us
  waiting for transfers between devices  122 us (32%)
  starting transfers between devices  100 us (26%)
  Pallas kernels  95.9 us (25%)
  local copies, waits for them, and re-layouts  32.5 us (8%)
  between operations  16.4 us (4%)
  other arithmetic  7.33 us (2%)
    ppermute x77, waiting for transfers between devices, swap(): return lax.ppermute(x, axis, [(i, i ^ distance) for i in range(size)])  122 us
    ppermute x77, starting transfers between devices, swap(): return lax.ppermute(x, axis, [(i, i ^ distance) for i in range(size)])  95.9 us
    pallas_call x27, Pallas kernels, local_call(): pl.pallas_call(kernel, out_shape=tuple(outs), in_specs=[spec(a) for a in...  59 us
    pallas_call x1, Pallas kernels, attention(): pl.pallas_call(functools.partial(attention_kernel, chunk=chunk, count=cou...  36.9 us
    unnamed x246, local copies, waits for them, and re-layouts  25 us
  transfers between devices with their start and end apart: 86, of which 49 were waited for; matrix products, arithmetic and copies ran while one was open for 4% of the time, Pallas kernels for 10%

profile of v4, /device:TPU:0, one launch (start us, length us, event | category | flops | bytes accessed | tf_op | source)
XLA Modules:
  0.0 377.2 jit_solution(9734183711810002564)
XLA Ops:
  11.5 5.0 %collective-permute-start.5 = (bf16[8,2,64,128]{3,2,1,0:T(8,128)(2,1)}, bf16[8,2,64,128]{3,2,1,0:T(8,128)(2,1)S(1)}, u32[]{:S(2)}, u32[]{:S(2)}) collective-permute-start(bf16[8,2,64,128]{3,2,1,0:T(8,128)(2,1)} %c0.1), channel_id=1, source_target_pairs={{0,3},{1,2},{2,1},{3,0},{4,7},{5,6},{6,5},{7,4},{8,11},{9,10},{10,... | collective-permute-start | bytes 786440 | tf_op jit(solution)/shard_map/ppermute | solution.py:34
  16.5 2.4 collective-permute-start.3
  23.9 5.2 %collective-permute-done.4 = bf16[8,2,64,128]{3,2,1,0:T(8,128)(2,1)S(1)} collective-permute-done((bf16[8,2,64,128]{3,2,1,0:T(8,128)(2,1)}, bf16[8,2,64,128]{3,2,1,0:T(8,128)(2,1)S(1)}, u32[]{:S(2)}, u32[]{:S(2)}) %collective-permute-start.4) | collective-permute-done | bytes 262176 | tf_op jit(solution)/shard_map/ppermute | solution.py:34
  31.8 1.7 collective-permute-start.7
  33.5 9.3 %collective-permute-done.7 = bf16[8,2,64,128]{3,2,1,0:T(8,128)(2,1)S(1)} collective-permute-done((bf16[8,2,64,128]{3,2,1,0:T(8,128)(2,1)S(1)}, bf16[8,2,64,128]{3,2,1,0:T(8,128)(2,1)S(1)}, u32[]{:S(2)}, u32[]{:S(2)}) %collective-permute-start.7) | collective-permute-done | bytes 262176 | tf_op jit(solution)/shard_map/ppermute | solution.py:34
  42.8 3.6 collective-permute-done.6
  48.8 6.7 %collective-permute-done.8 = bf16[8,2,64,128]{3,2,1,0:T(8,128)(2,1)S(1)} collective-permute-done((bf16[8,2,64,128]{3,2,1,0:T(8,128)(2,1)S(1)}, bf16[8,2,64,128]{3,2,1,0:T(8,128)(2,1)S(1)}, u32[]{:S(2)}, u32[]{:S(2)}) %collective-permute-start.8) | collective-permute-done | bytes 262176 | tf_op jit(solution)/shard_map/ppermute | solution.py:34
  56.5 2.7 collective-permute-start.9
  61.5 3.2 shard_map.501
  64.8 2.2 collective-permute-start.12
  67.9 3.0 collective-permute-start.15
  72.5 2.0 collective-permute-done.14
  74.9 3.5 collective-permute-start.20
  80.4 5.6 %collective-permute-done.20 = bf16[8,2,64,128]{3,2,1,0:T(8,128)(2,1)S(1)} collective-permute-done((bf16[8,2,64,128]{3,2,1,0:T(8,128)(2,1)S(1)}, bf16[8,2,64,128]{3,2,1,0:T(8,128)(2,1)S(1)}, u32[]{:S(2)}, u32[]{:S(2)}) %collective-permute-start.20) | collective-permute-done | bytes 262176 | tf_op jit(solution)/shard_map/ppermute | solution.py:34
  86.0 3.8 %collective-permute-start.21 = (bf16[8,2,64,128]{3,2,1,0:T(8,128)(2,1)S(1)}, bf16[8,2,64,128]{3,2,1,0:T(8,128)(2,1)S(1)}, u32[]{:S(2)}, u32[]{:S(2)}) collective-permute-start(bf16[8,2,64,128]{3,2,1,0:T(8,128)(2,1)S(1)} %collective-permute-done.20), channel_id=1, source_target_pairs={{0,1},{1,0},{2,3},{3,2},{4,5},{5,4},{6,7},{7,6},{8,9},{9,8},{10,11... | collective-permute-start | bytes 786440 | tf_op jit(solution)/shard_map/ppermute | solution.py:34
  93.2 1.8 collective-permute-start.17
  95.1 2.3 collective-permute-done.21
  97.5 2.9 collective-permute-done.17.w2
  101.0 3.3 shard_map.503.refs_3_
  105.6 2.8 collective-permute-start.22
  110.1 6.2 %shard_map.504 = (f32[8,2,64,128]{3,2,1,0:T(8,128)}, f32[4,128]{1,0:T(4,128)}) custom-call(s32[5]{0:T(128)} %copy-done.68, bf16[1024,128]{1,0:T(8,128)(2,1)} %bitcast.113, bf16[1024,128]{1,0:T(8,128)(2,1)} %bitcast.149, bf16[1024,128]{1,0:T(8,128)(2,1)} %bitcast.147, bf16[1024,128]{1,0:T(8,128)(2,1)} %bitcast.151, bf16[4,128,128]{2,1,0:T(8,128)(2,1)} %bitcast.166, ...), custom_call_target="tpu_custom_call" | custom-call | flops 1 | bytes 1 | tf_op jit(solution)/shard_map/pallas_call | solution.py:119
  116.3 2.2 collective-permute-start.24
  120.3 2.0 collective-permute-start.27
  127.6 1.7 collective-permute-start.29
  130.2 8.6 %collective-permute-done.29 = bf16[8,2,64,128]{3,2,1,0:T(8,128)(2,1)S(1)} collective-permute-done((bf16[8,2,64,128]{3,2,1,0:T(8,128)(2,1)S(1)}, bf16[8,2,64,128]{3,2,1,0:T(8,128)(2,1)S(1)}, u32[]{:S(2)}, u32[]{:S(2)}) %collective-permute-start.29) | collective-permute-done | bytes 262176 | tf_op jit(solution)/shard_map/ppermute | solution.py:34
  138.7 1.6 collective-permute-start.30
  140.4 1.7 fusion
  142.9 4.8 %collective-permute-done.30 = bf16[8,2,64,128]{3,2,1,0:T(8,128)(2,1)S(1)} collective-permute-done((bf16[8,2,64,128]{3,2,1,0:T(8,128)(2,1)S(1)}, bf16[8,2,64,128]{3,2,1,0:T(8,128)(2,1)S(1)}, u32[]{:S(2)}, u32[]{:S(2)}) %collective-permute-start.30) | collective-permute-done | bytes 262176 | tf_op jit(solution)/shard_map/ppermute | solution.py:34
  148.4 4.5 %shard_map.506 = (bf16[4,64,512]{2,1,0:T(8,128)(2,1)}, bf16[4,64,512]{2,1,0:T(8,128)(2,1)}, bf16[4,64,512]{2,1,0:T(8,128)(2,1)}, bf16[4,64,512]{2,1,0:T(8,128)(2,1)}) custom-call(s32[5]{0:T(128)} %copy-done.68, bf16[13,512,128]{2,1,0:T(8,128)(2,1)} %all-gather.6.cloned.1.call-done.w_far.refs_1_.w, f32[14,128]{1,0:T(8,128)} %refs_28_.1, ...), custom_call_target="tpu_custom_call" | custom-call | flops 1 | bytes 1 | tf_op jit(solution)/shard_map/pallas_call | solution.py:119
  154.3 1.7 collective-permute-start.32
  156.4 5.9 %collective-permute-done.31.refs_3_ = bf16[4,64,512]{2,1,0:T(8,128)(2,1)S(1)} collective-permute-done((bf16[4,64,512]{2,1,0:T(8,128)(2,1)}, bf16[4,64,512]{2,1,0:T(8,128)(2,1)S(1)}, u32[]{:S(2)}, u32[]{:S(2)}) %collective-permute-start.31) | collective-permute-done | bytes 262176 | tf_op jit(solution)/shard_map/ppermute | solution.py:34
  162.4 5.5 %collective-permute-done.32.refs_4_ = bf16[4,64,512]{2,1,0:T(8,128)(2,1)S(1)} collective-permute-done((bf16[4,64,512]{2,1,0:T(8,128)(2,1)}, bf16[4,64,512]{2,1,0:T(8,128)(2,1)S(1)}, u32[]{:S(2)}, u32[]{:S(2)}) %collective-permute-start.32) | collective-permute-done | bytes 262176 | tf_op jit(solution)/shard_map/ppermute | solution.py:34
  171.3 36.9 %shard_map.507 = (bf16[2,64,2048]{2,1,0:T(8,128)(2,1)}, bf16[2,64,2176]{2,1,0:T(8,128)(2,1)}, bf16[2,64,2176]{2,1,0:T(8,128)(2,1)}) custom-call(s32[1]{0:T(128)S(6)} %add_shard_map.4.refs_0_, bf16[2,64,128]{2,1,0:T(8,128)(2,1)} %pad.5.refs_1_, bf16[4,64,512]{2,1,0:T(8,128)(2,1)} %get-tuple-element.170.refs_2_, bf16[4,64,512]{2,1,0:T(8,128)(2,1)} %copy-done.111, ...), custom_call_target="tpu_custom_call" | custom-call | flops 6643777536 | bytes 2162688 | tf_op jit(solution)/shard_map/pallas_call | solution.py:571
  208.2 2.1 collective-permute-done.38.other_far
  211.1 2.5 shard_map.508
  217.1 4.5 %collective-permute-done.39.refs_3_ = bf16[3,64,512]{2,1,0:T(8,128)(2,1)S(1)} collective-permute-done((bf16[3,64,512]{2,1,0:T(8,128)(2,1)}, bf16[3,64,512]{2,1,0:T(8,128)(2,1)S(1)}, u32[]{:S(2)}, u32[]{:S(2)}) %collective-permute-start.39) | collective-permute-done | bytes 196640 | tf_op jit(solution)/shard_map/ppermute | solution.py:34
  221.6 2.8 collective-permute-done.40.refs_4_
  226.5 4.3 %shard_map.509 = (bf16[8,2,64,384]{3,2,1,0:T(8,128)(2,1)}, f32[8,2,64,128]{3,2,1,0:T(8,128)}, bf16[8,2,64,128]{3,2,1,0:T(8,128)(2,1)}, bf16[8,2,64,128]{3,2,1,0:...) custom-call(s32[5]{0:T(128)} %copy-done.68, ...), custom_call_target="tpu_custom_call" | custom-call | flops 1 | bytes 1 | tf_op jit(solution)/shard_map/pallas_call | solution.py:119
  231.0 2.0 collective-permute-start.45
  233.0 7.4 %collective-permute-done.46 = bf16[8,2,64,128]{3,2,1,0:T(8,128)(2,1)S(1)} collective-permute-done((bf16[8,2,64,128]{3,2,1,0:T(8,128)(2,1)}, bf16[8,2,64,128]{3,2,1,0:T(8,128)(2,1)S(1)}, u32[]{:S(2)}, u32[]{:S(2)}) %collective-permute-start.46) | collective-permute-done | bytes 262176 | tf_op jit(solution)/shard_map/ppermute | solution.py:34
  248.9 1.8 collective-permute-done.44.refs_4_
  254.5 1.8 collective-permute-start.50
  258.1 1.8 collective-permute-done.49
  261.5 1.9 collective-permute-start.52
  264.3 3.2 shard_map.513
  267.4 2.0 collective-permute-start.55
  270.9 6.8 %shard_map.515 = (bf16[4,13,64,128]{3,2,1,0:T(8,128)(2,1)}, bf16[4,13,64,128]{3,2,1,0:T(8,128)(2,1)}) custom-call(s32[5]{0:T(128)} %copy-done.68, bf16[1024,128]{1,0:T(8,128)(2,1)} %bitcast.114, bf16[1024,128]{1,0:T(8,128)(2,1)} %bitcast.150, bf16[1024,128]{1,0:T(8,128)(2,1)} %bitcast.148, bf16[1024,128]{1,0:T(8,128)(2,1)} %bitcast.152, ...), custom_call_target="tpu_custom_call" | custom-call | flops 1 | bytes 1 | tf_op jit(solution)/shard_map/pallas_call | solution.py:119
  278.4 2.5 collective-permute-start.56
  281.1 5.4 %collective-permute-done.54.t1 = bf16[8,2,64,128]{3,2,1,0:T(8,128)(2,1)S(1)} collective-permute-done((bf16[8,2,64,128]{3,2,1,0:T(8,128)(2,1)S(1)}, bf16[8,2,64,128]{3,2,1,0:T(8,128)(2,1)S(1)}, u32[]{:S(2)}, u32[]{:S(2)}) %collective-permute-start.54) | collective-permute-done | bytes 262176 | tf_op jit(solution)/shard_map/ppermute | solution.py:34
  286.5 6.4 %collective-permute-done.56.t2 = bf16[8,2,64,128]{3,2,1,0:T(8,128)(2,1)S(1)} collective-permute-done((bf16[8,2,64,128]{3,2,1,0:T(8,128)(2,1)S(1)}, bf16[8,2,64,128]{3,2,1,0:T(8,128)(2,1)S(1)}, u32[]{:S(2)}, u32[]{:S(2)}) %collective-permute-start.56) | collective-permute-done | bytes 262176 | tf_op jit(solution)/shard_map/ppermute | solution.py:34
  294.9 2.2 collective-permute-start.63
  299.3 1.7 collective-permute-start.58
  301.5 2.3 shard_map.516
  308.8 2.7 collective-permute-start.64
  315.1 3.2 shard_map.518
  320.2 5.4 %shard_map.519 = (bf16[4,9,64,128]{3,2,1,0:T(8,128)(2,1)}, bf16[4,9,64,128]{3,2,1,0:T(8,128)(2,1)}) custom-call(s32[5]{0:T(128)} %copy-done.68, bf16[1024,128]{1,0:T(8,128)(2,1)} %bitcast.116, bf16[1024,128]{1,0:T(8,128)(2,1)} %bitcast.122, bf16[1024,128]{1,0:T(8,128)(2,1)} %bitcast.120, bf16[1024,128]{1,0:T(8,128)(2,1)} %bitcast.124, ...), custom_call_target="tpu_custom_call" | custom-call | flops 1 | bytes 1 | tf_op jit(solution)/shard_map/pallas_call | solution.py:119
  326.7 2.2 collective-permute-start.68
  330.5 2.1 collective-permute-start.70
  334.1 2.8 collective-permute-done.70.refs_2_
  337.5 3.2 collective-permute-done.71.refs_3_
  350.0 1.8 collective-permute-start.76
  355.4 3.6 collective-permute-start.80
  360.8 3.6 shard_map.522
  365.8 4.6 %shard_map.526 = (f32[1,128]{1,0:T(1,128)}, f32[9,64,128]{2,1,0:T(8,128)}, f32[9,64,128]{2,1,0:T(8,128)}, f32[9,64,128]{2,1,0:T(8,128)}, bf16[9,64,128]{2,1,0:T(...) custom-call(f32[8,128]{1,0:T(8,128)S(1)} %get-tuple-element.232.refs, ...), custom_call_target="tpu_custom_call" | custom-call | flops 1 | bytes 1 | tf_op jit(solution)/shard_map/pallas_call | solution.py:119
  (459 shorter events, 103.7 us)
Async XLA Ops:
  7.2 53.0 %all-gather.8.cloned.1.call-start = ((), (), s32[]{:S(2)}) async-start(), calls=%async_computation.3 | async-start | bytes 1327104 | tf_op jit(solution)/shard_map/all_gather | solution.py:888
  11.5 78.5 %all-gather.6.cloned.1.call-start = ((), (), s32[]{:S(2)}) async-start(), calls=%async_computation.2 | async-start | bytes 1916928 | tf_op jit(solution)/shard_map/all_gather | solution.py:897
  11.5 12.4 %collective-permute-start.5 = (bf16[8,2,64,128]{3,2,1,0:T(8,128)(2,1)}, bf16[8,2,64,128]{3,2,1,0:T(8,128)(2,1)S(1)}, u32[]{:S(2)}, u32[]{:S(2)}) collective-permute-start(bf16[8,2,64,128]{3,2,1,0:T(8,128)(2,1)} %c0.1), channel_id=1, source_target_pairs={{0,3},{1,2},{2,1},{3,0},{4,7},{5,6},{6,5},{7,4},{8,11},{9,10},{10,... | collective-permute-start | bytes 786440 | tf_op jit(solution)/shard_map/ppermute | solution.py:34
  16.5 12.6 %collective-permute-start.4 = (bf16[8,2,64,128]{3,2,1,0:T(8,128)(2,1)}, bf16[8,2,64,128]{3,2,1,0:T(8,128)(2,1)S(1)}, u32[]{:S(2)}, u32[]{:S(2)}) collective-permute-start(bf16[8,2,64,128]{3,2,1,0:T(8,128)(2,1)} %c0.1), channel_id=1, source_target_pairs={{0,1},{1,0},{2,3},{3,2},{4,5},{5,4},{6,7},{7,6},{8,9},{9,8},{10,11... | collective-permute-start | bytes 786440 | tf_op jit(solution)/shard_map/ppermute | solution.py:34
  16.5 4.5 %collective-permute-start.3 = (f32[4,128]{1,0:T(4,128)S(1)}, f32[4,128]{1,0:T(4,128)S(1)}, u32[]{:S(2)}, u32[]{:S(2)}) collective-permute-start(f32[4,128]{1,0:T(4,128)S(1)} %add.173), channel_id=1, source_target_pairs={{0,24},{4,28},{8,16},{12,20},{16,8},{20,12},{24,0},{28,4},{1,25},{... | collective-permute-start | bytes 6152 | tf_op jit(solution)/shard_map/ppermute | solution.py:34
  31.8 11.0 %collective-permute-start.7 = (bf16[8,2,64,128]{3,2,1,0:T(8,128)(2,1)S(1)}, bf16[8,2,64,128]{3,2,1,0:T(8,128)(2,1)S(1)}, u32[]{:S(2)}, u32[]{:S(2)}) collective-permute-start(bf16[8,2,64,128]{3,2,1,0:T(8,128)(2,1)S(1)} %shard_map.500), channel_id=1, source_target_pairs={{0,3},{1,2},{2,1},{3,0},{4,7},{5,6},{6,5},{7,4},{8,11},{9,10},{10,... | collective-permute-start | bytes 786440 | tf_op jit(solution)/shard_map/ppermute | solution.py:34
  33.5 12.9 %collective-permute-start.6 = (bf16[8,2,64,128]{3,2,1,0:T(8,128)(2,1)S(1)}, bf16[8,2,64,128]{3,2,1,0:T(8,128)(2,1)S(1)}, u32[]{:S(2)}, u32[]{:S(2)}) collective-permute-start(bf16[8,2,64,128]{3,2,1,0:T(8,128)(2,1)S(1)} %shard_map.500), channel_id=1, source_target_pairs={{0,1},{1,0},{2,3},{3,2},{4,5},{5,4},{6,7},{7,6},{8,9},{9,8},{10,11... | collective-permute-start | bytes 786440 | tf_op jit(solution)/shard_map/ppermute | solution.py:34
  47.2 93.2 %all-gather.4.cloned.1.call-start = ((), (), s32[]{:S(2)}) async-start(), calls=%async_computation.1 | async-start | bytes 1179648 | tf_op jit(solution)/shard_map/all_gather | solution.py:900
  48.4 7.1 %collective-permute-start.8 = (bf16[8,2,64,128]{3,2,1,0:T(8,128)(2,1)S(1)}, bf16[8,2,64,128]{3,2,1,0:T(8,128)(2,1)S(1)}, u32[]{:S(2)}, u32[]{:S(2)}) collective-permute-start(bf16[8,2,64,128]{3,2,1,0:T(8,128)(2,1)S(1)} %collective-permute-done.7), channel_id=1, source_target_pairs={{0,1},{1,0},{2,3},{3,2},{4,5},{5,4},{6,7},{7,6},{8,9},{9,8},{10,11... | collective-permute-start | bytes 786440 | tf_op jit(solution)/shard_map/ppermute | solution.py:34
  55.5 9.3 %collective-permute-start.11 = (bf16[8,2,64,128]{3,2,1,0:T(8,128)(2,1)S(1)}, bf16[8,2,64,128]{3,2,1,0:T(8,128)(2,1)}, u32[]{:S(2)}, u32[]{:S(2)}) collective-permute-start(bf16[8,2,64,128]{3,2,1,0:T(8,128)(2,1)S(1)} %collective-permute-done.5), channel_id=1, source_target_pairs={{0,1},{1,0},{2,3},{3,2},{4,5},{5,4},{6,7},{7,6},{8,9},{9,8},{10,11... | collective-permute-start | bytes 786440 | tf_op jit(solution)/shard_map/ppermute | solution.py:34
  67.9 4.6 %collective-permute-start.15 = (f32[8,128]{1,0:T(8,128)S(1)}, f32[8,128]{1,0:T(8,128)S(1)}, u32[]{:S(2)}, u32[]{:S(2)}) collective-permute-start(f32[8,128]{1,0:T(8,128)S(1)} %fusion.20), channel_id=1, source_target_pairs={{0,24},{4,28},{8,16},{12,20},{16,8},{20,12},{24,0},{28,4},{1,25},{... | collective-permute-start | bytes 12296 | tf_op jit(solution)/shard_map/ppermute | solution.py:34
  74.9 11.1 %collective-permute-start.20 = (bf16[8,2,64,128]{3,2,1,0:T(8,128)(2,1)S(1)}, bf16[8,2,64,128]{3,2,1,0:T(8,128)(2,1)S(1)}, u32[]{:S(2)}, u32[]{:S(2)}) collective-permute-start(bf16[8,2,64,128]{3,2,1,0:T(8,128)(2,1)S(1)} %shard_map.502), channel_id=1, source_target_pairs={{0,3},{1,2},{2,1},{3,0},{4,7},{5,6},{6,5},{7,4},{8,11},{9,10},{10,... | collective-permute-start | bytes 786440 | tf_op jit(solution)/shard_map/ppermute | solution.py:34
  78.4 11.5 %collective-permute-start.19 = (bf16[8,2,64,128]{3,2,1,0:T(8,128)(2,1)S(1)}, bf16[8,2,64,128]{3,2,1,0:T(8,128)(2,1)S(1)}, u32[]{:S(2)}, u32[]{:S(2)}) collective-permute-start(bf16[8,2,64,128]{3,2,1,0:T(8,128)(2,1)S(1)} %shard_map.502), channel_id=1, source_target_pairs={{0,1},{1,0},{2,3},{3,2},{4,5},{5,4},{6,7},{7,6},{8,9},{9,8},{10,11... | collective-permute-start | bytes 786440 | tf_op jit(solution)/shard_map/ppermute | solution.py:34
  80.4 262.5 %reduce-scatter.4.cloned.1.call-start = ((), (), s32[]{:S(2)}) async-start(), calls=%async_computation.4 | async-start | bytes 1064960
  86.0 11.4 %collective-permute-start.21 = (bf16[8,2,64,128]{3,2,1,0:T(8,128)(2,1)S(1)}, bf16[8,2,64,128]{3,2,1,0:T(8,128)(2,1)S(1)}, u32[]{:S(2)}, u32[]{:S(2)}) collective-permute-start(bf16[8,2,64,128]{3,2,1,0:T(8,128)(2,1)S(1)} %collective-permute-done.20), channel_id=1, source_target_pairs={{0,1},{1,0},{2,3},{3,2},{4,5},{5,4},{6,7},{7,6},{8,9},{9,8},{10,11... | collective-permute-start | bytes 786440 | tf_op jit(solution)/shard_map/ppermute | solution.py:34
  91.6 5.9 %collective-permute-start.18 = (bf16[128,128]{1,0:T(8,128)(2,1)S(1)}, bf16[128,128]{1,0:T(8,128)(2,1)S(1)}, u32[]{:S(2)}, u32[]{:S(2)}) collective-permute-start(bf16[128,128]{1,0:T(8,128)(2,1)S(1)} %get-tuple-element.292), channel_id=1, source_target_pairs={{0,2},{1,3},{2,0},{3,1},{4,6},{5,7},{6,4},{7,5},{8,10},{9,11},{10,... | collective-permute-start | bytes 98312 | tf_op jit(solution)/shard_map/ppermute | solution.py:34
  93.2 7.2 %collective-permute-start.17 = (bf16[128,128]{1,0:T(8,128)(2,1)S(1)}, bf16[128,128]{1,0:T(8,128)(2,1)S(1)}, u32[]{:S(2)}, u32[]{:S(2)}) collective-permute-start(bf16[128,128]{1,0:T(8,128)(2,1)S(1)} %get-tuple-element.293), channel_id=1, source_target_pairs={{0,3},{1,2},{2,1},{3,0},{4,7},{5,6},{6,5},{7,4},{8,11},{9,10},{10,... | collective-permute-start | bytes 98312 | tf_op jit(solution)/shard_map/ppermute | solution.py:34
  95.0 5.4 %collective-permute-start.16 = (bf16[128,128]{1,0:T(8,128)(2,1)S(1)}, bf16[128,128]{1,0:T(8,128)(2,1)S(1)}, u32[]{:S(2)}, u32[]{:S(2)}) collective-permute-start(bf16[128,128]{1,0:T(8,128)(2,1)S(1)} %get-tuple-element.294), channel_id=1, source_target_pairs={{0,1},{1,0},{2,3},{3,2},{4,5},{5,4},{6,7},{7,6},{8,9},{9,8},{10,11... | collective-permute-start | bytes 98312 | tf_op jit(solution)/shard_map/ppermute | solution.py:34
  104.4 4.5 %collective-permute-start.23 = (bf16[4,2,64,128]{3,2,1,0:T(8,128)(2,1)S(1)}, bf16[4,2,64,128]{3,2,1,0:T(8,128)(2,1)S(1)}, u32[]{:S(2)}, u32[]{:S(2)}) collective-permute-start(bf16[4,2,64,128]{3,2,1,0:T(8,128)(2,1)S(1)} %get-tuple-element.272), channel_id=1, source_target_pairs={{4,8},{12,16},{20,24},{8,4},{16,12},{24,20},{5,9},{13,17},{21,25},... | collective-permute-start | bytes 393224 | tf_op jit(solution)/shard_map/ppermute | solution.py:72
  105.6 3.8 %collective-permute-start.22 = (bf16[4,2,64,128]{3,2,1,0:T(8,128)(2,1)S(1)}, bf16[4,2,64,128]{3,2,1,0:T(8,128)(2,1)S(1)}, u32[]{:S(2)}, u32[]{:S(2)}) collective-permute-start(bf16[4,2,64,128]{3,2,1,0:T(8,128)(2,1)S(1)} %get-tuple-element.273), channel_id=1, source_target_pairs={{0,4},{4,0},{8,12},{12,8},{16,20},{20,16},{24,28},{28,24},{1,5},{5... | collective-permute-start | bytes 393224 | tf_op jit(solution)/shard_map/ppermute | solution.py:34
  120.3 4.5 %collective-permute-start.27 = (f32[4,128]{1,0:T(4,128)S(1)}, f32[4,128]{1,0:T(4,128)S(1)}, u32[]{:S(2)}, u32[]{:S(2)}) collective-permute-start(f32[4,128]{1,0:T(4,128)S(1)} %add.195), channel_id=1, source_target_pairs={{0,24},{4,28},{8,16},{12,20},{16,8},{20,12},{24,0},{28,4},{1,25},{... | collective-permute-start | bytes 6152 | tf_op jit(solution)/shard_map/ppermute | solution.py:34
  127.6 11.2 %collective-permute-start.29 = (bf16[8,2,64,128]{3,2,1,0:T(8,128)(2,1)S(1)}, bf16[8,2,64,128]{3,2,1,0:T(8,128)(2,1)S(1)}, u32[]{:S(2)}, u32[]{:S(2)}) collective-permute-start(bf16[8,2,64,128]{3,2,1,0:T(8,128)(2,1)S(1)} %shard_map.505), channel_id=1, source_target_pairs={{0,3},{1,2},{2,1},{3,0},{4,7},{5,6},{6,5},{7,4},{8,11},{9,10},{10,... | collective-permute-start | bytes 786440 | tf_op jit(solution)/shard_map/ppermute | solution.py:34
  130.1 12.8 %collective-permute-start.28 = (bf16[8,2,64,128]{3,2,1,0:T(8,128)(2,1)S(1)}, bf16[8,2,64,128]{3,2,1,0:T(8,128)(2,1)S(1)}, u32[]{:S(2)}, u32[]{:S(2)}) collective-permute-start(bf16[8,2,64,128]{3,2,1,0:T(8,128)(2,1)S(1)} %shard_map.505), channel_id=1, source_target_pairs={{0,1},{1,0},{2,3},{3,2},{4,5},{5,4},{6,7},{7,6},{8,9},{9,8},{10,11... | collective-permute-start | bytes 786440 | tf_op jit(solution)/shard_map/ppermute | solution.py:34
  138.7 9.0 %collective-permute-start.30 = (bf16[8,2,64,128]{3,2,1,0:T(8,128)(2,1)S(1)}, bf16[8,2,64,128]{3,2,1,0:T(8,128)(2,1)S(1)}, u32[]{:S(2)}, u32[]{:S(2)}) collective-permute-start(bf16[8,2,64,128]{3,2,1,0:T(8,128)(2,1)S(1)} %collective-permute-done.29), channel_id=1, source_target_pairs={{0,1},{1,0},{2,3},{3,2},{4,5},{5,4},{6,7},{7,6},{8,9},{9,8},{10,11... | collective-permute-start | bytes 786440 | tf_op jit(solution)/shard_map/ppermute | solution.py:34
  152.9 9.5 %collective-permute-start.31 = (bf16[4,64,512]{2,1,0:T(8,128)(2,1)}, bf16[4,64,512]{2,1,0:T(8,128)(2,1)S(1)}, u32[]{:S(2)}, u32[]{:S(2)}) collective-permute-start(bf16[4,64,512]{2,1,0:T(8,128)(2,1)} %get-tuple-element.171), channel_id=1, source_target_pairs={{0,8},{4,12},{8,0},{12,4},{16,24},{20,28},{24,16},{28,20},{1,9},{5... | collective-permute-start | bytes 786440 | tf_op jit(solution)/shard_map/ppermute | solution.py:34
  154.3 13.6 %collective-permute-start.32 = (bf16[4,64,512]{2,1,0:T(8,128)(2,1)}, bf16[4,64,512]{2,1,0:T(8,128)(2,1)S(1)}, u32[]{:S(2)}, u32[]{:S(2)}) collective-permute-start(bf16[4,64,512]{2,1,0:T(8,128)(2,1)} %get-tuple-element.172), channel_id=1, source_target_pairs={{0,16},{4,20},{8,24},{12,28},{16,0},{20,4},{24,8},{28,12},{1,17},{... | collective-permute-start | bytes 786440 | tf_op jit(solution)/shard_map/ppermute | solution.py:34
  156.0 11.8 %collective-permute-start.33 = (bf16[4,64,512]{2,1,0:T(8,128)(2,1)}, bf16[4,64,512]{2,1,0:T(8,128)(2,1)S(1)}, u32[]{:S(2)}, u32[]{:S(2)}) collective-permute-start(bf16[4,64,512]{2,1,0:T(8,128)(2,1)} %get-tuple-element.173), channel_id=1, source_target_pairs={{0,24},{4,28},{8,16},{12,20},{16,8},{20,12},{24,0},{28,4},{1,25},{... | collective-permute-start | bytes 786440 | tf_op jit(solution)/shard_map/ppermute | solution.py:34
  156.4 13.2 %collective-permute-start.34 = (bf16[4,64,512]{2,1,0:T(8,128)(2,1)}, bf16[4,64,512]{2,1,0:T(8,128)(2,1)S(1)}, u32[]{:S(2)}, u32[]{:S(2)}) collective-permute-start(bf16[4,64,512]{2,1,0:T(8,128)(2,1)} %get-tuple-element.170.refs_2_), channel_id=1, source_target_pairs={{0,4},{4,0},{8,12},{12,8},{16,20},{20,16},{24,28},{28,24},{1,5},{5... | collective-permute-start | bytes 786440 | tf_op jit(solution)/shard_map/ppermute | solution.py:34
  162.4 7.3 %collective-permute-start.35 = (bf16[4,64,512]{2,1,0:T(8,128)(2,1)S(1)}, bf16[4,64,512]{2,1,0:T(8,128)(2,1)S(1)}, u32[]{:S(2)}, u32[]{:S(2)}) collective-permute-start(bf16[4,64,512]{2,1,0:T(8,128)(2,1)S(1)} %collective-permute-done.31.refs_3_), channel_id=1, source_target_pairs={{0,4},{4,0},{8,12},{12,8},{16,20},{20,16},{24,28},{28,24},{1,5},{5... | collective-permute-start | bytes 786440 | tf_op jit(solution)/shard_map/ppermute | solution.py:34
  213.5 8.0 %collective-permute-start.39 = (bf16[3,64,512]{2,1,0:T(8,128)(2,1)}, bf16[3,64,512]{2,1,0:T(8,128)(2,1)S(1)}, u32[]{:S(2)}, u32[]{:S(2)}) collective-permute-start(bf16[3,64,512]{2,1,0:T(8,128)(2,1)} %get-tuple-element.179), channel_id=1, source_target_pairs={{0,8},{4,12},{8,0},{12,4},{16,24},{20,28},{24,16},{28,20},{1,9},{5... | collective-permute-start | bytes 589832 | tf_op jit(solution)/shard_map/ppermute | solution.py:34
  214.4 10.0 %collective-permute-start.40 = (bf16[3,64,512]{2,1,0:T(8,128)(2,1)}, bf16[3,64,512]{2,1,0:T(8,128)(2,1)S(1)}, u32[]{:S(2)}, u32[]{:S(2)}) collective-permute-start(bf16[3,64,512]{2,1,0:T(8,128)(2,1)} %get-tuple-element.180), channel_id=1, source_target_pairs={{0,16},{4,20},{8,24},{12,28},{16,0},{20,4},{24,8},{28,12},{1,17},{... | collective-permute-start | bytes 589832 | tf_op jit(solution)/shard_map/ppermute | solution.py:34
  215.6 10.2 %collective-permute-start.41 = (bf16[3,64,512]{2,1,0:T(8,128)(2,1)}, bf16[3,64,512]{2,1,0:T(8,128)(2,1)S(1)}, u32[]{:S(2)}, u32[]{:S(2)}) collective-permute-start(bf16[3,64,512]{2,1,0:T(8,128)(2,1)} %get-tuple-element.181), channel_id=1, source_target_pairs={{0,24},{4,28},{8,16},{12,20},{16,8},{20,12},{24,0},{28,4},{1,25},{... | collective-permute-start | bytes 589832 | tf_op jit(solution)/shard_map/ppermute | solution.py:34
  230.9 9.5 %collective-permute-start.46 = (bf16[8,2,64,128]{3,2,1,0:T(8,128)(2,1)}, bf16[8,2,64,128]{3,2,1,0:T(8,128)(2,1)S(1)}, u32[]{:S(2)}, u32[]{:S(2)}) collective-permute-start(bf16[8,2,64,128]{3,2,1,0:T(8,128)(2,1)} %get-tuple-element.182), channel_id=1, source_target_pairs={{0,1},{1,0},{2,3},{3,2},{4,5},{5,4},{6,7},{7,6},{8,9},{9,8},{10,11... | collective-permute-start | bytes 786440 | tf_op jit(solution)/shard_map/ppermute | solution.py:34
  231.0 19.7 %collective-permute-start.45 = (bf16[8,2,64,128]{3,2,1,0:T(8,128)(2,1)}, bf16[8,2,64,128]{3,2,1,0:T(8,128)(2,1)S(1)}, u32[]{:S(2)}, u32[]{:S(2)}) collective-permute-start(bf16[8,2,64,128]{3,2,1,0:T(8,128)(2,1)} %get-tuple-element.192), channel_id=1, source_target_pairs={{0,1},{1,0},{2,3},{3,2},{4,5},{5,4},{6,7},{7,6},{8,9},{9,8},{10,11... | collective-permute-start | bytes 786440 | tf_op jit(solution)/shard_map/ppermute | solution.py:34
  241.5 9.2 %collective-permute-start.47 = (bf16[8,2,64,128]{3,2,1,0:T(8,128)(2,1)S(1)}, bf16[8,2,64,128]{3,2,1,0:T(8,128)(2,1)S(1)}, u32[]{:S(2)}, u32[]{:S(2)}) collective-permute-start(bf16[8,2,64,128]{3,2,1,0:T(8,128)(2,1)S(1)} %add_convert_fusion.2), channel_id=1, source_target_pairs={{0,3},{1,2},{2,1},{3,0},{4,7},{5,6},{6,5},{7,4},{8,11},{9,10},{10,... | collective-permute-start | bytes 786440 | tf_op jit(solution)/shard_map/ppermute | solution.py:34
  242.9 4.6 %collective-permute-start.42 = (bf16[64,768]{1,0:T(8,128)(2,1)S(1)}, bf16[64,768]{1,0:T(8,128)(2,1)S(1)}, u32[]{:S(2)}, u32[]{:S(2)}) collective-permute-start(bf16[64,768]{1,0:T(8,128)(2,1)S(1)} %copy-done.120), channel_id=1, source_target_pairs={{0,8},{4,12},{8,0},{12,4},{16,24},{20,28},{24,16},{28,20},{1,9},{5... | collective-permute-start | bytes 294920 | tf_op jit(solution)/shard_map/ppermute | solution.py:34
  244.3 4.6 %collective-permute-start.43 = (bf16[64,768]{1,0:T(8,128)(2,1)S(1)}, bf16[64,768]{1,0:T(8,128)(2,1)S(1)}, u32[]{:S(2)}, u32[]{:S(2)}) collective-permute-start(bf16[64,768]{1,0:T(8,128)(2,1)S(1)} %copy-done.119), channel_id=1, source_target_pairs={{0,16},{4,20},{8,24},{12,28},{16,0},{20,4},{24,8},{28,12},{1,17},{... | collective-permute-start | bytes 294920 | tf_op jit(solution)/shard_map/ppermute | solution.py:34
  245.2 5.5 %collective-permute-start.44 = (bf16[64,768]{1,0:T(8,128)(2,1)S(1)}, bf16[64,768]{1,0:T(8,128)(2,1)S(1)}, u32[]{:S(2)}, u32[]{:S(2)}) collective-permute-start(bf16[64,768]{1,0:T(8,128)(2,1)S(1)} %copy-done.118), channel_id=1, source_target_pairs={{0,24},{4,28},{8,16},{12,20},{16,8},{20,12},{24,0},{28,4},{1,25},{... | collective-permute-start | bytes 294920 | tf_op jit(solution)/shard_map/ppermute | solution.py:34
  253.3 4.5 %collective-permute-start.51 = (f32[4,128]{1,0:T(4,128)S(1)}, f32[4,128]{1,0:T(4,128)S(1)}, u32[]{:S(2)}, u32[]{:S(2)}) collective-permute-start(f32[4,128]{1,0:T(4,128)S(1)} %add.200), channel_id=1, source_target_pairs={{0,24},{4,28},{8,16},{12,20},{16,8},{20,12},{24,0},{28,4},{1,25},{... | collective-permute-start | bytes 6152 | tf_op jit(solution)/shard_map/ppermute | solution.py:34
  267.4 10.8 %collective-permute-start.55 = (bf16[8,2,64,128]{3,2,1,0:T(8,128)(2,1)S(1)}, bf16[8,2,64,128]{3,2,1,0:T(8,128)(2,1)S(1)}, u32[]{:S(2)}, u32[]{:S(2)}) collective-permute-start(bf16[8,2,64,128]{3,2,1,0:T(8,128)(2,1)S(1)} %get-tuple-element.201), channel_id=1, source_target_pairs={{0,1},{1,0},{2,3},{3,2},{4,5},{5,4},{6,7},{7,6},{8,9},{9,8},{10,11... | collective-permute-start | bytes 786440 | tf_op jit(solution)/shard_map/ppermute | solution.py:34
  277.7 23.3 %collective-permute-start.59 = (bf16[4,13,64,128]{3,2,1,0:T(8,128)(2,1)}, bf16[4,13,64,128]{3,2,1,0:T(8,128)(2,1)}, u32[]{:S(2)}, u32[]{:S(2)}) collective-permute-start(bf16[4,13,64,128]{3,2,1,0:T(8,128)(2,1)} %get-tuple-element.207), channel_id=1, source_target_pairs={{0,4},{4,0},{8,12},{12,8},{16,20},{20,16},{24,28},{28,24},{1,5},{5... | collective-permute-start | bytes 2555912 | tf_op jit(solution)/shard_map/ppermute | solution.py:34
  278.0 8.5 %collective-permute-start.54 = (bf16[8,2,64,128]{3,2,1,0:T(8,128)(2,1)S(1)}, bf16[8,2,64,128]{3,2,1,0:T(8,128)(2,1)S(1)}, u32[]{:S(2)}, u32[]{:S(2)}) collective-permute-start(bf16[8,2,64,128]{3,2,1,0:T(8,128)(2,1)S(1)} %get-tuple-element.199), channel_id=1, source_target_pairs={{0,1},{1,0},{2,3},{3,2},{4,5},{5,4},{6,7},{7,6},{8,9},{9,8},{10,11... | collective-permute-start | bytes 786440 | tf_op jit(solution)/shard_map/ppermute | solution.py:34
  278.4 14.6 %collective-permute-start.56 = (bf16[8,2,64,128]{3,2,1,0:T(8,128)(2,1)S(1)}, bf16[8,2,64,128]{3,2,1,0:T(8,128)(2,1)S(1)}, u32[]{:S(2)}, u32[]{:S(2)}) collective-permute-start(bf16[8,2,64,128]{3,2,1,0:T(8,128)(2,1)S(1)} %add_convert_fusion.1), channel_id=1, source_target_pairs={{0,3},{1,2},{2,1},{3,0},{4,7},{5,6},{6,5},{7,4},{8,11},{9,10},{10,... | collective-permute-start | bytes 786440 | tf_op jit(solution)/shard_map/ppermute | solution.py:34
  294.9 8.9 %collective-permute-start.63 = (f32[8,128]{1,0:T(8,128)S(1)}, f32[8,128]{1,0:T(8,128)S(1)}, u32[]{:S(2)}, u32[]{:S(2)}) collective-permute-start(f32[8,128]{1,0:T(8,128)S(1)} %fusion.21), channel_id=1, source_target_pairs={{0,24},{4,28},{8,16},{12,20},{16,8},{20,12},{24,0},{28,4},{1,25},{... | collective-permute-start | bytes 12296 | tf_op jit(solution)/shard_map/ppermute | solution.py:34
  297.1 6.7 %collective-permute-start.62 = (f32[8,128]{1,0:T(8,128)S(1)}, f32[8,128]{1,0:T(8,128)S(1)}, u32[]{:S(2)}, u32[]{:S(2)}) collective-permute-start(f32[8,128]{1,0:T(8,128)S(1)} %fusion.21), channel_id=1, source_target_pairs={{0,16},{4,20},{8,24},{12,28},{16,0},{20,4},{24,8},{28,12},{1,17},{... | collective-permute-start | bytes 12296 | tf_op jit(solution)/shard_map/ppermute | solution.py:34
  298.5 5.3 %collective-permute-start.61 = (f32[8,128]{1,0:T(8,128)S(1)}, f32[8,128]{1,0:T(8,128)S(1)}, u32[]{:S(2)}, u32[]{:S(2)}) collective-permute-start(f32[8,128]{1,0:T(8,128)S(1)} %fusion.21), channel_id=1, source_target_pairs={{0,8},{4,12},{8,0},{12,4},{16,24},{20,28},{24,16},{28,20},{1,9},{5... | collective-permute-start | bytes 12296 | tf_op jit(solution)/shard_map/ppermute | solution.py:34
  299.3 15.2 %collective-permute-start.58 = (bf16[8,2,64,128]{3,2,1,0:T(8,128)(2,1)S(1)}, bf16[8,2,64,128]{3,2,1,0:T(8,128)(2,1)}, u32[]{:S(2)}, u32[]{:S(2)}) collective-permute-start(bf16[8,2,64,128]{3,2,1,0:T(8,128)(2,1)S(1)} %copy-done.32), channel_id=1, source_target_pairs={{0,3},{1,2},{2,1},{3,0},{4,7},{5,6},{6,5},{7,4},{8,11},{9,10},{10,... | collective-permute-start | bytes 786440 | tf_op jit(solution)/shard_map/ppermute | solution.py:34
  301.0 13.5 %collective-permute-start.57 = (bf16[8,2,64,128]{3,2,1,0:T(8,128)(2,1)S(1)}, bf16[8,2,64,128]{3,2,1,0:T(8,128)(2,1)}, u32[]{:S(2)}, u32[]{:S(2)}) collective-permute-start(bf16[8,2,64,128]{3,2,1,0:T(8,128)(2,1)S(1)} %copy-done.32), channel_id=1, source_target_pairs={{0,1},{1,0},{2,3},{3,2},{4,5},{5,4},{6,7},{7,6},{8,9},{9,8},{10,11... | collective-permute-start | bytes 786440 | tf_op jit(solution)/shard_map/ppermute | solution.py:34
  307.9 6.6 %collective-permute-start.65 = (bf16[1,2,64,128]{3,2,1,0:T(8,128)(2,1)S(1)}, bf16[1,2,64,128]{3,2,1,0:T(8,128)(2,1)S(1)}, u32[]{:S(2)}, u32[]{:S(2)}) collective-permute-start(bf16[1,2,64,128]{3,2,1,0:T(8,128)(2,1)S(1)} %get-tuple-element.268), channel_id=1, source_target_pairs={{4,8},{12,16},{20,24},{8,4},{16,12},{24,20},{5,9},{13,17},{21,25},... | collective-permute-start | bytes 98312 | tf_op jit(solution)/shard_map/ppermute | solution.py:72
  308.8 5.7 %collective-permute-start.64 = (bf16[1,2,64,128]{3,2,1,0:T(8,128)(2,1)S(1)}, bf16[1,2,64,128]{3,2,1,0:T(8,128)(2,1)S(1)}, u32[]{:S(2)}, u32[]{:S(2)}) collective-permute-start(bf16[1,2,64,128]{3,2,1,0:T(8,128)(2,1)S(1)} %get-tuple-element.269), channel_id=1, source_target_pairs={{0,4},{4,0},{8,12},{12,8},{16,20},{20,16},{24,28},{28,24},{1,5},{5... | collective-permute-start | bytes 98312 | tf_op jit(solution)/shard_map/ppermute | solution.py:34
  318.3 8.3 %collective-permute-start.67 = (bf16[8,2,64,128]{3,2,1,0:T(8,128)(2,1)S(1)}, bf16[8,2,64,128]{3,2,1,0:T(8,128)(2,1)S(1)}, u32[]{:S(2)}, u32[]{:S(2)}) collective-permute-start(bf16[8,2,64,128]{3,2,1,0:T(8,128)(2,1)S(1)} %get-tuple-element.216), channel_id=1, source_target_pairs={{0,1},{1,0},{2,3},{3,2},{4,5},{5,4},{6,7},{7,6},{8,9},{9,8},{10,11... | collective-permute-start | bytes 786440 | tf_op jit(solution)/shard_map/ppermute | solution.py:34
  325.6 4.0 %collective-permute-start.69 = (bf16[4,9,64,128]{3,2,1,0:T(8,128)(2,1)}, bf16[4,9,64,128]{3,2,1,0:T(8,128)(2,1)S(1)}, u32[]{:S(2)}, u32[]{:S(2)}) collective-permute-start(bf16[4,9,64,128]{3,2,1,0:T(8,128)(2,1)} %get-tuple-element.218), channel_id=1, source_target_pairs={{0,4},{4,0},{8,12},{12,8},{16,20},{20,16},{24,28},{28,24},{1,5},{5... | collective-permute-start | bytes 1769480 | tf_op jit(solution)/shard_map/ppermute | solution.py:34
  325.7 16.4 %collective-permute-start.66 = (bf16[8,2,64,128]{3,2,1,0:T(8,128)(2,1)S(1)}, bf16[8,2,64,128]{3,2,1,0:T(8,128)(2,1)S(1)}, u32[]{:S(2)}, u32[]{:S(2)}) collective-permute-start(bf16[8,2,64,128]{3,2,1,0:T(8,128)(2,1)S(1)} %get-tuple-element.214), channel_id=1, source_target_pairs={{0,1},{1,0},{2,3},{3,2},{4,5},{5,4},{6,7},{7,6},{8,9},{9,8},{10,11... | collective-permute-start | bytes 786440 | tf_op jit(solution)/shard_map/ppermute | solution.py:34
  326.7 15.4 %collective-permute-start.68 = (bf16[8,2,64,128]{3,2,1,0:T(8,128)(2,1)S(1)}, bf16[8,2,64,128]{3,2,1,0:T(8,128)(2,1)S(1)}, u32[]{:S(2)}, u32[]{:S(2)}) collective-permute-start(bf16[8,2,64,128]{3,2,1,0:T(8,128)(2,1)S(1)} %add_convert_fusion), channel_id=1, source_target_pairs={{0,3},{1,2},{2,1},{3,0},{4,7},{5,6},{6,5},{7,4},{8,11},{9,10},{10,... | collective-permute-start | bytes 786440 | tf_op jit(solution)/shard_map/ppermute | solution.py:34
  330.5 6.4 %collective-permute-start.70 = (bf16[9,64,128]{2,1,0:T(8,128)(2,1)S(1)}, bf16[9,64,128]{2,1,0:T(8,128)(2,1)S(1)}, u32[]{:S(2)}, u32[]{:S(2)}) collective-permute-start(bf16[9,64,128]{2,1,0:T(8,128)(2,1)S(1)} %get-tuple-element.220), channel_id=1, source_target_pairs={{0,8},{4,12},{8,0},{12,4},{16,24},{20,28},{24,16},{28,20},{1,9},{5... | collective-permute-start | bytes 442376 | tf_op jit(solution)/shard_map/ppermute | solution.py:34
  332.6 8.2 %collective-permute-start.71 = (bf16[9,64,128]{2,1,0:T(8,128)(2,1)S(1)}, bf16[9,64,128]{2,1,0:T(8,128)(2,1)S(1)}, u32[]{:S(2)}, u32[]{:S(2)}) collective-permute-start(bf16[9,64,128]{2,1,0:T(8,128)(2,1)S(1)} %get-tuple-element.221), channel_id=1, source_target_pairs={{0,16},{4,20},{8,24},{12,28},{16,0},{20,4},{24,8},{28,12},{1,17},{... | collective-permute-start | bytes 442376 | tf_op jit(solution)/shard_map/ppermute | solution.py:34
  332.6 8.9 %collective-permute-start.72 = (bf16[9,64,128]{2,1,0:T(8,128)(2,1)S(1)}, bf16[9,64,128]{2,1,0:T(8,128)(2,1)S(1)}, u32[]{:S(2)}, u32[]{:S(2)}) collective-permute-start(bf16[9,64,128]{2,1,0:T(8,128)(2,1)S(1)} %get-tuple-element.222), channel_id=1, source_target_pairs={{0,24},{4,28},{8,16},{12,20},{16,8},{20,12},{24,0},{28,4},{1,25},{... | collective-permute-start | bytes 442376 | tf_op jit(solution)/shard_map/ppermute | solution.py:34
  348.3 11.6 %collective-permute-start.73 = (bf16[8,2,64,128]{3,2,1,0:T(8,128)(2,1)}, bf16[8,2,64,128]{3,2,1,0:T(8,128)(2,1)S(1)}, u32[]{:S(2)}, u32[]{:S(2)}) collective-permute-start(bf16[8,2,64,128]{3,2,1,0:T(8,128)(2,1)} %collective-permute-done.58), channel_id=1, source_target_pairs={{0,1},{1,0},{2,3},{3,2},{4,5},{5,4},{6,7},{7,6},{8,9},{9,8},{10,11... | collective-permute-start | bytes 786440 | tf_op jit(solution)/shard_map/ppermute | solution.py:34
  349.5 4.5 %collective-permute-start.77 = (f32[8,128]{1,0:T(8,128)S(1)}, f32[8,128]{1,0:T(8,128)S(1)}, u32[]{:S(2)}, u32[]{:S(2)}) collective-permute-start(f32[8,128]{1,0:T(8,128)S(1)} %add.213), channel_id=1, source_target_pairs={{0,24},{4,28},{8,16},{12,20},{16,8},{20,12},{24,0},{28,4},{1,25},{... | collective-permute-start | bytes 12296 | tf_op jit(solution)/shard_map/ppermute | solution.py:34
  350.0 4.0 %collective-permute-start.76 = (f32[8,128]{1,0:T(8,128)S(1)}, f32[8,128]{1,0:T(8,128)S(1)}, u32[]{:S(2)}, u32[]{:S(2)}) collective-permute-start(f32[8,128]{1,0:T(8,128)S(1)} %add.213), channel_id=1, source_target_pairs={{0,16},{4,20},{8,24},{12,28},{16,0},{20,4},{24,8},{28,12},{1,17},{... | collective-permute-start | bytes 12296 | tf_op jit(solution)/shard_map/ppermute | solution.py:34
  353.1 12.5 %collective-permute-start.81 = (f32[1,64,128]{2,1,0:T(8,128)S(1)}, f32[1,64,128]{2,1,0:T(8,128)S(1)}, u32[]{:S(2)}, u32[]{:S(2)}) collective-permute-start(f32[1,64,128]{2,1,0:T(8,128)S(1)} %get-tuple-element.236), channel_id=1, source_target_pairs={{0,0},{8,1},{16,2},{24,3},{4,4},{12,5},{20,6},{28,7},{1,8},{9,9},{... | collective-permute-start | bytes 98312 | tf_op jit(solution)/shard_map/ppermute | solution.py:827
  355.4 10.2 %collective-permute-start.80 = (f32[8,128]{1,0:T(8,128)S(1)}, f32[8,128]{1,0:T(8,128)S(1)}, u32[]{:S(2)}, u32[]{:S(2)}) collective-permute-start(f32[8,128]{1,0:T(8,128)S(1)} %get-tuple-element.232.refs_0_), channel_id=1, source_target_pairs={{0,3},{1,2},{2,1},{3,0},{4,7},{5,6},{6,5},{7,4},{8,11},{9,10},{10,... | collective-permute-start | bytes 12296 | tf_op jit(solution)/shard_map/ppermute | solution.py:34
  359.0 6.6 %collective-permute-start.79 = (f32[8,128]{1,0:T(8,128)S(1)}, f32[8,128]{1,0:T(8,128)S(1)}, u32[]{:S(2)}, u32[]{:S(2)}) collective-permute-start(f32[8,128]{1,0:T(8,128)S(1)} %get-tuple-element.232.refs_0_), channel_id=1, source_target_pairs={{0,2},{1,3},{2,0},{3,1},{4,6},{5,7},{6,4},{7,5},{8,10},{9,11},{10,... | collective-permute-start | bytes 12296 | tf_op jit(solution)/shard_map/ppermute | solution.py:34
  359.0 6.6 %collective-permute-start.78 = (f32[8,128]{1,0:T(8,128)S(1)}, f32[8,128]{1,0:T(8,128)S(1)}, u32[]{:S(2)}, u32[]{:S(2)}) collective-permute-start(f32[8,128]{1,0:T(8,128)S(1)} %get-tuple-element.232.refs_0_), channel_id=1, source_target_pairs={{0,1},{1,0},{2,3},{3,2},{4,5},{5,4},{6,7},{7,6},{8,9},{9,8},{10,11... | collective-permute-start | bytes 12296 | tf_op jit(solution)/shard_map/ppermute | solution.py:34
  (145 other events, 1576.2 us)
Sparse Core Ops, SparseCore 0:
  11.6 26.6 all-gather.7
  47.3 25.8 all-gather.5
  80.5 22.5 all-gather.3
  303.9 26.1 reduce-scatter.3

commit v5 on v4

--- a/solution.py
+++ b/solution.py
@@ -556,8 +556,8 @@
     _, depth, tokens = mine[0].shape
     queries = count * tokens
     total = 2 * queries + ctx.shape[2]
-    block = min(512, queries)
-    chunk = min(1024, 2 * queries)
+    block = min(1024, queries)
+    chunk = min(256, 2 * queries)
 
     def whole(a):
         return pl.BlockSpec(a.shape, lambda i: (0,) * len(a.shape))
@@ -1237,7 +1237,7 @@
         ctx_value_bias,
     )
     squares = [squares] + [swap(squares, "chan", k) for k in (1, 2, 3)]
-    squares[0] = after(squares[0], activations, pixel_grad)
+    squares[0] = after(squares[0], pixel_grad)
 
     def turn(x):
         return jnp.transpose(x, (1, 0, 2))

time: 384 us -> 382 us (level)
  no operation moved by 1% of the time
where the time goes in v5:
time: 382 us; the launch traced here: 376 us
  waiting for transfers between devices  122 us (32%)
  starting transfers between devices  101 us (26%)
  Pallas kernels  94.7 us (25%)
  local copies, waits for them, and re-layouts  32.5 us (9%)
  between operations  16.3 us (4%)
  other arithmetic  7.33 us (2%)
    ppermute x77, waiting for transfers between devices, swap(): return lax.ppermute(x, axis, [(i, i ^ distance) for i in range(size)])  122 us
    ppermute x77, starting transfers between devices, swap(): return lax.ppermute(x, axis, [(i, i ^ distance) for i in range(size)])  96.8 us
    pallas_call x27, Pallas kernels, local_call(): pl.pallas_call(kernel, out_shape=tuple(outs), in_specs=[spec(a) for a in...  59 us
    pallas_call x1, Pallas kernels, attention(): pl.pallas_call(functools.partial(attention_kernel, chunk=chunk, count=cou...  35.7 us
    unnamed x246, local copies, waits for them, and re-layouts  25 us
  transfers between devices with their start and end apart: 86, of which 49 were waited for; matrix products, arithmetic and copies ran while one was open for 4% of the time, Pallas kernels for 10%

profile of v5, /device:TPU:0, one launch (start us, length us, event | category | flops | bytes accessed | tf_op | source)
XLA Modules:
  0.0 376.1 jit_solution(17354411770955573412)
XLA Ops:
  9.8 1.6 convert_element_type.85
  11.5 5.0 %collective-permute-start.5 = (bf16[8,2,64,128]{3,2,1,0:T(8,128)(2,1)}, bf16[8,2,64,128]{3,2,1,0:T(8,128)(2,1)S(1)}, u32[]{:S(2)}, u32[]{:S(2)}) collective-permute-start(bf16[8,2,64,128]{3,2,1,0:T(8,128)(2,1)} %c0.1), channel_id=1, source_target_pairs={{0,3},{1,2},{2,1},{3,0},{4,7},{5,6},{6,5},{7,4},{8,11},{9,10},{10,... | collective-permute-start | bytes 786440 | tf_op jit(solution)/shard_map/ppermute | solution.py:34
  16.5 2.4 collective-permute-start.3
  23.9 5.2 %collective-permute-done.4 = bf16[8,2,64,128]{3,2,1,0:T(8,128)(2,1)S(1)} collective-permute-done((bf16[8,2,64,128]{3,2,1,0:T(8,128)(2,1)}, bf16[8,2,64,128]{3,2,1,0:T(8,128)(2,1)S(1)}, u32[]{:S(2)}, u32[]{:S(2)}) %collective-permute-start.4) | collective-permute-done | bytes 262176 | tf_op jit(solution)/shard_map/ppermute | solution.py:34
  31.8 1.7 collective-permute-start.7
  33.5 9.3 %collective-permute-done.7 = bf16[8,2,64,128]{3,2,1,0:T(8,128)(2,1)S(1)} collective-permute-done((bf16[8,2,64,128]{3,2,1,0:T(8,128)(2,1)S(1)}, bf16[8,2,64,128]{3,2,1,0:T(8,128)(2,1)S(1)}, u32[]{:S(2)}, u32[]{:S(2)}) %collective-permute-start.7) | collective-permute-done | bytes 262176 | tf_op jit(solution)/shard_map/ppermute | solution.py:34
  42.8 3.6 collective-permute-done.6
  48.8 6.7 %collective-permute-done.8 = bf16[8,2,64,128]{3,2,1,0:T(8,128)(2,1)S(1)} collective-permute-done((bf16[8,2,64,128]{3,2,1,0:T(8,128)(2,1)S(1)}, bf16[8,2,64,128]{3,2,1,0:T(8,128)(2,1)S(1)}, u32[]{:S(2)}, u32[]{:S(2)}) %collective-permute-start.8) | collective-permute-done | bytes 262176 | tf_op jit(solution)/shard_map/ppermute | solution.py:34
  56.5 2.7 collective-permute-start.9
  61.5 3.2 shard_map.501
  64.8 2.2 collective-permute-start.12
  67.9 3.0 collective-permute-start.15
  72.5 2.0 collective-permute-done.14
  74.9 3.5 collective-permute-start.20
  80.4 5.6 %collective-permute-done.20 = bf16[8,2,64,128]{3,2,1,0:T(8,128)(2,1)S(1)} collective-permute-done((bf16[8,2,64,128]{3,2,1,0:T(8,128)(2,1)S(1)}, bf16[8,2,64,128]{3,2,1,0:T(8,128)(2,1)S(1)}, u32[]{:S(2)}, u32[]{:S(2)}) %collective-permute-start.20) | collective-permute-done | bytes 262176 | tf_op jit(solution)/shard_map/ppermute | solution.py:34
  86.0 3.8 %collective-permute-start.21 = (bf16[8,2,64,128]{3,2,1,0:T(8,128)(2,1)S(1)}, bf16[8,2,64,128]{3,2,1,0:T(8,128)(2,1)S(1)}, u32[]{:S(2)}, u32[]{:S(2)}) collective-permute-start(bf16[8,2,64,128]{3,2,1,0:T(8,128)(2,1)S(1)} %collective-permute-done.20), channel_id=1, source_target_pairs={{0,1},{1,0},{2,3},{3,2},{4,5},{5,4},{6,7},{7,6},{8,9},{9,8},{10,11... | collective-permute-start | bytes 786440 | tf_op jit(solution)/shard_map/ppermute | solution.py:34
  93.2 1.8 collective-permute-start.17
  95.1 2.3 collective-permute-done.21
  97.5 2.9 collective-permute-done.17.w2
  101.0 3.4 shard_map.503.refs_3_
  105.4 2.8 collective-permute-start.22
  109.8 6.2 %shard_map.504 = (f32[8,2,64,128]{3,2,1,0:T(8,128)}, f32[4,128]{1,0:T(4,128)}) custom-call(s32[5]{0:T(128)} %copy-done.68, bf16[1024,128]{1,0:T(8,128)(2,1)} %bitcast.113, bf16[1024,128]{1,0:T(8,128)(2,1)} %bitcast.149, bf16[1024,128]{1,0:T(8,128)(2,1)} %bitcast.147, bf16[1024,128]{1,0:T(8,128)(2,1)} %bitcast.151, bf16[4,128,128]{2,1,0:T(8,128)(2,1)} %bitcast.166, ...), custom_call_target="tpu_custom_call" | custom-call | flops 1 | bytes 1 | tf_op jit(solution)/shard_map/pallas_call | solution.py:119
  116.0 2.6 collective-permute-start.24
  120.3 1.9 collective-permute-start.27
  127.6 1.7 collective-permute-start.29
  130.2 8.6 %collective-permute-done.29 = bf16[8,2,64,128]{3,2,1,0:T(8,128)(2,1)S(1)} collective-permute-done((bf16[8,2,64,128]{3,2,1,0:T(8,128)(2,1)S(1)}, bf16[8,2,64,128]{3,2,1,0:T(8,128)(2,1)S(1)}, u32[]{:S(2)}, u32[]{:S(2)}) %collective-permute-start.29) | collective-permute-done | bytes 262176 | tf_op jit(solution)/shard_map/ppermute | solution.py:34
  138.8 1.6 collective-permute-start.30
  140.4 1.8 fusion
  142.9 4.8 %collective-permute-done.30 = bf16[8,2,64,128]{3,2,1,0:T(8,128)(2,1)S(1)} collective-permute-done((bf16[8,2,64,128]{3,2,1,0:T(8,128)(2,1)S(1)}, bf16[8,2,64,128]{3,2,1,0:T(8,128)(2,1)S(1)}, u32[]{:S(2)}, u32[]{:S(2)}) %collective-permute-start.30) | collective-permute-done | bytes 262176 | tf_op jit(solution)/shard_map/ppermute | solution.py:34
  148.4 4.5 %shard_map.506 = (bf16[4,64,512]{2,1,0:T(8,128)(2,1)}, bf16[4,64,512]{2,1,0:T(8,128)(2,1)}, bf16[4,64,512]{2,1,0:T(8,128)(2,1)}, bf16[4,64,512]{2,1,0:T(8,128)(2,1)}) custom-call(s32[5]{0:T(128)} %copy-done.68, bf16[13,512,128]{2,1,0:T(8,128)(2,1)} %all-gather.6.cloned.1.call-done.w_far.refs_1_.w, f32[14,128]{1,0:T(8,128)} %refs_28_.1, ...), custom_call_target="tpu_custom_call" | custom-call | flops 1 | bytes 1 | tf_op jit(solution)/shard_map/pallas_call | solution.py:119
  154.3 1.7 collective-permute-start.32
  156.5 5.9 %collective-permute-done.31.refs_3_ = bf16[4,64,512]{2,1,0:T(8,128)(2,1)S(1)} collective-permute-done((bf16[4,64,512]{2,1,0:T(8,128)(2,1)}, bf16[4,64,512]{2,1,0:T(8,128)(2,1)S(1)}, u32[]{:S(2)}, u32[]{:S(2)}) %collective-permute-start.31) | collective-permute-done | bytes 262176 | tf_op jit(solution)/shard_map/ppermute | solution.py:34
  162.4 5.5 %collective-permute-done.32.refs_4_ = bf16[4,64,512]{2,1,0:T(8,128)(2,1)S(1)} collective-permute-done((bf16[4,64,512]{2,1,0:T(8,128)(2,1)}, bf16[4,64,512]{2,1,0:T(8,128)(2,1)S(1)}, u32[]{:S(2)}, u32[]{:S(2)}) %collective-permute-start.32) | collective-permute-done | bytes 262176 | tf_op jit(solution)/shard_map/ppermute | solution.py:34
  171.2 35.7 %shard_map.507 = (bf16[2,64,2048]{2,1,0:T(8,128)(2,1)}, bf16[2,64,2176]{2,1,0:T(8,128)(2,1)}, bf16[2,64,2176]{2,1,0:T(8,128)(2,1)}) custom-call(s32[1]{0:T(128)S(6)} %add_shard_map.4.refs_0_, bf16[2,64,128]{2,1,0:T(8,128)(2,1)} %pad.5.refs_1_, bf16[4,64,512]{2,1,0:T(8,128)(2,1)} %get-tuple-element.170.refs_2_, bf16[4,64,512]{2,1,0:T(8,128)(2,1)} %copy-done.111, ...), custom_call_target="tpu_custom_call" | custom-call | flops 6643777536 | bytes 2162688 | tf_op jit(solution)/shard_map/pallas_call | solution.py:571
  207.1 2.1 collective-permute-done.38.other_far
  209.9 2.5 shard_map.508
  215.9 4.5 %collective-permute-done.39.refs_3_ = bf16[3,64,512]{2,1,0:T(8,128)(2,1)S(1)} collective-permute-done((bf16[3,64,512]{2,1,0:T(8,128)(2,1)}, bf16[3,64,512]{2,1,0:T(8,128)(2,1)S(1)}, u32[]{:S(2)}, u32[]{:S(2)}) %collective-permute-start.39) | collective-permute-done | bytes 196640 | tf_op jit(solution)/shard_map/ppermute | solution.py:34
  220.4 2.9 collective-permute-done.40.refs_4_
  225.4 4.3 %shard_map.509 = (bf16[8,2,64,384]{3,2,1,0:T(8,128)(2,1)}, f32[8,2,64,128]{3,2,1,0:T(8,128)}, bf16[8,2,64,128]{3,2,1,0:T(8,128)(2,1)}, bf16[8,2,64,128]{3,2,1,0:...) custom-call(s32[5]{0:T(128)} %copy-done.68, ...), custom_call_target="tpu_custom_call" | custom-call | flops 1 | bytes 1 | tf_op jit(solution)/shard_map/pallas_call | solution.py:119
  229.8 2.0 collective-permute-start.45
  231.9 7.4 %collective-permute-done.46 = bf16[8,2,64,128]{3,2,1,0:T(8,128)(2,1)S(1)} collective-permute-done((bf16[8,2,64,128]{3,2,1,0:T(8,128)(2,1)}, bf16[8,2,64,128]{3,2,1,0:T(8,128)(2,1)S(1)}, u32[]{:S(2)}, u32[]{:S(2)}) %collective-permute-start.46) | collective-permute-done | bytes 262176 | tf_op jit(solution)/shard_map/ppermute | solution.py:34
  247.8 1.8 collective-permute-done.44.refs_4_
  253.4 1.8 collective-permute-start.50
  257.0 1.8 collective-permute-done.49
  260.1 1.9 collective-permute-start.52
  262.9 3.2 shard_map.513
  266.1 2.0 collective-permute-start.55
  269.6 6.8 %shard_map.515 = (bf16[4,13,64,128]{3,2,1,0:T(8,128)(2,1)}, bf16[4,13,64,128]{3,2,1,0:T(8,128)(2,1)}) custom-call(s32[5]{0:T(128)} %copy-done.68, bf16[1024,128]{1,0:T(8,128)(2,1)} %bitcast.114, bf16[1024,128]{1,0:T(8,128)(2,1)} %bitcast.150, bf16[1024,128]{1,0:T(8,128)(2,1)} %bitcast.148, bf16[1024,128]{1,0:T(8,128)(2,1)} %bitcast.152, ...), custom_call_target="tpu_custom_call" | custom-call | flops 1 | bytes 1 | tf_op jit(solution)/shard_map/pallas_call | solution.py:119
  277.2 2.5 collective-permute-start.56
  280.0 5.3 %collective-permute-done.54.t1 = bf16[8,2,64,128]{3,2,1,0:T(8,128)(2,1)S(1)} collective-permute-done((bf16[8,2,64,128]{3,2,1,0:T(8,128)(2,1)S(1)}, bf16[8,2,64,128]{3,2,1,0:T(8,128)(2,1)S(1)}, u32[]{:S(2)}, u32[]{:S(2)}) %collective-permute-start.54) | collective-permute-done | bytes 262176 | tf_op jit(solution)/shard_map/ppermute | solution.py:34
  285.3 6.3 %collective-permute-done.56.t2 = bf16[8,2,64,128]{3,2,1,0:T(8,128)(2,1)S(1)} collective-permute-done((bf16[8,2,64,128]{3,2,1,0:T(8,128)(2,1)S(1)}, bf16[8,2,64,128]{3,2,1,0:T(8,128)(2,1)S(1)}, u32[]{:S(2)}, u32[]{:S(2)}) %collective-permute-start.56) | collective-permute-done | bytes 262176 | tf_op jit(solution)/shard_map/ppermute | solution.py:34
  293.5 2.4 collective-permute-start.63
  298.2 1.7 collective-permute-start.58
  300.4 2.3 shard_map.516
  307.6 2.7 collective-permute-start.64
  314.0 3.2 shard_map.518
  319.0 5.4 %shard_map.519 = (bf16[4,9,64,128]{3,2,1,0:T(8,128)(2,1)}, bf16[4,9,64,128]{3,2,1,0:T(8,128)(2,1)}) custom-call(s32[5]{0:T(128)} %copy-done.68, bf16[1024,128]{1,0:T(8,128)(2,1)} %bitcast.116, bf16[1024,128]{1,0:T(8,128)(2,1)} %bitcast.122, bf16[1024,128]{1,0:T(8,128)(2,1)} %bitcast.120, bf16[1024,128]{1,0:T(8,128)(2,1)} %bitcast.124, ...), custom_call_target="tpu_custom_call" | custom-call | flops 1 | bytes 1 | tf_op jit(solution)/shard_map/pallas_call | solution.py:119
  325.6 2.3 collective-permute-start.68
  329.3 2.1 collective-permute-start.70
  332.9 2.8 collective-permute-done.70.refs_2_
  336.4 3.3 collective-permute-done.71.refs_3_
  354.3 3.9 %collective-permute-start.80 = (f32[8,128]{1,0:T(8,128)S(1)}, f32[8,128]{1,0:T(8,128)S(1)}, u32[]{:S(2)}, u32[]{:S(2)}) collective-permute-start(f32[8,128]{1,0:T(8,128)S(1)} %get-tuple-element.232.refs_0_), channel_id=1, source_target_pairs={{0,3},{1,2},{2,1},{3,0},{4,7},{5,6},{6,5},{7,4},{8,11},{9,10},{10,... | collective-permute-start | bytes 12296 | tf_op jit(solution)/shard_map/ppermute | solution.py:34
  359.7 3.6 shard_map.522
  364.7 4.6 %shard_map.526 = (f32[1,128]{1,0:T(1,128)}, f32[9,64,128]{2,1,0:T(8,128)}, f32[9,64,128]{2,1,0:T(8,128)}, f32[9,64,128]{2,1,0:T(8,128)}, bf16[9,64,128]{2,1,0:T(...) custom-call(f32[8,128]{1,0:T(8,128)S(1)} %get-tuple-element.232.refs, ...), custom_call_target="tpu_custom_call" | custom-call | flops 1 | bytes 1 | tf_op jit(solution)/shard_map/pallas_call | solution.py:119
  (459 shorter events, 103.2 us)
Async XLA Ops:
  7.2 53.0 %all-gather.8.cloned.1.call-start = ((), (), s32[]{:S(2)}) async-start(), calls=%async_computation.3 | async-start | bytes 1327104 | tf_op jit(solution)/shard_map/all_gather | solution.py:888
  11.5 78.5 %all-gather.6.cloned.1.call-start = ((), (), s32[]{:S(2)}) async-start(), calls=%async_computation.2 | async-start | bytes 1916928 | tf_op jit(solution)/shard_map/all_gather | solution.py:897
  11.5 12.4 %collective-permute-start.5 = (bf16[8,2,64,128]{3,2,1,0:T(8,128)(2,1)}, bf16[8,2,64,128]{3,2,1,0:T(8,128)(2,1)S(1)}, u32[]{:S(2)}, u32[]{:S(2)}) collective-permute-start(bf16[8,2,64,128]{3,2,1,0:T(8,128)(2,1)} %c0.1), channel_id=1, source_target_pairs={{0,3},{1,2},{2,1},{3,0},{4,7},{5,6},{6,5},{7,4},{8,11},{9,10},{10,... | collective-permute-start | bytes 786440 | tf_op jit(solution)/shard_map/ppermute | solution.py:34
  16.5 12.6 %collective-permute-start.4 = (bf16[8,2,64,128]{3,2,1,0:T(8,128)(2,1)}, bf16[8,2,64,128]{3,2,1,0:T(8,128)(2,1)S(1)}, u32[]{:S(2)}, u32[]{:S(2)}) collective-permute-start(bf16[8,2,64,128]{3,2,1,0:T(8,128)(2,1)} %c0.1), channel_id=1, source_target_pairs={{0,1},{1,0},{2,3},{3,2},{4,5},{5,4},{6,7},{7,6},{8,9},{9,8},{10,11... | collective-permute-start | bytes 786440 | tf_op jit(solution)/shard_map/ppermute | solution.py:34
  16.5 4.5 %collective-permute-start.3 = (f32[4,128]{1,0:T(4,128)S(1)}, f32[4,128]{1,0:T(4,128)S(1)}, u32[]{:S(2)}, u32[]{:S(2)}) collective-permute-start(f32[4,128]{1,0:T(4,128)S(1)} %add.173), channel_id=1, source_target_pairs={{0,24},{4,28},{8,16},{12,20},{16,8},{20,12},{24,0},{28,4},{1,25},{... | collective-permute-start | bytes 6152 | tf_op jit(solution)/shard_map/ppermute | solution.py:34
  31.8 11.0 %collective-permute-start.7 = (bf16[8,2,64,128]{3,2,1,0:T(8,128)(2,1)S(1)}, bf16[8,2,64,128]{3,2,1,0:T(8,128)(2,1)S(1)}, u32[]{:S(2)}, u32[]{:S(2)}) collective-permute-start(bf16[8,2,64,128]{3,2,1,0:T(8,128)(2,1)S(1)} %shard_map.500), channel_id=1, source_target_pairs={{0,3},{1,2},{2,1},{3,0},{4,7},{5,6},{6,5},{7,4},{8,11},{9,10},{10,... | collective-permute-start | bytes 786440 | tf_op jit(solution)/shard_map/ppermute | solution.py:34
  33.5 12.9 %collective-permute-start.6 = (bf16[8,2,64,128]{3,2,1,0:T(8,128)(2,1)S(1)}, bf16[8,2,64,128]{3,2,1,0:T(8,128)(2,1)S(1)}, u32[]{:S(2)}, u32[]{:S(2)}) collective-permute-start(bf16[8,2,64,128]{3,2,1,0:T(8,128)(2,1)S(1)} %shard_map.500), channel_id=1, source_target_pairs={{0,1},{1,0},{2,3},{3,2},{4,5},{5,4},{6,7},{7,6},{8,9},{9,8},{10,11... | collective-permute-start | bytes 786440 | tf_op jit(solution)/shard_map/ppermute | solution.py:34
  47.2 93.2 %all-gather.4.cloned.1.call-start = ((), (), s32[]{:S(2)}) async-start(), calls=%async_computation.1 | async-start | bytes 1179648 | tf_op jit(solution)/shard_map/all_gather | solution.py:900
  48.4 7.1 %collective-permute-start.8 = (bf16[8,2,64,128]{3,2,1,0:T(8,128)(2,1)S(1)}, bf16[8,2,64,128]{3,2,1,0:T(8,128)(2,1)S(1)}, u32[]{:S(2)}, u32[]{:S(2)}) collective-permute-start(bf16[8,2,64,128]{3,2,1,0:T(8,128)(2,1)S(1)} %collective-permute-done.7), channel_id=1, source_target_pairs={{0,1},{1,0},{2,3},{3,2},{4,5},{5,4},{6,7},{7,6},{8,9},{9,8},{10,11... | collective-permute-start | bytes 786440 | tf_op jit(solution)/shard_map/ppermute | solution.py:34
  55.5 9.3 %collective-permute-start.11 = (bf16[8,2,64,128]{3,2,1,0:T(8,128)(2,1)S(1)}, bf16[8,2,64,128]{3,2,1,0:T(8,128)(2,1)}, u32[]{:S(2)}, u32[]{:S(2)}) collective-permute-start(bf16[8,2,64,128]{3,2,1,0:T(8,128)(2,1)S(1)} %collective-permute-done.5), channel_id=1, source_target_pairs={{0,1},{1,0},{2,3},{3,2},{4,5},{5,4},{6,7},{7,6},{8,9},{9,8},{10,11... | collective-permute-start | bytes 786440 | tf_op jit(solution)/shard_map/ppermute | solution.py:34
  67.9 4.6 %collective-permute-start.15 = (f32[8,128]{1,0:T(8,128)S(1)}, f32[8,128]{1,0:T(8,128)S(1)}, u32[]{:S(2)}, u32[]{:S(2)}) collective-permute-start(f32[8,128]{1,0:T(8,128)S(1)} %fusion.20), channel_id=1, source_target_pairs={{0,24},{4,28},{8,16},{12,20},{16,8},{20,12},{24,0},{28,4},{1,25},{... | collective-permute-start | bytes 12296 | tf_op jit(solution)/shard_map/ppermute | solution.py:34
  74.9 11.1 %collective-permute-start.20 = (bf16[8,2,64,128]{3,2,1,0:T(8,128)(2,1)S(1)}, bf16[8,2,64,128]{3,2,1,0:T(8,128)(2,1)S(1)}, u32[]{:S(2)}, u32[]{:S(2)}) collective-permute-start(bf16[8,2,64,128]{3,2,1,0:T(8,128)(2,1)S(1)} %shard_map.502), channel_id=1, source_target_pairs={{0,3},{1,2},{2,1},{3,0},{4,7},{5,6},{6,5},{7,4},{8,11},{9,10},{10,... | collective-permute-start | bytes 786440 | tf_op jit(solution)/shard_map/ppermute | solution.py:34
  78.4 11.5 %collective-permute-start.19 = (bf16[8,2,64,128]{3,2,1,0:T(8,128)(2,1)S(1)}, bf16[8,2,64,128]{3,2,1,0:T(8,128)(2,1)S(1)}, u32[]{:S(2)}, u32[]{:S(2)}) collective-permute-start(bf16[8,2,64,128]{3,2,1,0:T(8,128)(2,1)S(1)} %shard_map.502), channel_id=1, source_target_pairs={{0,1},{1,0},{2,3},{3,2},{4,5},{5,4},{6,7},{7,6},{8,9},{9,8},{10,11... | collective-permute-start | bytes 786440 | tf_op jit(solution)/shard_map/ppermute | solution.py:34
  80.4 261.3 %reduce-scatter.4.cloned.1.call-start = ((), (), s32[]{:S(2)}) async-start(), calls=%async_computation.4 | async-start | bytes 1064960
  86.0 11.4 %collective-permute-start.21 = (bf16[8,2,64,128]{3,2,1,0:T(8,128)(2,1)S(1)}, bf16[8,2,64,128]{3,2,1,0:T(8,128)(2,1)S(1)}, u32[]{:S(2)}, u32[]{:S(2)}) collective-permute-start(bf16[8,2,64,128]{3,2,1,0:T(8,128)(2,1)S(1)} %collective-permute-done.20), channel_id=1, source_target_pairs={{0,1},{1,0},{2,3},{3,2},{4,5},{5,4},{6,7},{7,6},{8,9},{9,8},{10,11... | collective-permute-start | bytes 786440 | tf_op jit(solution)/shard_map/ppermute | solution.py:34
  91.6 5.9 %collective-permute-start.18 = (bf16[128,128]{1,0:T(8,128)(2,1)S(1)}, bf16[128,128]{1,0:T(8,128)(2,1)S(1)}, u32[]{:S(2)}, u32[]{:S(2)}) collective-permute-start(bf16[128,128]{1,0:T(8,128)(2,1)S(1)} %get-tuple-element.292), channel_id=1, source_target_pairs={{0,2},{1,3},{2,0},{3,1},{4,6},{5,7},{6,4},{7,5},{8,10},{9,11},{10,... | collective-permute-start | bytes 98312 | tf_op jit(solution)/shard_map/ppermute | solution.py:34
  93.2 7.2 %collective-permute-start.17 = (bf16[128,128]{1,0:T(8,128)(2,1)S(1)}, bf16[128,128]{1,0:T(8,128)(2,1)S(1)}, u32[]{:S(2)}, u32[]{:S(2)}) collective-permute-start(bf16[128,128]{1,0:T(8,128)(2,1)S(1)} %get-tuple-element.293), channel_id=1, source_target_pairs={{0,3},{1,2},{2,1},{3,0},{4,7},{5,6},{6,5},{7,4},{8,11},{9,10},{10,... | collective-permute-start | bytes 98312 | tf_op jit(solution)/shard_map/ppermute | solution.py:34
  95.0 5.4 %collective-permute-start.16 = (bf16[128,128]{1,0:T(8,128)(2,1)S(1)}, bf16[128,128]{1,0:T(8,128)(2,1)S(1)}, u32[]{:S(2)}, u32[]{:S(2)}) collective-permute-start(bf16[128,128]{1,0:T(8,128)(2,1)S(1)} %get-tuple-element.294), channel_id=1, source_target_pairs={{0,1},{1,0},{2,3},{3,2},{4,5},{5,4},{6,7},{7,6},{8,9},{9,8},{10,11... | collective-permute-start | bytes 98312 | tf_op jit(solution)/shard_map/ppermute | solution.py:34
  104.5 4.2 %collective-permute-start.23 = (bf16[4,2,64,128]{3,2,1,0:T(8,128)(2,1)S(1)}, bf16[4,2,64,128]{3,2,1,0:T(8,128)(2,1)S(1)}, u32[]{:S(2)}, u32[]{:S(2)}) collective-permute-start(bf16[4,2,64,128]{3,2,1,0:T(8,128)(2,1)S(1)} %get-tuple-element.272), channel_id=1, source_target_pairs={{4,8},{12,16},{20,24},{8,4},{16,12},{24,20},{5,9},{13,17},{21,25},... | collective-permute-start | bytes 393224 | tf_op jit(solution)/shard_map/ppermute | solution.py:72
  105.4 3.8 %collective-permute-start.22 = (bf16[4,2,64,128]{3,2,1,0:T(8,128)(2,1)S(1)}, bf16[4,2,64,128]{3,2,1,0:T(8,128)(2,1)S(1)}, u32[]{:S(2)}, u32[]{:S(2)}) collective-permute-start(bf16[4,2,64,128]{3,2,1,0:T(8,128)(2,1)S(1)} %get-tuple-element.273), channel_id=1, source_target_pairs={{0,4},{4,0},{8,12},{12,8},{16,20},{20,16},{24,28},{28,24},{1,5},{5... | collective-permute-start | bytes 393224 | tf_op jit(solution)/shard_map/ppermute | solution.py:34
  120.3 4.5 %collective-permute-start.27 = (f32[4,128]{1,0:T(4,128)S(1)}, f32[4,128]{1,0:T(4,128)S(1)}, u32[]{:S(2)}, u32[]{:S(2)}) collective-permute-start(f32[4,128]{1,0:T(4,128)S(1)} %add.195), channel_id=1, source_target_pairs={{0,24},{4,28},{8,16},{12,20},{16,8},{20,12},{24,0},{28,4},{1,25},{... | collective-permute-start | bytes 6152 | tf_op jit(solution)/shard_map/ppermute | solution.py:34
  127.6 11.2 %collective-permute-start.29 = (bf16[8,2,64,128]{3,2,1,0:T(8,128)(2,1)S(1)}, bf16[8,2,64,128]{3,2,1,0:T(8,128)(2,1)S(1)}, u32[]{:S(2)}, u32[]{:S(2)}) collective-permute-start(bf16[8,2,64,128]{3,2,1,0:T(8,128)(2,1)S(1)} %shard_map.505), channel_id=1, source_target_pairs={{0,3},{1,2},{2,1},{3,0},{4,7},{5,6},{6,5},{7,4},{8,11},{9,10},{10,... | collective-permute-start | bytes 786440 | tf_op jit(solution)/shard_map/ppermute | solution.py:34
  130.1 12.8 %collective-permute-start.28 = (bf16[8,2,64,128]{3,2,1,0:T(8,128)(2,1)S(1)}, bf16[8,2,64,128]{3,2,1,0:T(8,128)(2,1)S(1)}, u32[]{:S(2)}, u32[]{:S(2)}) collective-permute-start(bf16[8,2,64,128]{3,2,1,0:T(8,128)(2,1)S(1)} %shard_map.505), channel_id=1, source_target_pairs={{0,1},{1,0},{2,3},{3,2},{4,5},{5,4},{6,7},{7,6},{8,9},{9,8},{10,11... | collective-permute-start | bytes 786440 | tf_op jit(solution)/shard_map/ppermute | solution.py:34
  138.8 9.0 %collective-permute-start.30 = (bf16[8,2,64,128]{3,2,1,0:T(8,128)(2,1)S(1)}, bf16[8,2,64,128]{3,2,1,0:T(8,128)(2,1)S(1)}, u32[]{:S(2)}, u32[]{:S(2)}) collective-permute-start(bf16[8,2,64,128]{3,2,1,0:T(8,128)(2,1)S(1)} %collective-permute-done.29), channel_id=1, source_target_pairs={{0,1},{1,0},{2,3},{3,2},{4,5},{5,4},{6,7},{7,6},{8,9},{9,8},{10,11... | collective-permute-start | bytes 786440 | tf_op jit(solution)/shard_map/ppermute | solution.py:34
  152.9 9.5 %collective-permute-start.31 = (bf16[4,64,512]{2,1,0:T(8,128)(2,1)}, bf16[4,64,512]{2,1,0:T(8,128)(2,1)S(1)}, u32[]{:S(2)}, u32[]{:S(2)}) collective-permute-start(bf16[4,64,512]{2,1,0:T(8,128)(2,1)} %get-tuple-element.171), channel_id=1, source_target_pairs={{0,8},{4,12},{8,0},{12,4},{16,24},{20,28},{24,16},{28,20},{1,9},{5... | collective-permute-start | bytes 786440 | tf_op jit(solution)/shard_map/ppermute | solution.py:34
  154.3 13.5 %collective-permute-start.32 = (bf16[4,64,512]{2,1,0:T(8,128)(2,1)}, bf16[4,64,512]{2,1,0:T(8,128)(2,1)S(1)}, u32[]{:S(2)}, u32[]{:S(2)}) collective-permute-start(bf16[4,64,512]{2,1,0:T(8,128)(2,1)} %get-tuple-element.172), channel_id=1, source_target_pairs={{0,16},{4,20},{8,24},{12,28},{16,0},{20,4},{24,8},{28,12},{1,17},{... | collective-permute-start | bytes 786440 | tf_op jit(solution)/shard_map/ppermute | solution.py:34
  156.0 11.8 %collective-permute-start.33 = (bf16[4,64,512]{2,1,0:T(8,128)(2,1)}, bf16[4,64,512]{2,1,0:T(8,128)(2,1)S(1)}, u32[]{:S(2)}, u32[]{:S(2)}) collective-permute-start(bf16[4,64,512]{2,1,0:T(8,128)(2,1)} %get-tuple-element.173), channel_id=1, source_target_pairs={{0,24},{4,28},{8,16},{12,20},{16,8},{20,12},{24,0},{28,4},{1,25},{... | collective-permute-start | bytes 786440 | tf_op jit(solution)/shard_map/ppermute | solution.py:34
  156.5 13.1 %collective-permute-start.34 = (bf16[4,64,512]{2,1,0:T(8,128)(2,1)}, bf16[4,64,512]{2,1,0:T(8,128)(2,1)S(1)}, u32[]{:S(2)}, u32[]{:S(2)}) collective-permute-start(bf16[4,64,512]{2,1,0:T(8,128)(2,1)} %get-tuple-element.170.refs_2_), channel_id=1, source_target_pairs={{0,4},{4,0},{8,12},{12,8},{16,20},{20,16},{24,28},{28,24},{1,5},{5... | collective-permute-start | bytes 786440 | tf_op jit(solution)/shard_map/ppermute | solution.py:34
  162.4 7.2 %collective-permute-start.35 = (bf16[4,64,512]{2,1,0:T(8,128)(2,1)S(1)}, bf16[4,64,512]{2,1,0:T(8,128)(2,1)S(1)}, u32[]{:S(2)}, u32[]{:S(2)}) collective-permute-start(bf16[4,64,512]{2,1,0:T(8,128)(2,1)S(1)} %collective-permute-done.31.refs_3_), channel_id=1, source_target_pairs={{0,4},{4,0},{8,12},{12,8},{16,20},{20,16},{24,28},{28,24},{1,5},{5... | collective-permute-start | bytes 786440 | tf_op jit(solution)/shard_map/ppermute | solution.py:34
  212.4 8.0 %collective-permute-start.39 = (bf16[3,64,512]{2,1,0:T(8,128)(2,1)}, bf16[3,64,512]{2,1,0:T(8,128)(2,1)S(1)}, u32[]{:S(2)}, u32[]{:S(2)}) collective-permute-start(bf16[3,64,512]{2,1,0:T(8,128)(2,1)} %get-tuple-element.179), channel_id=1, source_target_pairs={{0,8},{4,12},{8,0},{12,4},{16,24},{20,28},{24,16},{28,20},{1,9},{5... | collective-permute-start | bytes 589832 | tf_op jit(solution)/shard_map/ppermute | solution.py:34
  213.3 10.0 %collective-permute-start.40 = (bf16[3,64,512]{2,1,0:T(8,128)(2,1)}, bf16[3,64,512]{2,1,0:T(8,128)(2,1)S(1)}, u32[]{:S(2)}, u32[]{:S(2)}) collective-permute-start(bf16[3,64,512]{2,1,0:T(8,128)(2,1)} %get-tuple-element.180), channel_id=1, source_target_pairs={{0,16},{4,20},{8,24},{12,28},{16,0},{20,4},{24,8},{28,12},{1,17},{... | collective-permute-start | bytes 589832 | tf_op jit(solution)/shard_map/ppermute | solution.py:34
  214.5 10.2 %collective-permute-start.41 = (bf16[3,64,512]{2,1,0:T(8,128)(2,1)}, bf16[3,64,512]{2,1,0:T(8,128)(2,1)S(1)}, u32[]{:S(2)}, u32[]{:S(2)}) collective-permute-start(bf16[3,64,512]{2,1,0:T(8,128)(2,1)} %get-tuple-element.181), channel_id=1, source_target_pairs={{0,24},{4,28},{8,16},{12,20},{16,8},{20,12},{24,0},{28,4},{1,25},{... | collective-permute-start | bytes 589832 | tf_op jit(solution)/shard_map/ppermute | solution.py:34
  229.8 9.5 %collective-permute-start.46 = (bf16[8,2,64,128]{3,2,1,0:T(8,128)(2,1)}, bf16[8,2,64,128]{3,2,1,0:T(8,128)(2,1)S(1)}, u32[]{:S(2)}, u32[]{:S(2)}) collective-permute-start(bf16[8,2,64,128]{3,2,1,0:T(8,128)(2,1)} %get-tuple-element.182), channel_id=1, source_target_pairs={{0,1},{1,0},{2,3},{3,2},{4,5},{5,4},{6,7},{7,6},{8,9},{9,8},{10,11... | collective-permute-start | bytes 786440 | tf_op jit(solution)/shard_map/ppermute | solution.py:34
  229.8 19.7 %collective-permute-start.45 = (bf16[8,2,64,128]{3,2,1,0:T(8,128)(2,1)}, bf16[8,2,64,128]{3,2,1,0:T(8,128)(2,1)S(1)}, u32[]{:S(2)}, u32[]{:S(2)}) collective-permute-start(bf16[8,2,64,128]{3,2,1,0:T(8,128)(2,1)} %get-tuple-element.192), channel_id=1, source_target_pairs={{0,1},{1,0},{2,3},{3,2},{4,5},{5,4},{6,7},{7,6},{8,9},{9,8},{10,11... | collective-permute-start | bytes 786440 | tf_op jit(solution)/shard_map/ppermute | solution.py:34
  240.4 9.2 %collective-permute-start.47 = (bf16[8,2,64,128]{3,2,1,0:T(8,128)(2,1)S(1)}, bf16[8,2,64,128]{3,2,1,0:T(8,128)(2,1)S(1)}, u32[]{:S(2)}, u32[]{:S(2)}) collective-permute-start(bf16[8,2,64,128]{3,2,1,0:T(8,128)(2,1)S(1)} %add_convert_fusion.2), channel_id=1, source_target_pairs={{0,3},{1,2},{2,1},{3,0},{4,7},{5,6},{6,5},{7,4},{8,11},{9,10},{10,... | collective-permute-start | bytes 786440 | tf_op jit(solution)/shard_map/ppermute | solution.py:34
  241.7 4.6 %collective-permute-start.42 = (bf16[64,768]{1,0:T(8,128)(2,1)S(1)}, bf16[64,768]{1,0:T(8,128)(2,1)S(1)}, u32[]{:S(2)}, u32[]{:S(2)}) collective-permute-start(bf16[64,768]{1,0:T(8,128)(2,1)S(1)} %copy-done.120), channel_id=1, source_target_pairs={{0,8},{4,12},{8,0},{12,4},{16,24},{20,28},{24,16},{28,20},{1,9},{5... | collective-permute-start | bytes 294920 | tf_op jit(solution)/shard_map/ppermute | solution.py:34
  243.2 4.6 %collective-permute-start.43 = (bf16[64,768]{1,0:T(8,128)(2,1)S(1)}, bf16[64,768]{1,0:T(8,128)(2,1)S(1)}, u32[]{:S(2)}, u32[]{:S(2)}) collective-permute-start(bf16[64,768]{1,0:T(8,128)(2,1)S(1)} %copy-done.119), channel_id=1, source_target_pairs={{0,16},{4,20},{8,24},{12,28},{16,0},{20,4},{24,8},{28,12},{1,17},{... | collective-permute-start | bytes 294920 | tf_op jit(solution)/shard_map/ppermute | solution.py:34
  244.0 5.5 %collective-permute-start.44 = (bf16[64,768]{1,0:T(8,128)(2,1)S(1)}, bf16[64,768]{1,0:T(8,128)(2,1)S(1)}, u32[]{:S(2)}, u32[]{:S(2)}) collective-permute-start(bf16[64,768]{1,0:T(8,128)(2,1)S(1)} %copy-done.118), channel_id=1, source_target_pairs={{0,24},{4,28},{8,16},{12,20},{16,8},{20,12},{24,0},{28,4},{1,25},{... | collective-permute-start | bytes 294920 | tf_op jit(solution)/shard_map/ppermute | solution.py:34
  252.2 4.5 %collective-permute-start.51 = (f32[4,128]{1,0:T(4,128)S(1)}, f32[4,128]{1,0:T(4,128)S(1)}, u32[]{:S(2)}, u32[]{:S(2)}) collective-permute-start(f32[4,128]{1,0:T(4,128)S(1)} %add.200), channel_id=1, source_target_pairs={{0,24},{4,28},{8,16},{12,20},{16,8},{20,12},{24,0},{28,4},{1,25},{... | collective-permute-start | bytes 6152 | tf_op jit(solution)/shard_map/ppermute | solution.py:34
  266.1 11.0 %collective-permute-start.55 = (bf16[8,2,64,128]{3,2,1,0:T(8,128)(2,1)S(1)}, bf16[8,2,64,128]{3,2,1,0:T(8,128)(2,1)S(1)}, u32[]{:S(2)}, u32[]{:S(2)}) collective-permute-start(bf16[8,2,64,128]{3,2,1,0:T(8,128)(2,1)S(1)} %get-tuple-element.201), channel_id=1, source_target_pairs={{0,1},{1,0},{2,3},{3,2},{4,5},{5,4},{6,7},{7,6},{8,9},{9,8},{10,11... | collective-permute-start | bytes 786440 | tf_op jit(solution)/shard_map/ppermute | solution.py:34
  276.4 23.5 %collective-permute-start.59 = (bf16[4,13,64,128]{3,2,1,0:T(8,128)(2,1)}, bf16[4,13,64,128]{3,2,1,0:T(8,128)(2,1)}, u32[]{:S(2)}, u32[]{:S(2)}) collective-permute-start(bf16[4,13,64,128]{3,2,1,0:T(8,128)(2,1)} %get-tuple-element.207), channel_id=1, source_target_pairs={{0,4},{4,0},{8,12},{12,8},{16,20},{20,16},{24,28},{28,24},{1,5},{5... | collective-permute-start | bytes 2555912 | tf_op jit(solution)/shard_map/ppermute | solution.py:34
  276.8 8.5 %collective-permute-start.54 = (bf16[8,2,64,128]{3,2,1,0:T(8,128)(2,1)S(1)}, bf16[8,2,64,128]{3,2,1,0:T(8,128)(2,1)S(1)}, u32[]{:S(2)}, u32[]{:S(2)}) collective-permute-start(bf16[8,2,64,128]{3,2,1,0:T(8,128)(2,1)S(1)} %get-tuple-element.199), channel_id=1, source_target_pairs={{0,1},{1,0},{2,3},{3,2},{4,5},{5,4},{6,7},{7,6},{8,9},{9,8},{10,11... | collective-permute-start | bytes 786440 | tf_op jit(solution)/shard_map/ppermute | solution.py:34
  277.2 14.4 %collective-permute-start.56 = (bf16[8,2,64,128]{3,2,1,0:T(8,128)(2,1)S(1)}, bf16[8,2,64,128]{3,2,1,0:T(8,128)(2,1)S(1)}, u32[]{:S(2)}, u32[]{:S(2)}) collective-permute-start(bf16[8,2,64,128]{3,2,1,0:T(8,128)(2,1)S(1)} %add_convert_fusion.1), channel_id=1, source_target_pairs={{0,3},{1,2},{2,1},{3,0},{4,7},{5,6},{6,5},{7,4},{8,11},{9,10},{10,... | collective-permute-start | bytes 786440 | tf_op jit(solution)/shard_map/ppermute | solution.py:34
  293.5 9.1 %collective-permute-start.63 = (f32[8,128]{1,0:T(8,128)S(1)}, f32[8,128]{1,0:T(8,128)S(1)}, u32[]{:S(2)}, u32[]{:S(2)}) collective-permute-start(f32[8,128]{1,0:T(8,128)S(1)} %fusion.21), channel_id=1, source_target_pairs={{0,24},{4,28},{8,16},{12,20},{16,8},{20,12},{24,0},{28,4},{1,25},{... | collective-permute-start | bytes 12296 | tf_op jit(solution)/shard_map/ppermute | solution.py:34
  296.0 6.7 %collective-permute-start.62 = (f32[8,128]{1,0:T(8,128)S(1)}, f32[8,128]{1,0:T(8,128)S(1)}, u32[]{:S(2)}, u32[]{:S(2)}) collective-permute-start(f32[8,128]{1,0:T(8,128)S(1)} %fusion.21), channel_id=1, source_target_pairs={{0,16},{4,20},{8,24},{12,28},{16,0},{20,4},{24,8},{28,12},{1,17},{... | collective-permute-start | bytes 12296 | tf_op jit(solution)/shard_map/ppermute | solution.py:34
  297.4 5.3 %collective-permute-start.61 = (f32[8,128]{1,0:T(8,128)S(1)}, f32[8,128]{1,0:T(8,128)S(1)}, u32[]{:S(2)}, u32[]{:S(2)}) collective-permute-start(f32[8,128]{1,0:T(8,128)S(1)} %fusion.21), channel_id=1, source_target_pairs={{0,8},{4,12},{8,0},{12,4},{16,24},{20,28},{24,16},{28,20},{1,9},{5... | collective-permute-start | bytes 12296 | tf_op jit(solution)/shard_map/ppermute | solution.py:34
  298.2 15.1 %collective-permute-start.58 = (bf16[8,2,64,128]{3,2,1,0:T(8,128)(2,1)S(1)}, bf16[8,2,64,128]{3,2,1,0:T(8,128)(2,1)}, u32[]{:S(2)}, u32[]{:S(2)}) collective-permute-start(bf16[8,2,64,128]{3,2,1,0:T(8,128)(2,1)S(1)} %copy-done.32), channel_id=1, source_target_pairs={{0,3},{1,2},{2,1},{3,0},{4,7},{5,6},{6,5},{7,4},{8,11},{9,10},{10,... | collective-permute-start | bytes 786440 | tf_op jit(solution)/shard_map/ppermute | solution.py:34
  299.9 13.5 %collective-permute-start.57 = (bf16[8,2,64,128]{3,2,1,0:T(8,128)(2,1)S(1)}, bf16[8,2,64,128]{3,2,1,0:T(8,128)(2,1)}, u32[]{:S(2)}, u32[]{:S(2)}) collective-permute-start(bf16[8,2,64,128]{3,2,1,0:T(8,128)(2,1)S(1)} %copy-done.32), channel_id=1, source_target_pairs={{0,1},{1,0},{2,3},{3,2},{4,5},{5,4},{6,7},{7,6},{8,9},{9,8},{10,11... | collective-permute-start | bytes 786440 | tf_op jit(solution)/shard_map/ppermute | solution.py:34
  306.7 6.6 %collective-permute-start.65 = (bf16[1,2,64,128]{3,2,1,0:T(8,128)(2,1)S(1)}, bf16[1,2,64,128]{3,2,1,0:T(8,128)(2,1)S(1)}, u32[]{:S(2)}, u32[]{:S(2)}) collective-permute-start(bf16[1,2,64,128]{3,2,1,0:T(8,128)(2,1)S(1)} %get-tuple-element.268), channel_id=1, source_target_pairs={{4,8},{12,16},{20,24},{8,4},{16,12},{24,20},{5,9},{13,17},{21,25},... | collective-permute-start | bytes 98312 | tf_op jit(solution)/shard_map/ppermute | solution.py:72
  307.6 5.7 %collective-permute-start.64 = (bf16[1,2,64,128]{3,2,1,0:T(8,128)(2,1)S(1)}, bf16[1,2,64,128]{3,2,1,0:T(8,128)(2,1)S(1)}, u32[]{:S(2)}, u32[]{:S(2)}) collective-permute-start(bf16[1,2,64,128]{3,2,1,0:T(8,128)(2,1)S(1)} %get-tuple-element.269), channel_id=1, source_target_pairs={{0,4},{4,0},{8,12},{12,8},{16,20},{20,16},{24,28},{28,24},{1,5},{5... | collective-permute-start | bytes 98312 | tf_op jit(solution)/shard_map/ppermute | solution.py:34
  317.2 8.3 %collective-permute-start.67 = (bf16[8,2,64,128]{3,2,1,0:T(8,128)(2,1)S(1)}, bf16[8,2,64,128]{3,2,1,0:T(8,128)(2,1)S(1)}, u32[]{:S(2)}, u32[]{:S(2)}) collective-permute-start(bf16[8,2,64,128]{3,2,1,0:T(8,128)(2,1)S(1)} %get-tuple-element.216), channel_id=1, source_target_pairs={{0,1},{1,0},{2,3},{3,2},{4,5},{5,4},{6,7},{7,6},{8,9},{9,8},{10,11... | collective-permute-start | bytes 786440 | tf_op jit(solution)/shard_map/ppermute | solution.py:34
  324.4 4.0 %collective-permute-start.69 = (bf16[4,9,64,128]{3,2,1,0:T(8,128)(2,1)}, bf16[4,9,64,128]{3,2,1,0:T(8,128)(2,1)S(1)}, u32[]{:S(2)}, u32[]{:S(2)}) collective-permute-start(bf16[4,9,64,128]{3,2,1,0:T(8,128)(2,1)} %get-tuple-element.218), channel_id=1, source_target_pairs={{0,4},{4,0},{8,12},{12,8},{16,20},{20,16},{24,28},{28,24},{1,5},{5... | collective-permute-start | bytes 1769480 | tf_op jit(solution)/shard_map/ppermute | solution.py:34
  324.5 16.4 %collective-permute-start.66 = (bf16[8,2,64,128]{3,2,1,0:T(8,128)(2,1)S(1)}, bf16[8,2,64,128]{3,2,1,0:T(8,128)(2,1)S(1)}, u32[]{:S(2)}, u32[]{:S(2)}) collective-permute-start(bf16[8,2,64,128]{3,2,1,0:T(8,128)(2,1)S(1)} %get-tuple-element.214), channel_id=1, source_target_pairs={{0,1},{1,0},{2,3},{3,2},{4,5},{5,4},{6,7},{7,6},{8,9},{9,8},{10,11... | collective-permute-start | bytes 786440 | tf_op jit(solution)/shard_map/ppermute | solution.py:34
  325.6 15.4 %collective-permute-start.68 = (bf16[8,2,64,128]{3,2,1,0:T(8,128)(2,1)S(1)}, bf16[8,2,64,128]{3,2,1,0:T(8,128)(2,1)S(1)}, u32[]{:S(2)}, u32[]{:S(2)}) collective-permute-start(bf16[8,2,64,128]{3,2,1,0:T(8,128)(2,1)S(1)} %add_convert_fusion), channel_id=1, source_target_pairs={{0,3},{1,2},{2,1},{3,0},{4,7},{5,6},{6,5},{7,4},{8,11},{9,10},{10,... | collective-permute-start | bytes 786440 | tf_op jit(solution)/shard_map/ppermute | solution.py:34
  329.3 6.4 %collective-permute-start.70 = (bf16[9,64,128]{2,1,0:T(8,128)(2,1)S(1)}, bf16[9,64,128]{2,1,0:T(8,128)(2,1)S(1)}, u32[]{:S(2)}, u32[]{:S(2)}) collective-permute-start(bf16[9,64,128]{2,1,0:T(8,128)(2,1)S(1)} %get-tuple-element.220), channel_id=1, source_target_pairs={{0,8},{4,12},{8,0},{12,4},{16,24},{20,28},{24,16},{28,20},{1,9},{5... | collective-permute-start | bytes 442376 | tf_op jit(solution)/shard_map/ppermute | solution.py:34
  331.4 8.2 %collective-permute-start.71 = (bf16[9,64,128]{2,1,0:T(8,128)(2,1)S(1)}, bf16[9,64,128]{2,1,0:T(8,128)(2,1)S(1)}, u32[]{:S(2)}, u32[]{:S(2)}) collective-permute-start(bf16[9,64,128]{2,1,0:T(8,128)(2,1)S(1)} %get-tuple-element.221), channel_id=1, source_target_pairs={{0,16},{4,20},{8,24},{12,28},{16,0},{20,4},{24,8},{28,12},{1,17},{... | collective-permute-start | bytes 442376 | tf_op jit(solution)/shard_map/ppermute | solution.py:34
  331.4 8.9 %collective-permute-start.72 = (bf16[9,64,128]{2,1,0:T(8,128)(2,1)S(1)}, bf16[9,64,128]{2,1,0:T(8,128)(2,1)S(1)}, u32[]{:S(2)}, u32[]{:S(2)}) collective-permute-start(bf16[9,64,128]{2,1,0:T(8,128)(2,1)S(1)} %get-tuple-element.222), channel_id=1, source_target_pairs={{0,24},{4,28},{8,16},{12,20},{16,8},{20,12},{24,0},{28,4},{1,25},{... | collective-permute-start | bytes 442376 | tf_op jit(solution)/shard_map/ppermute | solution.py:34
  347.1 11.6 %collective-permute-start.73 = (bf16[8,2,64,128]{3,2,1,0:T(8,128)(2,1)}, bf16[8,2,64,128]{3,2,1,0:T(8,128)(2,1)S(1)}, u32[]{:S(2)}, u32[]{:S(2)}) collective-permute-start(bf16[8,2,64,128]{3,2,1,0:T(8,128)(2,1)} %collective-permute-done.58), channel_id=1, source_target_pairs={{0,1},{1,0},{2,3},{3,2},{4,5},{5,4},{6,7},{7,6},{8,9},{9,8},{10,11... | collective-permute-start | bytes 786440 | tf_op jit(solution)/shard_map/ppermute | solution.py:34
  348.3 4.5 %collective-permute-start.77 = (f32[8,128]{1,0:T(8,128)S(1)}, f32[8,128]{1,0:T(8,128)S(1)}, u32[]{:S(2)}, u32[]{:S(2)}) collective-permute-start(f32[8,128]{1,0:T(8,128)S(1)} %add.213), channel_id=1, source_target_pairs={{0,24},{4,28},{8,16},{12,20},{16,8},{20,12},{24,0},{28,4},{1,25},{... | collective-permute-start | bytes 12296 | tf_op jit(solution)/shard_map/ppermute | solution.py:34
  349.1 3.7 collective-permute-start.76
  352.0 12.5 %collective-permute-start.81 = (f32[1,64,128]{2,1,0:T(8,128)S(1)}, f32[1,64,128]{2,1,0:T(8,128)S(1)}, u32[]{:S(2)}, u32[]{:S(2)}) collective-permute-start(f32[1,64,128]{2,1,0:T(8,128)S(1)} %get-tuple-element.236), channel_id=1, source_target_pairs={{0,0},{8,1},{16,2},{24,3},{4,4},{12,5},{20,6},{28,7},{1,8},{9,9},{... | collective-permute-start | bytes 98312 | tf_op jit(solution)/shard_map/ppermute | solution.py:827
  354.3 10.2 %collective-permute-start.80 = (f32[8,128]{1,0:T(8,128)S(1)}, f32[8,128]{1,0:T(8,128)S(1)}, u32[]{:S(2)}, u32[]{:S(2)}) collective-permute-start(f32[8,128]{1,0:T(8,128)S(1)} %get-tuple-element.232.refs_0_), channel_id=1, source_target_pairs={{0,3},{1,2},{2,1},{3,0},{4,7},{5,6},{6,5},{7,4},{8,11},{9,10},{10,... | collective-permute-start | bytes 12296 | tf_op jit(solution)/shard_map/ppermute | solution.py:34
  358.2 6.4 %collective-permute-start.79 = (f32[8,128]{1,0:T(8,128)S(1)}, f32[8,128]{1,0:T(8,128)S(1)}, u32[]{:S(2)}, u32[]{:S(2)}) collective-permute-start(f32[8,128]{1,0:T(8,128)S(1)} %get-tuple-element.232.refs_0_), channel_id=1, source_target_pairs={{0,2},{1,3},{2,0},{3,1},{4,6},{5,7},{6,4},{7,5},{8,10},{9,11},{10,... | collective-permute-start | bytes 12296 | tf_op jit(solution)/shard_map/ppermute | solution.py:34
  358.2 6.4 %collective-permute-start.78 = (f32[8,128]{1,0:T(8,128)S(1)}, f32[8,128]{1,0:T(8,128)S(1)}, u32[]{:S(2)}, u32[]{:S(2)}) collective-permute-start(f32[8,128]{1,0:T(8,128)S(1)} %get-tuple-element.232.refs_0_), channel_id=1, source_target_pairs={{0,1},{1,0},{2,3},{3,2},{4,5},{5,4},{6,7},{7,6},{8,9},{9,8},{10,11... | collective-permute-start | bytes 12296 | tf_op jit(solution)/shard_map/ppermute | solution.py:34
  (145 other events, 1575.1 us)
Sparse Core Ops, SparseCore 0:
  11.6 26.6 all-gather.7
  47.3 25.8 all-gather.5
  80.5 22.5 all-gather.3
  302.8 26.1 reduce-scatter.3
